TPU v7x, 32 devices: a whole 2x2x4 slice. The times are simulated.
32 devices in a mesh: groups: 2 (over x), row: 4 (over y, core), col: 4 (over z).
Axes of the slice: x: 2, y: 2, z: 4, core: 2. Of those that a mesh axis runs over, the one named last changes fastest.
Arguments:
- hamiltonian: bfloat16 [256, 64, 1536], P(('groups', 'row'), None, 'col'), parts along dimension 0, may hold values from -0.15625 to 0.15625
- columns: int32 [256, 24], P(('groups', 'row'), 'col'), parts along dimension 0, may hold values from 0 to 31
- vectors: bfloat16 [16384, 192], P(('groups', 'row', 'col')), parts along dimension 0, may hold values from -40 to 40
- lower: float32 [2], P('groups'), parts along dimension 0, may hold values from -2.4 to -1.6
- upper: float32 [2], P('groups'), parts along dimension 0, may hold values from 0.8 to 1.6
Outputs:
- basis: float32 [16384, 192], P(('groups', 'row', 'col')), parts along dimension 0
There are 2 independent parts, one for each index of `groups`. A program takes and returns all parts, laid end to end along the dimension named above; each array names one. Nothing has to cross between parts.
Inputs may be any that keep to these rules, and one draw needn't show every extreme that they name: Index of a block column among the 32 block columns of the slot's column group.
All inputs are finite; a program needn't handle non-finite values.
Results may differ from a plain program's by a relative error of at most 0.015.
Values may be sent and summed in bfloat16 or wider, within the bound.
No kernel may reach another device: no remote copies, remote signals or barrier semaphores. Data moves between devices by JAX's collectives and lax.ppermute only.
A program may use at most 64 MiB of HBM per device.

v0:
```python
import jax
import jax.numpy as jnp
from jax import lax
from jax.sharding import PartitionSpec as P


def make_term(hamiltonian, columns, source):
    orbitals = hamiltonian.shape[1]
    vector_count = source.shape[1]
    slot_count = columns.shape[1]
    gathered = lax.all_gather(source, "row", axis=0, tiled=True)
    blocks = gathered.reshape(-1, orbitals, vector_count)

    def panel_term(first_row, row_count):
        picked = jnp.take(blocks, columns, axis=0).reshape(
            row_count, slot_count * orbitals, vector_count
        )
        return jnp.einsum("rik,rkn->rin", hamiltonian, picked, preferred_element_type=jnp.float32)

    return panel_term


def per_device(hamiltonian, columns, vectors, lower, upper):
    orbitals = hamiltonian.shape[1]
    vector_count = vectors.shape[1]
    own_blocks = vectors.shape[0] // orbitals
    total_rows = vectors.shape[0] * lax.axis_size("row") * lax.axis_size("col")
    center = (upper[0] + lower[0]) * 0.5
    spread = (upper[0] - lower[0]) * 0.5
    start_vec = vectors.astype(jnp.float32)
    first_term = make_term(hamiltonian, columns, vectors)
    product = (
        lax.psum_scatter(
            first_term(jnp.int32(0), own_blocks * lax.axis_size("col")).astype(jnp.bfloat16),
            "col",
            scatter_dimension=0,
            tiled=True,
        )
        .astype(jnp.float32)
        .reshape(-1, vector_count)
    )
    first_filter = ((product - center * start_vec) / spread).astype(jnp.bfloat16)
    second_term = make_term(hamiltonian, columns, first_filter)
    summed = (
        lax.psum_scatter(
            second_term(jnp.int32(0), own_blocks * lax.axis_size("col")).astype(jnp.bfloat16),
            "col",
            scatter_dimension=0,
            tiled=True,
        )
        .astype(jnp.float32)
        .reshape(-1, vector_count)
    )
    second_filter = (
        2.0 * (summed - center * first_filter.astype(jnp.float32)) / spread - start_vec
    ).astype(jnp.bfloat16)
    local_gram = (
        jnp.dot(second_filter.T, second_filter, preferred_element_type=jnp.float32) / total_rows
    )
    gram = lax.psum(local_gram, ("row", "col"))
    lower_factor = jnp.linalg.cholesky(gram)
    filtered = second_filter.astype(jnp.float32)
    basis = lax.linalg.triangular_solve(
        lower_factor, filtered, left_side=False, lower=True, transpose_a=True
    )
    return basis


def solution(mesh):
    return jax.shard_map(
        per_device,
        mesh=mesh,
        in_specs=(
            P(("groups", "row"), None, "col"),
            P(("groups", "row"), "col"),
            P(("groups", "row", "col"), None),
            P("groups"),
            P("groups"),
        ),
        out_specs=P(("groups", "row", "col"), None),
        check_vma=False,
    )
```

profile of v0, /device:TPU:0, one launch (start us, length us, event | category | flops | bytes accessed | tf_op | source)
XLA Modules:
  0.0 266.3 jit_solution(522905540025122188)
XLA Ops:
  6.5 0.8 compare_select_fusion
  7.3 0.7 compare_and_fusion
  8.0 1.1 copy.16
  9.1 11.5 %all_gather.6 = bf16[2048,192]{1,0:T(8,128)(2,1)S(1)} all-gather(bf16[512,192]{1,0:T(8,128)(2,1)S(1)} %copy.16), channel_id=1, replica_groups=mesh['groups'=2,'row'=4,'col'=4] {'row'}, dimensions={0}, use_global_device_ids=true | all-gather | bytes 983040 | tf_op jit(solution)/shard_map/all_gather | solution.py:11
  20.9 8.0 %gather_fusion = bf16[192,64,192]{2,1,0:T(8,128)(2,1)} fusion(bf16[32,64,192]{2,1,0:T(8,128)(2,1)S(1)} %bitcast.51, s32[1024]{0:T(1024)S(1)} %pad_clamp_fusion), kind=kCustom, calls=%fused_computation.clone | custom fusion | bytes 9437952 | tf_op jit(solution)/shard_map/jit(_take)/gather | solution.py:15
  29.0 3.4 %broadcast_select_fusion = bf16[32,6,64,192]{3,2,1,0:T(8,128)(2,1)S(1)} fusion(bf16[32,6,64,192]{3,2,1,0:T(8,128)(2,1)} %bitcast.55, pred[32,6]{1,0:T(8,128)(4,1)S(1)} %copy.14), kind=kLoop, calls=%fused_computation.2 | loop fusion | flops 2359296 | bytes 9437376 | tf_op jit(solution)/shard_map/jit(_take)/select_n | solution.py:15
  32.4 2.3 fusion
  36.1 26.8 %reduce-scatter.3.cloned.1.call-done = bf16[8,64,192]{2,1,0:T(8,128)(2,1)} async-done(((bf16[32,64,192]{2,1,0:T(8,128)(2,1)}), bf16[8,64,192]{2,1,0:T(8,128)(2,1)}) %reduce-scatter.3.cloned.1.call-update) | async-done | bytes 196624 | tf_op jit(solution)/shard_map/reduce_scatter | solution.py:33
  62.9 1.0 fusion.4
  63.9 10.0 %all_gather.7 = bf16[2048,192]{1,0:T(8,128)(2,1)S(1)} all-gather(bf16[512,192]{1,0:T(8,128)(2,1)S(1)} %fusion.4), channel_id=1, replica_groups=mesh['groups'=2,'row'=4,'col'=4] {'row'}, dimensions={0}, use_global_device_ids=true | all-gather | bytes 983040 | tf_op jit(solution)/shard_map/all_gather | solution.py:11
  73.9 8.0 %gather_fusion.1 = bf16[192,64,192]{2,1,0:T(8,128)(2,1)} fusion(bf16[32,64,192]{2,1,0:T(8,128)(2,1)S(1)} %bitcast.52, s32[1024]{0:T(1024)S(1)} %pad_clamp_fusion), kind=kCustom, calls=%fused_computation.1.clone | custom fusion | bytes 9437952 | tf_op jit(solution)/shard_map/jit(_take)/gather | solution.py:15
  82.0 3.4 %broadcast_select_fusion.1 = bf16[32,6,64,192]{3,2,1,0:T(8,128)(2,1)S(1)} fusion(bf16[32,6,64,192]{3,2,1,0:T(8,128)(2,1)} %bitcast.53, pred[32,6]{1,0:T(8,128)(4,1)S(1)} %copy.14), kind=kLoop, calls=%fused_computation.3 | loop fusion | flops 2359296 | bytes 9437376 | tf_op jit(solution)/shard_map/jit(_take)/select_n | solution.py:15
  85.4 2.3 fusion.1
  87.8 0.2 all-reduce.5.cloned.1.call-start
  88.0 25.4 %reduce-scatter.5.cloned.1.call-done = bf16[8,64,192]{2,1,0:T(8,128)(2,1)} async-done(((bf16[32,64,192]{2,1,0:T(8,128)(2,1)}), bf16[8,64,192]{2,1,0:T(8,128)(2,1)}) %reduce-scatter.5.cloned.1.call-update) | async-done | bytes 196624 | tf_op jit(solution)/shard_map/reduce_scatter | solution.py:45
  113.4 1.2 fusion.5
  114.5 0.9 convolution_multiply_fusion
  115.5 89.7 %all-reduce.5.cloned.1.call-done = f32[192,192]{0,1:T(8,128)} async-done(((f32[192,192]{0,1:T(8,128)}), f32[192,192]{0,1:T(8,128)}) %all-reduce.5.cloned.1.call-update) | async-done | bytes 147472 | tf_op jit(solution)/shard_map/psum | solution.py:60
  205.2 1.0 copy.23
  206.3 1.0 fusion.8
  207.2 11.7 %cholesky.51 = f32[128,128]{1,0:T(8,128)S(1)} custom-call(f32[128,128]{1,0:T(8,128)S(1)} %cholesky.124), custom_call_target="Cholesky" | custom-call | tf_op jit(solution)/shard_map/jit(cholesky)/cholesky | solution.py:61
  219.0 9.8 %custom-call.14 = f32[1,128,128]{1,2,0:T(8,128)S(1)} custom-call(f32[1,128,128]{2,1,0:T(8,128)S(1)} %get-tuple-element.27), custom_call_target="InvertDiagBlocksLowerTriangular" | custom-call | tf_op jit(solution)/shard_map/jit(cholesky)/cholesky | solution.py:61
  228.8 0.2 constant_dynamic-update-slice_fusion.1
  229.0 0.2 convolution_subtract_fusion.1
  229.2 5.8 %cholesky.110 = f32[64,64]{1,0:T(8,128)S(1)} custom-call(f32[64,64]{1,0:T(8,128)S(1)} %convolution_subtract_fusion.1), custom_call_target="Cholesky" | custom-call | tf_op jit(solution)/shard_map/jit(cholesky)/cholesky | solution.py:61
  235.1 0.7 compare_reduce_fusion
  235.8 0.6 compare_reduce_fusion.1
  237.9 19.7 %custom-call.15 = f32[2,128,128]{1,2,0:T(8,128)S(1)} custom-call(f32[2,128,128]{2,1,0:T(8,128)S(1)} %pad_maximum_fusion.1), custom_call_target="InvertDiagBlocksLowerTriangular" | custom-call | tf_op jit(solution)/shard_map/triangular_solve | solution.py:63
  257.6 0.3 fusion.9
  257.9 0.6 convolution_subtract_fusion
  258.5 0.4 fusion.14
  259.0 0.8 pad_maximum_fusion
  (23 shorter events, 0.6 us)
Async XLA Ops:
  6.5 25.9 %copy-start = (bf16[32,64,384]{2,1,0:T(8,128)(2,1)S(1)}, bf16[32,64,384]{2,1,0:T(8,128)(2,1)}, u32[]{:S(2)}) copy-start(bf16[32,64,384]{2,1,0:T(8,128)(2,1)} %param.7) | copy-start | bytes 4718596
  6.5 56.4 %reduce-scatter.3.cloned.1.call-start = ((), (), s32[]{:S(2)}) async-start(), calls=%async_computation.2 | async-start | bytes 1310720 | tf_op jit(solution)/shard_map/reduce_scatter | solution.py:33
  34.7 78.6 %reduce-scatter.5.cloned.1.call-start = ((), (), s32[]{:S(2)}) async-start(), calls=%async_computation.3 | async-start | bytes 1310720 | tf_op jit(solution)/shard_map/reduce_scatter | solution.py:45
  85.4 28.0 %copy-start.1 = (bf16[8,64,192]{2,1,0:T(8,128)(2,1)S(1)}, bf16[8,64,192]{2,1,0:T(8,128)(2,1)}, u32[]{:S(2)}) copy-start(bf16[8,64,192]{2,1,0:T(8,128)(2,1)} %reduce-scatter.3.cloned.1.call-done) | copy-start | bytes 589828
  87.8 117.5 %all-reduce.5.cloned.1.call-start = ((), (), s32[]{:S(2)}) async-start(), calls=%async_computation.4 | async-start | bytes 393216 | tf_op jit(solution)/shard_map/psum | solution.py:60
Sparse Core Ops, SparseCore 0:
  34.9 27.9 reduce-scatter.2
  87.9 25.4 reduce-scatter.4
  116.8 88.3 all-reduce.4
where the time goes:
time: 267 us; the launch traced here: 266 us
  waiting for transfers between devices  142 us (53%)
  other arithmetic  60.9 us (23%)
  blocking collectives  21.5 us (8%)
  local copies, waits for them, and re-layouts  18.5 us (7%)
  between operations  15.9 us (6%)
  matrix products  7.23 us (3%)
    psum x1, waiting for transfers between devices, per_device(): gram = lax.psum(local_gram, ('row', 'col'))  89.7 us
    another operation x7, other arithmetic, per_device(): lower_factor = jnp.linalg.cholesky(gram)  28.8 us
    reduce_scatter x1, waiting for transfers between devices, per_device(): lax.psum_scatter(first_term(jnp.int32(0), own_blocks * lax.axis_size('col...  26.8 us
    reduce_scatter x1, waiting for transfers between devices, per_device(): lax.psum_scatter(second_term(jnp.int32(0), own_blocks * lax.axis_size('co...  25.4 us
    all_gather x2, blocking collectives, make_term(): gathered = lax.all_gather(source, 'row', axis=0, tiled=True)  21.5 us
    another operation x7, other arithmetic, per_device(): lax.linalg.triangular_solve(lower_factor, filtered, left_side=False, lowe...  20.6 us
    gather x2, local copies, waits for them, and re-layouts, panel_term(): jnp.take(blocks, columns, axis=0)  16.1 us
    select_n x3, other arithmetic, panel_term(): jnp.take(blocks, columns, axis=0)  7.65 us
  transfers between devices with their start and end apart: 3, of which 3 were waited for; matrix products, arithmetic and copies ran while one was open for 0% of the time, Pallas kernels for 0%

commit v1 on v0

v1 whole, which is shorter than its diff:
```python
import functools

import jax
import jax.numpy as jnp
from jax import lax
from jax.experimental import pallas as pl
from jax.experimental.pallas import tpu as pltpu
from jax.sharding import PartitionSpec as P

LANES = 128
F32 = jnp.float32
BF16 = jnp.bfloat16
VMEM = pl.BlockSpec(memory_space=pltpu.VMEM)
SMEM = pl.BlockSpec(memory_space=pltpu.SMEM)


def call(kernel, out_shape, in_specs, scratch=(), flops=1000, name=None):
    return pl.pallas_call(
        kernel,
        out_shape=out_shape,
        in_specs=in_specs,
        out_specs=jax.tree.map(lambda _: VMEM, out_shape),
        scratch_shapes=list(scratch),
        compiler_params=pltpu.CompilerParams(vmem_limit_bytes=40 * 1024 * 1024),
        cost_estimate=pl.CostEstimate(flops=flops, bytes_accessed=1000, transcendentals=0),
        name=name,
    )


def swap(x, axis, key):
    count = lax.axis_size(axis)
    return lax.ppermute(x, axis, [(i, i ^ key) for i in range(count)])


def gather_shards(own):
    shards = {0: own}
    bit = lax.axis_size("row") // 2
    while bit:
        for key in list(shards):
            shards[key | bit] = swap(shards[key], "row", bit)
        bit //= 2
    return [shards[key] for key in range(len(shards))]


def pack(vectors):
    half = vectors.shape[0] // 2
    return vectors[:, :LANES], jnp.concatenate(
        [vectors[:half, LANES:], vectors[half:, LANES:]], axis=1
    )


def product_kernel(n_row, n_col, orbitals, place_ref, ids_ref, ham_ref, *refs):
    wide, thin = refs[:n_row], refs[n_row : 2 * n_row]
    wide_out = refs[2 * n_row : 2 * n_row + n_col]
    thin_out = refs[2 * n_row + n_col : 2 * n_row + 2 * n_col]
    all_wide, left, right = refs[2 * n_row + 2 * n_col :]
    rows = wide[0].shape[0]
    half = rows // 2
    own_blocks = rows // orbitals
    slots = ids_ref.shape[1]
    row_at, col_at = place_ref[0], place_ref[1]
    low_lane = lax.broadcasted_iota(jnp.int32, (half, LANES), 1) < LANES // 2
    zero = jnp.zeros((half, LANES), BF16)
    for key in range(n_row):
        base = key * rows
        all_wide[pl.ds(base, rows), :] = wide[key][...]
        packed = thin[key][...]
        turned = jnp.concatenate([packed[:, LANES // 2 :], packed[:, : LANES // 2]], axis=1)
        left[pl.ds(base, half), :] = jnp.where(low_lane, packed, zero)
        right[pl.ds(base, half), :] = jnp.where(low_lane, zero, turned)
        left[pl.ds(base + half, half), :] = jnp.where(low_lane, turned, zero)
        right[pl.ds(base + half, half), :] = jnp.where(low_lane, zero, packed)

    def starts(block_row):
        out = []
        for slot in range(slots):
            index = ids_ref[block_row, slot]
            owner = lax.div(index, own_blocks)
            inner = index - owner * own_blocks
            out.append(pl.multiple_of(((owner ^ row_at) * own_blocks + inner) * orbitals, orbitals))
        return out

    def picked(ref, where):
        return jnp.concatenate([ref[pl.ds(at, orbitals), :] for at in where], axis=0)

    for key in range(n_col):
        first = (key ^ col_at) * own_blocks

        def body(step, carry, key=key, first=first):
            upper, lower = step, step + own_blocks // 2
            up_at, low_at = starts(first + upper), starts(first + lower)
            up_ham, low_ham = ham_ref[first + upper], ham_ref[first + lower]
            dot = functools.partial(jnp.dot, preferred_element_type=F32)
            up_rows = pl.ds(pl.multiple_of(upper * orbitals, orbitals), orbitals)
            low_rows = pl.ds(pl.multiple_of(lower * orbitals, orbitals), orbitals)
            wide_out[key][up_rows, :] = dot(up_ham, picked(all_wide, up_at)).astype(BF16)
            wide_out[key][low_rows, :] = dot(low_ham, picked(all_wide, low_at)).astype(BF16)
            thin_out[key][up_rows, :] = (
                dot(up_ham, picked(left, up_at)) + dot(low_ham, picked(right, low_at))
            ).astype(BF16)
            return carry

        lax.fori_loop(0, own_blocks // 2, body, 0, unroll=True)


def product(place, ids, ham, wide, thin):
    n_row, n_col = len(wide), lax.axis_size("col")
    rows = wide[0].shape[0]
    total = rows * n_row
    wide_shape = jax.ShapeDtypeStruct((rows, LANES), BF16)
    thin_shape = jax.ShapeDtypeStruct((rows // 2, LANES), BF16)
    outs = call(
        functools.partial(product_kernel, n_row, n_col, ham.shape[1]),
        [wide_shape] * n_col + [thin_shape] * n_col,
        [SMEM, SMEM, VMEM] + [VMEM] * (2 * n_row),
        [pltpu.VMEM((total, LANES), BF16)] * 3,
        flops=2 * ham.shape[0] * ham.shape[1] * ham.shape[2] * 256,
        name="product",
    )(place, ids, ham, *wide, *thin)
    return outs[:n_col], outs[n_col:]


def exchange(terms):
    got = {0: terms[0]}
    for key in reversed(range(1, len(terms))):
        got[key] = swap(terms[key], "col", key)
    return [got[key] for key in range(len(terms))]


def ends(lower_ref, upper_ref, shape):
    low = jnp.full(shape, lower_ref[0], F32)
    high = jnp.full(shape, upper_ref[0], F32)
    return (high + low) * 0.5, 1.0 / ((high - low) * 0.5)


def total_of(refs):
    acc = refs[0][...].astype(F32)
    for ref in refs[1:]:
        acc = acc + ref[...].astype(F32)
    return acc


def first_kernel(n_col, lower_ref, upper_ref, wide_v, thin_v, *refs):
    center, scale = ends(lower_ref, upper_ref, (1, LANES))
    parts = ((wide_v, refs[:n_col], refs[2 * n_col]), (thin_v, refs[n_col : 2 * n_col], refs[-1]))
    for start, terms, out in parts:
        out[...] = ((total_of(terms) - center * start[...].astype(F32)) * scale).astype(BF16)


def second_kernel(n_col, rows_all, place_ref, lower_ref, upper_ref, wide_v, thin_v, wide_f, thin_f, *refs):
    wide_terms, thin_terms = refs[:n_col], refs[n_col : 2 * n_col]
    wide_out, thin_out, keep_out, send_out, gram = refs[2 * n_col :]
    center, scale = ends(lower_ref, upper_ref, (1, LANES))
    parts = ((wide_v, wide_f, wide_terms, wide_out), (thin_v, thin_f, thin_terms, thin_out))
    for start, first, terms, out in parts:
        moved = total_of(terms) - center * first[...].astype(F32)
        out[...] = (2.0 * moved * scale - start[...].astype(F32)).astype(BF16)
    wide, thin = wide_out[...], thin_out[...]
    half = thin.shape[0]
    size = LANES // 2

    def cross(a, b):
        return lax.dot_general(a, b, (((0,), (0,)), ((), ())), preferred_element_type=F32)

    inv = 1.0 / rows_all
    aa = cross(wide, wide) * inv
    upper = cross(thin, wide[:half]) * inv
    lower = cross(thin, wide[half:]) * inv
    bb = cross(thin, thin) * inv
    turned = jnp.concatenate([bb[:size, size:], bb[:size, :size]], axis=1)
    low_lane = lax.broadcasted_iota(jnp.int32, (size, LANES), 1) < size
    gram[pl.ds(0, size), :] = jnp.where(low_lane, aa[:size], turned + bb[size:])
    gram[pl.ds(size, size), :] = aa[size:]
    gram[pl.ds(2 * size, size), :] = upper[:size] + lower[size:]
    part = 3 * size // 2
    mine = place_ref[0] & 1
    keep_out[...] = gram[pl.ds(pl.multiple_of(mine * part, 8), part), :]
    send_out[...] = gram[pl.ds(pl.multiple_of((1 - mine) * part, 8), part), :]


def inverse_factor(block, pivots):
    size = block.shape[0]
    tiles = size // 8
    rows = lax.broadcasted_iota(jnp.int32, (8, LANES), 0)
    lanes = lax.broadcasted_iota(jnp.int32, (8, LANES), 1)
    pad = jnp.concatenate([block, jnp.zeros((size, LANES - size), F32)], axis=1)
    a = [
        jnp.where(lanes == rows + (size + 8 * t), 1.0, pad[8 * t : 8 * t + 8]) for t in range(tiles)
    ]
    diag = [jnp.ones((8, LANES), F32) for _ in range(tiles)]
    full = (8, LANES)
    for j in range(0, size, pivots):
        t0, s0 = divmod(j, 8)
        cols = [
            [jnp.broadcast_to(a[t][:, j + k : j + k + 1], full) for t in range(t0, tiles)]
            for k in range(pivots)
        ]
        lines = [jnp.broadcast_to(a[t0][s0 + k : s0 + k + 1, :], full) for k in range(pivots)]
        small = [
            [jnp.broadcast_to(cols[q][0][s0 + k : s0 + k + 1, :], full) for q in range(k + 1)]
            for k in range(pivots)
        ]
        for k in range(pivots):
            d = small[k][k]
            diag[t0] = jnp.where(rows == s0 + k, d, diag[t0])
            r = 1.0 / d
            mult = {}
            for q in range(k + 1, pivots):
                mult[q] = small[q][k] * r
            for q in range(k + 1, pivots):
                lines[q] = lines[q] - mult[q] * lines[k]
                for p in range(k + 1, q + 1):
                    small[q][p] = small[q][p] - mult[q] * small[p][k]
            for i, t in enumerate(range(t0, tiles)):
                x = cols[k][i] * r
                if t == t0:
                    x = jnp.where(rows > s0 + k, x, 0.0)
                for q in range(k + 1, pivots):
                    cols[q][i] = cols[q][i] - cols[k][i] * mult[q]
                a[t] = a[t] - x * lines[k]
    out = jnp.concatenate([a[t] * lax.rsqrt(diag[t]) for t in range(tiles)], axis=0)
    return out[:, size:]


def last_kernel(pivots, place_ref, keep_ref, other_ref, wide_ref, thin_ref, out_ref, gram, factor):
    size = LANES // 2
    part = 3 * size // 2
    mine = place_ref[0] & 1
    gram[pl.ds(pl.multiple_of(mine * part, 8), part), :] = keep_ref[...]
    gram[pl.ds(pl.multiple_of((1 - mine) * part, 8), part), :] = other_ref[...]
    dot = functools.partial(
        jnp.dot, precision=lax.Precision.HIGHEST, preferred_element_type=F32
    )

    def dot_t(a, b):
        return lax.dot_general(
            a,
            b,
            (((1,), (1,)), ((), ())),
            precision=lax.Precision.HIGHEST,
            preferred_element_type=F32,
        )

    g00 = gram[pl.ds(0, size), :][:, :size]
    g22 = gram[pl.ds(0, size), :][:, size:]
    strip = gram[pl.ds(size, 2 * size), :]
    x0 = inverse_factor(g00, pivots)
    l_strip = dot_t(strip[:, :size], x0)
    rest = strip[:, size:] - dot_t(l_strip, l_strip[:size])
    x1 = inverse_factor(rest[:size], pivots)
    l10, l20 = l_strip[:size], l_strip[size:]
    l21 = dot_t(rest[size:], x1)
    x2 = inverse_factor(g22 - dot_t(l20, l20) - dot_t(l21, l21), pivots)
    n10 = -dot(x1, dot(l10, x0))
    n20 = -dot(x2, dot(l20, x0) + dot(l21, n10))
    n21 = -dot(x2, dot(l21, x1))
    zero = jnp.zeros((size, size), F32)
    factor[pl.ds(0, size), :] = jnp.concatenate([x0, zero], axis=1)
    factor[pl.ds(size, size), :] = jnp.concatenate([n10, x1], axis=1)
    factor[pl.ds(2 * size, size), :] = jnp.concatenate([n20, n21], axis=1)

    def apply(mat, vec):
        high = mat.astype(BF16)
        low = (mat - high.astype(F32)).astype(BF16)
        con = (((1,), (1,)), ((), ()))
        return lax.dot_general(high, vec, con, preferred_element_type=F32) + lax.dot_general(
            low, vec, con, preferred_element_type=F32
        )

    wide, thin = wide_ref[...], thin_ref[...]
    half = thin.shape[0]
    main = apply(factor[...], wide)
    out_ref[pl.ds(0, 2 * size), :] = main[: 2 * size]
    tail = jnp.concatenate(
        [
            apply(jnp.concatenate([x2, zero], axis=1), thin),
            apply(jnp.concatenate([zero, x2], axis=1), thin),
        ],
        axis=1,
    )
    out_ref[pl.ds(2 * size, size), :] = main[2 * size :] + tail


def sum_all(keep, send):
    acc = keep + swap(send, "row", 1)
    bit = 2
    while bit < lax.axis_size("row"):
        acc = acc + swap(acc, "row", bit)
        bit *= 2
    got = [swap(acc, "col", key) for key in range(1, lax.axis_size("col"))]
    for x in got:
        acc = acc + x
    return acc, swap(acc, "row", 1)


def per_device(hamiltonian, columns, vectors, lower, upper):
    rows = vectors.shape[0]
    n_col = lax.axis_size("col")
    place = jnp.stack([lax.axis_index("row"), lax.axis_index("col")]).astype(jnp.int32)
    wide_shape = jax.ShapeDtypeStruct((rows, LANES), BF16)
    thin_shape = jax.ShapeDtypeStruct((rows // 2, LANES), BF16)
    half_gram = jax.ShapeDtypeStruct((96, LANES), F32)

    def apply(wide, thin):
        terms = product(place, columns, hamiltonian, gather_shards(wide), gather_shards(thin))
        return [*exchange(terms[0]), *exchange(terms[1])]

    wide_v, thin_v = pack(vectors)
    terms = apply(wide_v, thin_v)
    wide_f, thin_f = call(
        functools.partial(first_kernel, n_col),
        [wide_shape, thin_shape],
        [SMEM, SMEM] + [VMEM] * (2 + 2 * n_col),
        name="first_filter",
    )(lower, upper, wide_v, thin_v, *terms)
    terms = apply(wide_f, thin_f)
    rows_all = rows * n_col * lax.axis_size("row")
    wide_s, thin_s, keep, send = call(
        functools.partial(second_kernel, n_col, rows_all),
        [wide_shape, thin_shape, half_gram, half_gram],
        [SMEM, SMEM, SMEM] + [VMEM] * (4 + 2 * n_col),
        [pltpu.VMEM((192, LANES), F32)],
        name="second_filter",
    )(place, lower, upper, wide_v, thin_v, wide_f, thin_f, *terms)
    keep, other = sum_all(keep, send)
    basis = call(
        functools.partial(last_kernel, 2),
        jax.ShapeDtypeStruct((192, rows), F32),
        [SMEM] + [VMEM] * 4,
        [pltpu.VMEM((192, LANES), F32), pltpu.VMEM((192, LANES), F32)],
        name="orthonormalize",
    )(place, keep, other, wide_s, thin_s)
    return basis.T


def solution(mesh):
    return jax.shard_map(
        per_device,
        mesh=mesh,
        in_specs=(
            P(("groups", "row"), None, "col"),
            P(("groups", "row"), "col"),
            P(("groups", "row", "col"), None),
            P("groups"),
            P("groups"),
        ),
        out_specs=P(("groups", "row", "col"), None),
        check_vma=False,
    )
```

time: 267 us -> 102 us (0.38)
  waiting for transfers between devices: 142 us -> 42 us
  other arithmetic: 60.9 us -> 0.2 us
  starting transfers between devices: 0.27 us -> 30.2 us
  Pallas kernels: 0 us -> 23.5 us
  blocking collectives: 21.5 us -> 0 us
  between operations: 15.9 us -> 1.44 us
  local copies, waits for them, and re-layouts: 18.5 us -> 4.22 us
  matrix products: 7.23 us -> 0 us
    psum x1 -> x0, waiting for transfers between devices: 89.7 us -> none  [per_device(): gram = lax.psum(local_gram, ('row', 'col'))]
    reduce_scatter x2 -> x0, waiting for transfers between devices: 52.2 us -> none  [the longest x1 26.8 us: per_device(): lax.psum_scatter(first_term(jnp.int32(0), own_blocks * lax.axis_size('col...]
    another operation x14 -> x1, other arithmetic: 49.4 us -> 0.07 us  [per_device(): jnp.stack([lax.axis_index('row'), lax.axis_index('col')]).astype(jnp.int32)]
    ppermute x0 -> x30, waiting for transfers between devices: none -> 42 us  [swap(): return lax.ppermute(x, axis, [(i, i ^ key) for i in range(count)])]
    ppermute x0 -> x30, starting transfers between devices: none -> 30.2 us  [swap(): return lax.ppermute(x, axis, [(i, i ^ key) for i in range(count)])]
    pallas_call x0 -> x5, Pallas kernels: none -> 23.5 us  [the longest x1 17.4 us: per_device(): call(functools.partial(last_kernel, 2), jax.ShapeDtypeStruct((192, rows),...]
    all_gather x2 -> x0, blocking collectives: 21.5 us -> none  [make_term(): gathered = lax.all_gather(source, 'row', axis=0, tiled=True)]
    gather x2 -> x0, local copies, waits for them, and re-layouts: 16.1 us -> none  [panel_term(): jnp.take(blocks, columns, axis=0)]
  transfers between devices with their start and end apart: 3 -> 30, of which waited for: 3 -> 14; matrix products, arithmetic and copies ran while one was open for 0% -> 2% of each run, Pallas kernels for 0% -> 0%
where the time goes in v1:
time: 102 us
  waiting for transfers between devices  42 us (41%)
  starting transfers between devices  30.2 us (30%)
  Pallas kernels  23.5 us (23%)
  local copies, waits for them, and re-layouts  4.22 us (4%)
  between operations  1.44 us (1%)
    ppermute x30, waiting for transfers between devices, swap(): return lax.ppermute(x, axis, [(i, i ^ key) for i in range(count)])  42 us
    ppermute x30, starting transfers between devices, swap(): return lax.ppermute(x, axis, [(i, i ^ key) for i in range(count)])  30.2 us
    pallas_call x1, Pallas kernels, per_device(): call(functools.partial(last_kernel, 2), jax.ShapeDtypeStruct((192, rows),...  17.4 us
    pallas_call x2, Pallas kernels, product(): call(functools.partial(product_kernel, n_row, n_col, ham.shape[1]), [wide...  4.87 us
    unnamed x8, local copies, waits for them, and re-layouts  2.53 us
  transfers between devices with their start and end apart: 30, of which 14 were waited for; matrix products, arithmetic and copies ran while one was open for 2% of the time, Pallas kernels for 0%

profile of v1, /device:TPU:0, one launch (start us, length us, event | category | flops | bytes accessed | tf_op | source)
XLA Modules:
  0.0 101.6 jit_solution(15065411747488278730)
XLA Ops:
  0.0 0.9 slice.9
  1.0 3.0 %collective-permute-start.1 = (bf16[512,128]{1,0:T(8,128)(2,1)S(1)}, bf16[512,128]{1,0:T(8,128)(2,1)S(1)}, u32[]{:S(2)}, u32[]{:S(2)}) collective-permute-start(bf16[512,128]{1,0:T(8,128)(2,1)S(1)} %copy.11.refs_0_.wide_v), channel_id=1, source_target_pairs={{0,8},{4,12},{8,0},{12,4},{1,9},{5,13},{9,1},{13,5},{2,10},{6,14},... | collective-permute-start | bytes 393224 | tf_op jit(solution)/shard_map/ppermute | solution.py:32
  4.1 0.8 fusion
  5.4 2.3 %collective-permute-done.1.refs_2_ = bf16[512,128]{1,0:T(8,128)(2,1)S(1)} collective-permute-done((bf16[512,128]{1,0:T(8,128)(2,1)S(1)}, bf16[512,128]{1,0:T(8,128)(2,1)S(1)}, u32[]{:S(2)}, u32[]{:S(2)}) %collective-permute-start.1) | collective-permute-done | bytes 131104 | tf_op jit(solution)/shard_map/ppermute | solution.py:32
  9.6 1.2 %collective-permute-done.5.refs_7_ = bf16[256,128]{1,0:T(8,128)(2,1)S(1)} collective-permute-done((bf16[256,128]{1,0:T(8,128)(2,1)S(1)}, bf16[256,128]{1,0:T(8,128)(2,1)S(1)}, u32[]{:S(2)}, u32[]{:S(2)}) %collective-permute-start.5) | collective-permute-done | bytes 65568 | tf_op jit(solution)/shard_map/ppermute | solution.py:32
  10.8 1.4 %copy-done = bf16[32,64,384]{2,1,0:T(8,128)(2,1)S(1)} copy-done((bf16[32,64,384]{2,1,0:T(8,128)(2,1)S(1)}, bf16[32,64,384]{2,1,0:T(8,128)(2,1)}, u32[]{:S(2)}) %copy-start) | copy-done | bytes 1572888
  12.2 2.4 %product.2 = (bf16[512,128]{1,0:T(8,128)(2,1)S(1)}, bf16[512,128]{1,0:T(8,128)(2,1)S(1)}, bf16[512,128]{1,0:T(8,128)(2,1)S(1)}, bf16[512,128]{1,0:T(8,128)(2,1)S...) custom-call(s32[2]{0:T(128)S(1)} %pad_add_fusion.place_ref, ...), custom_call_target="tpu_custom_call" | custom-call | flops 402653184 | bytes 1000 | tf_op jit(solution)/shard_map/product/pallas_call | solution.py:112
  14.6 1.6 %collective-permute-start.9 = (bf16[256,128]{1,0:T(8,128)(2,1)S(1)}, bf16[256,128]{1,0:T(8,128)(2,1)S(1)}, u32[]{:S(2)}, u32[]{:S(2)}) collective-permute-start(bf16[256,128]{1,0:T(8,128)(2,1)S(1)} %get-tuple-element.32), channel_id=1, source_target_pairs={{0,1},{1,0},{2,3},{3,2},{4,5},{5,4},{6,7},{7,6},{8,9},{9,8},{10,11... | collective-permute-start | bytes 196616 | tf_op jit(solution)/shard_map/ppermute | solution.py:32
  16.7 2.6 %collective-permute-start.7 = (bf16[512,128]{1,0:T(8,128)(2,1)S(1)}, bf16[512,128]{1,0:T(8,128)(2,1)S(1)}, u32[]{:S(2)}, u32[]{:S(2)}) collective-permute-start(bf16[512,128]{1,0:T(8,128)(2,1)S(1)} %get-tuple-element.29), channel_id=1, source_target_pairs={{0,2},{1,3},{2,0},{3,1},{4,6},{5,7},{6,4},{7,5},{8,10},{9,11},{10,... | collective-permute-start | bytes 393224 | tf_op jit(solution)/shard_map/ppermute | solution.py:32
  19.3 1.3 %collective-permute-start.8 = (bf16[512,128]{1,0:T(8,128)(2,1)S(1)}, bf16[512,128]{1,0:T(8,128)(2,1)S(1)}, u32[]{:S(2)}, u32[]{:S(2)}) collective-permute-start(bf16[512,128]{1,0:T(8,128)(2,1)S(1)} %get-tuple-element.30), channel_id=1, source_target_pairs={{0,3},{1,2},{2,1},{3,0},{4,7},{5,6},{6,5},{7,4},{8,11},{9,10},{10,... | collective-permute-start | bytes 393224 | tf_op jit(solution)/shard_map/ppermute | solution.py:32
  20.7 1.7 %collective-permute-start.10 = (bf16[256,128]{1,0:T(8,128)(2,1)S(1)}, bf16[256,128]{1,0:T(8,128)(2,1)S(1)}, u32[]{:S(2)}, u32[]{:S(2)}) collective-permute-start(bf16[256,128]{1,0:T(8,128)(2,1)S(1)} %get-tuple-element.33), channel_id=1, source_target_pairs={{0,2},{1,3},{2,0},{3,1},{4,6},{5,7},{6,4},{7,5},{8,10},{9,11},{10,... | collective-permute-start | bytes 196616 | tf_op jit(solution)/shard_map/ppermute | solution.py:32
  22.4 0.9 collective-permute-start.11
  24.6 11.4 %collective-permute-done.10.refs_6_ = bf16[256,128]{1,0:T(8,128)(2,1)S(1)} collective-permute-done((bf16[256,128]{1,0:T(8,128)(2,1)S(1)}, bf16[256,128]{1,0:T(8,128)(2,1)S(1)}, u32[]{:S(2)}, u32[]{:S(2)}) %collective-permute-start.10) | collective-permute-done | bytes 65568 | tf_op jit(solution)/shard_map/ppermute | solution.py:32
  36.2 1.8 %collective-permute-start.13 = (bf16[512,128]{1,0:T(8,128)(2,1)S(1)}, bf16[512,128]{1,0:T(8,128)(2,1)S(1)}, u32[]{:S(2)}, u32[]{:S(2)}) collective-permute-start(bf16[512,128]{1,0:T(8,128)(2,1)S(1)} %get-tuple-element.35.refs_0_.wide_f), channel_id=1, source_target_pairs={{0,8},{4,12},{8,0},{12,4},{1,9},{5,13},{9,1},{13,5},{2,10},{6,14},... | collective-permute-start | bytes 393224 | tf_op jit(solution)/shard_map/ppermute | solution.py:32
  38.3 2.9 %collective-permute-done.13.refs_2_ = bf16[512,128]{1,0:T(8,128)(2,1)S(1)} collective-permute-done((bf16[512,128]{1,0:T(8,128)(2,1)S(1)}, bf16[512,128]{1,0:T(8,128)(2,1)S(1)}, u32[]{:S(2)}, u32[]{:S(2)}) %collective-permute-start.13) | collective-permute-done | bytes 131104 | tf_op jit(solution)/shard_map/ppermute | solution.py:32
  42.7 0.9 collective-permute-done.17.refs_7_
  43.6 2.4 %product.3 = (bf16[512,128]{1,0:T(8,128)(2,1)S(1)}, bf16[512,128]{1,0:T(8,128)(2,1)S(1)}, bf16[512,128]{1,0:T(8,128)(2,1)S(1)}, bf16[512,128]{1,0:T(8,128)(2,1)S...) custom-call(s32[2]{0:T(128)S(1)} %pad_add_fusion.place_ref, ...), custom_call_target="tpu_custom_call" | custom-call | flops 402653184 | bytes 1000 | tf_op jit(solution)/shard_map/product/pallas_call | solution.py:112
  46.0 1.5 %collective-permute-start.21 = (bf16[256,128]{1,0:T(8,128)(2,1)S(1)}, bf16[256,128]{1,0:T(8,128)(2,1)S(1)}, u32[]{:S(2)}, u32[]{:S(2)}) collective-permute-start(bf16[256,128]{1,0:T(8,128)(2,1)S(1)} %get-tuple-element.42), channel_id=1, source_target_pairs={{0,1},{1,0},{2,3},{3,2},{4,5},{5,4},{6,7},{7,6},{8,9},{9,8},{10,11... | collective-permute-start | bytes 196616 | tf_op jit(solution)/shard_map/ppermute | solution.py:32
  48.1 3.3 %collective-permute-start.19 = (bf16[512,128]{1,0:T(8,128)(2,1)S(1)}, bf16[512,128]{1,0:T(8,128)(2,1)S(1)}, u32[]{:S(2)}, u32[]{:S(2)}) collective-permute-start(bf16[512,128]{1,0:T(8,128)(2,1)S(1)} %get-tuple-element.39), channel_id=1, source_target_pairs={{0,2},{1,3},{2,0},{3,1},{4,6},{5,7},{6,4},{7,5},{8,10},{9,11},{10,... | collective-permute-start | bytes 393224 | tf_op jit(solution)/shard_map/ppermute | solution.py:32
  51.9 1.8 %collective-permute-start.22 = (bf16[256,128]{1,0:T(8,128)(2,1)S(1)}, bf16[256,128]{1,0:T(8,128)(2,1)S(1)}, u32[]{:S(2)}, u32[]{:S(2)}) collective-permute-start(bf16[256,128]{1,0:T(8,128)(2,1)S(1)} %get-tuple-element.43), channel_id=1, source_target_pairs={{0,2},{1,3},{2,0},{3,1},{4,6},{5,7},{6,4},{7,5},{8,10},{9,11},{10,... | collective-permute-start | bytes 196616 | tf_op jit(solution)/shard_map/ppermute | solution.py:32
  53.7 1.6 %collective-permute-start.23 = (bf16[256,128]{1,0:T(8,128)(2,1)S(1)}, bf16[256,128]{1,0:T(8,128)(2,1)S(1)}, u32[]{:S(2)}, u32[]{:S(2)}) collective-permute-start(bf16[256,128]{1,0:T(8,128)(2,1)S(1)} %get-tuple-element.44), channel_id=1, source_target_pairs={{0,3},{1,2},{2,1},{3,0},{4,7},{5,6},{6,5},{7,4},{8,11},{9,10},{10,... | collective-permute-start | bytes 196616 | tf_op jit(solution)/shard_map/ppermute | solution.py:32
  55.3 12.8 %collective-permute-done.22.refs_6_ = bf16[256,128]{1,0:T(8,128)(2,1)S(1)} collective-permute-done((bf16[256,128]{1,0:T(8,128)(2,1)S(1)}, bf16[256,128]{1,0:T(8,128)(2,1)S(1)}, u32[]{:S(2)}, u32[]{:S(2)}) %collective-permute-start.22) | collective-permute-done | bytes 65568 | tf_op jit(solution)/shard_map/ppermute | solution.py:32
  68.1 1.1 %second_filter.1 = (bf16[512,128]{1,0:T(8,128)(2,1)S(1)}, bf16[256,128]{1,0:T(8,128)(2,1)S(1)}, f32[96,128]{1,0:T(8,128)S(1)}, f32[96,128]{1,0:T(8,128)S(1)}) custom-call(s32[2]{0:T(128)S(1)} %pad_add_fusion.place_ref, f32[1]{0:T(128)S(6)} %copy.14.lower_ref, f32[1]{0:T(128)S(6)} %copy.15.upper_ref, bf16[512,128]{1,0:T(8,128)(2,1)S(1)} %copy.11.refs_0_.wide_v, ...), custom_call_target="tpu_custom_call" | custom-call | flops 1000 | bytes 1000 | tf_op jit(solution)/shard_map/second_filter/pallas_call | solution.py:318
  69.3 1.2 %collective-permute-done.24 = f32[96,128]{1,0:T(8,128)S(1)} collective-permute-done((f32[96,128]{1,0:T(8,128)S(1)}, f32[96,128]{1,0:T(8,128)S(1)}, u32[]{:S(2)}, u32[]{:S(2)}) %collective-permute-start.24) | collective-permute-done | bytes 49184 | tf_op jit(solution)/shard_map/ppermute | solution.py:32
  70.5 1.5 %collective-permute-start.25 = (f32[96,128]{1,0:T(8,128)S(1)}, f32[96,128]{1,0:T(8,128)S(1)}, u32[]{:S(2)}, u32[]{:S(2)}) collective-permute-start(f32[96,128]{1,0:T(8,128)S(1)} %add.15), channel_id=1, source_target_pairs={{0,8},{4,12},{8,0},{12,4},{1,9},{5,13},{9,1},{13,5},{2,10},{6,14},... | collective-permute-start | bytes 147464 | tf_op jit(solution)/shard_map/ppermute | solution.py:32
  72.0 2.7 %collective-permute-done.25 = f32[96,128]{1,0:T(8,128)S(1)} collective-permute-done((f32[96,128]{1,0:T(8,128)S(1)}, f32[96,128]{1,0:T(8,128)S(1)}, u32[]{:S(2)}, u32[]{:S(2)}) %collective-permute-start.25) | collective-permute-done | bytes 49184 | tf_op jit(solution)/shard_map/ppermute | solution.py:32
  74.7 2.9 %collective-permute-start.28 = (f32[96,128]{1,0:T(8,128)S(1)}, f32[96,128]{1,0:T(8,128)S(1)}, u32[]{:S(2)}, u32[]{:S(2)}) collective-permute-start(f32[96,128]{1,0:T(8,128)S(1)} %add.16), channel_id=1, source_target_pairs={{0,3},{1,2},{2,1},{3,0},{4,7},{5,6},{6,5},{7,4},{8,11},{9,10},{10,... | collective-permute-start | bytes 147464 | tf_op jit(solution)/shard_map/ppermute | solution.py:32
  77.5 1.6 %collective-permute-start.26 = (f32[96,128]{1,0:T(8,128)S(1)}, f32[96,128]{1,0:T(8,128)S(1)}, u32[]{:S(2)}, u32[]{:S(2)}) collective-permute-start(f32[96,128]{1,0:T(8,128)S(1)} %add.16), channel_id=1, source_target_pairs={{0,1},{1,0},{2,3},{3,2},{4,5},{5,4},{6,7},{7,6},{8,9},{9,8},{10,11... | collective-permute-start | bytes 147464 | tf_op jit(solution)/shard_map/ppermute | solution.py:32
  79.1 1.5 %collective-permute-done.28 = f32[96,128]{1,0:T(8,128)S(1)} collective-permute-done((f32[96,128]{1,0:T(8,128)S(1)}, f32[96,128]{1,0:T(8,128)S(1)}, u32[]{:S(2)}, u32[]{:S(2)}) %collective-permute-start.28) | collective-permute-done | bytes 49184 | tf_op jit(solution)/shard_map/ppermute | solution.py:32
  80.6 2.2 %collective-permute-done.27 = f32[96,128]{1,0:T(8,128)S(1)} collective-permute-done((f32[96,128]{1,0:T(8,128)S(1)}, f32[96,128]{1,0:T(8,128)S(1)}, u32[]{:S(2)}, u32[]{:S(2)}) %collective-permute-start.27) | collective-permute-done | bytes 49184 | tf_op jit(solution)/shard_map/ppermute | solution.py:32
  82.9 1.2 %collective-permute-done.29.other_ref = f32[96,128]{1,0:T(8,128)S(1)} collective-permute-done((f32[96,128]{1,0:T(8,128)S(1)}, f32[96,128]{1,0:T(8,128)S(1)}, u32[]{:S(2)}, u32[]{:S(2)}) %collective-permute-start.29) | collective-permute-done | bytes 49184 | tf_op jit(solution)/shard_map/ppermute | solution.py:32
  84.1 17.4 %orthonormalize.1 = f32[192,512]{1,0:T(8,128)} custom-call(s32[2]{0:T(128)S(1)} %pad_add_fusion.place_ref, f32[96,128]{1,0:T(8,128)S(1)} %add_add_fusion.keep_ref, f32[96,128]{1,0:T(8,128)S(1)} %collective-permute-done.29.other_ref, bf16[512,128]{1,0:T(8,128)(2,1)S(1)} %get-tuple-element.47.wide_ref, bf16[256,128]{1,0:T(8,128)(2,1)S(1)} %get-tuple-element.48.thin_ref), custom_call_target="tpu_custom_call" | custom-call | flops 1000 | bytes 1000 | tf_op jit(solution)/shard_map/orthonormalize/pallas_call | solution.py:326
  (48 shorter events, 6.1 us)
Async XLA Ops:
  1.0 6.6 %collective-permute-start.1 = (bf16[512,128]{1,0:T(8,128)(2,1)S(1)}, bf16[512,128]{1,0:T(8,128)(2,1)S(1)}, u32[]{:S(2)}, u32[]{:S(2)}) collective-permute-start(bf16[512,128]{1,0:T(8,128)(2,1)S(1)} %copy.11.refs_0_.wide_v), channel_id=1, source_target_pairs={{0,8},{4,12},{8,0},{12,4},{1,9},{5,13},{9,1},{13,5},{2,10},{6,14},... | collective-permute-start | bytes 393224 | tf_op jit(solution)/shard_map/ppermute | solution.py:32
  5.2 4.3 %collective-permute-start.4 = (bf16[256,128]{1,0:T(8,128)(2,1)S(1)}, bf16[256,128]{1,0:T(8,128)(2,1)S(1)}, u32[]{:S(2)}, u32[]{:S(2)}) collective-permute-start(bf16[256,128]{1,0:T(8,128)(2,1)S(1)} %pad_maximum_fusion.refs_4_.thin_v), channel_id=1, source_target_pairs={{0,8},{4,12},{8,0},{12,4},{1,9},{5,13},{9,1},{13,5},{2,10},{6,14},... | collective-permute-start | bytes 196616 | tf_op jit(solution)/shard_map/ppermute | solution.py:32
  5.3 5.5 %collective-permute-start = (bf16[512,128]{1,0:T(8,128)(2,1)S(1)}, bf16[512,128]{1,0:T(8,128)(2,1)S(1)}, u32[]{:S(2)}, u32[]{:S(2)}) collective-permute-start(bf16[512,128]{1,0:T(8,128)(2,1)S(1)} %copy.11.refs_0_.wide_v), channel_id=1, source_target_pairs={{0,4},{4,0},{8,12},{12,8},{1,5},{5,1},{9,13},{13,9},{2,6},{6,2},{1... | collective-permute-start | bytes 393224 | tf_op jit(solution)/shard_map/ppermute | solution.py:32
  7.7 3.1 %collective-permute-start.2 = (bf16[512,128]{1,0:T(8,128)(2,1)S(1)}, bf16[512,128]{1,0:T(8,128)(2,1)S(1)}, u32[]{:S(2)}, u32[]{:S(2)}) collective-permute-start(bf16[512,128]{1,0:T(8,128)(2,1)S(1)} %collective-permute-done.1.refs_2_), channel_id=1, source_target_pairs={{0,4},{4,0},{8,12},{12,8},{1,5},{5,1},{9,13},{13,9},{2,6},{6,2},{1... | collective-permute-start | bytes 393224 | tf_op jit(solution)/shard_map/ppermute | solution.py:32
  7.7 1.9 %collective-permute-start.3 = (bf16[256,128]{1,0:T(8,128)(2,1)S(1)}, bf16[256,128]{1,0:T(8,128)(2,1)S(1)}, u32[]{:S(2)}, u32[]{:S(2)}) collective-permute-start(bf16[256,128]{1,0:T(8,128)(2,1)S(1)} %pad_maximum_fusion.refs_4_.thin_v), channel_id=1, source_target_pairs={{0,4},{4,0},{8,12},{12,8},{1,5},{5,1},{9,13},{13,9},{2,6},{6,2},{1... | collective-permute-start | bytes 196616 | tf_op jit(solution)/shard_map/ppermute | solution.py:32
  9.5 1.3 %collective-permute-start.5 = (bf16[256,128]{1,0:T(8,128)(2,1)S(1)}, bf16[256,128]{1,0:T(8,128)(2,1)S(1)}, u32[]{:S(2)}, u32[]{:S(2)}) collective-permute-start(bf16[256,128]{1,0:T(8,128)(2,1)S(1)} %collective-permute-done.4.refs_6_), channel_id=1, source_target_pairs={{0,4},{4,0},{8,12},{12,8},{1,5},{5,1},{9,13},{13,9},{2,6},{6,2},{1... | collective-permute-start | bytes 196616 | tf_op jit(solution)/shard_map/ppermute | solution.py:32
  10.8 1.4 %copy-start = (bf16[32,64,384]{2,1,0:T(8,128)(2,1)S(1)}, bf16[32,64,384]{2,1,0:T(8,128)(2,1)}, u32[]{:S(2)}) copy-start(bf16[32,64,384]{2,1,0:T(8,128)(2,1)} %ham_ref.3) | copy-start | bytes 4718596
  12.2 31.4 %copy-start.1 = (bf16[32,64,384]{2,1,0:T(8,128)(2,1)S(1)}, bf16[32,64,384]{2,1,0:T(8,128)(2,1)}, u32[]{:S(2)}) copy-start(bf16[32,64,384]{2,1,0:T(8,128)(2,1)} %ham_ref.3) | copy-start | bytes 4718596
  14.6 7.7 %collective-permute-start.9 = (bf16[256,128]{1,0:T(8,128)(2,1)S(1)}, bf16[256,128]{1,0:T(8,128)(2,1)S(1)}, u32[]{:S(2)}, u32[]{:S(2)}) collective-permute-start(bf16[256,128]{1,0:T(8,128)(2,1)S(1)} %get-tuple-element.32), channel_id=1, source_target_pairs={{0,1},{1,0},{2,3},{3,2},{4,5},{5,4},{6,7},{7,6},{8,9},{9,8},{10,11... | collective-permute-start | bytes 196616 | tf_op jit(solution)/shard_map/ppermute | solution.py:32
  16.3 19.7 %collective-permute-start.6 = (bf16[512,128]{1,0:T(8,128)(2,1)S(1)}, bf16[512,128]{1,0:T(8,128)(2,1)S(1)}, u32[]{:S(2)}, u32[]{:S(2)}) collective-permute-start(bf16[512,128]{1,0:T(8,128)(2,1)S(1)} %get-tuple-element.28), channel_id=1, source_target_pairs={{0,1},{1,0},{2,3},{3,2},{4,5},{5,4},{6,7},{7,6},{8,9},{9,8},{10,11... | collective-permute-start | bytes 393224 | tf_op jit(solution)/shard_map/ppermute | solution.py:32
  16.7 19.3 %collective-permute-start.7 = (bf16[512,128]{1,0:T(8,128)(2,1)S(1)}, bf16[512,128]{1,0:T(8,128)(2,1)S(1)}, u32[]{:S(2)}, u32[]{:S(2)}) collective-permute-start(bf16[512,128]{1,0:T(8,128)(2,1)S(1)} %get-tuple-element.29), channel_id=1, source_target_pairs={{0,2},{1,3},{2,0},{3,1},{4,6},{5,7},{6,4},{7,5},{8,10},{9,11},{10,... | collective-permute-start | bytes 393224 | tf_op jit(solution)/shard_map/ppermute | solution.py:32
  19.3 16.7 %collective-permute-start.8 = (bf16[512,128]{1,0:T(8,128)(2,1)S(1)}, bf16[512,128]{1,0:T(8,128)(2,1)S(1)}, u32[]{:S(2)}, u32[]{:S(2)}) collective-permute-start(bf16[512,128]{1,0:T(8,128)(2,1)S(1)} %get-tuple-element.30), channel_id=1, source_target_pairs={{0,3},{1,2},{2,1},{3,0},{4,7},{5,6},{6,5},{7,4},{8,11},{9,10},{10,... | collective-permute-start | bytes 393224 | tf_op jit(solution)/shard_map/ppermute | solution.py:32
  20.7 15.3 %collective-permute-start.10 = (bf16[256,128]{1,0:T(8,128)(2,1)S(1)}, bf16[256,128]{1,0:T(8,128)(2,1)S(1)}, u32[]{:S(2)}, u32[]{:S(2)}) collective-permute-start(bf16[256,128]{1,0:T(8,128)(2,1)S(1)} %get-tuple-element.33), channel_id=1, source_target_pairs={{0,2},{1,3},{2,0},{3,1},{4,6},{5,7},{6,4},{7,5},{8,10},{9,11},{10,... | collective-permute-start | bytes 196616 | tf_op jit(solution)/shard_map/ppermute | solution.py:32
  22.4 13.7 %collective-permute-start.11 = (bf16[256,128]{1,0:T(8,128)(2,1)S(1)}, bf16[256,128]{1,0:T(8,128)(2,1)S(1)}, u32[]{:S(2)}, u32[]{:S(2)}) collective-permute-start(bf16[256,128]{1,0:T(8,128)(2,1)S(1)} %get-tuple-element.34), channel_id=1, source_target_pairs={{0,3},{1,2},{2,1},{3,0},{4,7},{5,6},{6,5},{7,4},{8,11},{9,10},{10,... | collective-permute-start | bytes 196616 | tf_op jit(solution)/shard_map/ppermute | solution.py:32
  36.2 5.0 %collective-permute-start.13 = (bf16[512,128]{1,0:T(8,128)(2,1)S(1)}, bf16[512,128]{1,0:T(8,128)(2,1)S(1)}, u32[]{:S(2)}, u32[]{:S(2)}) collective-permute-start(bf16[512,128]{1,0:T(8,128)(2,1)S(1)} %get-tuple-element.35.refs_0_.wide_f), channel_id=1, source_target_pairs={{0,8},{4,12},{8,0},{12,4},{1,9},{5,13},{9,1},{13,5},{2,10},{6,14},... | collective-permute-start | bytes 393224 | tf_op jit(solution)/shard_map/ppermute | solution.py:32
  38.0 4.3 %collective-permute-start.16 = (bf16[256,128]{1,0:T(8,128)(2,1)S(1)}, bf16[256,128]{1,0:T(8,128)(2,1)S(1)}, u32[]{:S(2)}, u32[]{:S(2)}) collective-permute-start(bf16[256,128]{1,0:T(8,128)(2,1)S(1)} %get-tuple-element.36.refs_4_.thin_f), channel_id=1, source_target_pairs={{0,8},{4,12},{8,0},{12,4},{1,9},{5,13},{9,1},{13,5},{2,10},{6,14},... | collective-permute-start | bytes 196616 | tf_op jit(solution)/shard_map/ppermute | solution.py:32
  38.3 5.3 %collective-permute-start.12 = (bf16[512,128]{1,0:T(8,128)(2,1)S(1)}, bf16[512,128]{1,0:T(8,128)(2,1)S(1)}, u32[]{:S(2)}, u32[]{:S(2)}) collective-permute-start(bf16[512,128]{1,0:T(8,128)(2,1)S(1)} %get-tuple-element.35.refs_0_.wide_f), channel_id=1, source_target_pairs={{0,4},{4,0},{8,12},{12,8},{1,5},{5,1},{9,13},{13,9},{2,6},{6,2},{1... | collective-permute-start | bytes 393224 | tf_op jit(solution)/shard_map/ppermute | solution.py:32
  41.2 2.3 %collective-permute-start.14 = (bf16[512,128]{1,0:T(8,128)(2,1)S(1)}, bf16[512,128]{1,0:T(8,128)(2,1)S(1)}, u32[]{:S(2)}, u32[]{:S(2)}) collective-permute-start(bf16[512,128]{1,0:T(8,128)(2,1)S(1)} %collective-permute-done.13.refs_2_), channel_id=1, source_target_pairs={{0,4},{4,0},{8,12},{12,8},{1,5},{5,1},{9,13},{13,9},{2,6},{6,2},{1... | collective-permute-start | bytes 393224 | tf_op jit(solution)/shard_map/ppermute | solution.py:32
  41.2 1.4 %collective-permute-start.15 = (bf16[256,128]{1,0:T(8,128)(2,1)S(1)}, bf16[256,128]{1,0:T(8,128)(2,1)S(1)}, u32[]{:S(2)}, u32[]{:S(2)}) collective-permute-start(bf16[256,128]{1,0:T(8,128)(2,1)S(1)} %get-tuple-element.36.refs_4_.thin_f), channel_id=1, source_target_pairs={{0,4},{4,0},{8,12},{12,8},{1,5},{5,1},{9,13},{13,9},{2,6},{6,2},{1... | collective-permute-start | bytes 196616 | tf_op jit(solution)/shard_map/ppermute | solution.py:32
  42.3 1.3 %collective-permute-start.17 = (bf16[256,128]{1,0:T(8,128)(2,1)S(1)}, bf16[256,128]{1,0:T(8,128)(2,1)S(1)}, u32[]{:S(2)}, u32[]{:S(2)}) collective-permute-start(bf16[256,128]{1,0:T(8,128)(2,1)S(1)} %collective-permute-done.16.refs_6_), channel_id=1, source_target_pairs={{0,4},{4,0},{8,12},{12,8},{1,5},{5,1},{9,13},{13,9},{2,6},{6,2},{1... | collective-permute-start | bytes 196616 | tf_op jit(solution)/shard_map/ppermute | solution.py:32
  46.0 7.7 %collective-permute-start.21 = (bf16[256,128]{1,0:T(8,128)(2,1)S(1)}, bf16[256,128]{1,0:T(8,128)(2,1)S(1)}, u32[]{:S(2)}, u32[]{:S(2)}) collective-permute-start(bf16[256,128]{1,0:T(8,128)(2,1)S(1)} %get-tuple-element.42), channel_id=1, source_target_pairs={{0,1},{1,0},{2,3},{3,2},{4,5},{5,4},{6,7},{7,6},{8,9},{9,8},{10,11... | collective-permute-start | bytes 196616 | tf_op jit(solution)/shard_map/ppermute | solution.py:32
  47.5 20.6 %collective-permute-start.18 = (bf16[512,128]{1,0:T(8,128)(2,1)S(1)}, bf16[512,128]{1,0:T(8,128)(2,1)S(1)}, u32[]{:S(2)}, u32[]{:S(2)}) collective-permute-start(bf16[512,128]{1,0:T(8,128)(2,1)S(1)} %get-tuple-element.38), channel_id=1, source_target_pairs={{0,1},{1,0},{2,3},{3,2},{4,5},{5,4},{6,7},{7,6},{8,9},{9,8},{10,11... | collective-permute-start | bytes 393224 | tf_op jit(solution)/shard_map/ppermute | solution.py:32
  48.1 20.0 %collective-permute-start.19 = (bf16[512,128]{1,0:T(8,128)(2,1)S(1)}, bf16[512,128]{1,0:T(8,128)(2,1)S(1)}, u32[]{:S(2)}, u32[]{:S(2)}) collective-permute-start(bf16[512,128]{1,0:T(8,128)(2,1)S(1)} %get-tuple-element.39), channel_id=1, source_target_pairs={{0,2},{1,3},{2,0},{3,1},{4,6},{5,7},{6,4},{7,5},{8,10},{9,11},{10,... | collective-permute-start | bytes 393224 | tf_op jit(solution)/shard_map/ppermute | solution.py:32
  51.5 16.7 %collective-permute-start.20 = (bf16[512,128]{1,0:T(8,128)(2,1)S(1)}, bf16[512,128]{1,0:T(8,128)(2,1)S(1)}, u32[]{:S(2)}, u32[]{:S(2)}) collective-permute-start(bf16[512,128]{1,0:T(8,128)(2,1)S(1)} %get-tuple-element.40), channel_id=1, source_target_pairs={{0,3},{1,2},{2,1},{3,0},{4,7},{5,6},{6,5},{7,4},{8,11},{9,10},{10,... | collective-permute-start | bytes 393224 | tf_op jit(solution)/shard_map/ppermute | solution.py:32
  51.9 16.2 %collective-permute-start.22 = (bf16[256,128]{1,0:T(8,128)(2,1)S(1)}, bf16[256,128]{1,0:T(8,128)(2,1)S(1)}, u32[]{:S(2)}, u32[]{:S(2)}) collective-permute-start(bf16[256,128]{1,0:T(8,128)(2,1)S(1)} %get-tuple-element.43), channel_id=1, source_target_pairs={{0,2},{1,3},{2,0},{3,1},{4,6},{5,7},{6,4},{7,5},{8,10},{9,11},{10,... | collective-permute-start | bytes 196616 | tf_op jit(solution)/shard_map/ppermute | solution.py:32
  53.7 14.4 %collective-permute-start.23 = (bf16[256,128]{1,0:T(8,128)(2,1)S(1)}, bf16[256,128]{1,0:T(8,128)(2,1)S(1)}, u32[]{:S(2)}, u32[]{:S(2)}) collective-permute-start(bf16[256,128]{1,0:T(8,128)(2,1)S(1)} %get-tuple-element.44), channel_id=1, source_target_pairs={{0,3},{1,2},{2,1},{3,0},{4,7},{5,6},{6,5},{7,4},{8,11},{9,10},{10,... | collective-permute-start | bytes 196616 | tf_op jit(solution)/shard_map/ppermute | solution.py:32
  69.2 1.3 %collective-permute-start.24 = (f32[96,128]{1,0:T(8,128)S(1)}, f32[96,128]{1,0:T(8,128)S(1)}, u32[]{:S(2)}, u32[]{:S(2)}) collective-permute-start(f32[96,128]{1,0:T(8,128)S(1)} %get-tuple-element.46), channel_id=1, source_target_pairs={{0,4},{4,0},{8,12},{12,8},{1,5},{5,1},{9,13},{13,9},{2,6},{6,2},{1... | collective-permute-start | bytes 147464 | tf_op jit(solution)/shard_map/ppermute | solution.py:32
  70.5 4.2 %collective-permute-start.25 = (f32[96,128]{1,0:T(8,128)S(1)}, f32[96,128]{1,0:T(8,128)S(1)}, u32[]{:S(2)}, u32[]{:S(2)}) collective-permute-start(f32[96,128]{1,0:T(8,128)S(1)} %add.15), channel_id=1, source_target_pairs={{0,8},{4,12},{8,0},{12,4},{1,9},{5,13},{9,1},{13,5},{2,10},{6,14},... | collective-permute-start | bytes 147464 | tf_op jit(solution)/shard_map/ppermute | solution.py:32
  74.7 6.0 %collective-permute-start.28 = (f32[96,128]{1,0:T(8,128)S(1)}, f32[96,128]{1,0:T(8,128)S(1)}, u32[]{:S(2)}, u32[]{:S(2)}) collective-permute-start(f32[96,128]{1,0:T(8,128)S(1)} %add.16), channel_id=1, source_target_pairs={{0,3},{1,2},{2,1},{3,0},{4,7},{5,6},{6,5},{7,4},{8,11},{9,10},{10,... | collective-permute-start | bytes 147464 | tf_op jit(solution)/shard_map/ppermute | solution.py:32
  77.5 5.3 %collective-permute-start.27 = (f32[96,128]{1,0:T(8,128)S(1)}, f32[96,128]{1,0:T(8,128)S(1)}, u32[]{:S(2)}, u32[]{:S(2)}) collective-permute-start(f32[96,128]{1,0:T(8,128)S(1)} %add.16), channel_id=1, source_target_pairs={{0,2},{1,3},{2,0},{3,1},{4,6},{5,7},{6,4},{7,5},{8,10},{9,11},{10,... | collective-permute-start | bytes 147464 | tf_op jit(solution)/shard_map/ppermute | solution.py:32
  77.5 5.3 %collective-permute-start.26 = (f32[96,128]{1,0:T(8,128)S(1)}, f32[96,128]{1,0:T(8,128)S(1)}, u32[]{:S(2)}, u32[]{:S(2)}) collective-permute-start(f32[96,128]{1,0:T(8,128)S(1)} %add.16), channel_id=1, source_target_pairs={{0,1},{1,0},{2,3},{3,2},{4,5},{5,4},{6,7},{7,6},{8,9},{9,8},{10,11... | collective-permute-start | bytes 147464 | tf_op jit(solution)/shard_map/ppermute | solution.py:32
  82.9 1.3 %collective-permute-start.29 = (f32[96,128]{1,0:T(8,128)S(1)}, f32[96,128]{1,0:T(8,128)S(1)}, u32[]{:S(2)}, u32[]{:S(2)}) collective-permute-start(f32[96,128]{1,0:T(8,128)S(1)} %add_add_fusion.keep_ref), channel_id=1, source_target_pairs={{0,4},{4,0},{8,12},{12,8},{1,5},{5,1},{9,13},{13,9},{2,6},{6,2},{1... | collective-permute-start | bytes 147464 | tf_op jit(solution)/shard_map/ppermute | solution.py:32

commit v2 on v1

v2 whole, which is shorter than its diff:
```python
import functools

import jax
import jax.numpy as jnp
from jax import lax
from jax.experimental import pallas as pl
from jax.experimental.pallas import tpu as pltpu
from jax.sharding import PartitionSpec as P

LANES = 128
SIZE = LANES // 2
PIVOTS = 8
F32 = jnp.float32
BF16 = jnp.bfloat16
VMEM = pl.BlockSpec(memory_space=pltpu.VMEM)
SMEM = pl.BlockSpec(memory_space=pltpu.SMEM)


def call(kernel, out_shape, in_specs, scratch=(), flops=1000, name=None):
    return pl.pallas_call(
        kernel,
        out_shape=out_shape,
        in_specs=in_specs,
        out_specs=jax.tree.map(lambda _: VMEM, out_shape),
        scratch_shapes=list(scratch),
        compiler_params=pltpu.CompilerParams(vmem_limit_bytes=40 * 1024 * 1024),
        cost_estimate=pl.CostEstimate(flops=flops, bytes_accessed=1000, transcendentals=0),
        name=name,
    )


def swap(x, axis, key):
    count = lax.axis_size(axis)
    return lax.ppermute(x, axis, [(i, i ^ key) for i in range(count)])


def gather_shards(own, twin):
    shards = {0: own}
    bit = lax.axis_size("row") // 2
    while bit:
        for key in list(shards):
            late = key == 0 and bit == 1
            shards[key | bit] = swap(twin if late else shards[key], "row", bit)
        bit //= 2
    return [shards[key] for key in range(len(shards))]


def pack_kernel(turned_ref, out):
    rows = turned_ref.shape[1]
    half = rows // 2
    turned = turned_ref[...].astype(F32)
    out[pl.ds(0, rows), :] = turned[:LANES].T.astype(BF16)
    thin = jnp.concatenate([turned[LANES:, :half], turned[LANES:, half:]], axis=0)
    out[pl.ds(rows, half), :] = thin.T.astype(BF16)


def load_kernel(own_blocks, orbitals, vec_ref, ids_ref, ham_ref, out, at_out):
    out[...] = vec_ref[...]
    at_out[...] = (ids_ref[...] ^ (lax.axis_index("row") * own_blocks)) * orbitals


def product_kernel(keys, n_row, own_blocks, at_ref, ham_ref, *refs):
    parts, outs = refs[:n_row], refs[n_row : n_row + len(keys)]
    source = refs[-1]
    orbitals = ham_ref.shape[1]
    rows = own_blocks * orbitals
    half = rows // 2
    me = lax.axis_index("col")
    first = [(key ^ me) * own_blocks for key in keys]
    low_lane = lax.broadcasted_iota(jnp.int32, (orbitals, LANES), 1) < SIZE
    for key in range(n_row):
        base = key * rows
        source[pl.ds(base, rows), pl.ds(0, LANES)] = parts[key][pl.ds(0, rows), :]
        thin = parts[key][pl.ds(rows, half), :]
        source[pl.ds(base, half), pl.ds(LANES, LANES)] = thin
        source[pl.ds(base + half, half), pl.ds(LANES, LANES)] = jnp.concatenate(
            [thin[:, SIZE:], thin[:, :SIZE]], axis=1
        )

    def term(i, block):
        picked = [
            source[pl.ds(pl.multiple_of(at_ref[slot, first[i] + block], orbitals), orbitals), :]
            for slot in range(at_ref.shape[0])
        ]
        return jnp.dot(
            ham_ref[first[i] + block],
            jnp.concatenate(picked, axis=0),
            preferred_element_type=F32,
        )

    for i, out in enumerate(outs):
        for block in range(own_blocks // 2):
            upper, lower = term(i, block), term(i, block + own_blocks // 2)
            out[pl.ds(block * orbitals, orbitals), :] = upper[:, :LANES].astype(BF16)
            out[pl.ds(half + block * orbitals, orbitals), :] = lower[:, :LANES].astype(BF16)
            turned = jnp.concatenate([lower[:, LANES + SIZE :], lower[:, LANES : LANES + SIZE]], axis=1)
            out[pl.ds(rows + block * orbitals, orbitals), :] = jnp.where(
                low_lane, upper[:, LANES:], turned
            ).astype(BF16)


def product(keys, own_blocks, at, ham, parts):
    n_row = len(parts)
    orbitals = ham.shape[1]
    flops = 4 * own_blocks * len(keys) * orbitals * ham.shape[2] * LANES
    return call(
        functools.partial(product_kernel, keys, n_row, own_blocks),
        [jax.ShapeDtypeStruct(parts[0].shape, BF16)] * len(keys),
        [SMEM, VMEM] + [VMEM] * n_row,
        [pltpu.VMEM((own_blocks * n_row * orbitals, 2 * LANES), BF16)],
        flops=flops,
        name="product",
    )(at, ham, *parts)


def add_kernel(a, b, later, out, later_out):
    out[...] = (a[...].astype(F32) + b[...].astype(F32)).astype(BF16)
    later_out[...] = later[...]


def add(a, b, later):
    shape = jax.ShapeDtypeStruct(a.shape, BF16)
    return call(add_kernel, [shape, shape], [VMEM] * 3, name="add")(a, b, later)


def summands(own_blocks, at, ham, parts):
    n_col = lax.axis_size("col")
    if n_col != 4:
        terms = product(tuple(range(n_col)), own_blocks, at, ham, parts)
        return [terms[0]] + [swap(terms[key], "col", key) for key in range(1, n_col)]
    (far,) = product((3,), own_blocks, at, ham, parts)
    other = swap(far, "col", 1)
    across, near, own = product((2, 1, 0), own_blocks, at, ham, parts)
    across, near = add(across, other, near)
    near = swap(near, "col", 1)
    return [own, swap(across, "col", 2), near]


def ends(lower_ref, upper_ref, shape):
    low = jnp.full(shape, lower_ref[0], F32)
    high = jnp.full(shape, upper_ref[0], F32)
    return (high + low) * 0.5, 1.0 / ((high - low) * 0.5)


def total_of(refs):
    acc = refs[0][...].astype(F32)
    for ref in refs[1:]:
        acc = acc + ref[...].astype(F32)
    return acc


def first_kernel(lower_ref, upper_ref, start, *refs):
    center, scale = ends(lower_ref, upper_ref, (1, LANES))
    moved = total_of(refs[:-1]) - center * start[...].astype(F32)
    refs[-1][...] = (moved * scale).astype(BF16)


def cross(a, b):
    return lax.dot_general(a, b, (((0,), (0,)), ((), ())), preferred_element_type=F32)


def second_kernel(rows_all, lower_ref, upper_ref, start, first, *refs):
    out, keep_out, send_out, gram = refs[-4:]
    center, scale = ends(lower_ref, upper_ref, (1, LANES))
    moved = total_of(refs[:-4]) - center * first[...].astype(F32)
    filtered = (2.0 * moved * scale - start[...].astype(F32)).astype(BF16)
    out[...] = filtered
    rows = out.shape[0] * 2 // 3
    half = rows // 2
    wide, thin = filtered[:rows], filtered[rows:]
    inv = 1.0 / rows_all
    aa = cross(wide, wide) * inv
    upper = cross(thin, wide[:half]) * inv
    lower = cross(thin, wide[half:]) * inv
    bb = cross(thin, thin) * inv
    turned = jnp.concatenate([bb[:SIZE, SIZE:], bb[:SIZE, :SIZE]], axis=1)
    low_lane = lax.broadcasted_iota(jnp.int32, (SIZE, LANES), 1) < SIZE
    gram[pl.ds(0, SIZE), :] = jnp.where(low_lane, aa[:SIZE], turned + bb[SIZE:])
    gram[pl.ds(SIZE, SIZE), :] = aa[SIZE:]
    gram[pl.ds(2 * SIZE, SIZE), :] = upper[:SIZE] + lower[SIZE:]
    part = 3 * SIZE // 2
    mine = lax.axis_index("row") & 1
    keep_out[...] = gram[pl.ds(pl.multiple_of(mine * part, 8), part), :]
    send_out[...] = gram[pl.ds(pl.multiple_of((1 - mine) * part, 8), part), :]


def inverse_factor(block, pivots):
    size = block.shape[0]
    tiles = size // 8
    rows = lax.broadcasted_iota(jnp.int32, (8, LANES), 0)
    lanes = lax.broadcasted_iota(jnp.int32, (8, LANES), 1)
    pad = jnp.concatenate([block, jnp.zeros((size, LANES - size), F32)], axis=1)
    a = [
        jnp.where(lanes == rows + (size + 8 * t), 1.0, pad[8 * t : 8 * t + 8]) for t in range(tiles)
    ]
    diag = [jnp.ones((8, LANES), F32) for _ in range(tiles)]
    full = (8, LANES)
    for j in range(0, size, pivots):
        t0, s0 = divmod(j, 8)
        cols = [
            [jnp.broadcast_to(a[t][:, j + k : j + k + 1], full) for t in range(t0, tiles)]
            for k in range(pivots)
        ]
        lines = [jnp.broadcast_to(a[t0][s0 + k : s0 + k + 1, :], full) for k in range(pivots)]
        small = [
            [jnp.broadcast_to(cols[q][0][s0 + k : s0 + k + 1, :], full) for q in range(k + 1)]
            for k in range(pivots)
        ]
        for k in range(pivots):
            d = small[k][k]
            diag[t0] = jnp.where(rows == s0 + k, d, diag[t0])
            r = 1.0 / d
            mult = {}
            for q in range(k + 1, pivots):
                mult[q] = small[q][k] * r
            for q in range(k + 1, pivots):
                lines[q] = lines[q] - mult[q] * lines[k]
                for p in range(k + 1, q + 1):
                    small[q][p] = small[q][p] - mult[q] * small[p][k]
            for i, t in enumerate(range(t0, tiles)):
                x = cols[k][i] * r
                if t == t0:
                    x = jnp.where(rows > s0 + k, x, 0.0)
                for q in range(k + 1, pivots):
                    cols[q][i] = cols[q][i] - cols[k][i] * mult[q]
                a[t] = a[t] - x * lines[k]
    out = jnp.concatenate([a[t] * lax.rsqrt(diag[t]) for t in range(tiles)], axis=0)
    return out[:, size:]


def last_kernel(pivots, keep_ref, other_ref, vec_ref, out_ref, gram, factor):
    size = LANES // 2
    part = 3 * size // 2
    mine = lax.axis_index("row") & 1
    gram[pl.ds(pl.multiple_of(mine * part, 8), part), :] = keep_ref[...]
    gram[pl.ds(pl.multiple_of((1 - mine) * part, 8), part), :] = other_ref[...]
    dot = functools.partial(
        jnp.dot, precision=lax.Precision.HIGHEST, preferred_element_type=F32
    )

    def dot_t(a, b):
        return lax.dot_general(
            a,
            b,
            (((1,), (1,)), ((), ())),
            precision=lax.Precision.HIGHEST,
            preferred_element_type=F32,
        )

    g00 = gram[pl.ds(0, size), :][:, :size]
    g22 = gram[pl.ds(0, size), :][:, size:]
    strip = gram[pl.ds(size, 2 * size), :]
    x0 = inverse_factor(g00, pivots)
    l_strip = dot_t(strip[:, :size], x0)
    rest = strip[:, size:] - dot_t(l_strip, l_strip[:size])
    x1 = inverse_factor(rest[:size], pivots)
    l10, l20 = l_strip[:size], l_strip[size:]
    l21 = dot_t(rest[size:], x1)
    x2 = inverse_factor(g22 - dot_t(l20, l20) - dot_t(l21, l21), pivots)
    n10 = -dot(x1, dot(l10, x0))
    n20 = -dot(x2, dot(l20, x0) + dot(l21, n10))
    n21 = -dot(x2, dot(l21, x1))
    zero = jnp.zeros((size, size), F32)
    factor[pl.ds(0, size), :] = jnp.concatenate([x0, zero], axis=1)
    factor[pl.ds(size, size), :] = jnp.concatenate([n10, x1], axis=1)
    factor[pl.ds(2 * size, size), :] = jnp.concatenate([n20, n21], axis=1)

    def apply(mat, vec):
        high = mat.astype(BF16)
        low = (mat - high.astype(F32)).astype(BF16)
        con = (((1,), (1,)), ((), ()))
        return lax.dot_general(high, vec, con, preferred_element_type=F32) + lax.dot_general(
            low, vec, con, preferred_element_type=F32
        )

    rows = out_ref.shape[1]
    wide, thin = vec_ref[pl.ds(0, rows), :], vec_ref[pl.ds(rows, rows // 2), :]
    main = apply(factor[...], wide)
    out_ref[pl.ds(0, 2 * size), :] = main[: 2 * size]
    tail = jnp.concatenate(
        [
            apply(jnp.concatenate([x2, zero], axis=1), thin),
            apply(jnp.concatenate([zero, x2], axis=1), thin),
        ],
        axis=1,
    )
    out_ref[pl.ds(2 * size, size), :] = main[2 * size :] + tail


def sum_all(keep, send):
    acc = keep + swap(send, "row", 1)
    bit = 2
    while bit < lax.axis_size("row"):
        acc = acc + swap(acc, "row", bit)
        bit *= 2
    got = [swap(acc, "col", key) for key in range(1, lax.axis_size("col"))]
    for x in got:
        acc = acc + x
    return acc, swap(acc, "row", 1)


def per_device(hamiltonian, columns, vectors, lower, upper):
    rows = vectors.shape[0]
    orbitals = hamiltonian.shape[1]
    own_blocks = rows // orbitals
    rows_all = rows * lax.axis_size("col") * lax.axis_size("row")
    shape = jax.ShapeDtypeStruct((rows + rows // 2, LANES), BF16)
    half_gram = jax.ShapeDtypeStruct((3 * SIZE // 2, LANES), F32)
    gram = pltpu.VMEM((3 * SIZE, LANES), F32)

    start = call(pack_kernel, shape, [VMEM], name="pack")(vectors.T)
    twin, at = call(
        functools.partial(load_kernel, own_blocks, orbitals),
        [shape, jax.ShapeDtypeStruct(columns.shape[::-1], jnp.int32)],
        [VMEM, VMEM, VMEM],
        name="load",
    )(start, columns.T, hamiltonian)
    terms = summands(own_blocks, at, hamiltonian, gather_shards(start, twin))
    first = call(
        first_kernel, shape, [SMEM, SMEM] + [VMEM] * (1 + len(terms)), name="first_filter"
    )(lower, upper, start, *terms)
    terms = summands(own_blocks, at, hamiltonian, gather_shards(first, first))
    second, keep, send = call(
        functools.partial(second_kernel, rows_all),
        [shape, half_gram, half_gram],
        [SMEM, SMEM] + [VMEM] * (2 + len(terms)),
        [gram],
        name="second_filter",
    )(lower, upper, start, first, *terms)
    keep, other = sum_all(keep, send)
    basis = call(
        functools.partial(last_kernel, PIVOTS),
        jax.ShapeDtypeStruct((LANES + SIZE, rows), F32),
        [VMEM] * 3,
        [gram, gram],
        name="orthonormalize",
    )(keep, other, second)
    return basis.T


def solution(mesh):
    return jax.shard_map(
        per_device,
        mesh=mesh,
        in_specs=(
            P(("groups", "row"), None, "col"),
            P(("groups", "row"), "col"),
            P(("groups", "row", "col"), None),
            P("groups"),
            P("groups"),
        ),
        out_specs=P(("groups", "row", "col"), None),
        check_vma=False,
    )
```

time: 102 us -> 83.1 us (0.81)
  Pallas kernels: 23.5 us -> 15.8 us
  starting transfers between devices: 30.2 us -> 23.8 us
  waiting for transfers between devices: 42 us -> 38.9 us
  local copies, waits for them, and re-layouts: 4.22 us -> 3.02 us
    pallas_call x5 -> x11, Pallas kernels: 23.5 us -> 15.8 us  [the longest x1 8.82 us: per_device(): call(functools.partial(last_kernel, PIVOTS), jax.ShapeDtypeStruct((LANES...]
    ppermute x30 -> x18, starting transfers between devices: 30.2 us -> 23.8 us  [swap(): return lax.ppermute(x, axis, [(i, i ^ key) for i in range(count)])]
    ppermute x30 -> x18, waiting for transfers between devices: 42 us -> 38.9 us  [swap(): return lax.ppermute(x, axis, [(i, i ^ key) for i in range(count)])]
    slice x2 -> x0, local copies, waits for them, and re-layouts: 1.69 us -> none  [the longest x1 0.91 us: pack(): vectors[:, :LANES]]
  transfers between devices with their start and end apart: 30 -> 18, of which waited for: 14 -> 15; matrix products, arithmetic and copies ran while one was open for 2% -> 0% of each run, Pallas kernels for 0% -> 4%
where the time goes in v2:
time: 83.1 us; the launch traced here: 82.9 us
  waiting for transfers between devices  38.9 us (47%)
  starting transfers between devices  23.8 us (29%)
  Pallas kernels  15.8 us (19%)
  local copies, waits for them, and re-layouts  3.02 us (4%)
  between operations  1.38 us (2%)
    ppermute x18, waiting for transfers between devices, swap(): return lax.ppermute(x, axis, [(i, i ^ key) for i in range(count)])  38.9 us
    ppermute x18, starting transfers between devices, swap(): return lax.ppermute(x, axis, [(i, i ^ key) for i in range(count)])  23.8 us
    pallas_call x1, Pallas kernels, per_device(): call(functools.partial(last_kernel, PIVOTS), jax.ShapeDtypeStruct((LANES...  8.82 us
    pallas_call x4, Pallas kernels, product(): call(functools.partial(product_kernel, keys, n_row, own_blocks), [jax.Sha...  6.15 us
    unnamed x8, local copies, waits for them, and re-layouts  3.02 us
  transfers between devices with their start and end apart: 18, of which 15 were waited for; matrix products, arithmetic and copies ran while one was open for 0% of the time, Pallas kernels for 4%

profile of v2, /device:TPU:0, one launch (start us, length us, event | category | flops | bytes accessed | tf_op | source)
XLA Modules:
  0.0 82.9 jit_solution(5761686398052755426)
XLA Ops:
  0.0 0.9 %copy-done.2 = bf16[512,192]{0,1:T(8,128)(2,1)S(1)} copy-done((bf16[512,192]{0,1:T(8,128)(2,1)S(1)}, bf16[512,192]{0,1:T(8,128)(2,1)}, u32[]{:S(2)}) %copy-start.2) | copy-done | bytes 196632
  1.1 3.0 %collective-permute-start.1 = (bf16[768,128]{1,0:T(8,128)(2,1)S(1)}, bf16[768,128]{1,0:T(8,128)(2,1)S(1)}, u32[]{:S(2)}, u32[]{:S(2)}) collective-permute-start(bf16[768,128]{1,0:T(8,128)(2,1)S(1)} %pack.1.vec_ref.refs_0_.start), channel_id=1, source_target_pairs={{0,8},{4,12},{8,0},{12,4},{1,9},{5,13},{9,1},{13,5},{2,10},{6,14},... | collective-permute-start | bytes 589832 | tf_op jit(solution)/shard_map/ppermute | solution.py:34
  4.1 1.4 %copy-done = bf16[32,64,384]{2,1,0:T(8,128)(2,1)S(1)} copy-done((bf16[32,64,384]{2,1,0:T(8,128)(2,1)S(1)}, bf16[32,64,384]{2,1,0:T(8,128)(2,1)}, u32[]{:S(2)}) %copy-start) | copy-done | bytes 1572888
  5.5 0.7 copy-done.3
  6.3 2.7 %collective-permute-done.1.refs_2_ = bf16[768,128]{1,0:T(8,128)(2,1)S(1)} collective-permute-done((bf16[768,128]{1,0:T(8,128)(2,1)S(1)}, bf16[768,128]{1,0:T(8,128)(2,1)S(1)}, u32[]{:S(2)}, u32[]{:S(2)}) %collective-permute-start.1) | collective-permute-done | bytes 196640 | tf_op jit(solution)/shard_map/ppermute | solution.py:34
  9.0 1.4 %collective-permute-done.2.refs_3_ = bf16[768,128]{1,0:T(8,128)(2,1)S(1)} collective-permute-done((bf16[768,128]{1,0:T(8,128)(2,1)S(1)}, bf16[768,128]{1,0:T(8,128)(2,1)S(1)}, u32[]{:S(2)}, u32[]{:S(2)}) %collective-permute-start.2) | collective-permute-done | bytes 196640 | tf_op jit(solution)/shard_map/ppermute | solution.py:34
  10.4 1.2 %product.5 = bf16[768,128]{1,0:T(8,128)(2,1)S(1)} custom-call(s32[6,32]{1,0:T(8,128)S(1)} %get-tuple-element.20.at_ref, bf16[32,64,384]{2,1,0:T(8,128)(2,1)S(1)} %copy-done.1, bf16[768,128]{1,0:T(8,128)(2,1)S(1)} %pack.1.vec_ref.refs_0_.start, bf16[768,128]{1,0:T(8,128)(2,1)S(1)} %collective-permute-done.refs_1_, ...), custom_call_target="tpu_custom_call" | custom-call | flops 100663296 | bytes 1000 | tf_op jit(solution)/shard_map/product/pallas_call | solution.py:106
  11.7 1.9 %collective-permute-start.3 = (bf16[768,128]{1,0:T(8,128)(2,1)S(1)}, bf16[768,128]{1,0:T(8,128)(2,1)S(1)}, u32[]{:S(2)}, u32[]{:S(2)}) collective-permute-start(bf16[768,128]{1,0:T(8,128)(2,1)S(1)} %product.5), channel_id=1, source_target_pairs={{0,1},{1,0},{2,3},{3,2},{4,5},{5,4},{6,7},{7,6},{8,9},{9,8},{10,11... | collective-permute-start | bytes 589832 | tf_op jit(solution)/shard_map/ppermute | solution.py:34
  13.6 1.8 %product.4 = (bf16[768,128]{1,0:T(8,128)(2,1)S(1)}, bf16[768,128]{1,0:T(8,128)(2,1)S(1)}, bf16[768,128]{1,0:T(8,128)(2,1)S(1)}) custom-call(s32[6,32]{1,0:T(8,128)S(1)} %get-tuple-element.20.at_ref, bf16[32,64,384]{2,1,0:T(8,128)(2,1)S(1)} %copy-done.1, bf16[768,128]{1,0:T(8,128)(2,1)S(1)} %pack.1.vec_ref.refs_0_.start, ...), custom_call_target="tpu_custom_call" | custom-call | flops 301989888 | bytes 1000 | tf_op jit(solution)/shard_map/product/pallas_call | solution.py:106
  15.4 3.4 %collective-permute-done.3.b = bf16[768,128]{1,0:T(8,128)(2,1)S(1)} collective-permute-done((bf16[768,128]{1,0:T(8,128)(2,1)S(1)}, bf16[768,128]{1,0:T(8,128)(2,1)S(1)}, u32[]{:S(2)}, u32[]{:S(2)}) %collective-permute-start.3) | collective-permute-done | bytes 196640 | tf_op jit(solution)/shard_map/ppermute | solution.py:34
  18.8 2.8 %collective-permute-start.4 = (bf16[768,128]{1,0:T(8,128)(2,1)S(1)}, bf16[768,128]{1,0:T(8,128)(2,1)S(1)}, u32[]{:S(2)}, u32[]{:S(2)}) collective-permute-start(bf16[768,128]{1,0:T(8,128)(2,1)S(1)} %get-tuple-element.25), channel_id=1, source_target_pairs={{0,2},{1,3},{2,0},{3,1},{4,6},{5,7},{6,4},{7,5},{8,10},{9,11},{10,... | collective-permute-start | bytes 589832 | tf_op jit(solution)/shard_map/ppermute | solution.py:34
  21.6 1.6 %collective-permute-start.5 = (bf16[768,128]{1,0:T(8,128)(2,1)S(1)}, bf16[768,128]{1,0:T(8,128)(2,1)S(1)}, u32[]{:S(2)}, u32[]{:S(2)}) collective-permute-start(bf16[768,128]{1,0:T(8,128)(2,1)S(1)} %get-tuple-element.26), channel_id=1, source_target_pairs={{0,1},{1,0},{2,3},{3,2},{4,5},{5,4},{6,7},{7,6},{8,9},{9,8},{10,11... | collective-permute-start | bytes 589832 | tf_op jit(solution)/shard_map/ppermute | solution.py:34
  24.5 5.8 %collective-permute-done.4.refs_1_ = bf16[768,128]{1,0:T(8,128)(2,1)S(1)} collective-permute-done((bf16[768,128]{1,0:T(8,128)(2,1)S(1)}, bf16[768,128]{1,0:T(8,128)(2,1)S(1)}, u32[]{:S(2)}, u32[]{:S(2)}) %collective-permute-start.4) | collective-permute-done | bytes 196640 | tf_op jit(solution)/shard_map/ppermute | solution.py:34
  30.6 1.6 %collective-permute-start.7 = (bf16[768,128]{1,0:T(8,128)(2,1)S(1)}, bf16[768,128]{1,0:T(8,128)(2,1)S(1)}, u32[]{:S(2)}, u32[]{:S(2)}) collective-permute-start(bf16[768,128]{1,0:T(8,128)(2,1)S(1)} %first_filter.1.refs_0_.first), channel_id=1, source_target_pairs={{0,8},{4,12},{8,0},{12,4},{1,9},{5,13},{9,1},{13,5},{2,10},{6,14},... | collective-permute-start | bytes 589832 | tf_op jit(solution)/shard_map/ppermute | solution.py:34
  32.3 4.1 %collective-permute-done.7.refs_2_ = bf16[768,128]{1,0:T(8,128)(2,1)S(1)} collective-permute-done((bf16[768,128]{1,0:T(8,128)(2,1)S(1)}, bf16[768,128]{1,0:T(8,128)(2,1)S(1)}, u32[]{:S(2)}, u32[]{:S(2)}) %collective-permute-start.7) | collective-permute-done | bytes 196640 | tf_op jit(solution)/shard_map/ppermute | solution.py:34
  36.4 1.4 %collective-permute-done.8.refs_3_ = bf16[768,128]{1,0:T(8,128)(2,1)S(1)} collective-permute-done((bf16[768,128]{1,0:T(8,128)(2,1)S(1)}, bf16[768,128]{1,0:T(8,128)(2,1)S(1)}, u32[]{:S(2)}, u32[]{:S(2)}) %collective-permute-start.8) | collective-permute-done | bytes 196640 | tf_op jit(solution)/shard_map/ppermute | solution.py:34
  37.8 1.2 %product.7 = bf16[768,128]{1,0:T(8,128)(2,1)S(1)} custom-call(s32[6,32]{1,0:T(8,128)S(1)} %get-tuple-element.20.at_ref, bf16[32,64,384]{2,1,0:T(8,128)(2,1)S(1)} %copy-done.1, bf16[768,128]{1,0:T(8,128)(2,1)S(1)} %first_filter.1.refs_0_.first, bf16[768,128]{1,0:T(8,128)(2,1)S(1)} %collective-permute-done.6.refs_1_, ...), custom_call_target="tpu_custom_call" | custom-call | flops 100663296 | bytes 1000 | tf_op jit(solution)/shard_map/product/pallas_call | solution.py:106
  39.1 1.6 %collective-permute-start.9 = (bf16[768,128]{1,0:T(8,128)(2,1)S(1)}, bf16[768,128]{1,0:T(8,128)(2,1)S(1)}, u32[]{:S(2)}, u32[]{:S(2)}) collective-permute-start(bf16[768,128]{1,0:T(8,128)(2,1)S(1)} %product.7), channel_id=1, source_target_pairs={{0,1},{1,0},{2,3},{3,2},{4,5},{5,4},{6,7},{7,6},{8,9},{9,8},{10,11... | collective-permute-start | bytes 589832 | tf_op jit(solution)/shard_map/ppermute | solution.py:34
  40.7 1.8 %product.6 = (bf16[768,128]{1,0:T(8,128)(2,1)S(1)}, bf16[768,128]{1,0:T(8,128)(2,1)S(1)}, bf16[768,128]{1,0:T(8,128)(2,1)S(1)}) custom-call(s32[6,32]{1,0:T(8,128)S(1)} %get-tuple-element.20.at_ref, bf16[32,64,384]{2,1,0:T(8,128)(2,1)S(1)} %copy-done.1, bf16[768,128]{1,0:T(8,128)(2,1)S(1)} %first_filter.1.refs_0_.first, ...), custom_call_target="tpu_custom_call" | custom-call | flops 301989888 | bytes 1000 | tf_op jit(solution)/shard_map/product/pallas_call | solution.py:106
  42.6 3.5 %collective-permute-done.9.b = bf16[768,128]{1,0:T(8,128)(2,1)S(1)} collective-permute-done((bf16[768,128]{1,0:T(8,128)(2,1)S(1)}, bf16[768,128]{1,0:T(8,128)(2,1)S(1)}, u32[]{:S(2)}, u32[]{:S(2)}) %collective-permute-start.9) | collective-permute-done | bytes 196640 | tf_op jit(solution)/shard_map/ppermute | solution.py:34
  46.1 3.3 %collective-permute-start.10 = (bf16[768,128]{1,0:T(8,128)(2,1)S(1)}, bf16[768,128]{1,0:T(8,128)(2,1)S(1)}, u32[]{:S(2)}, u32[]{:S(2)}) collective-permute-start(bf16[768,128]{1,0:T(8,128)(2,1)S(1)} %get-tuple-element.30), channel_id=1, source_target_pairs={{0,2},{1,3},{2,0},{3,1},{4,6},{5,7},{6,4},{7,5},{8,10},{9,11},{10,... | collective-permute-start | bytes 589832 | tf_op jit(solution)/shard_map/ppermute | solution.py:34
  49.4 1.7 %collective-permute-start.11 = (bf16[768,128]{1,0:T(8,128)(2,1)S(1)}, bf16[768,128]{1,0:T(8,128)(2,1)S(1)}, u32[]{:S(2)}, u32[]{:S(2)}) collective-permute-start(bf16[768,128]{1,0:T(8,128)(2,1)S(1)} %get-tuple-element.31), channel_id=1, source_target_pairs={{0,1},{1,0},{2,3},{3,2},{4,5},{5,4},{6,7},{7,6},{8,9},{9,8},{10,11... | collective-permute-start | bytes 589832 | tf_op jit(solution)/shard_map/ppermute | solution.py:34
  51.2 7.3 %collective-permute-done.10.refs_1_ = bf16[768,128]{1,0:T(8,128)(2,1)S(1)} collective-permute-done((bf16[768,128]{1,0:T(8,128)(2,1)S(1)}, bf16[768,128]{1,0:T(8,128)(2,1)S(1)}, u32[]{:S(2)}, u32[]{:S(2)}) %collective-permute-start.10) | collective-permute-done | bytes 196640 | tf_op jit(solution)/shard_map/ppermute | solution.py:34
  59.3 1.2 %collective-permute-done.12 = f32[96,128]{1,0:T(8,128)S(1)} collective-permute-done((f32[96,128]{1,0:T(8,128)S(1)}, f32[96,128]{1,0:T(8,128)S(1)}, u32[]{:S(2)}, u32[]{:S(2)}) %collective-permute-start.12) | collective-permute-done | bytes 49184 | tf_op jit(solution)/shard_map/ppermute | solution.py:34
  60.6 1.6 %collective-permute-start.13 = (f32[96,128]{1,0:T(8,128)S(1)}, f32[96,128]{1,0:T(8,128)S(1)}, u32[]{:S(2)}, u32[]{:S(2)}) collective-permute-start(f32[96,128]{1,0:T(8,128)S(1)} %add.17), channel_id=1, source_target_pairs={{0,8},{4,12},{8,0},{12,4},{1,9},{5,13},{9,1},{13,5},{2,10},{6,14},... | collective-permute-start | bytes 147464 | tf_op jit(solution)/shard_map/ppermute | solution.py:34
  62.1 2.6 %collective-permute-done.13 = f32[96,128]{1,0:T(8,128)S(1)} collective-permute-done((f32[96,128]{1,0:T(8,128)S(1)}, f32[96,128]{1,0:T(8,128)S(1)}, u32[]{:S(2)}, u32[]{:S(2)}) %collective-permute-start.13) | collective-permute-done | bytes 49184 | tf_op jit(solution)/shard_map/ppermute | solution.py:34
  64.7 3.1 %collective-permute-start.16 = (f32[96,128]{1,0:T(8,128)S(1)}, f32[96,128]{1,0:T(8,128)S(1)}, u32[]{:S(2)}, u32[]{:S(2)}) collective-permute-start(f32[96,128]{1,0:T(8,128)S(1)} %add.18), channel_id=1, source_target_pairs={{0,3},{1,2},{2,1},{3,0},{4,7},{5,6},{6,5},{7,4},{8,11},{9,10},{10,... | collective-permute-start | bytes 147464 | tf_op jit(solution)/shard_map/ppermute | solution.py:34
  67.8 1.4 %collective-permute-start.14 = (f32[96,128]{1,0:T(8,128)S(1)}, f32[96,128]{1,0:T(8,128)S(1)}, u32[]{:S(2)}, u32[]{:S(2)}) collective-permute-start(f32[96,128]{1,0:T(8,128)S(1)} %add.18), channel_id=1, source_target_pairs={{0,1},{1,0},{2,3},{3,2},{4,5},{5,4},{6,7},{7,6},{8,9},{9,8},{10,11... | collective-permute-start | bytes 147464 | tf_op jit(solution)/shard_map/ppermute | solution.py:34
  69.2 1.6 %collective-permute-done.16 = f32[96,128]{1,0:T(8,128)S(1)} collective-permute-done((f32[96,128]{1,0:T(8,128)S(1)}, f32[96,128]{1,0:T(8,128)S(1)}, u32[]{:S(2)}, u32[]{:S(2)}) %collective-permute-start.16) | collective-permute-done | bytes 49184 | tf_op jit(solution)/shard_map/ppermute | solution.py:34
  70.8 2.0 %collective-permute-done.15 = f32[96,128]{1,0:T(8,128)S(1)} collective-permute-done((f32[96,128]{1,0:T(8,128)S(1)}, f32[96,128]{1,0:T(8,128)S(1)}, u32[]{:S(2)}, u32[]{:S(2)}) %collective-permute-start.15) | collective-permute-done | bytes 49184 | tf_op jit(solution)/shard_map/ppermute | solution.py:34
  72.9 1.2 %collective-permute-done.17.other_ref = f32[96,128]{1,0:T(8,128)S(1)} collective-permute-done((f32[96,128]{1,0:T(8,128)S(1)}, f32[96,128]{1,0:T(8,128)S(1)}, u32[]{:S(2)}, u32[]{:S(2)}) %collective-permute-start.17) | collective-permute-done | bytes 49184 | tf_op jit(solution)/shard_map/ppermute | solution.py:34
  74.1 8.8 %orthonormalize.1 = f32[192,512]{1,0:T(8,128)} custom-call(f32[96,128]{1,0:T(8,128)S(1)} %add_add_fusion.keep_ref, f32[96,128]{1,0:T(8,128)S(1)} %collective-permute-done.17.other_ref, bf16[768,128]{1,0:T(8,128)(2,1)S(1)} %get-tuple-element.34.vec_ref), custom_call_target="tpu_custom_call" | custom-call | flops 1000 | bytes 1000 | tf_op jit(solution)/shard_map/orthonormalize/pallas_call | solution.py:331
  (26 shorter events, 1.6 us)
Async XLA Ops:
  0.0 0.9 %copy-start.2 = (bf16[512,192]{0,1:T(8,128)(2,1)S(1)}, bf16[512,192]{0,1:T(8,128)(2,1)}, u32[]{:S(2)}) copy-start(bf16[512,192]{0,1:T(8,128)(2,1)} %param.7) | copy-start | bytes 589828
  1.1 7.9 %collective-permute-start.1 = (bf16[768,128]{1,0:T(8,128)(2,1)S(1)}, bf16[768,128]{1,0:T(8,128)(2,1)S(1)}, u32[]{:S(2)}, u32[]{:S(2)}) collective-permute-start(bf16[768,128]{1,0:T(8,128)(2,1)S(1)} %pack.1.vec_ref.refs_0_.start), channel_id=1, source_target_pairs={{0,8},{4,12},{8,0},{12,4},{1,9},{5,13},{9,1},{13,5},{2,10},{6,14},... | collective-permute-start | bytes 589832 | tf_op jit(solution)/shard_map/ppermute | solution.py:34
  4.1 1.4 %copy-start = (bf16[32,64,384]{2,1,0:T(8,128)(2,1)S(1)}, bf16[32,64,384]{2,1,0:T(8,128)(2,1)}, u32[]{:S(2)}) copy-start(bf16[32,64,384]{2,1,0:T(8,128)(2,1)} %ham_ref.9) | copy-start | bytes 4718596
  5.5 0.7 copy-start.3
  6.2 4.3 %copy-start.1 = (bf16[32,64,384]{2,1,0:T(8,128)(2,1)S(1)}, bf16[32,64,384]{2,1,0:T(8,128)(2,1)}, u32[]{:S(2)}) copy-start(bf16[32,64,384]{2,1,0:T(8,128)(2,1)} %ham_ref.9) | copy-start | bytes 4718596
  6.2 2.8 %collective-permute-start = (bf16[768,128]{1,0:T(8,128)(2,1)S(1)}, bf16[768,128]{1,0:T(8,128)(2,1)S(1)}, u32[]{:S(2)}, u32[]{:S(2)}) collective-permute-start(bf16[768,128]{1,0:T(8,128)(2,1)S(1)} %get-tuple-element.21), channel_id=1, source_target_pairs={{0,4},{4,0},{8,12},{12,8},{1,5},{5,1},{9,13},{13,9},{2,6},{6,2},{1... | collective-permute-start | bytes 589832 | tf_op jit(solution)/shard_map/ppermute | solution.py:34
  9.0 1.4 %collective-permute-start.2 = (bf16[768,128]{1,0:T(8,128)(2,1)S(1)}, bf16[768,128]{1,0:T(8,128)(2,1)S(1)}, u32[]{:S(2)}, u32[]{:S(2)}) collective-permute-start(bf16[768,128]{1,0:T(8,128)(2,1)S(1)} %collective-permute-done.1.refs_2_), channel_id=1, source_target_pairs={{0,4},{4,0},{8,12},{12,8},{1,5},{5,1},{9,13},{13,9},{2,6},{6,2},{1... | collective-permute-start | bytes 589832 | tf_op jit(solution)/shard_map/ppermute | solution.py:34
  11.7 7.1 %collective-permute-start.3 = (bf16[768,128]{1,0:T(8,128)(2,1)S(1)}, bf16[768,128]{1,0:T(8,128)(2,1)S(1)}, u32[]{:S(2)}, u32[]{:S(2)}) collective-permute-start(bf16[768,128]{1,0:T(8,128)(2,1)S(1)} %product.5), channel_id=1, source_target_pairs={{0,1},{1,0},{2,3},{3,2},{4,5},{5,4},{6,7},{7,6},{8,9},{9,8},{10,11... | collective-permute-start | bytes 589832 | tf_op jit(solution)/shard_map/ppermute | solution.py:34
  18.8 11.5 %collective-permute-start.4 = (bf16[768,128]{1,0:T(8,128)(2,1)S(1)}, bf16[768,128]{1,0:T(8,128)(2,1)S(1)}, u32[]{:S(2)}, u32[]{:S(2)}) collective-permute-start(bf16[768,128]{1,0:T(8,128)(2,1)S(1)} %get-tuple-element.25), channel_id=1, source_target_pairs={{0,2},{1,3},{2,0},{3,1},{4,6},{5,7},{6,4},{7,5},{8,10},{9,11},{10,... | collective-permute-start | bytes 589832 | tf_op jit(solution)/shard_map/ppermute | solution.py:34
  21.6 8.9 %collective-permute-start.5 = (bf16[768,128]{1,0:T(8,128)(2,1)S(1)}, bf16[768,128]{1,0:T(8,128)(2,1)S(1)}, u32[]{:S(2)}, u32[]{:S(2)}) collective-permute-start(bf16[768,128]{1,0:T(8,128)(2,1)S(1)} %get-tuple-element.26), channel_id=1, source_target_pairs={{0,1},{1,0},{2,3},{3,2},{4,5},{5,4},{6,7},{7,6},{8,9},{9,8},{10,11... | collective-permute-start | bytes 589832 | tf_op jit(solution)/shard_map/ppermute | solution.py:34
  30.6 5.7 %collective-permute-start.7 = (bf16[768,128]{1,0:T(8,128)(2,1)S(1)}, bf16[768,128]{1,0:T(8,128)(2,1)S(1)}, u32[]{:S(2)}, u32[]{:S(2)}) collective-permute-start(bf16[768,128]{1,0:T(8,128)(2,1)S(1)} %first_filter.1.refs_0_.first), channel_id=1, source_target_pairs={{0,8},{4,12},{8,0},{12,4},{1,9},{5,13},{9,1},{13,5},{2,10},{6,14},... | collective-permute-start | bytes 589832 | tf_op jit(solution)/shard_map/ppermute | solution.py:34
  32.3 4.1 %collective-permute-start.6 = (bf16[768,128]{1,0:T(8,128)(2,1)S(1)}, bf16[768,128]{1,0:T(8,128)(2,1)S(1)}, u32[]{:S(2)}, u32[]{:S(2)}) collective-permute-start(bf16[768,128]{1,0:T(8,128)(2,1)S(1)} %first_filter.1.refs_0_.first), channel_id=1, source_target_pairs={{0,4},{4,0},{8,12},{12,8},{1,5},{5,1},{9,13},{13,9},{2,6},{6,2},{1... | collective-permute-start | bytes 589832 | tf_op jit(solution)/shard_map/ppermute | solution.py:34
  36.4 1.4 %collective-permute-start.8 = (bf16[768,128]{1,0:T(8,128)(2,1)S(1)}, bf16[768,128]{1,0:T(8,128)(2,1)S(1)}, u32[]{:S(2)}, u32[]{:S(2)}) collective-permute-start(bf16[768,128]{1,0:T(8,128)(2,1)S(1)} %collective-permute-done.7.refs_2_), channel_id=1, source_target_pairs={{0,4},{4,0},{8,12},{12,8},{1,5},{5,1},{9,13},{13,9},{2,6},{6,2},{1... | collective-permute-start | bytes 589832 | tf_op jit(solution)/shard_map/ppermute | solution.py:34
  39.1 7.0 %collective-permute-start.9 = (bf16[768,128]{1,0:T(8,128)(2,1)S(1)}, bf16[768,128]{1,0:T(8,128)(2,1)S(1)}, u32[]{:S(2)}, u32[]{:S(2)}) collective-permute-start(bf16[768,128]{1,0:T(8,128)(2,1)S(1)} %product.7), channel_id=1, source_target_pairs={{0,1},{1,0},{2,3},{3,2},{4,5},{5,4},{6,7},{7,6},{8,9},{9,8},{10,11... | collective-permute-start | bytes 589832 | tf_op jit(solution)/shard_map/ppermute | solution.py:34
  46.1 12.3 %collective-permute-start.10 = (bf16[768,128]{1,0:T(8,128)(2,1)S(1)}, bf16[768,128]{1,0:T(8,128)(2,1)S(1)}, u32[]{:S(2)}, u32[]{:S(2)}) collective-permute-start(bf16[768,128]{1,0:T(8,128)(2,1)S(1)} %get-tuple-element.30), channel_id=1, source_target_pairs={{0,2},{1,3},{2,0},{3,1},{4,6},{5,7},{6,4},{7,5},{8,10},{9,11},{10,... | collective-permute-start | bytes 589832 | tf_op jit(solution)/shard_map/ppermute | solution.py:34
  49.4 9.4 %collective-permute-start.11 = (bf16[768,128]{1,0:T(8,128)(2,1)S(1)}, bf16[768,128]{1,0:T(8,128)(2,1)S(1)}, u32[]{:S(2)}, u32[]{:S(2)}) collective-permute-start(bf16[768,128]{1,0:T(8,128)(2,1)S(1)} %get-tuple-element.31), channel_id=1, source_target_pairs={{0,1},{1,0},{2,3},{3,2},{4,5},{5,4},{6,7},{7,6},{8,9},{9,8},{10,11... | collective-permute-start | bytes 589832 | tf_op jit(solution)/shard_map/ppermute | solution.py:34
  59.3 1.3 %collective-permute-start.12 = (f32[96,128]{1,0:T(8,128)S(1)}, f32[96,128]{1,0:T(8,128)S(1)}, u32[]{:S(2)}, u32[]{:S(2)}) collective-permute-start(f32[96,128]{1,0:T(8,128)S(1)} %get-tuple-element.33), channel_id=1, source_target_pairs={{0,4},{4,0},{8,12},{12,8},{1,5},{5,1},{9,13},{13,9},{2,6},{6,2},{1... | collective-permute-start | bytes 147464 | tf_op jit(solution)/shard_map/ppermute | solution.py:34
  60.6 4.2 %collective-permute-start.13 = (f32[96,128]{1,0:T(8,128)S(1)}, f32[96,128]{1,0:T(8,128)S(1)}, u32[]{:S(2)}, u32[]{:S(2)}) collective-permute-start(f32[96,128]{1,0:T(8,128)S(1)} %add.17), channel_id=1, source_target_pairs={{0,8},{4,12},{8,0},{12,4},{1,9},{5,13},{9,1},{13,5},{2,10},{6,14},... | collective-permute-start | bytes 147464 | tf_op jit(solution)/shard_map/ppermute | solution.py:34
  64.7 6.0 %collective-permute-start.16 = (f32[96,128]{1,0:T(8,128)S(1)}, f32[96,128]{1,0:T(8,128)S(1)}, u32[]{:S(2)}, u32[]{:S(2)}) collective-permute-start(f32[96,128]{1,0:T(8,128)S(1)} %add.18), channel_id=1, source_target_pairs={{0,3},{1,2},{2,1},{3,0},{4,7},{5,6},{6,5},{7,4},{8,11},{9,10},{10,... | collective-permute-start | bytes 147464 | tf_op jit(solution)/shard_map/ppermute | solution.py:34
  67.8 5.0 %collective-permute-start.15 = (f32[96,128]{1,0:T(8,128)S(1)}, f32[96,128]{1,0:T(8,128)S(1)}, u32[]{:S(2)}, u32[]{:S(2)}) collective-permute-start(f32[96,128]{1,0:T(8,128)S(1)} %add.18), channel_id=1, source_target_pairs={{0,2},{1,3},{2,0},{3,1},{4,6},{5,7},{6,4},{7,5},{8,10},{9,11},{10,... | collective-permute-start | bytes 147464 | tf_op jit(solution)/shard_map/ppermute | solution.py:34
  67.8 5.0 %collective-permute-start.14 = (f32[96,128]{1,0:T(8,128)S(1)}, f32[96,128]{1,0:T(8,128)S(1)}, u32[]{:S(2)}, u32[]{:S(2)}) collective-permute-start(f32[96,128]{1,0:T(8,128)S(1)} %add.18), channel_id=1, source_target_pairs={{0,1},{1,0},{2,3},{3,2},{4,5},{5,4},{6,7},{7,6},{8,9},{9,8},{10,11... | collective-permute-start | bytes 147464 | tf_op jit(solution)/shard_map/ppermute | solution.py:34
  72.8 1.3 %collective-permute-start.17 = (f32[96,128]{1,0:T(8,128)S(1)}, f32[96,128]{1,0:T(8,128)S(1)}, u32[]{:S(2)}, u32[]{:S(2)}) collective-permute-start(f32[96,128]{1,0:T(8,128)S(1)} %add_add_fusion.keep_ref), channel_id=1, source_target_pairs={{0,4},{4,0},{8,12},{12,8},{1,5},{5,1},{9,13},{13,9},{2,6},{6,2},{1... | collective-permute-start | bytes 147464 | tf_op jit(solution)/shard_map/ppermute | solution.py:34

commit v3 on v2

--- a/solution.py
+++ b/solution.py
@@ -10,6 +10,8 @@
 LANES = 128
 SIZE = LANES // 2
 PIVOTS = 8
+GIGA = 10**9
+COSTS = ((3, 1, 3), (3, 1, 0))
 F32 = jnp.float32
 BF16 = jnp.bfloat16
 VMEM = pl.BlockSpec(memory_space=pltpu.VMEM)
@@ -35,6 +37,10 @@
 
 
 def gather_shards(own, twin):
+    return list(zip(*(gather_one(*x) for x in zip(own, twin))))
+
+
+def gather_one(own, twin):
     shards = {0: own}
     bit = lax.axis_size("row") // 2
     while bit:
@@ -45,22 +51,24 @@
     return [shards[key] for key in range(len(shards))]
 
 
-def pack_kernel(turned_ref, out):
+def pack_kernel(turned_ref, wide_out, thin_out):
     rows = turned_ref.shape[1]
     half = rows // 2
     turned = turned_ref[...].astype(F32)
-    out[pl.ds(0, rows), :] = turned[:LANES].T.astype(BF16)
+    wide_out[...] = turned[:LANES].T.astype(BF16)
     thin = jnp.concatenate([turned[LANES:, :half], turned[LANES:, half:]], axis=0)
-    out[pl.ds(rows, half), :] = thin.T.astype(BF16)
-
-
-def load_kernel(own_blocks, orbitals, vec_ref, ids_ref, ham_ref, out, at_out):
-    out[...] = vec_ref[...]
+    thin_out[...] = thin.T.astype(BF16)
+
+
+def load_kernel(own_blocks, orbitals, wide_ref, thin_ref, ids_ref, ham_ref, wide_out, thin_out, at_out):
+    wide_out[...] = wide_ref[...]
+    thin_out[...] = thin_ref[...]
     at_out[...] = (ids_ref[...] ^ (lax.axis_index("row") * own_blocks)) * orbitals
 
 
 def product_kernel(keys, n_row, own_blocks, at_ref, ham_ref, *refs):
-    parts, outs = refs[:n_row], refs[n_row : n_row + len(keys)]
+    wide, thin = refs[:n_row], refs[n_row : 2 * n_row]
+    wide_out, thin_out = refs[2 * n_row : 2 * n_row + len(keys)], refs[2 * n_row + len(keys) : -1]
     source = refs[-1]
     orbitals = ham_ref.shape[1]
     rows = own_blocks * orbitals
@@ -70,11 +78,11 @@
     low_lane = lax.broadcasted_iota(jnp.int32, (orbitals, LANES), 1) < SIZE
     for key in range(n_row):
         base = key * rows
-        source[pl.ds(base, rows), pl.ds(0, LANES)] = parts[key][pl.ds(0, rows), :]
-        thin = parts[key][pl.ds(rows, half), :]
-        source[pl.ds(base, half), pl.ds(LANES, LANES)] = thin
+        source[pl.ds(base, rows), pl.ds(0, LANES)] = wide[key][...]
+        packed = thin[key][...]
+        source[pl.ds(base, half), pl.ds(LANES, LANES)] = packed
         source[pl.ds(base + half, half), pl.ds(LANES, LANES)] = jnp.concatenate(
-            [thin[:, SIZE:], thin[:, :SIZE]], axis=1
+            [packed[:, SIZE:], packed[:, :SIZE]], axis=1
         )
 
     def term(i, block):
@@ -88,52 +96,73 @@
             preferred_element_type=F32,
         )
 
-    for i, out in enumerate(outs):
+    for i in range(len(keys)):
         for block in range(own_blocks // 2):
             upper, lower = term(i, block), term(i, block + own_blocks // 2)
-            out[pl.ds(block * orbitals, orbitals), :] = upper[:, :LANES].astype(BF16)
-            out[pl.ds(half + block * orbitals, orbitals), :] = lower[:, :LANES].astype(BF16)
+            at = pl.ds(block * orbitals, orbitals)
+            wide_out[i][at, :] = upper[:, :LANES].astype(BF16)
+            wide_out[i][pl.ds(half + block * orbitals, orbitals), :] = lower[:, :LANES].astype(BF16)
             turned = jnp.concatenate([lower[:, LANES + SIZE :], lower[:, LANES : LANES + SIZE]], axis=1)
-            out[pl.ds(rows + block * orbitals, orbitals), :] = jnp.where(
-                low_lane, upper[:, LANES:], turned
-            ).astype(BF16)
+            thin_out[i][at, :] = jnp.where(low_lane, upper[:, LANES:], turned).astype(BF16)
 
 
 def product(keys, own_blocks, at, ham, parts):
     n_row = len(parts)
     orbitals = ham.shape[1]
     flops = 4 * own_blocks * len(keys) * orbitals * ham.shape[2] * LANES
-    return call(
+    wide, thin = zip(*parts)
+    outs = call(
         functools.partial(product_kernel, keys, n_row, own_blocks),
-        [jax.ShapeDtypeStruct(parts[0].shape, BF16)] * len(keys),
-        [SMEM, VMEM] + [VMEM] * n_row,
+        [jax.ShapeDtypeStruct(x.shape, BF16) for x in parts[0] for _ in keys],
+        [SMEM, VMEM] + [VMEM] * (2 * n_row),
         [pltpu.VMEM((own_blocks * n_row * orbitals, 2 * LANES), BF16)],
         flops=flops,
         name="product",
-    )(at, ham, *parts)
-
-
-def add_kernel(a, b, later, out, later_out):
-    out[...] = (a[...].astype(F32) + b[...].astype(F32)).astype(BF16)
-    later_out[...] = later[...]
-
-
-def add(a, b, later):
-    shape = jax.ShapeDtypeStruct(a.shape, BF16)
-    return call(add_kernel, [shape, shape], [VMEM] * 3, name="add")(a, b, later)
-
-
-def summands(own_blocks, at, ham, parts):
+    )(at, ham, *wide, *thin)
+    return list(zip(outs[: len(keys)], outs[len(keys) :]))
+
+
+def add_kernel(a, b, *refs):
+    count = len(refs) // 2
+    refs[count][...] = (a[...].astype(F32) + b[...].astype(F32)).astype(BF16)
+    for later, out in zip(refs[:count], refs[count + 1 :]):
+        out[...] = later[...]
+
+
+def add(a, b, *later, after=(), flops=1000):
+    shapes = [jax.ShapeDtypeStruct(x.shape, BF16) for x in (a, *later)]
+    count = len(after)
+    kernel = lambda *refs: add_kernel(*refs[count:])
+    specs = [VMEM] * (count + 2 + len(later))
+    return call(kernel, shapes, specs, flops=flops, name="add")(*after, a, b, *later)
+
+
+def partial_kernel(a, b, out):
+    out[...] = a[...].astype(F32) + b[...].astype(F32)
+
+
+def partial_sum(a, b, flops):
+    shape = jax.ShapeDtypeStruct(a.shape, F32)
+    return call(partial_kernel, shape, [VMEM] * 2, flops=flops, name="partial_sum")(a, b)
+
+
+def summands(own_blocks, at, ham, parts, costs):
     n_col = lax.axis_size("col")
     if n_col != 4:
         terms = product(tuple(range(n_col)), own_blocks, at, ham, parts)
-        return [terms[0]] + [swap(terms[key], "col", key) for key in range(1, n_col)]
-    (far,) = product((3,), own_blocks, at, ham, parts)
-    other = swap(far, "col", 1)
+        sent = [[swap(x, "col", key) for x in terms[key]] for key in range(1, n_col)]
+        return list(zip(terms[0], *sent))
+    ((wide, thin),) = product((3,), own_blocks, at, ham, parts)
+    wide, thin = swap(wide, "col", 1), swap(thin, "col", 1)
     across, near, own = product((2, 1, 0), own_blocks, at, ham, parts)
-    across, near = add(across, other, near)
-    near = swap(near, "col", 1)
-    return [own, swap(across, "col", 2), near]
+    (wide,) = add(across[0], wide)
+    thin, *near = add(across[1], thin, *near, after=[wide], flops=costs[0] * GIGA + 1000)
+    near = [swap(x, "col", 1) for x in near]
+    across = [swap(x, "col", 2) for x in (wide, thin)]
+    sums = [
+        partial_sum(a, b, cost * GIGA + 1000) for a, b, cost in zip(own, across, costs[1:])
+    ]
+    return list(zip(sums, near))
 
 
 def ends(lower_ref, upper_ref, shape):
@@ -159,15 +188,18 @@
     return lax.dot_general(a, b, (((0,), (0,)), ((), ())), preferred_element_type=F32)
 
 
-def second_kernel(rows_all, lower_ref, upper_ref, start, first, *refs):
-    out, keep_out, send_out, gram = refs[-4:]
+def second_kernel(rows_all, lower_ref, upper_ref, *refs):
+    wide_out, thin_out, keep_out, send_out, gram = refs[-5:]
+    count = (len(refs) - 5) // 2
     center, scale = ends(lower_ref, upper_ref, (1, LANES))
-    moved = total_of(refs[:-4]) - center * first[...].astype(F32)
-    filtered = (2.0 * moved * scale - start[...].astype(F32)).astype(BF16)
-    out[...] = filtered
-    rows = out.shape[0] * 2 // 3
-    half = rows // 2
-    wide, thin = filtered[:rows], filtered[rows:]
+    for out, (start, first, *terms) in (
+        (wide_out, refs[:count]),
+        (thin_out, refs[count : 2 * count]),
+    ):
+        moved = total_of(terms) - center * first[...].astype(F32)
+        out[...] = (2.0 * moved * scale - start[...].astype(F32)).astype(BF16)
+    wide, thin = wide_out[...], thin_out[...]
+    half = thin.shape[0]
     inv = 1.0 / rows_all
     aa = cross(wide, wide) * inv
     upper = cross(thin, wide[:half]) * inv
@@ -228,7 +260,7 @@
     return out[:, size:]
 
 
-def last_kernel(pivots, keep_ref, other_ref, vec_ref, out_ref, gram, factor):
+def last_kernel(pivots, keep_ref, other_ref, wide_ref, thin_ref, out_ref, gram, factor):
     size = LANES // 2
     part = 3 * size // 2
     mine = lax.axis_index("row") & 1
@@ -273,8 +305,8 @@
             low, vec, con, preferred_element_type=F32
         )
 
-    rows = out_ref.shape[1]
-    wide, thin = vec_ref[pl.ds(0, rows), :], vec_ref[pl.ds(rows, rows // 2), :]
+    wide, thin = wide_ref[...], thin_ref[...]
+    half = thin.shape[0]
     main = apply(factor[...], wide)
     out_ref[pl.ds(0, 2 * size), :] = main[: 2 * size]
     tail = jnp.concatenate(
@@ -304,37 +336,41 @@
     orbitals = hamiltonian.shape[1]
     own_blocks = rows // orbitals
     rows_all = rows * lax.axis_size("col") * lax.axis_size("row")
-    shape = jax.ShapeDtypeStruct((rows + rows // 2, LANES), BF16)
+    shapes = [jax.ShapeDtypeStruct((x, LANES), BF16) for x in (rows, rows // 2)]
     half_gram = jax.ShapeDtypeStruct((3 * SIZE // 2, LANES), F32)
     gram = pltpu.VMEM((3 * SIZE, LANES), F32)
 
-    start = call(pack_kernel, shape, [VMEM], name="pack")(vectors.T)
-    twin, at = call(
+    start = call(pack_kernel, shapes, [VMEM], name="pack")(vectors.T)
+    *twin, at = call(
         functools.partial(load_kernel, own_blocks, orbitals),
-        [shape, jax.ShapeDtypeStruct(columns.shape[::-1], jnp.int32)],
-        [VMEM, VMEM, VMEM],
+        [*shapes, jax.ShapeDtypeStruct(columns.shape[::-1], jnp.int32)],
+        [VMEM] * 4,
         name="load",
-    )(start, columns.T, hamiltonian)
-    terms = summands(own_blocks, at, hamiltonian, gather_shards(start, twin))
-    first = call(
-        first_kernel, shape, [SMEM, SMEM] + [VMEM] * (1 + len(terms)), name="first_filter"
-    )(lower, upper, start, *terms)
-    terms = summands(own_blocks, at, hamiltonian, gather_shards(first, first))
-    second, keep, send = call(
+    )(*start, columns.T, hamiltonian)
+    terms = summands(own_blocks, at, hamiltonian, gather_shards(start, twin), COSTS[0])
+    first = [
+        call(first_kernel, shape, [SMEM, SMEM] + [VMEM] * (1 + len(x)), name="first_filter")(
+            lower, upper, vec, *x
+        )
+        for shape, vec, x in zip(shapes, start, terms)
+    ]
+    terms = summands(own_blocks, at, hamiltonian, gather_shards(first, first), COSTS[1])
+    operands = [x for each in zip(start, first, terms) for x in (each[0], each[1], *each[2])]
+    wide, thin, keep, send = call(
         functools.partial(second_kernel, rows_all),
-        [shape, half_gram, half_gram],
-        [SMEM, SMEM] + [VMEM] * (2 + len(terms)),
+        [*shapes, half_gram, half_gram],
+        [SMEM, SMEM] + [VMEM] * len(operands),
         [gram],
         name="second_filter",
-    )(lower, upper, start, first, *terms)
+    )(lower, upper, *operands)
     keep, other = sum_all(keep, send)
     basis = call(
         functools.partial(last_kernel, PIVOTS),
         jax.ShapeDtypeStruct((LANES + SIZE, rows), F32),
-        [VMEM] * 3,
+        [VMEM] * 4,
         [gram, gram],
         name="orthonormalize",
-    )(keep, other, second)
+    )(keep, other, wide, thin)
     return basis.T
 
 

time: 83.1 us -> 79.7 us (0.959)
  waiting for transfers between devices: 38.9 us -> 30.6 us
  starting transfers between devices: 23.8 us -> 28.5 us
    ppermute x18 -> x30, waiting for transfers between devices: 38.9 us -> 30.6 us  [swap(): return lax.ppermute(x, axis, [(i, i ^ key) for i in range(count)])]
    ppermute x18 -> x30, starting transfers between devices: 23.8 us -> 28.5 us  [swap(): return lax.ppermute(x, axis, [(i, i ^ key) for i in range(count)])]
  transfers between devices with their start and end apart: 18 -> 30, of which waited for: 15 -> 18; matrix products, arithmetic and copies ran while one was open for 0% -> 0% of each run, Pallas kernels for 4% -> 5%
where the time goes in v3:
time: 79.7 us; the launch traced here: 79.5 us
  waiting for transfers between devices  30.6 us (38%)
  starting transfers between devices  28.5 us (36%)
  Pallas kernels  15.9 us (20%)
  local copies, waits for them, and re-layouts  3.02 us (4%)
  between operations  1.44 us (2%)
    ppermute x30, waiting for transfers between devices, swap(): return lax.ppermute(x, axis, [(i, i ^ key) for i in range(count)])  30.6 us
    ppermute x30, starting transfers between devices, swap(): return lax.ppermute(x, axis, [(i, i ^ key) for i in range(count)])  28.5 us
    pallas_call x1, Pallas kernels, per_device(): call(functools.partial(last_kernel, PIVOTS), jax.ShapeDtypeStruct((LANES...  8.83 us
    pallas_call x4, Pallas kernels, product(): call(functools.partial(product_kernel, keys, n_row, own_blocks), [jax.Sha...  6.16 us
    unnamed x8, local copies, waits for them, and re-layouts  3.02 us
  transfers between devices with their start and end apart: 30, of which 18 were waited for; matrix products, arithmetic and copies ran while one was open for 0% of the time, Pallas kernels for 5%

profile of v3, /device:TPU:0, one launch (start us, length us, event | category | flops | bytes accessed | tf_op | source)
XLA Modules:
  0.0 79.5 jit_solution(5257295286454198778)
XLA Ops:
  1.1 3.0 %collective-permute-start.1 = (bf16[512,128]{1,0:T(8,128)(2,1)S(1)}, bf16[512,128]{1,0:T(8,128)(2,1)S(1)}, u32[]{:S(2)}, u32[]{:S(2)}) collective-permute-start(bf16[512,128]{1,0:T(8,128)(2,1)S(1)} %get-tuple-element.36.wide_ref.refs_0_.start), channel_id=1, source_target_pairs={{0,8},{4,12},{8,0},{12,4},{1,9},{5,13},{9,1},{13,5},{2,10},{6,14},... | collective-permute-start | bytes 393224 | tf_op jit(solution)/shard_map/ppermute | solution.py:36
  4.2 1.4 %copy-done = bf16[32,64,384]{2,1,0:T(8,128)(2,1)S(1)} copy-done((bf16[32,64,384]{2,1,0:T(8,128)(2,1)S(1)}, bf16[32,64,384]{2,1,0:T(8,128)(2,1)}, u32[]{:S(2)}) %copy-start) | copy-done | bytes 1572888
  6.4 1.9 %collective-permute-done.1.refs_2_ = bf16[512,128]{1,0:T(8,128)(2,1)S(1)} collective-permute-done((bf16[512,128]{1,0:T(8,128)(2,1)S(1)}, bf16[512,128]{1,0:T(8,128)(2,1)S(1)}, u32[]{:S(2)}, u32[]{:S(2)}) %collective-permute-start.1) | collective-permute-done | bytes 131104 | tf_op jit(solution)/shard_map/ppermute | solution.py:36
  10.3 1.3 %product.5 = (bf16[512,128]{1,0:T(8,128)(2,1)S(1)}, bf16[256,128]{1,0:T(8,128)(2,1)S(1)}) custom-call(s32[6,32]{1,0:T(8,128)S(1)} %get-tuple-element.38.at_ref, bf16[32,64,384]{2,1,0:T(8,128)(2,1)S(1)} %copy-done.1, bf16[512,128]{1,0:T(8,128)(2,1)S(1)} %get-tuple-element.36.wide_ref.refs_0_.start, bf16[512,128]{1,0:T(8,128)(2,1)S(1)} %collective-permute-done.refs_1_, ...), custom_call_target="tpu_custom_call" | custom-call | flops 100663296 | bytes 1000 | tf_op jit(solution)/shard_map/product/pallas_call | solution.py:114
  11.5 1.9 %collective-permute-start.6 = (bf16[512,128]{1,0:T(8,128)(2,1)S(1)}, bf16[512,128]{1,0:T(8,128)(2,1)S(1)}, u32[]{:S(2)}, u32[]{:S(2)}) collective-permute-start(bf16[512,128]{1,0:T(8,128)(2,1)S(1)} %get-tuple-element.43), channel_id=1, source_target_pairs={{0,1},{1,0},{2,3},{3,2},{4,5},{5,4},{6,7},{7,6},{8,9},{9,8},{10,11... | collective-permute-start | bytes 393224 | tf_op jit(solution)/shard_map/ppermute | solution.py:36
  13.6 1.8 %product.4 = (bf16[512,128]{1,0:T(8,128)(2,1)S(1)}, bf16[512,128]{1,0:T(8,128)(2,1)S(1)}, bf16[512,128]{1,0:T(8,128)(2,1)S(1)}, bf16[256,128]{1,0:T(8,128)(2,1)S...) custom-call(s32[6,32]{1,0:T(8,128)S(1)} %get-tuple-element.38.at_ref, ...), custom_call_target="tpu_custom_call" | custom-call | flops 301989888 | bytes 1000 | tf_op jit(solution)/shard_map/product/pallas_call | solution.py:114
  15.4 2.5 %collective-permute-done.6.refs_1_ = bf16[512,128]{1,0:T(8,128)(2,1)S(1)} collective-permute-done((bf16[512,128]{1,0:T(8,128)(2,1)S(1)}, bf16[512,128]{1,0:T(8,128)(2,1)S(1)}, u32[]{:S(2)}, u32[]{:S(2)}) %collective-permute-start.6) | collective-permute-done | bytes 131104 | tf_op jit(solution)/shard_map/ppermute | solution.py:36
  17.9 2.8 %collective-permute-start.7 = (bf16[512,128]{1,0:T(8,128)(2,1)S(1)}, bf16[512,128]{1,0:T(8,128)(2,1)S(1)}, u32[]{:S(2)}, u32[]{:S(2)}) collective-permute-start(bf16[512,128]{1,0:T(8,128)(2,1)S(1)} %add.27.refs_0_), channel_id=1, source_target_pairs={{0,2},{1,3},{2,0},{3,1},{4,6},{5,7},{6,4},{7,5},{8,10},{9,11},{10,... | collective-permute-start | bytes 393224 | tf_op jit(solution)/shard_map/ppermute | solution.py:36
  20.8 1.6 %collective-permute-start.9 = (bf16[512,128]{1,0:T(8,128)(2,1)S(1)}, bf16[512,128]{1,0:T(8,128)(2,1)S(1)}, u32[]{:S(2)}, u32[]{:S(2)}) collective-permute-start(bf16[512,128]{1,0:T(8,128)(2,1)S(1)} %get-tuple-element.48), channel_id=1, source_target_pairs={{0,1},{1,0},{2,3},{3,2},{4,5},{5,4},{6,7},{7,6},{8,9},{9,8},{10,11... | collective-permute-start | bytes 393224 | tf_op jit(solution)/shard_map/ppermute | solution.py:36
  24.8 2.0 %collective-permute-done.7.b = bf16[512,128]{1,0:T(8,128)(2,1)S(1)} collective-permute-done((bf16[512,128]{1,0:T(8,128)(2,1)S(1)}, bf16[512,128]{1,0:T(8,128)(2,1)S(1)}, u32[]{:S(2)}, u32[]{:S(2)}) %collective-permute-start.7) | collective-permute-done | bytes 131104 | tf_op jit(solution)/shard_map/ppermute | solution.py:36
  26.9 1.7 %collective-permute-start.11 = (bf16[512,128]{1,0:T(8,128)(2,1)S(1)}, bf16[512,128]{1,0:T(8,128)(2,1)S(1)}, u32[]{:S(2)}, u32[]{:S(2)}) collective-permute-start(bf16[512,128]{1,0:T(8,128)(2,1)S(1)} %first_filter.2.refs_0_.refs_1_), channel_id=1, source_target_pairs={{0,8},{4,12},{8,0},{12,4},{1,9},{5,13},{9,1},{13,5},{2,10},{6,14},... | collective-permute-start | bytes 393224 | tf_op jit(solution)/shard_map/ppermute | solution.py:36
  28.6 1.0 %collective-permute-done.13.b = bf16[256,128]{1,0:T(8,128)(2,1)S(1)} collective-permute-done((bf16[256,128]{1,0:T(8,128)(2,1)S(1)}, bf16[256,128]{1,0:T(8,128)(2,1)S(1)}, u32[]{:S(2)}, u32[]{:S(2)}) %collective-permute-start.13) | collective-permute-done | bytes 65568 | tf_op jit(solution)/shard_map/ppermute | solution.py:36
  29.7 1.6 %collective-permute-start.16 = (bf16[256,128]{1,0:T(8,128)(2,1)S(1)}, bf16[256,128]{1,0:T(8,128)(2,1)S(1)}, u32[]{:S(2)}, u32[]{:S(2)}) collective-permute-start(bf16[256,128]{1,0:T(8,128)(2,1)S(1)} %first_filter.3.refs_4_.refs_5_), channel_id=1, source_target_pairs={{0,8},{4,12},{8,0},{12,4},{1,9},{5,13},{9,1},{13,5},{2,10},{6,14},... | collective-permute-start | bytes 196616 | tf_op jit(solution)/shard_map/ppermute | solution.py:36
  32.8 1.3 %collective-permute-done.16.refs_6_ = bf16[256,128]{1,0:T(8,128)(2,1)S(1)} collective-permute-done((bf16[256,128]{1,0:T(8,128)(2,1)S(1)}, bf16[256,128]{1,0:T(8,128)(2,1)S(1)}, u32[]{:S(2)}, u32[]{:S(2)}) %collective-permute-start.16) | collective-permute-done | bytes 65568 | tf_op jit(solution)/shard_map/ppermute | solution.py:36
  34.1 1.2 %collective-permute-done.17.refs_7_ = bf16[256,128]{1,0:T(8,128)(2,1)S(1)} collective-permute-done((bf16[256,128]{1,0:T(8,128)(2,1)S(1)}, bf16[256,128]{1,0:T(8,128)(2,1)S(1)}, u32[]{:S(2)}, u32[]{:S(2)}) %collective-permute-start.17) | collective-permute-done | bytes 65568 | tf_op jit(solution)/shard_map/ppermute | solution.py:36
  35.3 1.2 %product.7 = (bf16[512,128]{1,0:T(8,128)(2,1)S(1)}, bf16[256,128]{1,0:T(8,128)(2,1)S(1)}) custom-call(s32[6,32]{1,0:T(8,128)S(1)} %get-tuple-element.38.at_ref, bf16[32,64,384]{2,1,0:T(8,128)(2,1)S(1)} %copy-done.1, bf16[512,128]{1,0:T(8,128)(2,1)S(1)} %first_filter.2.refs_0_.refs_1_, bf16[512,128]{1,0:T(8,128)(2,1)S(1)} %collective-permute-done.10.refs_1_, ...), custom_call_target="tpu_custom_call" | custom-call | flops 100663296 | bytes 1000 | tf_op jit(solution)/shard_map/product/pallas_call | solution.py:114
  36.6 1.1 %collective-permute-start.18 = (bf16[512,128]{1,0:T(8,128)(2,1)S(1)}, bf16[512,128]{1,0:T(8,128)(2,1)S(1)}, u32[]{:S(2)}, u32[]{:S(2)}) collective-permute-start(bf16[512,128]{1,0:T(8,128)(2,1)S(1)} %get-tuple-element.54), channel_id=1, source_target_pairs={{0,1},{1,0},{2,3},{3,2},{4,5},{5,4},{6,7},{7,6},{8,9},{9,8},{10,11... | collective-permute-start | bytes 393224 | tf_op jit(solution)/shard_map/ppermute | solution.py:36
  37.7 1.0 %collective-permute-start.20 = (bf16[256,128]{1,0:T(8,128)(2,1)S(1)}, bf16[256,128]{1,0:T(8,128)(2,1)S(1)}, u32[]{:S(2)}, u32[]{:S(2)}) collective-permute-start(bf16[256,128]{1,0:T(8,128)(2,1)S(1)} %get-tuple-element.56), channel_id=1, source_target_pairs={{0,1},{1,0},{2,3},{3,2},{4,5},{5,4},{6,7},{7,6},{8,9},{9,8},{10,11... | collective-permute-start | bytes 196616 | tf_op jit(solution)/shard_map/ppermute | solution.py:36
  38.7 1.8 %product.6 = (bf16[512,128]{1,0:T(8,128)(2,1)S(1)}, bf16[512,128]{1,0:T(8,128)(2,1)S(1)}, bf16[512,128]{1,0:T(8,128)(2,1)S(1)}, bf16[256,128]{1,0:T(8,128)(2,1)S...) custom-call(s32[6,32]{1,0:T(8,128)S(1)} %get-tuple-element.38.at_ref, ...), custom_call_target="tpu_custom_call" | custom-call | flops 301989888 | bytes 1000 | tf_op jit(solution)/shard_map/product/pallas_call | solution.py:114
  40.5 2.4 %collective-permute-done.18.refs_1_ = bf16[512,128]{1,0:T(8,128)(2,1)S(1)} collective-permute-done((bf16[512,128]{1,0:T(8,128)(2,1)S(1)}, bf16[512,128]{1,0:T(8,128)(2,1)S(1)}, u32[]{:S(2)}, u32[]{:S(2)}) %collective-permute-start.18) | collective-permute-done | bytes 131104 | tf_op jit(solution)/shard_map/ppermute | solution.py:36
  42.9 2.1 %collective-permute-start.19 = (bf16[512,128]{1,0:T(8,128)(2,1)S(1)}, bf16[512,128]{1,0:T(8,128)(2,1)S(1)}, u32[]{:S(2)}, u32[]{:S(2)}) collective-permute-start(bf16[512,128]{1,0:T(8,128)(2,1)S(1)} %add.29.refs_0_), channel_id=1, source_target_pairs={{0,2},{1,3},{2,0},{3,1},{4,6},{5,7},{6,4},{7,5},{8,10},{9,11},{10,... | collective-permute-start | bytes 393224 | tf_op jit(solution)/shard_map/ppermute | solution.py:36
  46.0 1.7 %collective-permute-start.21 = (bf16[512,128]{1,0:T(8,128)(2,1)S(1)}, bf16[512,128]{1,0:T(8,128)(2,1)S(1)}, u32[]{:S(2)}, u32[]{:S(2)}) collective-permute-start(bf16[512,128]{1,0:T(8,128)(2,1)S(1)} %get-tuple-element.59), channel_id=1, source_target_pairs={{0,1},{1,0},{2,3},{3,2},{4,5},{5,4},{6,7},{7,6},{8,9},{9,8},{10,11... | collective-permute-start | bytes 393224 | tf_op jit(solution)/shard_map/ppermute | solution.py:36
  48.1 5.6 %collective-permute-done.22.b = bf16[256,128]{1,0:T(8,128)(2,1)S(1)} collective-permute-done((bf16[256,128]{1,0:T(8,128)(2,1)S(1)}, bf16[256,128]{1,0:T(8,128)(2,1)S(1)}, u32[]{:S(2)}, u32[]{:S(2)}) %collective-permute-start.22) | collective-permute-done | bytes 65568 | tf_op jit(solution)/shard_map/ppermute | solution.py:36
  53.7 1.3 %collective-permute-done.23.refs_7_ = bf16[256,128]{1,0:T(8,128)(2,1)S(1)} collective-permute-done((bf16[256,128]{1,0:T(8,128)(2,1)S(1)}, bf16[256,128]{1,0:T(8,128)(2,1)S(1)}, u32[]{:S(2)}, u32[]{:S(2)}) %collective-permute-start.23) | collective-permute-done | bytes 65568 | tf_op jit(solution)/shard_map/ppermute | solution.py:36
  55.5 1.2 %collective-permute-done.24 = f32[96,128]{1,0:T(8,128)S(1)} collective-permute-done((f32[96,128]{1,0:T(8,128)S(1)}, f32[96,128]{1,0:T(8,128)S(1)}, u32[]{:S(2)}, u32[]{:S(2)}) %collective-permute-start.24) | collective-permute-done | bytes 49184 | tf_op jit(solution)/shard_map/ppermute | solution.py:36
  56.7 1.6 %collective-permute-start.25 = (f32[96,128]{1,0:T(8,128)S(1)}, f32[96,128]{1,0:T(8,128)S(1)}, u32[]{:S(2)}, u32[]{:S(2)}) collective-permute-start(f32[96,128]{1,0:T(8,128)S(1)} %add.19), channel_id=1, source_target_pairs={{0,8},{4,12},{8,0},{12,4},{1,9},{5,13},{9,1},{13,5},{2,10},{6,14},... | collective-permute-start | bytes 147464 | tf_op jit(solution)/shard_map/ppermute | solution.py:36
  58.3 2.6 %collective-permute-done.25 = f32[96,128]{1,0:T(8,128)S(1)} collective-permute-done((f32[96,128]{1,0:T(8,128)S(1)}, f32[96,128]{1,0:T(8,128)S(1)}, u32[]{:S(2)}, u32[]{:S(2)}) %collective-permute-start.25) | collective-permute-done | bytes 49184 | tf_op jit(solution)/shard_map/ppermute | solution.py:36
  60.9 3.5 %collective-permute-start.28 = (f32[96,128]{1,0:T(8,128)S(1)}, f32[96,128]{1,0:T(8,128)S(1)}, u32[]{:S(2)}, u32[]{:S(2)}) collective-permute-start(f32[96,128]{1,0:T(8,128)S(1)} %add.20), channel_id=1, source_target_pairs={{0,3},{1,2},{2,1},{3,0},{4,7},{5,6},{6,5},{7,4},{8,11},{9,10},{10,... | collective-permute-start | bytes 147464 | tf_op jit(solution)/shard_map/ppermute | solution.py:36
  65.3 1.5 %collective-permute-done.28 = f32[96,128]{1,0:T(8,128)S(1)} collective-permute-done((f32[96,128]{1,0:T(8,128)S(1)}, f32[96,128]{1,0:T(8,128)S(1)}, u32[]{:S(2)}, u32[]{:S(2)}) %collective-permute-start.28) | collective-permute-done | bytes 49184 | tf_op jit(solution)/shard_map/ppermute | solution.py:36
  66.8 2.5 %collective-permute-done.27 = f32[96,128]{1,0:T(8,128)S(1)} collective-permute-done((f32[96,128]{1,0:T(8,128)S(1)}, f32[96,128]{1,0:T(8,128)S(1)}, u32[]{:S(2)}, u32[]{:S(2)}) %collective-permute-start.27) | collective-permute-done | bytes 49184 | tf_op jit(solution)/shard_map/ppermute | solution.py:36
  69.5 1.2 %collective-permute-done.29.other_ref = f32[96,128]{1,0:T(8,128)S(1)} collective-permute-done((f32[96,128]{1,0:T(8,128)S(1)}, f32[96,128]{1,0:T(8,128)S(1)}, u32[]{:S(2)}, u32[]{:S(2)}) %collective-permute-start.29) | collective-permute-done | bytes 49184 | tf_op jit(solution)/shard_map/ppermute | solution.py:36
  70.7 8.8 %orthonormalize.1 = f32[192,512]{1,0:T(8,128)} custom-call(f32[96,128]{1,0:T(8,128)S(1)} %add_add_fusion.keep_ref, f32[96,128]{1,0:T(8,128)S(1)} %collective-permute-done.29.other_ref, bf16[512,128]{1,0:T(8,128)(2,1)S(1)} %get-tuple-element.65.wide_ref, bf16[256,128]{1,0:T(8,128)(2,1)S(1)} %get-tuple-element.66.thin_ref), custom_call_target="tpu_custom_call" | custom-call | flops 1000 | bytes 1000 | tf_op jit(solution)/shard_map/orthonormalize/pallas_call | solution.py:367
  (57 shorter events, 9.8 us)
Async XLA Ops:
  1.1 7.2 %collective-permute-start.1 = (bf16[512,128]{1,0:T(8,128)(2,1)S(1)}, bf16[512,128]{1,0:T(8,128)(2,1)S(1)}, u32[]{:S(2)}, u32[]{:S(2)}) collective-permute-start(bf16[512,128]{1,0:T(8,128)(2,1)S(1)} %get-tuple-element.36.wide_ref.refs_0_.start), channel_id=1, source_target_pairs={{0,8},{4,12},{8,0},{12,4},{1,9},{5,13},{9,1},{13,5},{2,10},{6,14},... | collective-permute-start | bytes 393224 | tf_op jit(solution)/shard_map/ppermute | solution.py:36
  4.1 4.9 %collective-permute-start.4 = (bf16[256,128]{1,0:T(8,128)(2,1)S(1)}, bf16[256,128]{1,0:T(8,128)(2,1)S(1)}, u32[]{:S(2)}, u32[]{:S(2)}) collective-permute-start(bf16[256,128]{1,0:T(8,128)(2,1)S(1)} %get-tuple-element.37.thin_ref.refs_4_.start), channel_id=1, source_target_pairs={{0,8},{4,12},{8,0},{12,4},{1,9},{5,13},{9,1},{13,5},{2,10},{6,14},... | collective-permute-start | bytes 196616 | tf_op jit(solution)/shard_map/ppermute | solution.py:36
  4.2 1.4 %copy-start = (bf16[32,64,384]{2,1,0:T(8,128)(2,1)S(1)}, bf16[32,64,384]{2,1,0:T(8,128)(2,1)}, u32[]{:S(2)}) copy-start(bf16[32,64,384]{2,1,0:T(8,128)(2,1)} %ham_ref.9) | copy-start | bytes 4718596
  6.3 4.0 %copy-start.1 = (bf16[32,64,384]{2,1,0:T(8,128)(2,1)S(1)}, bf16[32,64,384]{2,1,0:T(8,128)(2,1)}, u32[]{:S(2)}) copy-start(bf16[32,64,384]{2,1,0:T(8,128)(2,1)} %ham_ref.9) | copy-start | bytes 4718596
  6.3 4.0 %collective-permute-start = (bf16[512,128]{1,0:T(8,128)(2,1)S(1)}, bf16[512,128]{1,0:T(8,128)(2,1)S(1)}, u32[]{:S(2)}, u32[]{:S(2)}) collective-permute-start(bf16[512,128]{1,0:T(8,128)(2,1)S(1)} %get-tuple-element.39), channel_id=1, source_target_pairs={{0,4},{4,0},{8,12},{12,8},{1,5},{5,1},{9,13},{13,9},{2,6},{6,2},{1... | collective-permute-start | bytes 393224 | tf_op jit(solution)/shard_map/ppermute | solution.py:36
  8.3 2.0 %collective-permute-start.2 = (bf16[512,128]{1,0:T(8,128)(2,1)S(1)}, bf16[512,128]{1,0:T(8,128)(2,1)S(1)}, u32[]{:S(2)}, u32[]{:S(2)}) collective-permute-start(bf16[512,128]{1,0:T(8,128)(2,1)S(1)} %collective-permute-done.1.refs_2_), channel_id=1, source_target_pairs={{0,4},{4,0},{8,12},{12,8},{1,5},{5,1},{9,13},{13,9},{2,6},{6,2},{1... | collective-permute-start | bytes 393224 | tf_op jit(solution)/shard_map/ppermute | solution.py:36
  8.3 1.4 %collective-permute-start.3 = (bf16[256,128]{1,0:T(8,128)(2,1)S(1)}, bf16[256,128]{1,0:T(8,128)(2,1)S(1)}, u32[]{:S(2)}, u32[]{:S(2)}) collective-permute-start(bf16[256,128]{1,0:T(8,128)(2,1)S(1)} %get-tuple-element.40), channel_id=1, source_target_pairs={{0,4},{4,0},{8,12},{12,8},{1,5},{5,1},{9,13},{13,9},{2,6},{6,2},{1... | collective-permute-start | bytes 196616 | tf_op jit(solution)/shard_map/ppermute | solution.py:36
  9.0 1.3 %collective-permute-start.5 = (bf16[256,128]{1,0:T(8,128)(2,1)S(1)}, bf16[256,128]{1,0:T(8,128)(2,1)S(1)}, u32[]{:S(2)}, u32[]{:S(2)}) collective-permute-start(bf16[256,128]{1,0:T(8,128)(2,1)S(1)} %collective-permute-done.4.refs_6_), channel_id=1, source_target_pairs={{0,4},{4,0},{8,12},{12,8},{1,5},{5,1},{9,13},{13,9},{2,6},{6,2},{1... | collective-permute-start | bytes 196616 | tf_op jit(solution)/shard_map/ppermute | solution.py:36
  11.5 6.4 %collective-permute-start.6 = (bf16[512,128]{1,0:T(8,128)(2,1)S(1)}, bf16[512,128]{1,0:T(8,128)(2,1)S(1)}, u32[]{:S(2)}, u32[]{:S(2)}) collective-permute-start(bf16[512,128]{1,0:T(8,128)(2,1)S(1)} %get-tuple-element.43), channel_id=1, source_target_pairs={{0,1},{1,0},{2,3},{3,2},{4,5},{5,4},{6,7},{7,6},{8,9},{9,8},{10,11... | collective-permute-start | bytes 393224 | tf_op jit(solution)/shard_map/ppermute | solution.py:36
  13.4 7.4 %collective-permute-start.8 = (bf16[256,128]{1,0:T(8,128)(2,1)S(1)}, bf16[256,128]{1,0:T(8,128)(2,1)S(1)}, u32[]{:S(2)}, u32[]{:S(2)}) collective-permute-start(bf16[256,128]{1,0:T(8,128)(2,1)S(1)} %get-tuple-element.45), channel_id=1, source_target_pairs={{0,1},{1,0},{2,3},{3,2},{4,5},{5,4},{6,7},{7,6},{8,9},{9,8},{10,11... | collective-permute-start | bytes 196616 | tf_op jit(solution)/shard_map/ppermute | solution.py:36
  17.9 8.9 %collective-permute-start.7 = (bf16[512,128]{1,0:T(8,128)(2,1)S(1)}, bf16[512,128]{1,0:T(8,128)(2,1)S(1)}, u32[]{:S(2)}, u32[]{:S(2)}) collective-permute-start(bf16[512,128]{1,0:T(8,128)(2,1)S(1)} %add.27.refs_0_), channel_id=1, source_target_pairs={{0,2},{1,3},{2,0},{3,1},{4,6},{5,7},{6,4},{7,5},{8,10},{9,11},{10,... | collective-permute-start | bytes 393224 | tf_op jit(solution)/shard_map/ppermute | solution.py:36
  20.8 6.1 %collective-permute-start.9 = (bf16[512,128]{1,0:T(8,128)(2,1)S(1)}, bf16[512,128]{1,0:T(8,128)(2,1)S(1)}, u32[]{:S(2)}, u32[]{:S(2)}) collective-permute-start(bf16[512,128]{1,0:T(8,128)(2,1)S(1)} %get-tuple-element.48), channel_id=1, source_target_pairs={{0,1},{1,0},{2,3},{3,2},{4,5},{5,4},{6,7},{7,6},{8,9},{9,8},{10,11... | collective-permute-start | bytes 393224 | tf_op jit(solution)/shard_map/ppermute | solution.py:36
  23.7 5.9 %collective-permute-start.13 = (bf16[256,128]{1,0:T(8,128)(2,1)S(1)}, bf16[256,128]{1,0:T(8,128)(2,1)S(1)}, u32[]{:S(2)}, u32[]{:S(2)}) collective-permute-start(bf16[256,128]{1,0:T(8,128)(2,1)S(1)} %get-tuple-element.50), channel_id=1, source_target_pairs={{0,2},{1,3},{2,0},{3,1},{4,6},{5,7},{6,4},{7,5},{8,10},{9,11},{10,... | collective-permute-start | bytes 196616 | tf_op jit(solution)/shard_map/ppermute | solution.py:36
  24.4 5.3 %collective-permute-start.14 = (bf16[256,128]{1,0:T(8,128)(2,1)S(1)}, bf16[256,128]{1,0:T(8,128)(2,1)S(1)}, u32[]{:S(2)}, u32[]{:S(2)}) collective-permute-start(bf16[256,128]{1,0:T(8,128)(2,1)S(1)} %get-tuple-element.51), channel_id=1, source_target_pairs={{0,1},{1,0},{2,3},{3,2},{4,5},{5,4},{6,7},{7,6},{8,9},{9,8},{10,11... | collective-permute-start | bytes 196616 | tf_op jit(solution)/shard_map/ppermute | solution.py:36
  26.9 5.3 %collective-permute-start.11 = (bf16[512,128]{1,0:T(8,128)(2,1)S(1)}, bf16[512,128]{1,0:T(8,128)(2,1)S(1)}, u32[]{:S(2)}, u32[]{:S(2)}) collective-permute-start(bf16[512,128]{1,0:T(8,128)(2,1)S(1)} %first_filter.2.refs_0_.refs_1_), channel_id=1, source_target_pairs={{0,8},{4,12},{8,0},{12,4},{1,9},{5,13},{9,1},{13,5},{2,10},{6,14},... | collective-permute-start | bytes 393224 | tf_op jit(solution)/shard_map/ppermute | solution.py:36
  29.7 4.3 %collective-permute-start.16 = (bf16[256,128]{1,0:T(8,128)(2,1)S(1)}, bf16[256,128]{1,0:T(8,128)(2,1)S(1)}, u32[]{:S(2)}, u32[]{:S(2)}) collective-permute-start(bf16[256,128]{1,0:T(8,128)(2,1)S(1)} %first_filter.3.refs_4_.refs_5_), channel_id=1, source_target_pairs={{0,8},{4,12},{8,0},{12,4},{1,9},{5,13},{9,1},{13,5},{2,10},{6,14},... | collective-permute-start | bytes 196616 | tf_op jit(solution)/shard_map/ppermute | solution.py:36
  31.3 4.0 %collective-permute-start.10 = (bf16[512,128]{1,0:T(8,128)(2,1)S(1)}, bf16[512,128]{1,0:T(8,128)(2,1)S(1)}, u32[]{:S(2)}, u32[]{:S(2)}) collective-permute-start(bf16[512,128]{1,0:T(8,128)(2,1)S(1)} %first_filter.2.refs_0_.refs_1_), channel_id=1, source_target_pairs={{0,4},{4,0},{8,12},{12,8},{1,5},{5,1},{9,13},{13,9},{2,6},{6,2},{1... | collective-permute-start | bytes 393224 | tf_op jit(solution)/shard_map/ppermute | solution.py:36
  32.3 3.0 %collective-permute-start.12 = (bf16[512,128]{1,0:T(8,128)(2,1)S(1)}, bf16[512,128]{1,0:T(8,128)(2,1)S(1)}, u32[]{:S(2)}, u32[]{:S(2)}) collective-permute-start(bf16[512,128]{1,0:T(8,128)(2,1)S(1)} %collective-permute-done.11.refs_2_), channel_id=1, source_target_pairs={{0,4},{4,0},{8,12},{12,8},{1,5},{5,1},{9,13},{13,9},{2,6},{6,2},{1... | collective-permute-start | bytes 393224 | tf_op jit(solution)/shard_map/ppermute | solution.py:36
  32.3 1.8 %collective-permute-start.15 = (bf16[256,128]{1,0:T(8,128)(2,1)S(1)}, bf16[256,128]{1,0:T(8,128)(2,1)S(1)}, u32[]{:S(2)}, u32[]{:S(2)}) collective-permute-start(bf16[256,128]{1,0:T(8,128)(2,1)S(1)} %first_filter.3.refs_4_.refs_5_), channel_id=1, source_target_pairs={{0,4},{4,0},{8,12},{12,8},{1,5},{5,1},{9,13},{13,9},{2,6},{6,2},{1... | collective-permute-start | bytes 196616 | tf_op jit(solution)/shard_map/ppermute | solution.py:36
  34.1 1.3 %collective-permute-start.17 = (bf16[256,128]{1,0:T(8,128)(2,1)S(1)}, bf16[256,128]{1,0:T(8,128)(2,1)S(1)}, u32[]{:S(2)}, u32[]{:S(2)}) collective-permute-start(bf16[256,128]{1,0:T(8,128)(2,1)S(1)} %collective-permute-done.16.refs_6_), channel_id=1, source_target_pairs={{0,4},{4,0},{8,12},{12,8},{1,5},{5,1},{9,13},{13,9},{2,6},{6,2},{1... | collective-permute-start | bytes 196616 | tf_op jit(solution)/shard_map/ppermute | solution.py:36
  36.6 6.3 %collective-permute-start.18 = (bf16[512,128]{1,0:T(8,128)(2,1)S(1)}, bf16[512,128]{1,0:T(8,128)(2,1)S(1)}, u32[]{:S(2)}, u32[]{:S(2)}) collective-permute-start(bf16[512,128]{1,0:T(8,128)(2,1)S(1)} %get-tuple-element.54), channel_id=1, source_target_pairs={{0,1},{1,0},{2,3},{3,2},{4,5},{5,4},{6,7},{7,6},{8,9},{9,8},{10,11... | collective-permute-start | bytes 393224 | tf_op jit(solution)/shard_map/ppermute | solution.py:36
  37.7 7.4 %collective-permute-start.20 = (bf16[256,128]{1,0:T(8,128)(2,1)S(1)}, bf16[256,128]{1,0:T(8,128)(2,1)S(1)}, u32[]{:S(2)}, u32[]{:S(2)}) collective-permute-start(bf16[256,128]{1,0:T(8,128)(2,1)S(1)} %get-tuple-element.56), channel_id=1, source_target_pairs={{0,1},{1,0},{2,3},{3,2},{4,5},{5,4},{6,7},{7,6},{8,9},{9,8},{10,11... | collective-permute-start | bytes 196616 | tf_op jit(solution)/shard_map/ppermute | solution.py:36
  42.9 10.7 %collective-permute-start.19 = (bf16[512,128]{1,0:T(8,128)(2,1)S(1)}, bf16[512,128]{1,0:T(8,128)(2,1)S(1)}, u32[]{:S(2)}, u32[]{:S(2)}) collective-permute-start(bf16[512,128]{1,0:T(8,128)(2,1)S(1)} %add.29.refs_0_), channel_id=1, source_target_pairs={{0,2},{1,3},{2,0},{3,1},{4,6},{5,7},{6,4},{7,5},{8,10},{9,11},{10,... | collective-permute-start | bytes 393224 | tf_op jit(solution)/shard_map/ppermute | solution.py:36
  45.1 8.5 %collective-permute-start.22 = (bf16[256,128]{1,0:T(8,128)(2,1)S(1)}, bf16[256,128]{1,0:T(8,128)(2,1)S(1)}, u32[]{:S(2)}, u32[]{:S(2)}) collective-permute-start(bf16[256,128]{1,0:T(8,128)(2,1)S(1)} %get-tuple-element.61), channel_id=1, source_target_pairs={{0,2},{1,3},{2,0},{3,1},{4,6},{5,7},{6,4},{7,5},{8,10},{9,11},{10,... | collective-permute-start | bytes 196616 | tf_op jit(solution)/shard_map/ppermute | solution.py:36
  46.0 8.9 %collective-permute-start.21 = (bf16[512,128]{1,0:T(8,128)(2,1)S(1)}, bf16[512,128]{1,0:T(8,128)(2,1)S(1)}, u32[]{:S(2)}, u32[]{:S(2)}) collective-permute-start(bf16[512,128]{1,0:T(8,128)(2,1)S(1)} %get-tuple-element.59), channel_id=1, source_target_pairs={{0,1},{1,0},{2,3},{3,2},{4,5},{5,4},{6,7},{7,6},{8,9},{9,8},{10,11... | collective-permute-start | bytes 393224 | tf_op jit(solution)/shard_map/ppermute | solution.py:36
  47.7 7.2 %collective-permute-start.23 = (bf16[256,128]{1,0:T(8,128)(2,1)S(1)}, bf16[256,128]{1,0:T(8,128)(2,1)S(1)}, u32[]{:S(2)}, u32[]{:S(2)}) collective-permute-start(bf16[256,128]{1,0:T(8,128)(2,1)S(1)} %get-tuple-element.62), channel_id=1, source_target_pairs={{0,1},{1,0},{2,3},{3,2},{4,5},{5,4},{6,7},{7,6},{8,9},{9,8},{10,11... | collective-permute-start | bytes 196616 | tf_op jit(solution)/shard_map/ppermute | solution.py:36
  55.4 1.3 %collective-permute-start.24 = (f32[96,128]{1,0:T(8,128)S(1)}, f32[96,128]{1,0:T(8,128)S(1)}, u32[]{:S(2)}, u32[]{:S(2)}) collective-permute-start(f32[96,128]{1,0:T(8,128)S(1)} %get-tuple-element.64), channel_id=1, source_target_pairs={{0,4},{4,0},{8,12},{12,8},{1,5},{5,1},{9,13},{13,9},{2,6},{6,2},{1... | collective-permute-start | bytes 147464 | tf_op jit(solution)/shard_map/ppermute | solution.py:36
  56.7 4.2 %collective-permute-start.25 = (f32[96,128]{1,0:T(8,128)S(1)}, f32[96,128]{1,0:T(8,128)S(1)}, u32[]{:S(2)}, u32[]{:S(2)}) collective-permute-start(f32[96,128]{1,0:T(8,128)S(1)} %add.19), channel_id=1, source_target_pairs={{0,8},{4,12},{8,0},{12,4},{1,9},{5,13},{9,1},{13,5},{2,10},{6,14},... | collective-permute-start | bytes 147464 | tf_op jit(solution)/shard_map/ppermute | solution.py:36
  60.9 6.0 %collective-permute-start.28 = (f32[96,128]{1,0:T(8,128)S(1)}, f32[96,128]{1,0:T(8,128)S(1)}, u32[]{:S(2)}, u32[]{:S(2)}) collective-permute-start(f32[96,128]{1,0:T(8,128)S(1)} %add.20), channel_id=1, source_target_pairs={{0,3},{1,2},{2,1},{3,0},{4,7},{5,6},{6,5},{7,4},{8,11},{9,10},{10,... | collective-permute-start | bytes 147464 | tf_op jit(solution)/shard_map/ppermute | solution.py:36
  64.4 5.0 %collective-permute-start.27 = (f32[96,128]{1,0:T(8,128)S(1)}, f32[96,128]{1,0:T(8,128)S(1)}, u32[]{:S(2)}, u32[]{:S(2)}) collective-permute-start(f32[96,128]{1,0:T(8,128)S(1)} %add.20), channel_id=1, source_target_pairs={{0,2},{1,3},{2,0},{3,1},{4,6},{5,7},{6,4},{7,5},{8,10},{9,11},{10,... | collective-permute-start | bytes 147464 | tf_op jit(solution)/shard_map/ppermute | solution.py:36
  64.4 5.0 %collective-permute-start.26 = (f32[96,128]{1,0:T(8,128)S(1)}, f32[96,128]{1,0:T(8,128)S(1)}, u32[]{:S(2)}, u32[]{:S(2)}) collective-permute-start(f32[96,128]{1,0:T(8,128)S(1)} %add.20), channel_id=1, source_target_pairs={{0,1},{1,0},{2,3},{3,2},{4,5},{5,4},{6,7},{7,6},{8,9},{9,8},{10,11... | collective-permute-start | bytes 147464 | tf_op jit(solution)/shard_map/ppermute | solution.py:36
  69.4 1.3 %collective-permute-start.29 = (f32[96,128]{1,0:T(8,128)S(1)}, f32[96,128]{1,0:T(8,128)S(1)}, u32[]{:S(2)}, u32[]{:S(2)}) collective-permute-start(f32[96,128]{1,0:T(8,128)S(1)} %add_add_fusion.keep_ref), channel_id=1, source_target_pairs={{0,4},{4,0},{8,12},{12,8},{1,5},{5,1},{9,13},{13,9},{2,6},{6,2},{1... | collective-permute-start | bytes 147464 | tf_op jit(solution)/shard_map/ppermute | solution.py:36
  (2 other events, 1.6 us)

commit v4 on v3

--- a/solution.py
+++ b/solution.py
@@ -9,7 +9,6 @@
 
 LANES = 128
 SIZE = LANES // 2
-PIVOTS = 8
 GIGA = 10**9
 COSTS = ((3, 1, 3), (3, 1, 0))
 F32 = jnp.float32
@@ -18,12 +17,12 @@
 SMEM = pl.BlockSpec(memory_space=pltpu.SMEM)
 
 
-def call(kernel, out_shape, in_specs, scratch=(), flops=1000, name=None):
+def call(kernel, out_shape, in_specs, scratch=(), flops=1000, name=None, out_specs=None):
     return pl.pallas_call(
         kernel,
         out_shape=out_shape,
         in_specs=in_specs,
-        out_specs=jax.tree.map(lambda _: VMEM, out_shape),
+        out_specs=out_specs or jax.tree.map(lambda _: VMEM, out_shape),
         scratch_shapes=list(scratch),
         compiler_params=pltpu.CompilerParams(vmem_limit_bytes=40 * 1024 * 1024),
         cost_estimate=pl.CostEstimate(flops=flops, bytes_accessed=1000, transcendentals=0),
@@ -60,9 +59,26 @@
     thin_out[...] = thin.T.astype(BF16)
 
 
-def load_kernel(own_blocks, orbitals, wide_ref, thin_ref, ids_ref, ham_ref, wide_out, thin_out, at_out):
+def load_kernel(
+    own_blocks,
+    orbitals,
+    lower_ref,
+    upper_ref,
+    wide_ref,
+    thin_ref,
+    ids_ref,
+    ham_ref,
+    wide_out,
+    thin_out,
+    at_out,
+    ends_out,
+):
     wide_out[...] = wide_ref[...]
     thin_out[...] = thin_ref[...]
+    low = jnp.full((8, LANES), lower_ref[0], F32)
+    high = jnp.full((8, LANES), upper_ref[0], F32)
+    ends_out[pl.ds(0, 8), :] = (high + low) * 0.5
+    ends_out[pl.ds(8, 8), :] = 1.0 / ((high - low) * 0.5)
     at_out[...] = (ids_ref[...] ^ (lax.axis_index("row") * own_blocks)) * orbitals
 
 
@@ -165,12 +181,6 @@
     return list(zip(sums, near))
 
 
-def ends(lower_ref, upper_ref, shape):
-    low = jnp.full(shape, lower_ref[0], F32)
-    high = jnp.full(shape, upper_ref[0], F32)
-    return (high + low) * 0.5, 1.0 / ((high - low) * 0.5)
-
-
 def total_of(refs):
     acc = refs[0][...].astype(F32)
     for ref in refs[1:]:
@@ -178,8 +188,8 @@
     return acc
 
 
-def first_kernel(lower_ref, upper_ref, start, *refs):
-    center, scale = ends(lower_ref, upper_ref, (1, LANES))
+def first_kernel(ends_ref, start, *refs):
+    center, scale = ends_ref[pl.ds(0, 1), :], ends_ref[pl.ds(8, 1), :]
     moved = total_of(refs[:-1]) - center * start[...].astype(F32)
     refs[-1][...] = (moved * scale).astype(BF16)
 
@@ -188,10 +198,10 @@
     return lax.dot_general(a, b, (((0,), (0,)), ((), ())), preferred_element_type=F32)
 
 
-def second_kernel(rows_all, lower_ref, upper_ref, *refs):
+def second_kernel(rows_all, ends_ref, *refs):
     wide_out, thin_out, keep_out, send_out, gram = refs[-5:]
     count = (len(refs) - 5) // 2
-    center, scale = ends(lower_ref, upper_ref, (1, LANES))
+    center, scale = ends_ref[pl.ds(0, 1), :], ends_ref[pl.ds(8, 1), :]
     for out, (start, first, *terms) in (
         (wide_out, refs[:count]),
         (thin_out, refs[count : 2 * count]),
@@ -216,7 +226,7 @@
     send_out[...] = gram[pl.ds(pl.multiple_of((1 - mine) * part, 8), part), :]
 
 
-def inverse_factor(block, pivots):
+def inverse_factor(block):
     size = block.shape[0]
     tiles = size // 8
     rows = lax.broadcasted_iota(jnp.int32, (8, LANES), 0)
@@ -227,40 +237,53 @@
     ]
     diag = [jnp.ones((8, LANES), F32) for _ in range(tiles)]
     full = (8, LANES)
-    for j in range(0, size, pivots):
-        t0, s0 = divmod(j, 8)
-        cols = [
-            [jnp.broadcast_to(a[t][:, j + k : j + k + 1], full) for t in range(t0, tiles)]
-            for k in range(pivots)
-        ]
-        lines = [jnp.broadcast_to(a[t0][s0 + k : s0 + k + 1, :], full) for k in range(pivots)]
-        small = [
-            [jnp.broadcast_to(cols[q][0][s0 + k : s0 + k + 1, :], full) for q in range(k + 1)]
-            for k in range(pivots)
-        ]
-        for k in range(pivots):
+    def row(x, at):
+        return jnp.broadcast_to(x[at : at + 1, :], full)
+
+    def column(x, at):
+        return jnp.broadcast_to(x[:, at : at + 1], full)
+
+    def corner(columns):
+        return [[row(columns[q], k) for q in range(k + 1)] for k in range(8)]
+
+    small = corner([column(a[0], k) for k in range(8)])
+    for t0 in range(tiles):
+        j = 8 * t0
+        cols = [[column(a[t], j + k) for t in range(t0, tiles)] for k in range(8)]
+        lines = [row(a[t0], k) for k in range(8)]
+        ahead = t0 + 1 < tiles
+        if ahead:
+            later = corner([column(a[t0 + 1], j + 8 + k) for k in range(8)])
+        for k in range(8):
             d = small[k][k]
-            diag[t0] = jnp.where(rows == s0 + k, d, diag[t0])
+            diag[t0] = jnp.where(rows == k, d, diag[t0])
             r = 1.0 / d
-            mult = {}
-            for q in range(k + 1, pivots):
-                mult[q] = small[q][k] * r
-            for q in range(k + 1, pivots):
-                lines[q] = lines[q] - mult[q] * lines[k]
+            mult = {q: small[q][k] * r for q in range(k + 1, 8)}
+            for q in range(k + 1, 8):
                 for p in range(k + 1, q + 1):
                     small[q][p] = small[q][p] - mult[q] * small[p][k]
+            if ahead:
+                below = [row(cols[k][1], q) for q in range(8)]
+                for q in range(8):
+                    scaled = below[q] * r
+                    for p in range(q + 1):
+                        later[q][p] = later[q][p] - scaled * below[p]
+            for q in range(k + 1, 8):
+                lines[q] = lines[q] - mult[q] * lines[k]
             for i, t in enumerate(range(t0, tiles)):
                 x = cols[k][i] * r
                 if t == t0:
-                    x = jnp.where(rows > s0 + k, x, 0.0)
-                for q in range(k + 1, pivots):
+                    x = jnp.where(rows > k, x, 0.0)
+                for q in range(k + 1, 8):
                     cols[q][i] = cols[q][i] - cols[k][i] * mult[q]
                 a[t] = a[t] - x * lines[k]
+        if ahead:
+            small = later
     out = jnp.concatenate([a[t] * lax.rsqrt(diag[t]) for t in range(tiles)], axis=0)
     return out[:, size:]
 
 
-def last_kernel(pivots, keep_ref, other_ref, wide_ref, thin_ref, out_ref, gram, factor):
+def last_kernel(keep_ref, other_ref, wide_ref, thin_ref, out_ref, gram, factor, result, sems):
     size = LANES // 2
     part = 3 * size // 2
     mine = lax.axis_index("row") & 1
@@ -282,20 +305,19 @@
     g00 = gram[pl.ds(0, size), :][:, :size]
     g22 = gram[pl.ds(0, size), :][:, size:]
     strip = gram[pl.ds(size, 2 * size), :]
-    x0 = inverse_factor(g00, pivots)
+    x0 = inverse_factor(g00)
     l_strip = dot_t(strip[:, :size], x0)
     rest = strip[:, size:] - dot_t(l_strip, l_strip[:size])
-    x1 = inverse_factor(rest[:size], pivots)
+    x1 = inverse_factor(rest[:size])
     l10, l20 = l_strip[:size], l_strip[size:]
     l21 = dot_t(rest[size:], x1)
-    x2 = inverse_factor(g22 - dot_t(l20, l20) - dot_t(l21, l21), pivots)
+    last = g22 - dot_t(l20, l20) - dot_t(l21, l21)
     n10 = -dot(x1, dot(l10, x0))
-    n20 = -dot(x2, dot(l20, x0) + dot(l21, n10))
-    n21 = -dot(x2, dot(l21, x1))
+    below0 = dot(l20, x0) + dot(l21, n10)
+    below1 = dot(l21, x1)
     zero = jnp.zeros((size, size), F32)
     factor[pl.ds(0, size), :] = jnp.concatenate([x0, zero], axis=1)
     factor[pl.ds(size, size), :] = jnp.concatenate([n10, x1], axis=1)
-    factor[pl.ds(2 * size, size), :] = jnp.concatenate([n20, n21], axis=1)
 
     def apply(mat, vec):
         high = mat.astype(BF16)
@@ -307,8 +329,14 @@
 
     wide, thin = wide_ref[...], thin_ref[...]
     half = thin.shape[0]
-    main = apply(factor[...], wide)
-    out_ref[pl.ds(0, 2 * size), :] = main[: 2 * size]
+    head, foot = pl.ds(0, 2 * size), pl.ds(2 * size, size)
+    result[head, :] = apply(factor[head, :], wide)
+    early = pltpu.make_async_copy(result.at[head], out_ref.at[head], sems.at[0])
+    early.start()
+    x2 = inverse_factor(last)
+    n20 = -dot(x2, below0)
+    n21 = -dot(x2, below1)
+    factor[foot, :] = jnp.concatenate([n20, n21], axis=1)
     tail = jnp.concatenate(
         [
             apply(jnp.concatenate([x2, zero], axis=1), thin),
@@ -316,7 +344,11 @@
         ],
         axis=1,
     )
-    out_ref[pl.ds(2 * size, size), :] = main[2 * size :] + tail
+    result[foot, :] = apply(factor[foot, :], wide) + tail
+    late = pltpu.make_async_copy(result.at[foot], out_ref.at[foot], sems.at[1])
+    late.start()
+    early.wait()
+    late.wait()
 
 
 def sum_all(keep, send):
@@ -339,18 +371,19 @@
     shapes = [jax.ShapeDtypeStruct((x, LANES), BF16) for x in (rows, rows // 2)]
     half_gram = jax.ShapeDtypeStruct((3 * SIZE // 2, LANES), F32)
     gram = pltpu.VMEM((3 * SIZE, LANES), F32)
+    ends_shape = jax.ShapeDtypeStruct((16, LANES), F32)
 
     start = call(pack_kernel, shapes, [VMEM], name="pack")(vectors.T)
-    *twin, at = call(
+    *twin, at, ends = call(
         functools.partial(load_kernel, own_blocks, orbitals),
-        [*shapes, jax.ShapeDtypeStruct(columns.shape[::-1], jnp.int32)],
-        [VMEM] * 4,
+        [*shapes, jax.ShapeDtypeStruct(columns.shape[::-1], jnp.int32), ends_shape],
+        [SMEM] * 2 + [VMEM] * 4,
         name="load",
-    )(*start, columns.T, hamiltonian)
+    )(lower, upper, *start, columns.T, hamiltonian)
     terms = summands(own_blocks, at, hamiltonian, gather_shards(start, twin), COSTS[0])
     first = [
-        call(first_kernel, shape, [SMEM, SMEM] + [VMEM] * (1 + len(x)), name="first_filter")(
-            lower, upper, vec, *x
+        call(first_kernel, shape, [VMEM] * (2 + len(x)), name="first_filter")(
+            ends, vec, *x
         )
         for shape, vec, x in zip(shapes, start, terms)
     ]
@@ -359,17 +392,18 @@
     wide, thin, keep, send = call(
         functools.partial(second_kernel, rows_all),
         [*shapes, half_gram, half_gram],
-        [SMEM, SMEM] + [VMEM] * len(operands),
+        [VMEM] * (1 + len(operands)),
         [gram],
         name="second_filter",
-    )(lower, upper, *operands)
+    )(ends, *operands)
     keep, other = sum_all(keep, send)
     basis = call(
-        functools.partial(last_kernel, PIVOTS),
+        last_kernel,
         jax.ShapeDtypeStruct((LANES + SIZE, rows), F32),
         [VMEM] * 4,
-        [gram, gram],
+        [gram, gram, pltpu.VMEM((LANES + SIZE, rows), F32), pltpu.SemaphoreType.DMA((2,))],
         name="orthonormalize",
+        out_specs=pl.BlockSpec(memory_space=pl.ANY),
     )(keep, other, wide, thin)
     return basis.T
 

time: 79.7 us -> 78.8 us (0.989)
  waiting for transfers between devices: 30.6 us -> 32.1 us
  starting transfers between devices: 28.5 us -> 27.1 us
  Pallas kernels: 15.9 us -> 15 us
    ppermute x30, waiting for transfers between devices: 30.6 us -> 32.1 us  [swap(): return lax.ppermute(x, axis, [(i, i ^ key) for i in range(count)])]
    ppermute x30, starting transfers between devices: 28.5 us -> 27.1 us  [swap(): return lax.ppermute(x, axis, [(i, i ^ key) for i in range(count)])]
    pallas_call x3, Pallas kernels: 8.94 us -> 8.01 us  [the longest x1 7.9 us: per_device(): call(last_kernel, jax.ShapeDtypeStruct((LANES + SIZE, rows), F32), [VMEM]...]
  transfers between devices with their start and end apart: 30 -> 30, of which waited for: 18 -> 19; matrix products, arithmetic and copies ran while one was open for 0% -> 0% of each run, Pallas kernels for 5% -> 5%
where the time goes in v4:
time: 78.8 us; the launch traced here: 78.6 us
  waiting for transfers between devices  32.1 us (41%)
  starting transfers between devices  27.1 us (34%)
  Pallas kernels  15 us (19%)
  local copies, waits for them, and re-layouts  3.02 us (4%)
  between operations  1.44 us (2%)
    ppermute x30, waiting for transfers between devices, swap(): return lax.ppermute(x, axis, [(i, i ^ key) for i in range(count)])  32.1 us
    ppermute x30, starting transfers between devices, swap(): return lax.ppermute(x, axis, [(i, i ^ key) for i in range(count)])  27.1 us
    pallas_call x1, Pallas kernels, per_device(): call(last_kernel, jax.ShapeDtypeStruct((LANES + SIZE, rows), F32), [VMEM]...  7.9 us
    pallas_call x4, Pallas kernels, product(): call(functools.partial(product_kernel, keys, n_row, own_blocks), [jax.Sha...  6.16 us
    unnamed x8, local copies, waits for them, and re-layouts  3.02 us
  transfers between devices with their start and end apart: 30, of which 19 were waited for; matrix products, arithmetic and copies ran while one was open for 0% of the time, Pallas kernels for 5%

profile of v4, /device:TPU:0, one launch (start us, length us, event | category | flops | bytes accessed | tf_op | source)
XLA Modules:
  0.0 78.6 jit_solution(3485100549480127069)
XLA Ops:
  0.0 0.9 %copy-done.2 = bf16[512,192]{0,1:T(8,128)(2,1)S(1)} copy-done((bf16[512,192]{0,1:T(8,128)(2,1)S(1)}, bf16[512,192]{0,1:T(8,128)(2,1)}, u32[]{:S(2)}) %copy-start.2) | copy-done | bytes 196632
  1.1 3.0 %collective-permute-start.1 = (bf16[512,128]{1,0:T(8,128)(2,1)S(1)}, bf16[512,128]{1,0:T(8,128)(2,1)S(1)}, u32[]{:S(2)}, u32[]{:S(2)}) collective-permute-start(bf16[512,128]{1,0:T(8,128)(2,1)S(1)} %get-tuple-element.37.wide_ref.refs_0_.start), channel_id=1, source_target_pairs={{0,8},{4,12},{8,0},{12,4},{1,9},{5,13},{9,1},{13,5},{2,10},{6,14},... | collective-permute-start | bytes 393224 | tf_op jit(solution)/shard_map/ppermute | solution.py:35
  5.5 1.4 %copy-done = bf16[32,64,384]{2,1,0:T(8,128)(2,1)S(1)} copy-done((bf16[32,64,384]{2,1,0:T(8,128)(2,1)S(1)}, bf16[32,64,384]{2,1,0:T(8,128)(2,1)}, u32[]{:S(2)}) %copy-start) | copy-done | bytes 1572888
  10.3 1.3 %product.5 = (bf16[512,128]{1,0:T(8,128)(2,1)S(1)}, bf16[256,128]{1,0:T(8,128)(2,1)S(1)}) custom-call(s32[6,32]{1,0:T(8,128)S(1)} %get-tuple-element.40.at_ref, bf16[32,64,384]{2,1,0:T(8,128)(2,1)S(1)} %copy-done.1, bf16[512,128]{1,0:T(8,128)(2,1)S(1)} %get-tuple-element.37.wide_ref.refs_0_.start, bf16[512,128]{1,0:T(8,128)(2,1)S(1)} %collective-permute-done.refs_1_, ...), custom_call_target="tpu_custom_call" | custom-call | flops 100663296 | bytes 1000 | tf_op jit(solution)/shard_map/product/pallas_call | solution.py:130
  11.5 1.9 %collective-permute-start.6 = (bf16[512,128]{1,0:T(8,128)(2,1)S(1)}, bf16[512,128]{1,0:T(8,128)(2,1)S(1)}, u32[]{:S(2)}, u32[]{:S(2)}) collective-permute-start(bf16[512,128]{1,0:T(8,128)(2,1)S(1)} %get-tuple-element.45), channel_id=1, source_target_pairs={{0,1},{1,0},{2,3},{3,2},{4,5},{5,4},{6,7},{7,6},{8,9},{9,8},{10,11... | collective-permute-start | bytes 393224 | tf_op jit(solution)/shard_map/ppermute | solution.py:35
  13.6 1.8 %product.4 = (bf16[512,128]{1,0:T(8,128)(2,1)S(1)}, bf16[512,128]{1,0:T(8,128)(2,1)S(1)}, bf16[512,128]{1,0:T(8,128)(2,1)S(1)}, bf16[256,128]{1,0:T(8,128)(2,1)S...) custom-call(s32[6,32]{1,0:T(8,128)S(1)} %get-tuple-element.40.at_ref, ...), custom_call_target="tpu_custom_call" | custom-call | flops 301989888 | bytes 1000 | tf_op jit(solution)/shard_map/product/pallas_call | solution.py:130
  15.4 2.5 %collective-permute-done.6.refs_1_ = bf16[512,128]{1,0:T(8,128)(2,1)S(1)} collective-permute-done((bf16[512,128]{1,0:T(8,128)(2,1)S(1)}, bf16[512,128]{1,0:T(8,128)(2,1)S(1)}, u32[]{:S(2)}, u32[]{:S(2)}) %collective-permute-start.6) | collective-permute-done | bytes 131104 | tf_op jit(solution)/shard_map/ppermute | solution.py:35
  17.9 2.8 %collective-permute-start.7 = (bf16[512,128]{1,0:T(8,128)(2,1)S(1)}, bf16[512,128]{1,0:T(8,128)(2,1)S(1)}, u32[]{:S(2)}, u32[]{:S(2)}) collective-permute-start(bf16[512,128]{1,0:T(8,128)(2,1)S(1)} %add.27.refs_0_), channel_id=1, source_target_pairs={{0,2},{1,3},{2,0},{3,1},{4,6},{5,7},{6,4},{7,5},{8,10},{9,11},{10,... | collective-permute-start | bytes 393224 | tf_op jit(solution)/shard_map/ppermute | solution.py:35
  20.8 1.6 %collective-permute-start.9 = (bf16[512,128]{1,0:T(8,128)(2,1)S(1)}, bf16[512,128]{1,0:T(8,128)(2,1)S(1)}, u32[]{:S(2)}, u32[]{:S(2)}) collective-permute-start(bf16[512,128]{1,0:T(8,128)(2,1)S(1)} %get-tuple-element.50), channel_id=1, source_target_pairs={{0,1},{1,0},{2,3},{3,2},{4,5},{5,4},{6,7},{7,6},{8,9},{9,8},{10,11... | collective-permute-start | bytes 393224 | tf_op jit(solution)/shard_map/ppermute | solution.py:35
  23.5 3.8 %collective-permute-done.7.b = bf16[512,128]{1,0:T(8,128)(2,1)S(1)} collective-permute-done((bf16[512,128]{1,0:T(8,128)(2,1)S(1)}, bf16[512,128]{1,0:T(8,128)(2,1)S(1)}, u32[]{:S(2)}, u32[]{:S(2)}) %collective-permute-start.7) | collective-permute-done | bytes 131104 | tf_op jit(solution)/shard_map/ppermute | solution.py:35
  27.3 1.1 %collective-permute-done.9.refs_1_ = bf16[512,128]{1,0:T(8,128)(2,1)S(1)} collective-permute-done((bf16[512,128]{1,0:T(8,128)(2,1)S(1)}, bf16[512,128]{1,0:T(8,128)(2,1)S(1)}, u32[]{:S(2)}, u32[]{:S(2)}) %collective-permute-start.9) | collective-permute-done | bytes 131104 | tf_op jit(solution)/shard_map/ppermute | solution.py:35
  28.4 1.6 %collective-permute-start.11 = (bf16[512,128]{1,0:T(8,128)(2,1)S(1)}, bf16[512,128]{1,0:T(8,128)(2,1)S(1)}, u32[]{:S(2)}, u32[]{:S(2)}) collective-permute-start(bf16[512,128]{1,0:T(8,128)(2,1)S(1)} %first_filter.2.refs_0_.refs_1_), channel_id=1, source_target_pairs={{0,8},{4,12},{8,0},{12,4},{1,9},{5,13},{9,1},{13,5},{2,10},{6,14},... | collective-permute-start | bytes 393224 | tf_op jit(solution)/shard_map/ppermute | solution.py:35
  30.7 2.7 %collective-permute-done.11.refs_2_ = bf16[512,128]{1,0:T(8,128)(2,1)S(1)} collective-permute-done((bf16[512,128]{1,0:T(8,128)(2,1)S(1)}, bf16[512,128]{1,0:T(8,128)(2,1)S(1)}, u32[]{:S(2)}, u32[]{:S(2)}) %collective-permute-start.11) | collective-permute-done | bytes 131104 | tf_op jit(solution)/shard_map/ppermute | solution.py:35
  34.9 0.8 %collective-permute-done.17.refs_7_ = bf16[256,128]{1,0:T(8,128)(2,1)S(1)} collective-permute-done((bf16[256,128]{1,0:T(8,128)(2,1)S(1)}, bf16[256,128]{1,0:T(8,128)(2,1)S(1)}, u32[]{:S(2)}, u32[]{:S(2)}) %collective-permute-start.17) | collective-permute-done | bytes 65568 | tf_op jit(solution)/shard_map/ppermute | solution.py:35
  35.7 1.2 %product.7 = (bf16[512,128]{1,0:T(8,128)(2,1)S(1)}, bf16[256,128]{1,0:T(8,128)(2,1)S(1)}) custom-call(s32[6,32]{1,0:T(8,128)S(1)} %get-tuple-element.40.at_ref, bf16[32,64,384]{2,1,0:T(8,128)(2,1)S(1)} %copy-done.1, bf16[512,128]{1,0:T(8,128)(2,1)S(1)} %first_filter.2.refs_0_.refs_1_, bf16[512,128]{1,0:T(8,128)(2,1)S(1)} %collective-permute-done.10.refs_1_, ...), custom_call_target="tpu_custom_call" | custom-call | flops 100663296 | bytes 1000 | tf_op jit(solution)/shard_map/product/pallas_call | solution.py:130
  37.7 1.4 %collective-permute-start.20 = (bf16[256,128]{1,0:T(8,128)(2,1)S(1)}, bf16[256,128]{1,0:T(8,128)(2,1)S(1)}, u32[]{:S(2)}, u32[]{:S(2)}) collective-permute-start(bf16[256,128]{1,0:T(8,128)(2,1)S(1)} %get-tuple-element.58), channel_id=1, source_target_pairs={{0,1},{1,0},{2,3},{3,2},{4,5},{5,4},{6,7},{7,6},{8,9},{9,8},{10,11... | collective-permute-start | bytes 196616 | tf_op jit(solution)/shard_map/ppermute | solution.py:35
  39.1 1.8 %product.6 = (bf16[512,128]{1,0:T(8,128)(2,1)S(1)}, bf16[512,128]{1,0:T(8,128)(2,1)S(1)}, bf16[512,128]{1,0:T(8,128)(2,1)S(1)}, bf16[256,128]{1,0:T(8,128)(2,1)S...) custom-call(s32[6,32]{1,0:T(8,128)S(1)} %get-tuple-element.40.at_ref, ...), custom_call_target="tpu_custom_call" | custom-call | flops 301989888 | bytes 1000 | tf_op jit(solution)/shard_map/product/pallas_call | solution.py:130
  40.9 2.4 %collective-permute-done.18.refs_1_ = bf16[512,128]{1,0:T(8,128)(2,1)S(1)} collective-permute-done((bf16[512,128]{1,0:T(8,128)(2,1)S(1)}, bf16[512,128]{1,0:T(8,128)(2,1)S(1)}, u32[]{:S(2)}, u32[]{:S(2)}) %collective-permute-start.18) | collective-permute-done | bytes 131104 | tf_op jit(solution)/shard_map/ppermute | solution.py:35
  43.3 1.7 %collective-permute-start.19 = (bf16[512,128]{1,0:T(8,128)(2,1)S(1)}, bf16[512,128]{1,0:T(8,128)(2,1)S(1)}, u32[]{:S(2)}, u32[]{:S(2)}) collective-permute-start(bf16[512,128]{1,0:T(8,128)(2,1)S(1)} %add.29.refs_0_), channel_id=1, source_target_pairs={{0,2},{1,3},{2,0},{3,1},{4,6},{5,7},{6,4},{7,5},{8,10},{9,11},{10,... | collective-permute-start | bytes 393224 | tf_op jit(solution)/shard_map/ppermute | solution.py:35
  45.1 1.3 %collective-permute-start.22 = (bf16[256,128]{1,0:T(8,128)(2,1)S(1)}, bf16[256,128]{1,0:T(8,128)(2,1)S(1)}, u32[]{:S(2)}, u32[]{:S(2)}) collective-permute-start(bf16[256,128]{1,0:T(8,128)(2,1)S(1)} %get-tuple-element.63), channel_id=1, source_target_pairs={{0,2},{1,3},{2,0},{3,1},{4,6},{5,7},{6,4},{7,5},{8,10},{9,11},{10,... | collective-permute-start | bytes 196616 | tf_op jit(solution)/shard_map/ppermute | solution.py:35
  46.4 1.3 %collective-permute-start.21 = (bf16[512,128]{1,0:T(8,128)(2,1)S(1)}, bf16[512,128]{1,0:T(8,128)(2,1)S(1)}, u32[]{:S(2)}, u32[]{:S(2)}) collective-permute-start(bf16[512,128]{1,0:T(8,128)(2,1)S(1)} %get-tuple-element.61), channel_id=1, source_target_pairs={{0,1},{1,0},{2,3},{3,2},{4,5},{5,4},{6,7},{7,6},{8,9},{9,8},{10,11... | collective-permute-start | bytes 393224 | tf_op jit(solution)/shard_map/ppermute | solution.py:35
  48.5 5.6 %collective-permute-done.22.b = bf16[256,128]{1,0:T(8,128)(2,1)S(1)} collective-permute-done((bf16[256,128]{1,0:T(8,128)(2,1)S(1)}, bf16[256,128]{1,0:T(8,128)(2,1)S(1)}, u32[]{:S(2)}, u32[]{:S(2)}) %collective-permute-start.22) | collective-permute-done | bytes 65568 | tf_op jit(solution)/shard_map/ppermute | solution.py:35
  54.1 1.3 %collective-permute-done.23.refs_7_ = bf16[256,128]{1,0:T(8,128)(2,1)S(1)} collective-permute-done((bf16[256,128]{1,0:T(8,128)(2,1)S(1)}, bf16[256,128]{1,0:T(8,128)(2,1)S(1)}, u32[]{:S(2)}, u32[]{:S(2)}) %collective-permute-start.23) | collective-permute-done | bytes 65568 | tf_op jit(solution)/shard_map/ppermute | solution.py:35
  55.9 1.2 %collective-permute-done.24 = f32[96,128]{1,0:T(8,128)S(1)} collective-permute-done((f32[96,128]{1,0:T(8,128)S(1)}, f32[96,128]{1,0:T(8,128)S(1)}, u32[]{:S(2)}, u32[]{:S(2)}) %collective-permute-start.24) | collective-permute-done | bytes 49184 | tf_op jit(solution)/shard_map/ppermute | solution.py:35
  57.1 1.3 %collective-permute-start.25 = (f32[96,128]{1,0:T(8,128)S(1)}, f32[96,128]{1,0:T(8,128)S(1)}, u32[]{:S(2)}, u32[]{:S(2)}) collective-permute-start(f32[96,128]{1,0:T(8,128)S(1)} %add.19), channel_id=1, source_target_pairs={{0,8},{4,12},{8,0},{12,4},{1,9},{5,13},{9,1},{13,5},{2,10},{6,14},... | collective-permute-start | bytes 147464 | tf_op jit(solution)/shard_map/ppermute | solution.py:35
  58.4 2.8 %collective-permute-done.25 = f32[96,128]{1,0:T(8,128)S(1)} collective-permute-done((f32[96,128]{1,0:T(8,128)S(1)}, f32[96,128]{1,0:T(8,128)S(1)}, u32[]{:S(2)}, u32[]{:S(2)}) %collective-permute-start.25) | collective-permute-done | bytes 49184 | tf_op jit(solution)/shard_map/ppermute | solution.py:35
  61.3 3.1 %collective-permute-start.28 = (f32[96,128]{1,0:T(8,128)S(1)}, f32[96,128]{1,0:T(8,128)S(1)}, u32[]{:S(2)}, u32[]{:S(2)}) collective-permute-start(f32[96,128]{1,0:T(8,128)S(1)} %add.20), channel_id=1, source_target_pairs={{0,3},{1,2},{2,1},{3,0},{4,7},{5,6},{6,5},{7,4},{8,11},{9,10},{10,... | collective-permute-start | bytes 147464 | tf_op jit(solution)/shard_map/ppermute | solution.py:35
  64.4 1.3 %collective-permute-start.26 = (f32[96,128]{1,0:T(8,128)S(1)}, f32[96,128]{1,0:T(8,128)S(1)}, u32[]{:S(2)}, u32[]{:S(2)}) collective-permute-start(f32[96,128]{1,0:T(8,128)S(1)} %add.20), channel_id=1, source_target_pairs={{0,1},{1,0},{2,3},{3,2},{4,5},{5,4},{6,7},{7,6},{8,9},{9,8},{10,11... | collective-permute-start | bytes 147464 | tf_op jit(solution)/shard_map/ppermute | solution.py:35
  65.7 1.6 %collective-permute-done.28 = f32[96,128]{1,0:T(8,128)S(1)} collective-permute-done((f32[96,128]{1,0:T(8,128)S(1)}, f32[96,128]{1,0:T(8,128)S(1)}, u32[]{:S(2)}, u32[]{:S(2)}) %collective-permute-start.28) | collective-permute-done | bytes 49184 | tf_op jit(solution)/shard_map/ppermute | solution.py:35
  67.3 2.1 %collective-permute-done.27 = f32[96,128]{1,0:T(8,128)S(1)} collective-permute-done((f32[96,128]{1,0:T(8,128)S(1)}, f32[96,128]{1,0:T(8,128)S(1)}, u32[]{:S(2)}, u32[]{:S(2)}) %collective-permute-start.27) | collective-permute-done | bytes 49184 | tf_op jit(solution)/shard_map/ppermute | solution.py:35
  69.5 1.2 %collective-permute-done.29.other_ref = f32[96,128]{1,0:T(8,128)S(1)} collective-permute-done((f32[96,128]{1,0:T(8,128)S(1)}, f32[96,128]{1,0:T(8,128)S(1)}, u32[]{:S(2)}, u32[]{:S(2)}) %collective-permute-start.29) | collective-permute-done | bytes 49184 | tf_op jit(solution)/shard_map/ppermute | solution.py:35
  70.7 7.9 %orthonormalize.1 = f32[192,512]{1,0:T(8,128)} custom-call(f32[96,128]{1,0:T(8,128)S(1)} %add_add_fusion.keep_ref, f32[96,128]{1,0:T(8,128)S(1)} %collective-permute-done.29.other_ref, bf16[512,128]{1,0:T(8,128)(2,1)S(1)} %get-tuple-element.67.wide_ref, bf16[256,128]{1,0:T(8,128)(2,1)S(1)} %get-tuple-element.68.thin_ref), custom_call_target="tpu_custom_call" | custom-call | flops 1000 | bytes 1000 | tf_op jit(solution)/shard_map/orthonormalize/pallas_call | solution.py:400
  (57 shorter events, 9.3 us)
Async XLA Ops:
  1.1 7.2 %collective-permute-start.1 = (bf16[512,128]{1,0:T(8,128)(2,1)S(1)}, bf16[512,128]{1,0:T(8,128)(2,1)S(1)}, u32[]{:S(2)}, u32[]{:S(2)}) collective-permute-start(bf16[512,128]{1,0:T(8,128)(2,1)S(1)} %get-tuple-element.37.wide_ref.refs_0_.start), channel_id=1, source_target_pairs={{0,8},{4,12},{8,0},{12,4},{1,9},{5,13},{9,1},{13,5},{2,10},{6,14},... | collective-permute-start | bytes 393224 | tf_op jit(solution)/shard_map/ppermute | solution.py:35
  4.1 4.9 %collective-permute-start.4 = (bf16[256,128]{1,0:T(8,128)(2,1)S(1)}, bf16[256,128]{1,0:T(8,128)(2,1)S(1)}, u32[]{:S(2)}, u32[]{:S(2)}) collective-permute-start(bf16[256,128]{1,0:T(8,128)(2,1)S(1)} %get-tuple-element.38.thin_ref.refs_4_.start), channel_id=1, source_target_pairs={{0,8},{4,12},{8,0},{12,4},{1,9},{5,13},{9,1},{13,5},{2,10},{6,14},... | collective-permute-start | bytes 196616 | tf_op jit(solution)/shard_map/ppermute | solution.py:35
  5.5 1.4 %copy-start = (bf16[32,64,384]{2,1,0:T(8,128)(2,1)S(1)}, bf16[32,64,384]{2,1,0:T(8,128)(2,1)}, u32[]{:S(2)}) copy-start(bf16[32,64,384]{2,1,0:T(8,128)(2,1)} %ham_ref.9) | copy-start | bytes 4718596
  7.6 2.7 %copy-start.1 = (bf16[32,64,384]{2,1,0:T(8,128)(2,1)S(1)}, bf16[32,64,384]{2,1,0:T(8,128)(2,1)}, u32[]{:S(2)}) copy-start(bf16[32,64,384]{2,1,0:T(8,128)(2,1)} %ham_ref.9) | copy-start | bytes 4718596
  7.6 2.7 %collective-permute-start = (bf16[512,128]{1,0:T(8,128)(2,1)S(1)}, bf16[512,128]{1,0:T(8,128)(2,1)S(1)}, u32[]{:S(2)}, u32[]{:S(2)}) collective-permute-start(bf16[512,128]{1,0:T(8,128)(2,1)S(1)} %get-tuple-element.41), channel_id=1, source_target_pairs={{0,4},{4,0},{8,12},{12,8},{1,5},{5,1},{9,13},{13,9},{2,6},{6,2},{1... | collective-permute-start | bytes 393224 | tf_op jit(solution)/shard_map/ppermute | solution.py:35
  8.3 2.0 %collective-permute-start.2 = (bf16[512,128]{1,0:T(8,128)(2,1)S(1)}, bf16[512,128]{1,0:T(8,128)(2,1)S(1)}, u32[]{:S(2)}, u32[]{:S(2)}) collective-permute-start(bf16[512,128]{1,0:T(8,128)(2,1)S(1)} %collective-permute-done.1.refs_2_), channel_id=1, source_target_pairs={{0,4},{4,0},{8,12},{12,8},{1,5},{5,1},{9,13},{13,9},{2,6},{6,2},{1... | collective-permute-start | bytes 393224 | tf_op jit(solution)/shard_map/ppermute | solution.py:35
  8.3 1.4 %collective-permute-start.3 = (bf16[256,128]{1,0:T(8,128)(2,1)S(1)}, bf16[256,128]{1,0:T(8,128)(2,1)S(1)}, u32[]{:S(2)}, u32[]{:S(2)}) collective-permute-start(bf16[256,128]{1,0:T(8,128)(2,1)S(1)} %get-tuple-element.42), channel_id=1, source_target_pairs={{0,4},{4,0},{8,12},{12,8},{1,5},{5,1},{9,13},{13,9},{2,6},{6,2},{1... | collective-permute-start | bytes 196616 | tf_op jit(solution)/shard_map/ppermute | solution.py:35
  9.0 1.3 %collective-permute-start.5 = (bf16[256,128]{1,0:T(8,128)(2,1)S(1)}, bf16[256,128]{1,0:T(8,128)(2,1)S(1)}, u32[]{:S(2)}, u32[]{:S(2)}) collective-permute-start(bf16[256,128]{1,0:T(8,128)(2,1)S(1)} %collective-permute-done.4.refs_6_), channel_id=1, source_target_pairs={{0,4},{4,0},{8,12},{12,8},{1,5},{5,1},{9,13},{13,9},{2,6},{6,2},{1... | collective-permute-start | bytes 196616 | tf_op jit(solution)/shard_map/ppermute | solution.py:35
  11.5 6.4 %collective-permute-start.6 = (bf16[512,128]{1,0:T(8,128)(2,1)S(1)}, bf16[512,128]{1,0:T(8,128)(2,1)S(1)}, u32[]{:S(2)}, u32[]{:S(2)}) collective-permute-start(bf16[512,128]{1,0:T(8,128)(2,1)S(1)} %get-tuple-element.45), channel_id=1, source_target_pairs={{0,1},{1,0},{2,3},{3,2},{4,5},{5,4},{6,7},{7,6},{8,9},{9,8},{10,11... | collective-permute-start | bytes 393224 | tf_op jit(solution)/shard_map/ppermute | solution.py:35
  13.4 7.4 %collective-permute-start.8 = (bf16[256,128]{1,0:T(8,128)(2,1)S(1)}, bf16[256,128]{1,0:T(8,128)(2,1)S(1)}, u32[]{:S(2)}, u32[]{:S(2)}) collective-permute-start(bf16[256,128]{1,0:T(8,128)(2,1)S(1)} %get-tuple-element.47), channel_id=1, source_target_pairs={{0,1},{1,0},{2,3},{3,2},{4,5},{5,4},{6,7},{7,6},{8,9},{9,8},{10,11... | collective-permute-start | bytes 196616 | tf_op jit(solution)/shard_map/ppermute | solution.py:35
  17.9 9.3 %collective-permute-start.7 = (bf16[512,128]{1,0:T(8,128)(2,1)S(1)}, bf16[512,128]{1,0:T(8,128)(2,1)S(1)}, u32[]{:S(2)}, u32[]{:S(2)}) collective-permute-start(bf16[512,128]{1,0:T(8,128)(2,1)S(1)} %add.27.refs_0_), channel_id=1, source_target_pairs={{0,2},{1,3},{2,0},{3,1},{4,6},{5,7},{6,4},{7,5},{8,10},{9,11},{10,... | collective-permute-start | bytes 393224 | tf_op jit(solution)/shard_map/ppermute | solution.py:35
  20.8 7.6 %collective-permute-start.9 = (bf16[512,128]{1,0:T(8,128)(2,1)S(1)}, bf16[512,128]{1,0:T(8,128)(2,1)S(1)}, u32[]{:S(2)}, u32[]{:S(2)}) collective-permute-start(bf16[512,128]{1,0:T(8,128)(2,1)S(1)} %get-tuple-element.50), channel_id=1, source_target_pairs={{0,1},{1,0},{2,3},{3,2},{4,5},{5,4},{6,7},{7,6},{8,9},{9,8},{10,11... | collective-permute-start | bytes 393224 | tf_op jit(solution)/shard_map/ppermute | solution.py:35
  22.4 7.6 %collective-permute-start.13 = (bf16[256,128]{1,0:T(8,128)(2,1)S(1)}, bf16[256,128]{1,0:T(8,128)(2,1)S(1)}, u32[]{:S(2)}, u32[]{:S(2)}) collective-permute-start(bf16[256,128]{1,0:T(8,128)(2,1)S(1)} %get-tuple-element.52), channel_id=1, source_target_pairs={{0,2},{1,3},{2,0},{3,1},{4,6},{5,7},{6,4},{7,5},{8,10},{9,11},{10,... | collective-permute-start | bytes 196616 | tf_op jit(solution)/shard_map/ppermute | solution.py:35
  23.0 7.1 %collective-permute-start.14 = (bf16[256,128]{1,0:T(8,128)(2,1)S(1)}, bf16[256,128]{1,0:T(8,128)(2,1)S(1)}, u32[]{:S(2)}, u32[]{:S(2)}) collective-permute-start(bf16[256,128]{1,0:T(8,128)(2,1)S(1)} %get-tuple-element.53), channel_id=1, source_target_pairs={{0,1},{1,0},{2,3},{3,2},{4,5},{5,4},{6,7},{7,6},{8,9},{9,8},{10,11... | collective-permute-start | bytes 196616 | tf_op jit(solution)/shard_map/ppermute | solution.py:35
  28.4 5.0 %collective-permute-start.11 = (bf16[512,128]{1,0:T(8,128)(2,1)S(1)}, bf16[512,128]{1,0:T(8,128)(2,1)S(1)}, u32[]{:S(2)}, u32[]{:S(2)}) collective-permute-start(bf16[512,128]{1,0:T(8,128)(2,1)S(1)} %first_filter.2.refs_0_.refs_1_), channel_id=1, source_target_pairs={{0,8},{4,12},{8,0},{12,4},{1,9},{5,13},{9,1},{13,5},{2,10},{6,14},... | collective-permute-start | bytes 393224 | tf_op jit(solution)/shard_map/ppermute | solution.py:35
  30.1 4.3 %collective-permute-start.16 = (bf16[256,128]{1,0:T(8,128)(2,1)S(1)}, bf16[256,128]{1,0:T(8,128)(2,1)S(1)}, u32[]{:S(2)}, u32[]{:S(2)}) collective-permute-start(bf16[256,128]{1,0:T(8,128)(2,1)S(1)} %first_filter.3.refs_4_.refs_5_), channel_id=1, source_target_pairs={{0,8},{4,12},{8,0},{12,4},{1,9},{5,13},{9,1},{13,5},{2,10},{6,14},... | collective-permute-start | bytes 196616 | tf_op jit(solution)/shard_map/ppermute | solution.py:35
  30.7 5.0 %collective-permute-start.10 = (bf16[512,128]{1,0:T(8,128)(2,1)S(1)}, bf16[512,128]{1,0:T(8,128)(2,1)S(1)}, u32[]{:S(2)}, u32[]{:S(2)}) collective-permute-start(bf16[512,128]{1,0:T(8,128)(2,1)S(1)} %first_filter.2.refs_0_.refs_1_), channel_id=1, source_target_pairs={{0,4},{4,0},{8,12},{12,8},{1,5},{5,1},{9,13},{13,9},{2,6},{6,2},{1... | collective-permute-start | bytes 393224 | tf_op jit(solution)/shard_map/ppermute | solution.py:35
  33.5 2.3 %collective-permute-start.12 = (bf16[512,128]{1,0:T(8,128)(2,1)S(1)}, bf16[512,128]{1,0:T(8,128)(2,1)S(1)}, u32[]{:S(2)}, u32[]{:S(2)}) collective-permute-start(bf16[512,128]{1,0:T(8,128)(2,1)S(1)} %collective-permute-done.11.refs_2_), channel_id=1, source_target_pairs={{0,4},{4,0},{8,12},{12,8},{1,5},{5,1},{9,13},{13,9},{2,6},{6,2},{1... | collective-permute-start | bytes 393224 | tf_op jit(solution)/shard_map/ppermute | solution.py:35
  33.5 1.4 %collective-permute-start.15 = (bf16[256,128]{1,0:T(8,128)(2,1)S(1)}, bf16[256,128]{1,0:T(8,128)(2,1)S(1)}, u32[]{:S(2)}, u32[]{:S(2)}) collective-permute-start(bf16[256,128]{1,0:T(8,128)(2,1)S(1)} %first_filter.3.refs_4_.refs_5_), channel_id=1, source_target_pairs={{0,4},{4,0},{8,12},{12,8},{1,5},{5,1},{9,13},{13,9},{2,6},{6,2},{1... | collective-permute-start | bytes 196616 | tf_op jit(solution)/shard_map/ppermute | solution.py:35
  34.5 1.3 %collective-permute-start.17 = (bf16[256,128]{1,0:T(8,128)(2,1)S(1)}, bf16[256,128]{1,0:T(8,128)(2,1)S(1)}, u32[]{:S(2)}, u32[]{:S(2)}) collective-permute-start(bf16[256,128]{1,0:T(8,128)(2,1)S(1)} %collective-permute-done.16.refs_6_), channel_id=1, source_target_pairs={{0,4},{4,0},{8,12},{12,8},{1,5},{5,1},{9,13},{13,9},{2,6},{6,2},{1... | collective-permute-start | bytes 196616 | tf_op jit(solution)/shard_map/ppermute | solution.py:35
  37.0 6.3 %collective-permute-start.18 = (bf16[512,128]{1,0:T(8,128)(2,1)S(1)}, bf16[512,128]{1,0:T(8,128)(2,1)S(1)}, u32[]{:S(2)}, u32[]{:S(2)}) collective-permute-start(bf16[512,128]{1,0:T(8,128)(2,1)S(1)} %get-tuple-element.56), channel_id=1, source_target_pairs={{0,1},{1,0},{2,3},{3,2},{4,5},{5,4},{6,7},{7,6},{8,9},{9,8},{10,11... | collective-permute-start | bytes 393224 | tf_op jit(solution)/shard_map/ppermute | solution.py:35
  37.7 7.4 %collective-permute-start.20 = (bf16[256,128]{1,0:T(8,128)(2,1)S(1)}, bf16[256,128]{1,0:T(8,128)(2,1)S(1)}, u32[]{:S(2)}, u32[]{:S(2)}) collective-permute-start(bf16[256,128]{1,0:T(8,128)(2,1)S(1)} %get-tuple-element.58), channel_id=1, source_target_pairs={{0,1},{1,0},{2,3},{3,2},{4,5},{5,4},{6,7},{7,6},{8,9},{9,8},{10,11... | collective-permute-start | bytes 196616 | tf_op jit(solution)/shard_map/ppermute | solution.py:35
  43.3 10.7 %collective-permute-start.19 = (bf16[512,128]{1,0:T(8,128)(2,1)S(1)}, bf16[512,128]{1,0:T(8,128)(2,1)S(1)}, u32[]{:S(2)}, u32[]{:S(2)}) collective-permute-start(bf16[512,128]{1,0:T(8,128)(2,1)S(1)} %add.29.refs_0_), channel_id=1, source_target_pairs={{0,2},{1,3},{2,0},{3,1},{4,6},{5,7},{6,4},{7,5},{8,10},{9,11},{10,... | collective-permute-start | bytes 393224 | tf_op jit(solution)/shard_map/ppermute | solution.py:35
  45.1 8.9 %collective-permute-start.22 = (bf16[256,128]{1,0:T(8,128)(2,1)S(1)}, bf16[256,128]{1,0:T(8,128)(2,1)S(1)}, u32[]{:S(2)}, u32[]{:S(2)}) collective-permute-start(bf16[256,128]{1,0:T(8,128)(2,1)S(1)} %get-tuple-element.63), channel_id=1, source_target_pairs={{0,2},{1,3},{2,0},{3,1},{4,6},{5,7},{6,4},{7,5},{8,10},{9,11},{10,... | collective-permute-start | bytes 196616 | tf_op jit(solution)/shard_map/ppermute | solution.py:35
  46.4 8.9 %collective-permute-start.21 = (bf16[512,128]{1,0:T(8,128)(2,1)S(1)}, bf16[512,128]{1,0:T(8,128)(2,1)S(1)}, u32[]{:S(2)}, u32[]{:S(2)}) collective-permute-start(bf16[512,128]{1,0:T(8,128)(2,1)S(1)} %get-tuple-element.61), channel_id=1, source_target_pairs={{0,1},{1,0},{2,3},{3,2},{4,5},{5,4},{6,7},{7,6},{8,9},{9,8},{10,11... | collective-permute-start | bytes 393224 | tf_op jit(solution)/shard_map/ppermute | solution.py:35
  47.7 7.6 %collective-permute-start.23 = (bf16[256,128]{1,0:T(8,128)(2,1)S(1)}, bf16[256,128]{1,0:T(8,128)(2,1)S(1)}, u32[]{:S(2)}, u32[]{:S(2)}) collective-permute-start(bf16[256,128]{1,0:T(8,128)(2,1)S(1)} %get-tuple-element.64), channel_id=1, source_target_pairs={{0,1},{1,0},{2,3},{3,2},{4,5},{5,4},{6,7},{7,6},{8,9},{9,8},{10,11... | collective-permute-start | bytes 196616 | tf_op jit(solution)/shard_map/ppermute | solution.py:35
  55.8 1.3 %collective-permute-start.24 = (f32[96,128]{1,0:T(8,128)S(1)}, f32[96,128]{1,0:T(8,128)S(1)}, u32[]{:S(2)}, u32[]{:S(2)}) collective-permute-start(f32[96,128]{1,0:T(8,128)S(1)} %get-tuple-element.66), channel_id=1, source_target_pairs={{0,4},{4,0},{8,12},{12,8},{1,5},{5,1},{9,13},{13,9},{2,6},{6,2},{1... | collective-permute-start | bytes 147464 | tf_op jit(solution)/shard_map/ppermute | solution.py:35
  57.1 4.2 %collective-permute-start.25 = (f32[96,128]{1,0:T(8,128)S(1)}, f32[96,128]{1,0:T(8,128)S(1)}, u32[]{:S(2)}, u32[]{:S(2)}) collective-permute-start(f32[96,128]{1,0:T(8,128)S(1)} %add.19), channel_id=1, source_target_pairs={{0,8},{4,12},{8,0},{12,4},{1,9},{5,13},{9,1},{13,5},{2,10},{6,14},... | collective-permute-start | bytes 147464 | tf_op jit(solution)/shard_map/ppermute | solution.py:35
  61.3 6.1 %collective-permute-start.28 = (f32[96,128]{1,0:T(8,128)S(1)}, f32[96,128]{1,0:T(8,128)S(1)}, u32[]{:S(2)}, u32[]{:S(2)}) collective-permute-start(f32[96,128]{1,0:T(8,128)S(1)} %add.20), channel_id=1, source_target_pairs={{0,3},{1,2},{2,1},{3,0},{4,7},{5,6},{6,5},{7,4},{8,11},{9,10},{10,... | collective-permute-start | bytes 147464 | tf_op jit(solution)/shard_map/ppermute | solution.py:35
  64.4 5.0 %collective-permute-start.27 = (f32[96,128]{1,0:T(8,128)S(1)}, f32[96,128]{1,0:T(8,128)S(1)}, u32[]{:S(2)}, u32[]{:S(2)}) collective-permute-start(f32[96,128]{1,0:T(8,128)S(1)} %add.20), channel_id=1, source_target_pairs={{0,2},{1,3},{2,0},{3,1},{4,6},{5,7},{6,4},{7,5},{8,10},{9,11},{10,... | collective-permute-start | bytes 147464 | tf_op jit(solution)/shard_map/ppermute | solution.py:35
  64.4 5.0 %collective-permute-start.26 = (f32[96,128]{1,0:T(8,128)S(1)}, f32[96,128]{1,0:T(8,128)S(1)}, u32[]{:S(2)}, u32[]{:S(2)}) collective-permute-start(f32[96,128]{1,0:T(8,128)S(1)} %add.20), channel_id=1, source_target_pairs={{0,1},{1,0},{2,3},{3,2},{4,5},{5,4},{6,7},{7,6},{8,9},{9,8},{10,11... | collective-permute-start | bytes 147464 | tf_op jit(solution)/shard_map/ppermute | solution.py:35
  69.4 1.3 %collective-permute-start.29 = (f32[96,128]{1,0:T(8,128)S(1)}, f32[96,128]{1,0:T(8,128)S(1)}, u32[]{:S(2)}, u32[]{:S(2)}) collective-permute-start(f32[96,128]{1,0:T(8,128)S(1)} %add_add_fusion.keep_ref), channel_id=1, source_target_pairs={{0,4},{4,0},{8,12},{12,8},{1,5},{5,1},{9,13},{13,9},{2,6},{6,2},{1... | collective-permute-start | bytes 147464 | tf_op jit(solution)/shard_map/ppermute | solution.py:35
  (2 other events, 1.6 us)

commit v5 on v4

--- a/solution.py
+++ b/solution.py
@@ -10,7 +10,7 @@
 LANES = 128
 SIZE = LANES // 2
 GIGA = 10**9
-COSTS = ((3, 1, 3), (3, 1, 0))
+COSTS = ((3, 1, 3), (3, 0, 0))
 F32 = jnp.float32
 BF16 = jnp.bfloat16
 VMEM = pl.BlockSpec(memory_space=pltpu.VMEM)
@@ -35,10 +35,6 @@
     return lax.ppermute(x, axis, [(i, i ^ key) for i in range(count)])
 
 
-def gather_shards(own, twin):
-    return list(zip(*(gather_one(*x) for x in zip(own, twin))))
-
-
 def gather_one(own, twin):
     shards = {0: own}
     bit = lax.axis_size("row") // 2
@@ -64,17 +60,14 @@
     orbitals,
     lower_ref,
     upper_ref,
-    wide_ref,
-    thin_ref,
+    vec_ref,
     ids_ref,
     ham_ref,
-    wide_out,
-    thin_out,
+    vec_out,
     at_out,
     ends_out,
 ):
-    wide_out[...] = wide_ref[...]
-    thin_out[...] = thin_ref[...]
+    vec_out[...] = vec_ref[...]
     low = jnp.full((8, LANES), lower_ref[0], F32)
     high = jnp.full((8, LANES), upper_ref[0], F32)
     ends_out[pl.ds(0, 8), :] = (high + low) * 0.5
@@ -371,23 +364,30 @@
     shapes = [jax.ShapeDtypeStruct((x, LANES), BF16) for x in (rows, rows // 2)]
     half_gram = jax.ShapeDtypeStruct((3 * SIZE // 2, LANES), F32)
     gram = pltpu.VMEM((3 * SIZE, LANES), F32)
-    ends_shape = jax.ShapeDtypeStruct((16, LANES), F32)
-
-    start = call(pack_kernel, shapes, [VMEM], name="pack")(vectors.T)
-    *twin, at, ends = call(
+
+    turned = vectors.T
+    twin, at, ends = call(
         functools.partial(load_kernel, own_blocks, orbitals),
-        [*shapes, jax.ShapeDtypeStruct(columns.shape[::-1], jnp.int32), ends_shape],
-        [SMEM] * 2 + [VMEM] * 4,
+        [
+            jax.ShapeDtypeStruct(turned.shape, BF16),
+            jax.ShapeDtypeStruct(columns.shape[::-1], jnp.int32),
+            jax.ShapeDtypeStruct((16, LANES), F32),
+        ],
+        [SMEM] * 2 + [VMEM] * 3,
         name="load",
-    )(lower, upper, *start, columns.T, hamiltonian)
-    terms = summands(own_blocks, at, hamiltonian, gather_shards(start, twin), COSTS[0])
+    )(lower, upper, turned, columns.T, hamiltonian)
+    parts = [
+        call(pack_kernel, shapes, [VMEM], name="pack")(x) for x in gather_one(turned, twin)
+    ]
+    start = parts[0]
+    terms = summands(own_blocks, at, hamiltonian, parts, COSTS[0])
     first = [
         call(first_kernel, shape, [VMEM] * (2 + len(x)), name="first_filter")(
             ends, vec, *x
         )
         for shape, vec, x in zip(shapes, start, terms)
     ]
-    terms = summands(own_blocks, at, hamiltonian, gather_shards(first, first), COSTS[1])
+    terms = summands(own_blocks, at, hamiltonian, list(zip(*(gather_one(x, x) for x in first))), COSTS[1])
     operands = [x for each in zip(start, first, terms) for x in (each[0], each[1], *each[2])]
     wide, thin, keep, send = call(
         functools.partial(second_kernel, rows_all),

time: 78.8 us -> 77.1 us (0.978)
  waiting for transfers between devices: 32.1 us -> 30.6 us
    ppermute x30 -> x27, waiting for transfers between devices: 32.1 us -> 30.6 us  [swap(): return lax.ppermute(x, axis, [(i, i ^ key) for i in range(count)])]
    ppermute x30 -> x27, starting transfers between devices: 27.1 us -> 26.5 us  [swap(): return lax.ppermute(x, axis, [(i, i ^ key) for i in range(count)])]
  transfers between devices with their start and end apart: 30 -> 27, of which waited for: 19 -> 18; matrix products, arithmetic and copies ran while one was open for 0% -> 0% of each run, Pallas kernels for 5% -> 6%
where the time goes in v5:
time: 77.1 us; the launch traced here: 76.9 us
  waiting for transfers between devices  30.6 us (40%)
  starting transfers between devices  26.5 us (34%)
  Pallas kernels  15.4 us (20%)
  local copies, waits for them, and re-layouts  3.02 us (4%)
  between operations  1.45 us (2%)
    ppermute x27, waiting for transfers between devices, swap(): return lax.ppermute(x, axis, [(i, i ^ key) for i in range(count)])  30.6 us
    ppermute x27, starting transfers between devices, swap(): return lax.ppermute(x, axis, [(i, i ^ key) for i in range(count)])  26.5 us
    pallas_call x1, Pallas kernels, per_device(): call(last_kernel, jax.ShapeDtypeStruct((LANES + SIZE, rows), F32), [VMEM]...  7.91 us
    pallas_call x4, Pallas kernels, product(): call(functools.partial(product_kernel, keys, n_row, own_blocks), [jax.Sha...  6.17 us
    unnamed x8, local copies, waits for them, and re-layouts  3.02 us
  transfers between devices with their start and end apart: 27, of which 18 were waited for; matrix products, arithmetic and copies ran while one was open for 0% of the time, Pallas kernels for 6%

profile of v5, /device:TPU:0, one launch (start us, length us, event | category | flops | bytes accessed | tf_op | source)
XLA Modules:
  0.0 76.9 jit_solution(16570390341557493781)
XLA Ops:
  0.0 3.0 %collective-permute-start.1 = (bf16[192,512]{1,0:T(8,128)(2,1)}, bf16[192,512]{1,0:T(8,128)(2,1)S(1)}, u32[]{:S(2)}, u32[]{:S(2)}) collective-permute-start(bf16[192,512]{1,0:T(8,128)(2,1)} %bitcast.3), channel_id=1, source_target_pairs={{0,8},{4,12},{8,0},{12,4},{1,9},{5,13},{9,1},{13,5},{2,10},{6,14},... | collective-permute-start | bytes 589832 | tf_op jit(solution)/shard_map/ppermute | solution.py:35
  4.3 1.4 %copy-done = bf16[32,64,384]{2,1,0:T(8,128)(2,1)S(1)} copy-done((bf16[32,64,384]{2,1,0:T(8,128)(2,1)S(1)}, bf16[32,64,384]{2,1,0:T(8,128)(2,1)}, u32[]{:S(2)}) %copy-start) | copy-done | bytes 1572888
  5.7 0.9 %copy-done.2 = bf16[512,192]{0,1:T(8,128)(2,1)S(1)} copy-done((bf16[512,192]{0,1:T(8,128)(2,1)S(1)}, bf16[512,192]{0,1:T(8,128)(2,1)}, u32[]{:S(2)}) %copy-start.2) | copy-done | bytes 196632
  9.7 1.3 %product.5 = (bf16[512,128]{1,0:T(8,128)(2,1)S(1)}, bf16[256,128]{1,0:T(8,128)(2,1)S(1)}) custom-call(s32[6,32]{1,0:T(8,128)S(1)} %get-tuple-element.44.at_ref, bf16[32,64,384]{2,1,0:T(8,128)(2,1)S(1)} %copy-done.1, bf16[512,128]{1,0:T(8,128)(2,1)S(1)} %get-tuple-element.43.refs_0_.start, bf16[512,128]{1,0:T(8,128)(2,1)S(1)} %get-tuple-element.46.refs_1_, ...), custom_call_target="tpu_custom_call" | custom-call | flops 100663296 | bytes 1000 | tf_op jit(solution)/shard_map/product/pallas_call | solution.py:123
  10.9 1.9 %collective-permute-start.3 = (bf16[512,128]{1,0:T(8,128)(2,1)S(1)}, bf16[512,128]{1,0:T(8,128)(2,1)S(1)}, u32[]{:S(2)}, u32[]{:S(2)}) collective-permute-start(bf16[512,128]{1,0:T(8,128)(2,1)S(1)} %get-tuple-element.55), channel_id=1, source_target_pairs={{0,1},{1,0},{2,3},{3,2},{4,5},{5,4},{6,7},{7,6},{8,9},{9,8},{10,11... | collective-permute-start | bytes 393224 | tf_op jit(solution)/shard_map/ppermute | solution.py:35
  13.0 1.8 %product.4 = (bf16[512,128]{1,0:T(8,128)(2,1)S(1)}, bf16[512,128]{1,0:T(8,128)(2,1)S(1)}, bf16[512,128]{1,0:T(8,128)(2,1)S(1)}, bf16[256,128]{1,0:T(8,128)(2,1)S...) custom-call(s32[6,32]{1,0:T(8,128)S(1)} %get-tuple-element.44.at_ref, ...), custom_call_target="tpu_custom_call" | custom-call | flops 301989888 | bytes 1000 | tf_op jit(solution)/shard_map/product/pallas_call | solution.py:123
  14.8 2.4 %collective-permute-done.3.refs_1_ = bf16[512,128]{1,0:T(8,128)(2,1)S(1)} collective-permute-done((bf16[512,128]{1,0:T(8,128)(2,1)S(1)}, bf16[512,128]{1,0:T(8,128)(2,1)S(1)}, u32[]{:S(2)}, u32[]{:S(2)}) %collective-permute-start.3) | collective-permute-done | bytes 131104 | tf_op jit(solution)/shard_map/ppermute | solution.py:35
  17.3 2.8 %collective-permute-start.4 = (bf16[512,128]{1,0:T(8,128)(2,1)S(1)}, bf16[512,128]{1,0:T(8,128)(2,1)S(1)}, u32[]{:S(2)}, u32[]{:S(2)}) collective-permute-start(bf16[512,128]{1,0:T(8,128)(2,1)S(1)} %add.27.refs_0_), channel_id=1, source_target_pairs={{0,2},{1,3},{2,0},{3,1},{4,6},{5,7},{6,4},{7,5},{8,10},{9,11},{10,... | collective-permute-start | bytes 393224 | tf_op jit(solution)/shard_map/ppermute | solution.py:35
  20.2 1.6 %collective-permute-start.6 = (bf16[512,128]{1,0:T(8,128)(2,1)S(1)}, bf16[512,128]{1,0:T(8,128)(2,1)S(1)}, u32[]{:S(2)}, u32[]{:S(2)}) collective-permute-start(bf16[512,128]{1,0:T(8,128)(2,1)S(1)} %get-tuple-element.60), channel_id=1, source_target_pairs={{0,1},{1,0},{2,3},{3,2},{4,5},{5,4},{6,7},{7,6},{8,9},{9,8},{10,11... | collective-permute-start | bytes 393224 | tf_op jit(solution)/shard_map/ppermute | solution.py:35
  22.9 3.7 %collective-permute-done.4.b = bf16[512,128]{1,0:T(8,128)(2,1)S(1)} collective-permute-done((bf16[512,128]{1,0:T(8,128)(2,1)S(1)}, bf16[512,128]{1,0:T(8,128)(2,1)S(1)}, u32[]{:S(2)}, u32[]{:S(2)}) %collective-permute-start.4) | collective-permute-done | bytes 131104 | tf_op jit(solution)/shard_map/ppermute | solution.py:35
  26.6 1.1 %collective-permute-done.6.refs_1_ = bf16[512,128]{1,0:T(8,128)(2,1)S(1)} collective-permute-done((bf16[512,128]{1,0:T(8,128)(2,1)S(1)}, bf16[512,128]{1,0:T(8,128)(2,1)S(1)}, u32[]{:S(2)}, u32[]{:S(2)}) %collective-permute-start.6) | collective-permute-done | bytes 131104 | tf_op jit(solution)/shard_map/ppermute | solution.py:35
  27.8 1.6 %collective-permute-start.8 = (bf16[512,128]{1,0:T(8,128)(2,1)S(1)}, bf16[512,128]{1,0:T(8,128)(2,1)S(1)}, u32[]{:S(2)}, u32[]{:S(2)}) collective-permute-start(bf16[512,128]{1,0:T(8,128)(2,1)S(1)} %first_filter.2.refs_0_.refs_1_), channel_id=1, source_target_pairs={{0,8},{4,12},{8,0},{12,4},{1,9},{5,13},{9,1},{13,5},{2,10},{6,14},... | collective-permute-start | bytes 393224 | tf_op jit(solution)/shard_map/ppermute | solution.py:35
  30.1 2.7 %collective-permute-done.8.refs_2_ = bf16[512,128]{1,0:T(8,128)(2,1)S(1)} collective-permute-done((bf16[512,128]{1,0:T(8,128)(2,1)S(1)}, bf16[512,128]{1,0:T(8,128)(2,1)S(1)}, u32[]{:S(2)}, u32[]{:S(2)}) %collective-permute-start.8) | collective-permute-done | bytes 131104 | tf_op jit(solution)/shard_map/ppermute | solution.py:35
  34.3 0.8 %collective-permute-done.14.refs_7_ = bf16[256,128]{1,0:T(8,128)(2,1)S(1)} collective-permute-done((bf16[256,128]{1,0:T(8,128)(2,1)S(1)}, bf16[256,128]{1,0:T(8,128)(2,1)S(1)}, u32[]{:S(2)}, u32[]{:S(2)}) %collective-permute-start.14) | collective-permute-done | bytes 65568 | tf_op jit(solution)/shard_map/ppermute | solution.py:35
  35.1 1.2 %product.7 = (bf16[512,128]{1,0:T(8,128)(2,1)S(1)}, bf16[256,128]{1,0:T(8,128)(2,1)S(1)}) custom-call(s32[6,32]{1,0:T(8,128)S(1)} %get-tuple-element.44.at_ref, bf16[32,64,384]{2,1,0:T(8,128)(2,1)S(1)} %copy-done.1, bf16[512,128]{1,0:T(8,128)(2,1)S(1)} %first_filter.2.refs_0_.refs_1_, bf16[512,128]{1,0:T(8,128)(2,1)S(1)} %collective-permute-done.7.refs_1_, ...), custom_call_target="tpu_custom_call" | custom-call | flops 100663296 | bytes 1000 | tf_op jit(solution)/shard_map/product/pallas_call | solution.py:123
  37.1 1.4 %collective-permute-start.17 = (bf16[256,128]{1,0:T(8,128)(2,1)S(1)}, bf16[256,128]{1,0:T(8,128)(2,1)S(1)}, u32[]{:S(2)}, u32[]{:S(2)}) collective-permute-start(bf16[256,128]{1,0:T(8,128)(2,1)S(1)} %get-tuple-element.68), channel_id=1, source_target_pairs={{0,1},{1,0},{2,3},{3,2},{4,5},{5,4},{6,7},{7,6},{8,9},{9,8},{10,11... | collective-permute-start | bytes 196616 | tf_op jit(solution)/shard_map/ppermute | solution.py:35
  38.4 1.8 %product.6 = (bf16[512,128]{1,0:T(8,128)(2,1)S(1)}, bf16[512,128]{1,0:T(8,128)(2,1)S(1)}, bf16[512,128]{1,0:T(8,128)(2,1)S(1)}, bf16[256,128]{1,0:T(8,128)(2,1)S...) custom-call(s32[6,32]{1,0:T(8,128)S(1)} %get-tuple-element.44.at_ref, ...), custom_call_target="tpu_custom_call" | custom-call | flops 301989888 | bytes 1000 | tf_op jit(solution)/shard_map/product/pallas_call | solution.py:123
  40.3 2.4 %collective-permute-done.15.refs_1_ = bf16[512,128]{1,0:T(8,128)(2,1)S(1)} collective-permute-done((bf16[512,128]{1,0:T(8,128)(2,1)S(1)}, bf16[512,128]{1,0:T(8,128)(2,1)S(1)}, u32[]{:S(2)}, u32[]{:S(2)}) %collective-permute-start.15) | collective-permute-done | bytes 131104 | tf_op jit(solution)/shard_map/ppermute | solution.py:35
  42.7 1.7 %collective-permute-start.16 = (bf16[512,128]{1,0:T(8,128)(2,1)S(1)}, bf16[512,128]{1,0:T(8,128)(2,1)S(1)}, u32[]{:S(2)}, u32[]{:S(2)}) collective-permute-start(bf16[512,128]{1,0:T(8,128)(2,1)S(1)} %add.29.refs_0_), channel_id=1, source_target_pairs={{0,2},{1,3},{2,0},{3,1},{4,6},{5,7},{6,4},{7,5},{8,10},{9,11},{10,... | collective-permute-start | bytes 393224 | tf_op jit(solution)/shard_map/ppermute | solution.py:35
  44.4 2.0 %collective-permute-start.18 = (bf16[512,128]{1,0:T(8,128)(2,1)S(1)}, bf16[512,128]{1,0:T(8,128)(2,1)S(1)}, u32[]{:S(2)}, u32[]{:S(2)}) collective-permute-start(bf16[512,128]{1,0:T(8,128)(2,1)S(1)} %get-tuple-element.71), channel_id=1, source_target_pairs={{0,1},{1,0},{2,3},{3,2},{4,5},{5,4},{6,7},{7,6},{8,9},{9,8},{10,11... | collective-permute-start | bytes 393224 | tf_op jit(solution)/shard_map/ppermute | solution.py:35
  47.1 0.7 collective-permute-start.20
  47.8 4.9 %collective-permute-done.19.b = bf16[256,128]{1,0:T(8,128)(2,1)S(1)} collective-permute-done((bf16[256,128]{1,0:T(8,128)(2,1)S(1)}, bf16[256,128]{1,0:T(8,128)(2,1)S(1)}, u32[]{:S(2)}, u32[]{:S(2)}) %collective-permute-start.19) | collective-permute-done | bytes 65568 | tf_op jit(solution)/shard_map/ppermute | solution.py:35
  52.8 1.1 %collective-permute-done.20.refs_7_ = bf16[256,128]{1,0:T(8,128)(2,1)S(1)} collective-permute-done((bf16[256,128]{1,0:T(8,128)(2,1)S(1)}, bf16[256,128]{1,0:T(8,128)(2,1)S(1)}, u32[]{:S(2)}, u32[]{:S(2)}) %collective-permute-start.20) | collective-permute-done | bytes 65568 | tf_op jit(solution)/shard_map/ppermute | solution.py:35
  54.4 1.2 %collective-permute-done.21 = f32[96,128]{1,0:T(8,128)S(1)} collective-permute-done((f32[96,128]{1,0:T(8,128)S(1)}, f32[96,128]{1,0:T(8,128)S(1)}, u32[]{:S(2)}, u32[]{:S(2)}) %collective-permute-start.21) | collective-permute-done | bytes 49184 | tf_op jit(solution)/shard_map/ppermute | solution.py:35
  55.7 1.3 %collective-permute-start.22 = (f32[96,128]{1,0:T(8,128)S(1)}, f32[96,128]{1,0:T(8,128)S(1)}, u32[]{:S(2)}, u32[]{:S(2)}) collective-permute-start(f32[96,128]{1,0:T(8,128)S(1)} %add.19), channel_id=1, source_target_pairs={{0,8},{4,12},{8,0},{12,4},{1,9},{5,13},{9,1},{13,5},{2,10},{6,14},... | collective-permute-start | bytes 147464 | tf_op jit(solution)/shard_map/ppermute | solution.py:35
  57.0 2.8 %collective-permute-done.22 = f32[96,128]{1,0:T(8,128)S(1)} collective-permute-done((f32[96,128]{1,0:T(8,128)S(1)}, f32[96,128]{1,0:T(8,128)S(1)}, u32[]{:S(2)}, u32[]{:S(2)}) %collective-permute-start.22) | collective-permute-done | bytes 49184 | tf_op jit(solution)/shard_map/ppermute | solution.py:35
  59.8 2.9 %collective-permute-start.25 = (f32[96,128]{1,0:T(8,128)S(1)}, f32[96,128]{1,0:T(8,128)S(1)}, u32[]{:S(2)}, u32[]{:S(2)}) collective-permute-start(f32[96,128]{1,0:T(8,128)S(1)} %add.20), channel_id=1, source_target_pairs={{0,3},{1,2},{2,1},{3,0},{4,7},{5,6},{6,5},{7,4},{8,11},{9,10},{10,... | collective-permute-start | bytes 147464 | tf_op jit(solution)/shard_map/ppermute | solution.py:35
  62.7 1.6 %collective-permute-start.23 = (f32[96,128]{1,0:T(8,128)S(1)}, f32[96,128]{1,0:T(8,128)S(1)}, u32[]{:S(2)}, u32[]{:S(2)}) collective-permute-start(f32[96,128]{1,0:T(8,128)S(1)} %add.20), channel_id=1, source_target_pairs={{0,1},{1,0},{2,3},{3,2},{4,5},{5,4},{6,7},{7,6},{8,9},{9,8},{10,11... | collective-permute-start | bytes 147464 | tf_op jit(solution)/shard_map/ppermute | solution.py:35
  64.3 1.6 %collective-permute-done.25 = f32[96,128]{1,0:T(8,128)S(1)} collective-permute-done((f32[96,128]{1,0:T(8,128)S(1)}, f32[96,128]{1,0:T(8,128)S(1)}, u32[]{:S(2)}, u32[]{:S(2)}) %collective-permute-start.25) | collective-permute-done | bytes 49184 | tf_op jit(solution)/shard_map/ppermute | solution.py:35
  65.9 1.8 %collective-permute-done.24 = f32[96,128]{1,0:T(8,128)S(1)} collective-permute-done((f32[96,128]{1,0:T(8,128)S(1)}, f32[96,128]{1,0:T(8,128)S(1)}, u32[]{:S(2)}, u32[]{:S(2)}) %collective-permute-start.24) | collective-permute-done | bytes 49184 | tf_op jit(solution)/shard_map/ppermute | solution.py:35
  67.8 1.2 %collective-permute-done.26.other_ref = f32[96,128]{1,0:T(8,128)S(1)} collective-permute-done((f32[96,128]{1,0:T(8,128)S(1)}, f32[96,128]{1,0:T(8,128)S(1)}, u32[]{:S(2)}, u32[]{:S(2)}) %collective-permute-start.26) | collective-permute-done | bytes 49184 | tf_op jit(solution)/shard_map/ppermute | solution.py:35
  69.0 7.9 %orthonormalize.1 = f32[192,512]{1,0:T(8,128)} custom-call(f32[96,128]{1,0:T(8,128)S(1)} %add_add_fusion.keep_ref, f32[96,128]{1,0:T(8,128)S(1)} %collective-permute-done.26.other_ref, bf16[512,128]{1,0:T(8,128)(2,1)S(1)} %get-tuple-element.77.wide_ref, bf16[256,128]{1,0:T(8,128)(2,1)S(1)} %get-tuple-element.78.thin_ref), custom_call_target="tpu_custom_call" | custom-call | flops 1000 | bytes 1000 | tf_op jit(solution)/shard_map/orthonormalize/pallas_call | solution.py:400
  (54 shorter events, 8.6 us)
Async XLA Ops:
  0.0 8.1 %collective-permute-start.1 = (bf16[192,512]{1,0:T(8,128)(2,1)}, bf16[192,512]{1,0:T(8,128)(2,1)S(1)}, u32[]{:S(2)}, u32[]{:S(2)}) collective-permute-start(bf16[192,512]{1,0:T(8,128)(2,1)} %bitcast.3), channel_id=1, source_target_pairs={{0,8},{4,12},{8,0},{12,4},{1,9},{5,13},{9,1},{13,5},{2,10},{6,14},... | collective-permute-start | bytes 589832 | tf_op jit(solution)/shard_map/ppermute | solution.py:35
  4.3 1.4 %copy-start = (bf16[32,64,384]{2,1,0:T(8,128)(2,1)S(1)}, bf16[32,64,384]{2,1,0:T(8,128)(2,1)}, u32[]{:S(2)}) copy-start(bf16[32,64,384]{2,1,0:T(8,128)(2,1)} %ham_ref.9) | copy-start | bytes 4718596
  5.7 0.9 %copy-start.2 = (bf16[512,192]{0,1:T(8,128)(2,1)S(1)}, bf16[512,192]{0,1:T(8,128)(2,1)}, u32[]{:S(2)}) copy-start(bf16[512,192]{0,1:T(8,128)(2,1)} %param.7) | copy-start | bytes 589828
  6.6 0.7 copy-start.3
  7.3 2.4 %copy-start.1 = (bf16[32,64,384]{2,1,0:T(8,128)(2,1)S(1)}, bf16[32,64,384]{2,1,0:T(8,128)(2,1)}, u32[]{:S(2)}) copy-start(bf16[32,64,384]{2,1,0:T(8,128)(2,1)} %ham_ref.9) | copy-start | bytes 4718596
  7.3 1.5 %collective-permute-start = (bf16[192,512]{1,0:T(8,128)(2,1)S(1)}, bf16[192,512]{1,0:T(8,128)(2,1)S(1)}, u32[]{:S(2)}, u32[]{:S(2)}) collective-permute-start(bf16[192,512]{1,0:T(8,128)(2,1)S(1)} %get-tuple-element.45), channel_id=1, source_target_pairs={{0,4},{4,0},{8,12},{12,8},{1,5},{5,1},{9,13},{13,9},{2,6},{6,2},{1... | collective-permute-start | bytes 589832 | tf_op jit(solution)/shard_map/ppermute | solution.py:35
  8.1 1.4 %collective-permute-start.2 = (bf16[192,512]{1,0:T(8,128)(2,1)S(1)}, bf16[192,512]{1,0:T(8,128)(2,1)S(1)}, u32[]{:S(2)}, u32[]{:S(2)}) collective-permute-start(bf16[192,512]{1,0:T(8,128)(2,1)S(1)} %collective-permute-done.1.turned_ref), channel_id=1, source_target_pairs={{0,4},{4,0},{8,12},{12,8},{1,5},{5,1},{9,13},{13,9},{2,6},{6,2},{1... | collective-permute-start | bytes 589832 | tf_op jit(solution)/shard_map/ppermute | solution.py:35
  10.9 6.4 %collective-permute-start.3 = (bf16[512,128]{1,0:T(8,128)(2,1)S(1)}, bf16[512,128]{1,0:T(8,128)(2,1)S(1)}, u32[]{:S(2)}, u32[]{:S(2)}) collective-permute-start(bf16[512,128]{1,0:T(8,128)(2,1)S(1)} %get-tuple-element.55), channel_id=1, source_target_pairs={{0,1},{1,0},{2,3},{3,2},{4,5},{5,4},{6,7},{7,6},{8,9},{9,8},{10,11... | collective-permute-start | bytes 393224 | tf_op jit(solution)/shard_map/ppermute | solution.py:35
  12.8 7.4 %collective-permute-start.5 = (bf16[256,128]{1,0:T(8,128)(2,1)S(1)}, bf16[256,128]{1,0:T(8,128)(2,1)S(1)}, u32[]{:S(2)}, u32[]{:S(2)}) collective-permute-start(bf16[256,128]{1,0:T(8,128)(2,1)S(1)} %get-tuple-element.57), channel_id=1, source_target_pairs={{0,1},{1,0},{2,3},{3,2},{4,5},{5,4},{6,7},{7,6},{8,9},{9,8},{10,11... | collective-permute-start | bytes 196616 | tf_op jit(solution)/shard_map/ppermute | solution.py:35
  17.3 9.3 %collective-permute-start.4 = (bf16[512,128]{1,0:T(8,128)(2,1)S(1)}, bf16[512,128]{1,0:T(8,128)(2,1)S(1)}, u32[]{:S(2)}, u32[]{:S(2)}) collective-permute-start(bf16[512,128]{1,0:T(8,128)(2,1)S(1)} %add.27.refs_0_), channel_id=1, source_target_pairs={{0,2},{1,3},{2,0},{3,1},{4,6},{5,7},{6,4},{7,5},{8,10},{9,11},{10,... | collective-permute-start | bytes 393224 | tf_op jit(solution)/shard_map/ppermute | solution.py:35
  20.2 7.5 %collective-permute-start.6 = (bf16[512,128]{1,0:T(8,128)(2,1)S(1)}, bf16[512,128]{1,0:T(8,128)(2,1)S(1)}, u32[]{:S(2)}, u32[]{:S(2)}) collective-permute-start(bf16[512,128]{1,0:T(8,128)(2,1)S(1)} %get-tuple-element.60), channel_id=1, source_target_pairs={{0,1},{1,0},{2,3},{3,2},{4,5},{5,4},{6,7},{7,6},{8,9},{9,8},{10,11... | collective-permute-start | bytes 393224 | tf_op jit(solution)/shard_map/ppermute | solution.py:35
  21.8 7.6 %collective-permute-start.10 = (bf16[256,128]{1,0:T(8,128)(2,1)S(1)}, bf16[256,128]{1,0:T(8,128)(2,1)S(1)}, u32[]{:S(2)}, u32[]{:S(2)}) collective-permute-start(bf16[256,128]{1,0:T(8,128)(2,1)S(1)} %get-tuple-element.62), channel_id=1, source_target_pairs={{0,2},{1,3},{2,0},{3,1},{4,6},{5,7},{6,4},{7,5},{8,10},{9,11},{10,... | collective-permute-start | bytes 196616 | tf_op jit(solution)/shard_map/ppermute | solution.py:35
  22.4 7.0 %collective-permute-start.11 = (bf16[256,128]{1,0:T(8,128)(2,1)S(1)}, bf16[256,128]{1,0:T(8,128)(2,1)S(1)}, u32[]{:S(2)}, u32[]{:S(2)}) collective-permute-start(bf16[256,128]{1,0:T(8,128)(2,1)S(1)} %get-tuple-element.63), channel_id=1, source_target_pairs={{0,1},{1,0},{2,3},{3,2},{4,5},{5,4},{6,7},{7,6},{8,9},{9,8},{10,11... | collective-permute-start | bytes 196616 | tf_op jit(solution)/shard_map/ppermute | solution.py:35
  27.8 5.0 %collective-permute-start.8 = (bf16[512,128]{1,0:T(8,128)(2,1)S(1)}, bf16[512,128]{1,0:T(8,128)(2,1)S(1)}, u32[]{:S(2)}, u32[]{:S(2)}) collective-permute-start(bf16[512,128]{1,0:T(8,128)(2,1)S(1)} %first_filter.2.refs_0_.refs_1_), channel_id=1, source_target_pairs={{0,8},{4,12},{8,0},{12,4},{1,9},{5,13},{9,1},{13,5},{2,10},{6,14},... | collective-permute-start | bytes 393224 | tf_op jit(solution)/shard_map/ppermute | solution.py:35
  29.5 4.3 %collective-permute-start.13 = (bf16[256,128]{1,0:T(8,128)(2,1)S(1)}, bf16[256,128]{1,0:T(8,128)(2,1)S(1)}, u32[]{:S(2)}, u32[]{:S(2)}) collective-permute-start(bf16[256,128]{1,0:T(8,128)(2,1)S(1)} %first_filter.3.refs_4_.refs_5_), channel_id=1, source_target_pairs={{0,8},{4,12},{8,0},{12,4},{1,9},{5,13},{9,1},{13,5},{2,10},{6,14},... | collective-permute-start | bytes 196616 | tf_op jit(solution)/shard_map/ppermute | solution.py:35
  30.1 5.0 %collective-permute-start.7 = (bf16[512,128]{1,0:T(8,128)(2,1)S(1)}, bf16[512,128]{1,0:T(8,128)(2,1)S(1)}, u32[]{:S(2)}, u32[]{:S(2)}) collective-permute-start(bf16[512,128]{1,0:T(8,128)(2,1)S(1)} %first_filter.2.refs_0_.refs_1_), channel_id=1, source_target_pairs={{0,4},{4,0},{8,12},{12,8},{1,5},{5,1},{9,13},{13,9},{2,6},{6,2},{1... | collective-permute-start | bytes 393224 | tf_op jit(solution)/shard_map/ppermute | solution.py:35
  32.8 2.3 %collective-permute-start.9 = (bf16[512,128]{1,0:T(8,128)(2,1)S(1)}, bf16[512,128]{1,0:T(8,128)(2,1)S(1)}, u32[]{:S(2)}, u32[]{:S(2)}) collective-permute-start(bf16[512,128]{1,0:T(8,128)(2,1)S(1)} %collective-permute-done.8.refs_2_), channel_id=1, source_target_pairs={{0,4},{4,0},{8,12},{12,8},{1,5},{5,1},{9,13},{13,9},{2,6},{6,2},{1... | collective-permute-start | bytes 393224 | tf_op jit(solution)/shard_map/ppermute | solution.py:35
  32.8 1.4 %collective-permute-start.12 = (bf16[256,128]{1,0:T(8,128)(2,1)S(1)}, bf16[256,128]{1,0:T(8,128)(2,1)S(1)}, u32[]{:S(2)}, u32[]{:S(2)}) collective-permute-start(bf16[256,128]{1,0:T(8,128)(2,1)S(1)} %first_filter.3.refs_4_.refs_5_), channel_id=1, source_target_pairs={{0,4},{4,0},{8,12},{12,8},{1,5},{5,1},{9,13},{13,9},{2,6},{6,2},{1... | collective-permute-start | bytes 196616 | tf_op jit(solution)/shard_map/ppermute | solution.py:35
  33.8 1.3 %collective-permute-start.14 = (bf16[256,128]{1,0:T(8,128)(2,1)S(1)}, bf16[256,128]{1,0:T(8,128)(2,1)S(1)}, u32[]{:S(2)}, u32[]{:S(2)}) collective-permute-start(bf16[256,128]{1,0:T(8,128)(2,1)S(1)} %collective-permute-done.13.refs_6_), channel_id=1, source_target_pairs={{0,4},{4,0},{8,12},{12,8},{1,5},{5,1},{9,13},{13,9},{2,6},{6,2},{1... | collective-permute-start | bytes 196616 | tf_op jit(solution)/shard_map/ppermute | solution.py:35
  36.3 6.3 %collective-permute-start.15 = (bf16[512,128]{1,0:T(8,128)(2,1)S(1)}, bf16[512,128]{1,0:T(8,128)(2,1)S(1)}, u32[]{:S(2)}, u32[]{:S(2)}) collective-permute-start(bf16[512,128]{1,0:T(8,128)(2,1)S(1)} %get-tuple-element.66), channel_id=1, source_target_pairs={{0,1},{1,0},{2,3},{3,2},{4,5},{5,4},{6,7},{7,6},{8,9},{9,8},{10,11... | collective-permute-start | bytes 393224 | tf_op jit(solution)/shard_map/ppermute | solution.py:35
  37.1 7.4 %collective-permute-start.17 = (bf16[256,128]{1,0:T(8,128)(2,1)S(1)}, bf16[256,128]{1,0:T(8,128)(2,1)S(1)}, u32[]{:S(2)}, u32[]{:S(2)}) collective-permute-start(bf16[256,128]{1,0:T(8,128)(2,1)S(1)} %get-tuple-element.68), channel_id=1, source_target_pairs={{0,1},{1,0},{2,3},{3,2},{4,5},{5,4},{6,7},{7,6},{8,9},{9,8},{10,11... | collective-permute-start | bytes 196616 | tf_op jit(solution)/shard_map/ppermute | solution.py:35
  42.7 10.0 %collective-permute-start.16 = (bf16[512,128]{1,0:T(8,128)(2,1)S(1)}, bf16[512,128]{1,0:T(8,128)(2,1)S(1)}, u32[]{:S(2)}, u32[]{:S(2)}) collective-permute-start(bf16[512,128]{1,0:T(8,128)(2,1)S(1)} %add.29.refs_0_), channel_id=1, source_target_pairs={{0,2},{1,3},{2,0},{3,1},{4,6},{5,7},{6,4},{7,5},{8,10},{9,11},{10,... | collective-permute-start | bytes 393224 | tf_op jit(solution)/shard_map/ppermute | solution.py:35
  44.4 9.5 %collective-permute-start.18 = (bf16[512,128]{1,0:T(8,128)(2,1)S(1)}, bf16[512,128]{1,0:T(8,128)(2,1)S(1)}, u32[]{:S(2)}, u32[]{:S(2)}) collective-permute-start(bf16[512,128]{1,0:T(8,128)(2,1)S(1)} %get-tuple-element.71), channel_id=1, source_target_pairs={{0,1},{1,0},{2,3},{3,2},{4,5},{5,4},{6,7},{7,6},{8,9},{9,8},{10,11... | collective-permute-start | bytes 393224 | tf_op jit(solution)/shard_map/ppermute | solution.py:35
  46.5 6.2 %collective-permute-start.19 = (bf16[256,128]{1,0:T(8,128)(2,1)S(1)}, bf16[256,128]{1,0:T(8,128)(2,1)S(1)}, u32[]{:S(2)}, u32[]{:S(2)}) collective-permute-start(bf16[256,128]{1,0:T(8,128)(2,1)S(1)} %get-tuple-element.73), channel_id=1, source_target_pairs={{0,2},{1,3},{2,0},{3,1},{4,6},{5,7},{6,4},{7,5},{8,10},{9,11},{10,... | collective-permute-start | bytes 196616 | tf_op jit(solution)/shard_map/ppermute | solution.py:35
  47.1 6.8 %collective-permute-start.20 = (bf16[256,128]{1,0:T(8,128)(2,1)S(1)}, bf16[256,128]{1,0:T(8,128)(2,1)S(1)}, u32[]{:S(2)}, u32[]{:S(2)}) collective-permute-start(bf16[256,128]{1,0:T(8,128)(2,1)S(1)} %get-tuple-element.74), channel_id=1, source_target_pairs={{0,1},{1,0},{2,3},{3,2},{4,5},{5,4},{6,7},{7,6},{8,9},{9,8},{10,11... | collective-permute-start | bytes 196616 | tf_op jit(solution)/shard_map/ppermute | solution.py:35
  54.4 1.3 %collective-permute-start.21 = (f32[96,128]{1,0:T(8,128)S(1)}, f32[96,128]{1,0:T(8,128)S(1)}, u32[]{:S(2)}, u32[]{:S(2)}) collective-permute-start(f32[96,128]{1,0:T(8,128)S(1)} %get-tuple-element.76), channel_id=1, source_target_pairs={{0,4},{4,0},{8,12},{12,8},{1,5},{5,1},{9,13},{13,9},{2,6},{6,2},{1... | collective-permute-start | bytes 147464 | tf_op jit(solution)/shard_map/ppermute | solution.py:35
  55.7 4.2 %collective-permute-start.22 = (f32[96,128]{1,0:T(8,128)S(1)}, f32[96,128]{1,0:T(8,128)S(1)}, u32[]{:S(2)}, u32[]{:S(2)}) collective-permute-start(f32[96,128]{1,0:T(8,128)S(1)} %add.19), channel_id=1, source_target_pairs={{0,8},{4,12},{8,0},{12,4},{1,9},{5,13},{9,1},{13,5},{2,10},{6,14},... | collective-permute-start | bytes 147464 | tf_op jit(solution)/shard_map/ppermute | solution.py:35
  59.8 6.1 %collective-permute-start.25 = (f32[96,128]{1,0:T(8,128)S(1)}, f32[96,128]{1,0:T(8,128)S(1)}, u32[]{:S(2)}, u32[]{:S(2)}) collective-permute-start(f32[96,128]{1,0:T(8,128)S(1)} %add.20), channel_id=1, source_target_pairs={{0,3},{1,2},{2,1},{3,0},{4,7},{5,6},{6,5},{7,4},{8,11},{9,10},{10,... | collective-permute-start | bytes 147464 | tf_op jit(solution)/shard_map/ppermute | solution.py:35
  62.7 5.0 %collective-permute-start.24 = (f32[96,128]{1,0:T(8,128)S(1)}, f32[96,128]{1,0:T(8,128)S(1)}, u32[]{:S(2)}, u32[]{:S(2)}) collective-permute-start(f32[96,128]{1,0:T(8,128)S(1)} %add.20), channel_id=1, source_target_pairs={{0,2},{1,3},{2,0},{3,1},{4,6},{5,7},{6,4},{7,5},{8,10},{9,11},{10,... | collective-permute-start | bytes 147464 | tf_op jit(solution)/shard_map/ppermute | solution.py:35
  62.7 5.0 %collective-permute-start.23 = (f32[96,128]{1,0:T(8,128)S(1)}, f32[96,128]{1,0:T(8,128)S(1)}, u32[]{:S(2)}, u32[]{:S(2)}) collective-permute-start(f32[96,128]{1,0:T(8,128)S(1)} %add.20), channel_id=1, source_target_pairs={{0,1},{1,0},{2,3},{3,2},{4,5},{5,4},{6,7},{7,6},{8,9},{9,8},{10,11... | collective-permute-start | bytes 147464 | tf_op jit(solution)/shard_map/ppermute | solution.py:35
  67.7 1.3 %collective-permute-start.26 = (f32[96,128]{1,0:T(8,128)S(1)}, f32[96,128]{1,0:T(8,128)S(1)}, u32[]{:S(2)}, u32[]{:S(2)}) collective-permute-start(f32[96,128]{1,0:T(8,128)S(1)} %add_add_fusion.keep_ref), channel_id=1, source_target_pairs={{0,4},{4,0},{8,12},{12,8},{1,5},{5,1},{9,13},{13,9},{2,6},{6,2},{1... | collective-permute-start | bytes 147464 | tf_op jit(solution)/shard_map/ppermute | solution.py:35

commit v6 on v5

--- a/solution.py
+++ b/solution.py
@@ -208,15 +208,24 @@
     upper = cross(thin, wide[:half]) * inv
     lower = cross(thin, wide[half:]) * inv
     bb = cross(thin, thin) * inv
-    turned = jnp.concatenate([bb[:SIZE, SIZE:], bb[:SIZE, :SIZE]], axis=1)
-    low_lane = lax.broadcasted_iota(jnp.int32, (SIZE, LANES), 1) < SIZE
-    gram[pl.ds(0, SIZE), :] = jnp.where(low_lane, aa[:SIZE], turned + bb[SIZE:])
-    gram[pl.ds(SIZE, SIZE), :] = aa[SIZE:]
-    gram[pl.ds(2 * SIZE, SIZE), :] = upper[:SIZE] + lower[SIZE:]
-    part = 3 * SIZE // 2
+    bb = bb[:SIZE, :SIZE] + bb[SIZE:, SIZE:]
+    corner = fold(aa[:SIZE, :SIZE])
+    gram[pl.ds(0, SIZE // 2), :] = fold(bb)
+    gram[pl.ds(SIZE // 2, SIZE), :] = aa[SIZE:]
+    gram[pl.ds(3 * SIZE // 2, SIZE), :] = upper[:SIZE] + lower[SIZE:]
+    part = gram.shape[0] // 2
     mine = lax.axis_index("row") & 1
-    keep_out[...] = gram[pl.ds(pl.multiple_of(mine * part, 8), part), :]
-    send_out[...] = gram[pl.ds(pl.multiple_of((1 - mine) * part, 8), part), :]
+    for out, half_at in ((keep_out, mine), (send_out, 1 - mine)):
+        out[pl.ds(0, SIZE // 2), :] = corner
+        out[pl.ds(SIZE // 2, part), :] = gram[pl.ds(pl.multiple_of(half_at * part, 8), part), :]
+
+
+def fold(block):
+    return jnp.concatenate([block[: SIZE // 2], block[SIZE // 2 :]], axis=1)
+
+
+def unfold(rows):
+    return jnp.concatenate([rows[:, :SIZE], rows[:, SIZE:]], axis=0)
 
 
 def inverse_factor(block):
@@ -276,12 +285,18 @@
     return out[:, size:]
 
 
-def last_kernel(keep_ref, other_ref, wide_ref, thin_ref, out_ref, gram, factor, result, sems):
+def corner_kernel(keep_ref, out_ref):
+    out_ref[...] = inverse_factor(unfold(keep_ref[pl.ds(0, SIZE // 2), :]))
+
+
+def last_kernel(
+    keep_ref, other_ref, corner_ref, wide_ref, thin_ref, out_ref, gram, factor, result, sems
+):
     size = LANES // 2
-    part = 3 * size // 2
+    part = gram.shape[0] // 2
     mine = lax.axis_index("row") & 1
-    gram[pl.ds(pl.multiple_of(mine * part, 8), part), :] = keep_ref[...]
-    gram[pl.ds(pl.multiple_of((1 - mine) * part, 8), part), :] = other_ref[...]
+    for ref, half_at in ((keep_ref, mine), (other_ref, 1 - mine)):
+        gram[pl.ds(pl.multiple_of(half_at * part, 8), part), :] = ref[pl.ds(size // 2, part), :]
     dot = functools.partial(
         jnp.dot, precision=lax.Precision.HIGHEST, preferred_element_type=F32
     )
@@ -295,10 +310,9 @@
             preferred_element_type=F32,
         )
 
-    g00 = gram[pl.ds(0, size), :][:, :size]
-    g22 = gram[pl.ds(0, size), :][:, size:]
-    strip = gram[pl.ds(size, 2 * size), :]
-    x0 = inverse_factor(g00)
+    g22 = unfold(gram[pl.ds(0, size // 2), :])
+    strip = gram[pl.ds(size // 2, 2 * size), :]
+    x0 = corner_ref[...]
     l_strip = dot_t(strip[:, :size], x0)
     rest = strip[:, size:] - dot_t(l_strip, l_strip[:size])
     x1 = inverse_factor(rest[:size])
@@ -362,8 +376,9 @@
     own_blocks = rows // orbitals
     rows_all = rows * lax.axis_size("col") * lax.axis_size("row")
     shapes = [jax.ShapeDtypeStruct((x, LANES), BF16) for x in (rows, rows // 2)]
-    half_gram = jax.ShapeDtypeStruct((3 * SIZE // 2, LANES), F32)
-    gram = pltpu.VMEM((3 * SIZE, LANES), F32)
+    half_gram = jax.ShapeDtypeStruct((7 * SIZE // 4, LANES), F32)
+    gram = pltpu.VMEM((5 * SIZE // 2, LANES), F32)
+    factor = pltpu.VMEM((3 * SIZE, LANES), F32)
 
     turned = vectors.T
     twin, at, ends = call(
@@ -397,14 +412,17 @@
         name="second_filter",
     )(ends, *operands)
     keep, other = sum_all(keep, send)
+    corner = call(
+        corner_kernel, jax.ShapeDtypeStruct((SIZE, SIZE), F32), [VMEM], flops=10**9, name="corner"
+    )(keep)
     basis = call(
         last_kernel,
         jax.ShapeDtypeStruct((LANES + SIZE, rows), F32),
-        [VMEM] * 4,
-        [gram, gram, pltpu.VMEM((LANES + SIZE, rows), F32), pltpu.SemaphoreType.DMA((2,))],
+        [VMEM] * 5,
+        [gram, factor, pltpu.VMEM((LANES + SIZE, rows), F32), pltpu.SemaphoreType.DMA((2,))],
         name="orthonormalize",
         out_specs=pl.BlockSpec(memory_space=pl.ANY),
-    )(keep, other, wide, thin)
+    )(keep, other, corner, wide, thin)
     return basis.T
 
 

time: 77.1 us -> 76.2 us (0.988)
  waiting for transfers between devices: 30.6 us -> 29.6 us
    pallas_call x1, Pallas kernels: 7.91 us -> 5.97 us  [per_device(): call(last_kernel, jax.ShapeDtypeStruct((LANES + SIZE, rows), F32), [VMEM]...]
    pallas_call x0 -> x1, Pallas kernels: none -> 1.88 us  [per_device(): call(corner_kernel, jax.ShapeDtypeStruct((SIZE, SIZE), F32), [VMEM], flop...]
    ppermute x27, waiting for transfers between devices: 30.6 us -> 29.6 us  [swap(): return lax.ppermute(x, axis, [(i, i ^ key) for i in range(count)])]
  transfers between devices with their start and end apart: 27 -> 27, of which waited for: 18 -> 17; matrix products, arithmetic and copies ran while one was open for 0% -> 0% of each run, Pallas kernels for 6% -> 8%
where the time goes in v6:
time: 76.2 us; the launch traced here: 76 us
  waiting for transfers between devices  29.6 us (39%)
  starting transfers between devices  26.5 us (35%)
  Pallas kernels  15.4 us (20%)
  local copies, waits for them, and re-layouts  3.02 us (4%)
  between operations  1.45 us (2%)
    ppermute x27, waiting for transfers between devices, swap(): return lax.ppermute(x, axis, [(i, i ^ key) for i in range(count)])  29.6 us
    ppermute x27, starting transfers between devices, swap(): return lax.ppermute(x, axis, [(i, i ^ key) for i in range(count)])  26.5 us
    pallas_call x4, Pallas kernels, product(): call(functools.partial(product_kernel, keys, n_row, own_blocks), [jax.Sha...  6.17 us
    pallas_call x1, Pallas kernels, per_device(): call(last_kernel, jax.ShapeDtypeStruct((LANES + SIZE, rows), F32), [VMEM]...  5.97 us
    unnamed x8, local copies, waits for them, and re-layouts  3.02 us
    pallas_call x1, Pallas kernels, per_device(): call(corner_kernel, jax.ShapeDtypeStruct((SIZE, SIZE), F32), [VMEM], flop...  1.88 us
  transfers between devices with their start and end apart: 27, of which 17 were waited for; matrix products, arithmetic and copies ran while one was open for 0% of the time, Pallas kernels for 8%

profile of v6, /device:TPU:0, one launch (start us, length us, event | category | flops | bytes accessed | tf_op | source)
XLA Modules:
  0.0 76.0 jit_solution(229832928083906987)
XLA Ops:
  0.0 3.0 %collective-permute-start.1 = (bf16[192,512]{1,0:T(8,128)(2,1)}, bf16[192,512]{1,0:T(8,128)(2,1)S(1)}, u32[]{:S(2)}, u32[]{:S(2)}) collective-permute-start(bf16[192,512]{1,0:T(8,128)(2,1)} %bitcast.3), channel_id=1, source_target_pairs={{0,8},{4,12},{8,0},{12,4},{1,9},{5,13},{9,1},{13,5},{2,10},{6,14},... | collective-permute-start | bytes 589832 | tf_op jit(solution)/shard_map/ppermute | solution.py:35
  4.3 1.4 %copy-done = bf16[32,64,384]{2,1,0:T(8,128)(2,1)S(1)} copy-done((bf16[32,64,384]{2,1,0:T(8,128)(2,1)S(1)}, bf16[32,64,384]{2,1,0:T(8,128)(2,1)}, u32[]{:S(2)}) %copy-start) | copy-done | bytes 1572888
  5.7 0.9 %copy-done.2 = bf16[512,192]{0,1:T(8,128)(2,1)S(1)} copy-done((bf16[512,192]{0,1:T(8,128)(2,1)S(1)}, bf16[512,192]{0,1:T(8,128)(2,1)}, u32[]{:S(2)}) %copy-start.2) | copy-done | bytes 196632
  9.7 1.3 %product.5 = (bf16[512,128]{1,0:T(8,128)(2,1)S(1)}, bf16[256,128]{1,0:T(8,128)(2,1)S(1)}) custom-call(s32[6,32]{1,0:T(8,128)S(1)} %get-tuple-element.44.at_ref, bf16[32,64,384]{2,1,0:T(8,128)(2,1)S(1)} %copy-done.1, bf16[512,128]{1,0:T(8,128)(2,1)S(1)} %get-tuple-element.43.refs_0_.start, bf16[512,128]{1,0:T(8,128)(2,1)S(1)} %get-tuple-element.46.refs_1_, ...), custom_call_target="tpu_custom_call" | custom-call | flops 100663296 | bytes 1000 | tf_op jit(solution)/shard_map/product/pallas_call | solution.py:123
  10.9 1.9 %collective-permute-start.3 = (bf16[512,128]{1,0:T(8,128)(2,1)S(1)}, bf16[512,128]{1,0:T(8,128)(2,1)S(1)}, u32[]{:S(2)}, u32[]{:S(2)}) collective-permute-start(bf16[512,128]{1,0:T(8,128)(2,1)S(1)} %get-tuple-element.55), channel_id=1, source_target_pairs={{0,1},{1,0},{2,3},{3,2},{4,5},{5,4},{6,7},{7,6},{8,9},{9,8},{10,11... | collective-permute-start | bytes 393224 | tf_op jit(solution)/shard_map/ppermute | solution.py:35
  13.0 1.8 %product.4 = (bf16[512,128]{1,0:T(8,128)(2,1)S(1)}, bf16[512,128]{1,0:T(8,128)(2,1)S(1)}, bf16[512,128]{1,0:T(8,128)(2,1)S(1)}, bf16[256,128]{1,0:T(8,128)(2,1)S...) custom-call(s32[6,32]{1,0:T(8,128)S(1)} %get-tuple-element.44.at_ref, ...), custom_call_target="tpu_custom_call" | custom-call | flops 301989888 | bytes 1000 | tf_op jit(solution)/shard_map/product/pallas_call | solution.py:123
  14.8 2.4 %collective-permute-done.3.refs_1_ = bf16[512,128]{1,0:T(8,128)(2,1)S(1)} collective-permute-done((bf16[512,128]{1,0:T(8,128)(2,1)S(1)}, bf16[512,128]{1,0:T(8,128)(2,1)S(1)}, u32[]{:S(2)}, u32[]{:S(2)}) %collective-permute-start.3) | collective-permute-done | bytes 131104 | tf_op jit(solution)/shard_map/ppermute | solution.py:35
  17.3 2.8 %collective-permute-start.4 = (bf16[512,128]{1,0:T(8,128)(2,1)S(1)}, bf16[512,128]{1,0:T(8,128)(2,1)S(1)}, u32[]{:S(2)}, u32[]{:S(2)}) collective-permute-start(bf16[512,128]{1,0:T(8,128)(2,1)S(1)} %add.27.refs_0_), channel_id=1, source_target_pairs={{0,2},{1,3},{2,0},{3,1},{4,6},{5,7},{6,4},{7,5},{8,10},{9,11},{10,... | collective-permute-start | bytes 393224 | tf_op jit(solution)/shard_map/ppermute | solution.py:35
  20.2 1.6 %collective-permute-start.6 = (bf16[512,128]{1,0:T(8,128)(2,1)S(1)}, bf16[512,128]{1,0:T(8,128)(2,1)S(1)}, u32[]{:S(2)}, u32[]{:S(2)}) collective-permute-start(bf16[512,128]{1,0:T(8,128)(2,1)S(1)} %get-tuple-element.60), channel_id=1, source_target_pairs={{0,1},{1,0},{2,3},{3,2},{4,5},{5,4},{6,7},{7,6},{8,9},{9,8},{10,11... | collective-permute-start | bytes 393224 | tf_op jit(solution)/shard_map/ppermute | solution.py:35
  22.9 3.7 %collective-permute-done.4.b = bf16[512,128]{1,0:T(8,128)(2,1)S(1)} collective-permute-done((bf16[512,128]{1,0:T(8,128)(2,1)S(1)}, bf16[512,128]{1,0:T(8,128)(2,1)S(1)}, u32[]{:S(2)}, u32[]{:S(2)}) %collective-permute-start.4) | collective-permute-done | bytes 131104 | tf_op jit(solution)/shard_map/ppermute | solution.py:35
  26.6 1.1 %collective-permute-done.6.refs_1_ = bf16[512,128]{1,0:T(8,128)(2,1)S(1)} collective-permute-done((bf16[512,128]{1,0:T(8,128)(2,1)S(1)}, bf16[512,128]{1,0:T(8,128)(2,1)S(1)}, u32[]{:S(2)}, u32[]{:S(2)}) %collective-permute-start.6) | collective-permute-done | bytes 131104 | tf_op jit(solution)/shard_map/ppermute | solution.py:35
  27.8 1.6 %collective-permute-start.8 = (bf16[512,128]{1,0:T(8,128)(2,1)S(1)}, bf16[512,128]{1,0:T(8,128)(2,1)S(1)}, u32[]{:S(2)}, u32[]{:S(2)}) collective-permute-start(bf16[512,128]{1,0:T(8,128)(2,1)S(1)} %first_filter.2.refs_0_.refs_1_), channel_id=1, source_target_pairs={{0,8},{4,12},{8,0},{12,4},{1,9},{5,13},{9,1},{13,5},{2,10},{6,14},... | collective-permute-start | bytes 393224 | tf_op jit(solution)/shard_map/ppermute | solution.py:35
  30.1 2.7 %collective-permute-done.8.refs_2_ = bf16[512,128]{1,0:T(8,128)(2,1)S(1)} collective-permute-done((bf16[512,128]{1,0:T(8,128)(2,1)S(1)}, bf16[512,128]{1,0:T(8,128)(2,1)S(1)}, u32[]{:S(2)}, u32[]{:S(2)}) %collective-permute-start.8) | collective-permute-done | bytes 131104 | tf_op jit(solution)/shard_map/ppermute | solution.py:35
  34.3 0.8 %collective-permute-done.14.refs_7_ = bf16[256,128]{1,0:T(8,128)(2,1)S(1)} collective-permute-done((bf16[256,128]{1,0:T(8,128)(2,1)S(1)}, bf16[256,128]{1,0:T(8,128)(2,1)S(1)}, u32[]{:S(2)}, u32[]{:S(2)}) %collective-permute-start.14) | collective-permute-done | bytes 65568 | tf_op jit(solution)/shard_map/ppermute | solution.py:35
  35.1 1.2 %product.7 = (bf16[512,128]{1,0:T(8,128)(2,1)S(1)}, bf16[256,128]{1,0:T(8,128)(2,1)S(1)}) custom-call(s32[6,32]{1,0:T(8,128)S(1)} %get-tuple-element.44.at_ref, bf16[32,64,384]{2,1,0:T(8,128)(2,1)S(1)} %copy-done.1, bf16[512,128]{1,0:T(8,128)(2,1)S(1)} %first_filter.2.refs_0_.refs_1_, bf16[512,128]{1,0:T(8,128)(2,1)S(1)} %collective-permute-done.7.refs_1_, ...), custom_call_target="tpu_custom_call" | custom-call | flops 100663296 | bytes 1000 | tf_op jit(solution)/shard_map/product/pallas_call | solution.py:123
  37.1 1.4 %collective-permute-start.17 = (bf16[256,128]{1,0:T(8,128)(2,1)S(1)}, bf16[256,128]{1,0:T(8,128)(2,1)S(1)}, u32[]{:S(2)}, u32[]{:S(2)}) collective-permute-start(bf16[256,128]{1,0:T(8,128)(2,1)S(1)} %get-tuple-element.68), channel_id=1, source_target_pairs={{0,1},{1,0},{2,3},{3,2},{4,5},{5,4},{6,7},{7,6},{8,9},{9,8},{10,11... | collective-permute-start | bytes 196616 | tf_op jit(solution)/shard_map/ppermute | solution.py:35
  38.4 1.8 %product.6 = (bf16[512,128]{1,0:T(8,128)(2,1)S(1)}, bf16[512,128]{1,0:T(8,128)(2,1)S(1)}, bf16[512,128]{1,0:T(8,128)(2,1)S(1)}, bf16[256,128]{1,0:T(8,128)(2,1)S...) custom-call(s32[6,32]{1,0:T(8,128)S(1)} %get-tuple-element.44.at_ref, ...), custom_call_target="tpu_custom_call" | custom-call | flops 301989888 | bytes 1000 | tf_op jit(solution)/shard_map/product/pallas_call | solution.py:123
  40.3 2.4 %collective-permute-done.15.refs_1_ = bf16[512,128]{1,0:T(8,128)(2,1)S(1)} collective-permute-done((bf16[512,128]{1,0:T(8,128)(2,1)S(1)}, bf16[512,128]{1,0:T(8,128)(2,1)S(1)}, u32[]{:S(2)}, u32[]{:S(2)}) %collective-permute-start.15) | collective-permute-done | bytes 131104 | tf_op jit(solution)/shard_map/ppermute | solution.py:35
  42.7 1.7 %collective-permute-start.16 = (bf16[512,128]{1,0:T(8,128)(2,1)S(1)}, bf16[512,128]{1,0:T(8,128)(2,1)S(1)}, u32[]{:S(2)}, u32[]{:S(2)}) collective-permute-start(bf16[512,128]{1,0:T(8,128)(2,1)S(1)} %add.29.refs_0_), channel_id=1, source_target_pairs={{0,2},{1,3},{2,0},{3,1},{4,6},{5,7},{6,4},{7,5},{8,10},{9,11},{10,... | collective-permute-start | bytes 393224 | tf_op jit(solution)/shard_map/ppermute | solution.py:35
  44.4 2.0 %collective-permute-start.18 = (bf16[512,128]{1,0:T(8,128)(2,1)S(1)}, bf16[512,128]{1,0:T(8,128)(2,1)S(1)}, u32[]{:S(2)}, u32[]{:S(2)}) collective-permute-start(bf16[512,128]{1,0:T(8,128)(2,1)S(1)} %get-tuple-element.71), channel_id=1, source_target_pairs={{0,1},{1,0},{2,3},{3,2},{4,5},{5,4},{6,7},{7,6},{8,9},{9,8},{10,11... | collective-permute-start | bytes 393224 | tf_op jit(solution)/shard_map/ppermute | solution.py:35
  47.1 0.7 collective-permute-start.20
  47.8 4.9 %collective-permute-done.19.b = bf16[256,128]{1,0:T(8,128)(2,1)S(1)} collective-permute-done((bf16[256,128]{1,0:T(8,128)(2,1)S(1)}, bf16[256,128]{1,0:T(8,128)(2,1)S(1)}, u32[]{:S(2)}, u32[]{:S(2)}) %collective-permute-start.19) | collective-permute-done | bytes 65568 | tf_op jit(solution)/shard_map/ppermute | solution.py:35
  52.8 1.1 %collective-permute-done.20.refs_7_ = bf16[256,128]{1,0:T(8,128)(2,1)S(1)} collective-permute-done((bf16[256,128]{1,0:T(8,128)(2,1)S(1)}, bf16[256,128]{1,0:T(8,128)(2,1)S(1)}, u32[]{:S(2)}, u32[]{:S(2)}) %collective-permute-start.20) | collective-permute-done | bytes 65568 | tf_op jit(solution)/shard_map/ppermute | solution.py:35
  54.5 1.2 %collective-permute-done.21 = f32[112,128]{1,0:T(8,128)S(1)} collective-permute-done((f32[112,128]{1,0:T(8,128)S(1)}, f32[112,128]{1,0:T(8,128)S(1)}, u32[]{:S(2)}, u32[]{:S(2)}) %collective-permute-start.21) | collective-permute-done | bytes 57376 | tf_op jit(solution)/shard_map/ppermute | solution.py:35
  55.8 1.3 %collective-permute-start.22 = (f32[112,128]{1,0:T(8,128)S(1)}, f32[112,128]{1,0:T(8,128)S(1)}, u32[]{:S(2)}, u32[]{:S(2)}) collective-permute-start(f32[112,128]{1,0:T(8,128)S(1)} %add.19), channel_id=1, source_target_pairs={{0,8},{4,12},{8,0},{12,4},{1,9},{5,13},{9,1},{13,5},{2,10},{6,14},... | collective-permute-start | bytes 172040 | tf_op jit(solution)/shard_map/ppermute | solution.py:35
  57.1 2.9 %collective-permute-done.22 = f32[112,128]{1,0:T(8,128)S(1)} collective-permute-done((f32[112,128]{1,0:T(8,128)S(1)}, f32[112,128]{1,0:T(8,128)S(1)}, u32[]{:S(2)}, u32[]{:S(2)}) %collective-permute-start.22) | collective-permute-done | bytes 57376 | tf_op jit(solution)/shard_map/ppermute | solution.py:35
  60.0 2.9 %collective-permute-start.25 = (f32[112,128]{1,0:T(8,128)S(1)}, f32[112,128]{1,0:T(8,128)S(1)}, u32[]{:S(2)}, u32[]{:S(2)}) collective-permute-start(f32[112,128]{1,0:T(8,128)S(1)} %add.20), channel_id=1, source_target_pairs={{0,3},{1,2},{2,1},{3,0},{4,7},{5,6},{6,5},{7,4},{8,11},{9,10},{10,... | collective-permute-start | bytes 172040 | tf_op jit(solution)/shard_map/ppermute | solution.py:35
  62.9 1.6 %collective-permute-start.23 = (f32[112,128]{1,0:T(8,128)S(1)}, f32[112,128]{1,0:T(8,128)S(1)}, u32[]{:S(2)}, u32[]{:S(2)}) collective-permute-start(f32[112,128]{1,0:T(8,128)S(1)} %add.20), channel_id=1, source_target_pairs={{0,1},{1,0},{2,3},{3,2},{4,5},{5,4},{6,7},{7,6},{8,9},{9,8},{10,11... | collective-permute-start | bytes 172040 | tf_op jit(solution)/shard_map/ppermute | solution.py:35
  64.5 1.7 %collective-permute-done.25 = f32[112,128]{1,0:T(8,128)S(1)} collective-permute-done((f32[112,128]{1,0:T(8,128)S(1)}, f32[112,128]{1,0:T(8,128)S(1)}, u32[]{:S(2)}, u32[]{:S(2)}) %collective-permute-start.25) | collective-permute-done | bytes 57376 | tf_op jit(solution)/shard_map/ppermute | solution.py:35
  66.1 1.9 %collective-permute-done.24 = f32[112,128]{1,0:T(8,128)S(1)} collective-permute-done((f32[112,128]{1,0:T(8,128)S(1)}, f32[112,128]{1,0:T(8,128)S(1)}, u32[]{:S(2)}, u32[]{:S(2)}) %collective-permute-start.24) | collective-permute-done | bytes 57376 | tf_op jit(solution)/shard_map/ppermute | solution.py:35
  68.1 1.9 %corner.1.corner_ref = f32[64,64]{1,0:T(8,128)S(1)} custom-call(f32[112,128]{1,0:T(8,128)S(1)} %add_add_fusion.keep_ref), custom_call_target="tpu_custom_call" | custom-call | flops 1000000000 | bytes 1000 | tf_op jit(solution)/shard_map/corner/pallas_call | solution.py:415
  70.0 6.0 %orthonormalize.1 = f32[192,512]{1,0:T(8,128)} custom-call(f32[112,128]{1,0:T(8,128)S(1)} %add_add_fusion.keep_ref, f32[112,128]{1,0:T(8,128)S(1)} %collective-permute-done.26.other_ref, f32[64,64]{1,0:T(8,128)S(1)} %corner.1.corner_ref, bf16[512,128]{1,0:T(8,128)(2,1)S(1)} %get-tuple-element.77.wide_ref, bf16[256,128]{1,0:T(8,128)(2,1)S(1)} %get-tuple-element.78.thin_ref), custom_call_target="tpu_custom_call" | custom-call | flops 1000 | bytes 1000 | tf_op jit(solution)/shard_map/orthonormalize/pallas_call | solution.py:418
  (55 shorter events, 8.7 us)
Async XLA Ops:
  0.0 8.1 %collective-permute-start.1 = (bf16[192,512]{1,0:T(8,128)(2,1)}, bf16[192,512]{1,0:T(8,128)(2,1)S(1)}, u32[]{:S(2)}, u32[]{:S(2)}) collective-permute-start(bf16[192,512]{1,0:T(8,128)(2,1)} %bitcast.3), channel_id=1, source_target_pairs={{0,8},{4,12},{8,0},{12,4},{1,9},{5,13},{9,1},{13,5},{2,10},{6,14},... | collective-permute-start | bytes 589832 | tf_op jit(solution)/shard_map/ppermute | solution.py:35
  4.3 1.4 %copy-start = (bf16[32,64,384]{2,1,0:T(8,128)(2,1)S(1)}, bf16[32,64,384]{2,1,0:T(8,128)(2,1)}, u32[]{:S(2)}) copy-start(bf16[32,64,384]{2,1,0:T(8,128)(2,1)} %ham_ref.9) | copy-start | bytes 4718596
  5.7 0.9 %copy-start.2 = (bf16[512,192]{0,1:T(8,128)(2,1)S(1)}, bf16[512,192]{0,1:T(8,128)(2,1)}, u32[]{:S(2)}) copy-start(bf16[512,192]{0,1:T(8,128)(2,1)} %param.7) | copy-start | bytes 589828
  6.6 0.7 copy-start.3
  7.3 2.4 %copy-start.1 = (bf16[32,64,384]{2,1,0:T(8,128)(2,1)S(1)}, bf16[32,64,384]{2,1,0:T(8,128)(2,1)}, u32[]{:S(2)}) copy-start(bf16[32,64,384]{2,1,0:T(8,128)(2,1)} %ham_ref.9) | copy-start | bytes 4718596
  7.3 1.5 %collective-permute-start = (bf16[192,512]{1,0:T(8,128)(2,1)S(1)}, bf16[192,512]{1,0:T(8,128)(2,1)S(1)}, u32[]{:S(2)}, u32[]{:S(2)}) collective-permute-start(bf16[192,512]{1,0:T(8,128)(2,1)S(1)} %get-tuple-element.45), channel_id=1, source_target_pairs={{0,4},{4,0},{8,12},{12,8},{1,5},{5,1},{9,13},{13,9},{2,6},{6,2},{1... | collective-permute-start | bytes 589832 | tf_op jit(solution)/shard_map/ppermute | solution.py:35
  8.1 1.4 %collective-permute-start.2 = (bf16[192,512]{1,0:T(8,128)(2,1)S(1)}, bf16[192,512]{1,0:T(8,128)(2,1)S(1)}, u32[]{:S(2)}, u32[]{:S(2)}) collective-permute-start(bf16[192,512]{1,0:T(8,128)(2,1)S(1)} %collective-permute-done.1.turned_ref), channel_id=1, source_target_pairs={{0,4},{4,0},{8,12},{12,8},{1,5},{5,1},{9,13},{13,9},{2,6},{6,2},{1... | collective-permute-start | bytes 589832 | tf_op jit(solution)/shard_map/ppermute | solution.py:35
  10.9 6.4 %collective-permute-start.3 = (bf16[512,128]{1,0:T(8,128)(2,1)S(1)}, bf16[512,128]{1,0:T(8,128)(2,1)S(1)}, u32[]{:S(2)}, u32[]{:S(2)}) collective-permute-start(bf16[512,128]{1,0:T(8,128)(2,1)S(1)} %get-tuple-element.55), channel_id=1, source_target_pairs={{0,1},{1,0},{2,3},{3,2},{4,5},{5,4},{6,7},{7,6},{8,9},{9,8},{10,11... | collective-permute-start | bytes 393224 | tf_op jit(solution)/shard_map/ppermute | solution.py:35
  12.8 7.4 %collective-permute-start.5 = (bf16[256,128]{1,0:T(8,128)(2,1)S(1)}, bf16[256,128]{1,0:T(8,128)(2,1)S(1)}, u32[]{:S(2)}, u32[]{:S(2)}) collective-permute-start(bf16[256,128]{1,0:T(8,128)(2,1)S(1)} %get-tuple-element.57), channel_id=1, source_target_pairs={{0,1},{1,0},{2,3},{3,2},{4,5},{5,4},{6,7},{7,6},{8,9},{9,8},{10,11... | collective-permute-start | bytes 196616 | tf_op jit(solution)/shard_map/ppermute | solution.py:35
  17.3 9.3 %collective-permute-start.4 = (bf16[512,128]{1,0:T(8,128)(2,1)S(1)}, bf16[512,128]{1,0:T(8,128)(2,1)S(1)}, u32[]{:S(2)}, u32[]{:S(2)}) collective-permute-start(bf16[512,128]{1,0:T(8,128)(2,1)S(1)} %add.27.refs_0_), channel_id=1, source_target_pairs={{0,2},{1,3},{2,0},{3,1},{4,6},{5,7},{6,4},{7,5},{8,10},{9,11},{10,... | collective-permute-start | bytes 393224 | tf_op jit(solution)/shard_map/ppermute | solution.py:35
  20.2 7.5 %collective-permute-start.6 = (bf16[512,128]{1,0:T(8,128)(2,1)S(1)}, bf16[512,128]{1,0:T(8,128)(2,1)S(1)}, u32[]{:S(2)}, u32[]{:S(2)}) collective-permute-start(bf16[512,128]{1,0:T(8,128)(2,1)S(1)} %get-tuple-element.60), channel_id=1, source_target_pairs={{0,1},{1,0},{2,3},{3,2},{4,5},{5,4},{6,7},{7,6},{8,9},{9,8},{10,11... | collective-permute-start | bytes 393224 | tf_op jit(solution)/shard_map/ppermute | solution.py:35
  21.8 7.6 %collective-permute-start.10 = (bf16[256,128]{1,0:T(8,128)(2,1)S(1)}, bf16[256,128]{1,0:T(8,128)(2,1)S(1)}, u32[]{:S(2)}, u32[]{:S(2)}) collective-permute-start(bf16[256,128]{1,0:T(8,128)(2,1)S(1)} %get-tuple-element.62), channel_id=1, source_target_pairs={{0,2},{1,3},{2,0},{3,1},{4,6},{5,7},{6,4},{7,5},{8,10},{9,11},{10,... | collective-permute-start | bytes 196616 | tf_op jit(solution)/shard_map/ppermute | solution.py:35
  22.4 7.0 %collective-permute-start.11 = (bf16[256,128]{1,0:T(8,128)(2,1)S(1)}, bf16[256,128]{1,0:T(8,128)(2,1)S(1)}, u32[]{:S(2)}, u32[]{:S(2)}) collective-permute-start(bf16[256,128]{1,0:T(8,128)(2,1)S(1)} %get-tuple-element.63), channel_id=1, source_target_pairs={{0,1},{1,0},{2,3},{3,2},{4,5},{5,4},{6,7},{7,6},{8,9},{9,8},{10,11... | collective-permute-start | bytes 196616 | tf_op jit(solution)/shard_map/ppermute | solution.py:35
  27.8 5.0 %collective-permute-start.8 = (bf16[512,128]{1,0:T(8,128)(2,1)S(1)}, bf16[512,128]{1,0:T(8,128)(2,1)S(1)}, u32[]{:S(2)}, u32[]{:S(2)}) collective-permute-start(bf16[512,128]{1,0:T(8,128)(2,1)S(1)} %first_filter.2.refs_0_.refs_1_), channel_id=1, source_target_pairs={{0,8},{4,12},{8,0},{12,4},{1,9},{5,13},{9,1},{13,5},{2,10},{6,14},... | collective-permute-start | bytes 393224 | tf_op jit(solution)/shard_map/ppermute | solution.py:35
  29.5 4.3 %collective-permute-start.13 = (bf16[256,128]{1,0:T(8,128)(2,1)S(1)}, bf16[256,128]{1,0:T(8,128)(2,1)S(1)}, u32[]{:S(2)}, u32[]{:S(2)}) collective-permute-start(bf16[256,128]{1,0:T(8,128)(2,1)S(1)} %first_filter.3.refs_4_.refs_5_), channel_id=1, source_target_pairs={{0,8},{4,12},{8,0},{12,4},{1,9},{5,13},{9,1},{13,5},{2,10},{6,14},... | collective-permute-start | bytes 196616 | tf_op jit(solution)/shard_map/ppermute | solution.py:35
  30.1 5.0 %collective-permute-start.7 = (bf16[512,128]{1,0:T(8,128)(2,1)S(1)}, bf16[512,128]{1,0:T(8,128)(2,1)S(1)}, u32[]{:S(2)}, u32[]{:S(2)}) collective-permute-start(bf16[512,128]{1,0:T(8,128)(2,1)S(1)} %first_filter.2.refs_0_.refs_1_), channel_id=1, source_target_pairs={{0,4},{4,0},{8,12},{12,8},{1,5},{5,1},{9,13},{13,9},{2,6},{6,2},{1... | collective-permute-start | bytes 393224 | tf_op jit(solution)/shard_map/ppermute | solution.py:35
  32.8 2.3 %collective-permute-start.9 = (bf16[512,128]{1,0:T(8,128)(2,1)S(1)}, bf16[512,128]{1,0:T(8,128)(2,1)S(1)}, u32[]{:S(2)}, u32[]{:S(2)}) collective-permute-start(bf16[512,128]{1,0:T(8,128)(2,1)S(1)} %collective-permute-done.8.refs_2_), channel_id=1, source_target_pairs={{0,4},{4,0},{8,12},{12,8},{1,5},{5,1},{9,13},{13,9},{2,6},{6,2},{1... | collective-permute-start | bytes 393224 | tf_op jit(solution)/shard_map/ppermute | solution.py:35
  32.8 1.4 %collective-permute-start.12 = (bf16[256,128]{1,0:T(8,128)(2,1)S(1)}, bf16[256,128]{1,0:T(8,128)(2,1)S(1)}, u32[]{:S(2)}, u32[]{:S(2)}) collective-permute-start(bf16[256,128]{1,0:T(8,128)(2,1)S(1)} %first_filter.3.refs_4_.refs_5_), channel_id=1, source_target_pairs={{0,4},{4,0},{8,12},{12,8},{1,5},{5,1},{9,13},{13,9},{2,6},{6,2},{1... | collective-permute-start | bytes 196616 | tf_op jit(solution)/shard_map/ppermute | solution.py:35
  33.8 1.3 %collective-permute-start.14 = (bf16[256,128]{1,0:T(8,128)(2,1)S(1)}, bf16[256,128]{1,0:T(8,128)(2,1)S(1)}, u32[]{:S(2)}, u32[]{:S(2)}) collective-permute-start(bf16[256,128]{1,0:T(8,128)(2,1)S(1)} %collective-permute-done.13.refs_6_), channel_id=1, source_target_pairs={{0,4},{4,0},{8,12},{12,8},{1,5},{5,1},{9,13},{13,9},{2,6},{6,2},{1... | collective-permute-start | bytes 196616 | tf_op jit(solution)/shard_map/ppermute | solution.py:35
  36.3 6.3 %collective-permute-start.15 = (bf16[512,128]{1,0:T(8,128)(2,1)S(1)}, bf16[512,128]{1,0:T(8,128)(2,1)S(1)}, u32[]{:S(2)}, u32[]{:S(2)}) collective-permute-start(bf16[512,128]{1,0:T(8,128)(2,1)S(1)} %get-tuple-element.66), channel_id=1, source_target_pairs={{0,1},{1,0},{2,3},{3,2},{4,5},{5,4},{6,7},{7,6},{8,9},{9,8},{10,11... | collective-permute-start | bytes 393224 | tf_op jit(solution)/shard_map/ppermute | solution.py:35
  37.1 7.4 %collective-permute-start.17 = (bf16[256,128]{1,0:T(8,128)(2,1)S(1)}, bf16[256,128]{1,0:T(8,128)(2,1)S(1)}, u32[]{:S(2)}, u32[]{:S(2)}) collective-permute-start(bf16[256,128]{1,0:T(8,128)(2,1)S(1)} %get-tuple-element.68), channel_id=1, source_target_pairs={{0,1},{1,0},{2,3},{3,2},{4,5},{5,4},{6,7},{7,6},{8,9},{9,8},{10,11... | collective-permute-start | bytes 196616 | tf_op jit(solution)/shard_map/ppermute | solution.py:35
  42.7 10.0 %collective-permute-start.16 = (bf16[512,128]{1,0:T(8,128)(2,1)S(1)}, bf16[512,128]{1,0:T(8,128)(2,1)S(1)}, u32[]{:S(2)}, u32[]{:S(2)}) collective-permute-start(bf16[512,128]{1,0:T(8,128)(2,1)S(1)} %add.29.refs_0_), channel_id=1, source_target_pairs={{0,2},{1,3},{2,0},{3,1},{4,6},{5,7},{6,4},{7,5},{8,10},{9,11},{10,... | collective-permute-start | bytes 393224 | tf_op jit(solution)/shard_map/ppermute | solution.py:35
  44.4 9.5 %collective-permute-start.18 = (bf16[512,128]{1,0:T(8,128)(2,1)S(1)}, bf16[512,128]{1,0:T(8,128)(2,1)S(1)}, u32[]{:S(2)}, u32[]{:S(2)}) collective-permute-start(bf16[512,128]{1,0:T(8,128)(2,1)S(1)} %get-tuple-element.71), channel_id=1, source_target_pairs={{0,1},{1,0},{2,3},{3,2},{4,5},{5,4},{6,7},{7,6},{8,9},{9,8},{10,11... | collective-permute-start | bytes 393224 | tf_op jit(solution)/shard_map/ppermute | solution.py:35
  46.5 6.2 %collective-permute-start.19 = (bf16[256,128]{1,0:T(8,128)(2,1)S(1)}, bf16[256,128]{1,0:T(8,128)(2,1)S(1)}, u32[]{:S(2)}, u32[]{:S(2)}) collective-permute-start(bf16[256,128]{1,0:T(8,128)(2,1)S(1)} %get-tuple-element.73), channel_id=1, source_target_pairs={{0,2},{1,3},{2,0},{3,1},{4,6},{5,7},{6,4},{7,5},{8,10},{9,11},{10,... | collective-permute-start | bytes 196616 | tf_op jit(solution)/shard_map/ppermute | solution.py:35
  47.1 6.8 %collective-permute-start.20 = (bf16[256,128]{1,0:T(8,128)(2,1)S(1)}, bf16[256,128]{1,0:T(8,128)(2,1)S(1)}, u32[]{:S(2)}, u32[]{:S(2)}) collective-permute-start(bf16[256,128]{1,0:T(8,128)(2,1)S(1)} %get-tuple-element.74), channel_id=1, source_target_pairs={{0,1},{1,0},{2,3},{3,2},{4,5},{5,4},{6,7},{7,6},{8,9},{9,8},{10,11... | collective-permute-start | bytes 196616 | tf_op jit(solution)/shard_map/ppermute | solution.py:35
  54.4 1.3 %collective-permute-start.21 = (f32[112,128]{1,0:T(8,128)S(1)}, f32[112,128]{1,0:T(8,128)S(1)}, u32[]{:S(2)}, u32[]{:S(2)}) collective-permute-start(f32[112,128]{1,0:T(8,128)S(1)} %get-tuple-element.76), channel_id=1, source_target_pairs={{0,4},{4,0},{8,12},{12,8},{1,5},{5,1},{9,13},{13,9},{2,6},{6,2},{1... | collective-permute-start | bytes 172040 | tf_op jit(solution)/shard_map/ppermute | solution.py:35
  55.8 4.2 %collective-permute-start.22 = (f32[112,128]{1,0:T(8,128)S(1)}, f32[112,128]{1,0:T(8,128)S(1)}, u32[]{:S(2)}, u32[]{:S(2)}) collective-permute-start(f32[112,128]{1,0:T(8,128)S(1)} %add.19), channel_id=1, source_target_pairs={{0,8},{4,12},{8,0},{12,4},{1,9},{5,13},{9,1},{13,5},{2,10},{6,14},... | collective-permute-start | bytes 172040 | tf_op jit(solution)/shard_map/ppermute | solution.py:35
  60.0 6.1 %collective-permute-start.25 = (f32[112,128]{1,0:T(8,128)S(1)}, f32[112,128]{1,0:T(8,128)S(1)}, u32[]{:S(2)}, u32[]{:S(2)}) collective-permute-start(f32[112,128]{1,0:T(8,128)S(1)} %add.20), channel_id=1, source_target_pairs={{0,3},{1,2},{2,1},{3,0},{4,7},{5,6},{6,5},{7,4},{8,11},{9,10},{10,... | collective-permute-start | bytes 172040 | tf_op jit(solution)/shard_map/ppermute | solution.py:35
  62.9 5.1 %collective-permute-start.24 = (f32[112,128]{1,0:T(8,128)S(1)}, f32[112,128]{1,0:T(8,128)S(1)}, u32[]{:S(2)}, u32[]{:S(2)}) collective-permute-start(f32[112,128]{1,0:T(8,128)S(1)} %add.20), channel_id=1, source_target_pairs={{0,2},{1,3},{2,0},{3,1},{4,6},{5,7},{6,4},{7,5},{8,10},{9,11},{10,... | collective-permute-start | bytes 172040 | tf_op jit(solution)/shard_map/ppermute | solution.py:35
  62.9 5.1 %collective-permute-start.23 = (f32[112,128]{1,0:T(8,128)S(1)}, f32[112,128]{1,0:T(8,128)S(1)}, u32[]{:S(2)}, u32[]{:S(2)}) collective-permute-start(f32[112,128]{1,0:T(8,128)S(1)} %add.20), channel_id=1, source_target_pairs={{0,1},{1,0},{2,3},{3,2},{4,5},{5,4},{6,7},{7,6},{8,9},{9,8},{10,11... | collective-permute-start | bytes 172040 | tf_op jit(solution)/shard_map/ppermute | solution.py:35
  68.0 2.0 %collective-permute-start.26 = (f32[112,128]{1,0:T(8,128)S(1)}, f32[112,128]{1,0:T(8,128)S(1)}, u32[]{:S(2)}, u32[]{:S(2)}) collective-permute-start(f32[112,128]{1,0:T(8,128)S(1)} %add_add_fusion.keep_ref), channel_id=1, source_target_pairs={{0,4},{4,0},{8,12},{12,8},{1,5},{5,1},{9,13},{13,9},{2,6},{6,2},{1... | collective-permute-start | bytes 172040 | tf_op jit(solution)/shard_map/ppermute | solution.py:35

commit v7 on v6

--- a/solution.py
+++ b/solution.py
@@ -75,10 +75,12 @@
     at_out[...] = (ids_ref[...] ^ (lax.axis_index("row") * own_blocks)) * orbitals
 
 
-def product_kernel(keys, n_row, own_blocks, at_ref, ham_ref, *refs):
+def product_kernel(keys, n_row, own_blocks, at_vmem, ham_ref, *refs):
     wide, thin = refs[:n_row], refs[n_row : 2 * n_row]
-    wide_out, thin_out = refs[2 * n_row : 2 * n_row + len(keys)], refs[2 * n_row + len(keys) : -1]
-    source = refs[-1]
+    wide_out, thin_out = refs[2 * n_row : 2 * n_row + len(keys)], refs[2 * n_row + len(keys) : -3]
+    source, at_ref, sem = refs[-3:]
+    copy = pltpu.make_async_copy(at_vmem, at_ref, sem)
+    copy.start()
     orbitals = ham_ref.shape[1]
     rows = own_blocks * orbitals
     half = rows // 2
@@ -94,6 +96,8 @@
             [packed[:, SIZE:], packed[:, :SIZE]], axis=1
         )
 
+    copy.wait()
+
     def term(i, block):
         picked = [
             source[pl.ds(pl.multiple_of(at_ref[slot, first[i] + block], orbitals), orbitals), :]
@@ -123,8 +127,12 @@
     outs = call(
         functools.partial(product_kernel, keys, n_row, own_blocks),
         [jax.ShapeDtypeStruct(x.shape, BF16) for x in parts[0] for _ in keys],
-        [SMEM, VMEM] + [VMEM] * (2 * n_row),
-        [pltpu.VMEM((own_blocks * n_row * orbitals, 2 * LANES), BF16)],
+        [VMEM, VMEM] + [VMEM] * (2 * n_row),
+        [
+            pltpu.VMEM((own_blocks * n_row * orbitals, 2 * LANES), BF16),
+            pltpu.SMEM(at.shape, jnp.int32),
+            pltpu.SemaphoreType.DMA,
+        ],
         flops=flops,
         name="product",
     )(at, ham, *wide, *thin)

time: 76.2 us -> 75.9 us (level)
  Pallas kernels: 15.4 us -> 14.6 us
    pallas_call x4, Pallas kernels: 6.17 us -> 5.33 us  [product(): call(functools.partial(product_kernel, keys, n_row, own_blocks), [jax.Sha...]
where the time goes in v7:
time: 75.9 us; the launch traced here: 75.7 us
  waiting for transfers between devices  30.1 us (40%)
  starting transfers between devices  26.5 us (35%)
  Pallas kernels  14.6 us (19%)
  local copies, waits for them, and re-layouts  3.02 us (4%)
  between operations  1.47 us (2%)
    ppermute x27, waiting for transfers between devices, swap(): return lax.ppermute(x, axis, [(i, i ^ key) for i in range(count)])  30.1 us
    ppermute x27, starting transfers between devices, swap(): return lax.ppermute(x, axis, [(i, i ^ key) for i in range(count)])  26.5 us
    pallas_call x1, Pallas kernels, per_device(): call(last_kernel, jax.ShapeDtypeStruct((LANES + SIZE, rows), F32), [VMEM]...  5.97 us
    pallas_call x4, Pallas kernels, product(): call(functools.partial(product_kernel, keys, n_row, own_blocks), [jax.Sha...  5.33 us
    unnamed x8, local copies, waits for them, and re-layouts  3.02 us
    pallas_call x1, Pallas kernels, per_device(): call(corner_kernel, jax.ShapeDtypeStruct((SIZE, SIZE), F32), [VMEM], flop...  1.88 us
  transfers between devices with their start and end apart: 27, of which 17 were waited for; matrix products, arithmetic and copies ran while one was open for 0% of the time, Pallas kernels for 8%

profile of v7, /device:TPU:0, one launch (start us, length us, event | category | flops | bytes accessed | tf_op | source)
XLA Modules:
  0.0 75.7 jit_solution(83592449200203535)
XLA Ops:
  0.0 3.0 %collective-permute-start.1 = (bf16[192,512]{1,0:T(8,128)(2,1)}, bf16[192,512]{1,0:T(8,128)(2,1)S(1)}, u32[]{:S(2)}, u32[]{:S(2)}) collective-permute-start(bf16[192,512]{1,0:T(8,128)(2,1)} %bitcast.3), channel_id=1, source_target_pairs={{0,8},{4,12},{8,0},{12,4},{1,9},{5,13},{9,1},{13,5},{2,10},{6,14},... | collective-permute-start | bytes 589832 | tf_op jit(solution)/shard_map/ppermute | solution.py:35
  4.3 1.4 %copy-done = bf16[32,64,384]{2,1,0:T(8,128)(2,1)S(1)} copy-done((bf16[32,64,384]{2,1,0:T(8,128)(2,1)S(1)}, bf16[32,64,384]{2,1,0:T(8,128)(2,1)}, u32[]{:S(2)}) %copy-start) | copy-done | bytes 1572888
  5.7 0.9 %copy-done.2 = bf16[512,192]{0,1:T(8,128)(2,1)S(1)} copy-done((bf16[512,192]{0,1:T(8,128)(2,1)S(1)}, bf16[512,192]{0,1:T(8,128)(2,1)}, u32[]{:S(2)}) %copy-start.2) | copy-done | bytes 196632
  9.7 1.1 %product.5 = (bf16[512,128]{1,0:T(8,128)(2,1)S(1)}, bf16[256,128]{1,0:T(8,128)(2,1)S(1)}) custom-call(s32[6,32]{1,0:T(8,128)S(1)} %get-tuple-element.44.at_vmem, bf16[32,64,384]{2,1,0:T(8,128)(2,1)S(1)} %copy-done.1, bf16[512,128]{1,0:T(8,128)(2,1)S(1)} %get-tuple-element.43.refs_0_.start, bf16[512,128]{1,0:T(8,128)(2,1)S(1)} %get-tuple-element.46.refs_1_, ...), custom_call_target="tpu_custom_call" | custom-call | flops 100663296 | bytes 1000 | tf_op jit(solution)/shard_map/product/pallas_call | solution.py:127
  10.8 1.9 %collective-permute-start.3 = (bf16[512,128]{1,0:T(8,128)(2,1)S(1)}, bf16[512,128]{1,0:T(8,128)(2,1)S(1)}, u32[]{:S(2)}, u32[]{:S(2)}) collective-permute-start(bf16[512,128]{1,0:T(8,128)(2,1)S(1)} %get-tuple-element.55), channel_id=1, source_target_pairs={{0,1},{1,0},{2,3},{3,2},{4,5},{5,4},{6,7},{7,6},{8,9},{9,8},{10,11... | collective-permute-start | bytes 393224 | tf_op jit(solution)/shard_map/ppermute | solution.py:35
  12.9 1.6 %product.4 = (bf16[512,128]{1,0:T(8,128)(2,1)S(1)}, bf16[512,128]{1,0:T(8,128)(2,1)S(1)}, bf16[512,128]{1,0:T(8,128)(2,1)S(1)}, bf16[256,128]{1,0:T(8,128)(2,1)S...) custom-call(s32[6,32]{1,0:T(8,128)S(1)} %get-tuple-element.44.at_vmem, ...), custom_call_target="tpu_custom_call" | custom-call | flops 301989888 | bytes 1000 | tf_op jit(solution)/shard_map/product/pallas_call | solution.py:127
  14.4 2.7 %collective-permute-done.3.refs_1_ = bf16[512,128]{1,0:T(8,128)(2,1)S(1)} collective-permute-done((bf16[512,128]{1,0:T(8,128)(2,1)S(1)}, bf16[512,128]{1,0:T(8,128)(2,1)S(1)}, u32[]{:S(2)}, u32[]{:S(2)}) %collective-permute-start.3) | collective-permute-done | bytes 131104 | tf_op jit(solution)/shard_map/ppermute | solution.py:35
  17.2 2.8 %collective-permute-start.4 = (bf16[512,128]{1,0:T(8,128)(2,1)S(1)}, bf16[512,128]{1,0:T(8,128)(2,1)S(1)}, u32[]{:S(2)}, u32[]{:S(2)}) collective-permute-start(bf16[512,128]{1,0:T(8,128)(2,1)S(1)} %add.27.refs_0_), channel_id=1, source_target_pairs={{0,2},{1,3},{2,0},{3,1},{4,6},{5,7},{6,4},{7,5},{8,10},{9,11},{10,... | collective-permute-start | bytes 393224 | tf_op jit(solution)/shard_map/ppermute | solution.py:35
  20.0 1.6 %collective-permute-start.6 = (bf16[512,128]{1,0:T(8,128)(2,1)S(1)}, bf16[512,128]{1,0:T(8,128)(2,1)S(1)}, u32[]{:S(2)}, u32[]{:S(2)}) collective-permute-start(bf16[512,128]{1,0:T(8,128)(2,1)S(1)} %get-tuple-element.60), channel_id=1, source_target_pairs={{0,1},{1,0},{2,3},{3,2},{4,5},{5,4},{6,7},{7,6},{8,9},{9,8},{10,11... | collective-permute-start | bytes 393224 | tf_op jit(solution)/shard_map/ppermute | solution.py:35
  22.7 3.7 %collective-permute-done.4.b = bf16[512,128]{1,0:T(8,128)(2,1)S(1)} collective-permute-done((bf16[512,128]{1,0:T(8,128)(2,1)S(1)}, bf16[512,128]{1,0:T(8,128)(2,1)S(1)}, u32[]{:S(2)}, u32[]{:S(2)}) %collective-permute-start.4) | collective-permute-done | bytes 131104 | tf_op jit(solution)/shard_map/ppermute | solution.py:35
  26.5 1.1 %collective-permute-done.6.refs_1_ = bf16[512,128]{1,0:T(8,128)(2,1)S(1)} collective-permute-done((bf16[512,128]{1,0:T(8,128)(2,1)S(1)}, bf16[512,128]{1,0:T(8,128)(2,1)S(1)}, u32[]{:S(2)}, u32[]{:S(2)}) %collective-permute-start.6) | collective-permute-done | bytes 131104 | tf_op jit(solution)/shard_map/ppermute | solution.py:35
  27.6 1.6 %collective-permute-start.8 = (bf16[512,128]{1,0:T(8,128)(2,1)S(1)}, bf16[512,128]{1,0:T(8,128)(2,1)S(1)}, u32[]{:S(2)}, u32[]{:S(2)}) collective-permute-start(bf16[512,128]{1,0:T(8,128)(2,1)S(1)} %first_filter.2.refs_0_.refs_1_), channel_id=1, source_target_pairs={{0,8},{4,12},{8,0},{12,4},{1,9},{5,13},{9,1},{13,5},{2,10},{6,14},... | collective-permute-start | bytes 393224 | tf_op jit(solution)/shard_map/ppermute | solution.py:35
  30.0 2.7 %collective-permute-done.8.refs_2_ = bf16[512,128]{1,0:T(8,128)(2,1)S(1)} collective-permute-done((bf16[512,128]{1,0:T(8,128)(2,1)S(1)}, bf16[512,128]{1,0:T(8,128)(2,1)S(1)}, u32[]{:S(2)}, u32[]{:S(2)}) %collective-permute-start.8) | collective-permute-done | bytes 131104 | tf_op jit(solution)/shard_map/ppermute | solution.py:35
  34.1 0.8 %collective-permute-done.14.refs_7_ = bf16[256,128]{1,0:T(8,128)(2,1)S(1)} collective-permute-done((bf16[256,128]{1,0:T(8,128)(2,1)S(1)}, bf16[256,128]{1,0:T(8,128)(2,1)S(1)}, u32[]{:S(2)}, u32[]{:S(2)}) %collective-permute-start.14) | collective-permute-done | bytes 65568 | tf_op jit(solution)/shard_map/ppermute | solution.py:35
  34.9 1.1 %product.7 = (bf16[512,128]{1,0:T(8,128)(2,1)S(1)}, bf16[256,128]{1,0:T(8,128)(2,1)S(1)}) custom-call(s32[6,32]{1,0:T(8,128)S(1)} %get-tuple-element.44.at_vmem, bf16[32,64,384]{2,1,0:T(8,128)(2,1)S(1)} %copy-done.1, bf16[512,128]{1,0:T(8,128)(2,1)S(1)} %first_filter.2.refs_0_.refs_1_, bf16[512,128]{1,0:T(8,128)(2,1)S(1)} %collective-permute-done.7.refs_1_, ...), custom_call_target="tpu_custom_call" | custom-call | flops 100663296 | bytes 1000 | tf_op jit(solution)/shard_map/product/pallas_call | solution.py:127
  36.8 1.4 %collective-permute-start.17 = (bf16[256,128]{1,0:T(8,128)(2,1)S(1)}, bf16[256,128]{1,0:T(8,128)(2,1)S(1)}, u32[]{:S(2)}, u32[]{:S(2)}) collective-permute-start(bf16[256,128]{1,0:T(8,128)(2,1)S(1)} %get-tuple-element.68), channel_id=1, source_target_pairs={{0,1},{1,0},{2,3},{3,2},{4,5},{5,4},{6,7},{7,6},{8,9},{9,8},{10,11... | collective-permute-start | bytes 196616 | tf_op jit(solution)/shard_map/ppermute | solution.py:35
  38.1 1.6 %product.6 = (bf16[512,128]{1,0:T(8,128)(2,1)S(1)}, bf16[512,128]{1,0:T(8,128)(2,1)S(1)}, bf16[512,128]{1,0:T(8,128)(2,1)S(1)}, bf16[256,128]{1,0:T(8,128)(2,1)S...) custom-call(s32[6,32]{1,0:T(8,128)S(1)} %get-tuple-element.44.at_vmem, ...), custom_call_target="tpu_custom_call" | custom-call | flops 301989888 | bytes 1000 | tf_op jit(solution)/shard_map/product/pallas_call | solution.py:127
  39.7 2.7 %collective-permute-done.15.refs_1_ = bf16[512,128]{1,0:T(8,128)(2,1)S(1)} collective-permute-done((bf16[512,128]{1,0:T(8,128)(2,1)S(1)}, bf16[512,128]{1,0:T(8,128)(2,1)S(1)}, u32[]{:S(2)}, u32[]{:S(2)}) %collective-permute-start.15) | collective-permute-done | bytes 131104 | tf_op jit(solution)/shard_map/ppermute | solution.py:35
  42.4 1.7 %collective-permute-start.16 = (bf16[512,128]{1,0:T(8,128)(2,1)S(1)}, bf16[512,128]{1,0:T(8,128)(2,1)S(1)}, u32[]{:S(2)}, u32[]{:S(2)}) collective-permute-start(bf16[512,128]{1,0:T(8,128)(2,1)S(1)} %add.29.refs_0_), channel_id=1, source_target_pairs={{0,2},{1,3},{2,0},{3,1},{4,6},{5,7},{6,4},{7,5},{8,10},{9,11},{10,... | collective-permute-start | bytes 393224 | tf_op jit(solution)/shard_map/ppermute | solution.py:35
  44.2 2.0 %collective-permute-start.18 = (bf16[512,128]{1,0:T(8,128)(2,1)S(1)}, bf16[512,128]{1,0:T(8,128)(2,1)S(1)}, u32[]{:S(2)}, u32[]{:S(2)}) collective-permute-start(bf16[512,128]{1,0:T(8,128)(2,1)S(1)} %get-tuple-element.71), channel_id=1, source_target_pairs={{0,1},{1,0},{2,3},{3,2},{4,5},{5,4},{6,7},{7,6},{8,9},{9,8},{10,11... | collective-permute-start | bytes 393224 | tf_op jit(solution)/shard_map/ppermute | solution.py:35
  46.8 0.7 collective-permute-start.20
  47.5 4.9 %collective-permute-done.19.b = bf16[256,128]{1,0:T(8,128)(2,1)S(1)} collective-permute-done((bf16[256,128]{1,0:T(8,128)(2,1)S(1)}, bf16[256,128]{1,0:T(8,128)(2,1)S(1)}, u32[]{:S(2)}, u32[]{:S(2)}) %collective-permute-start.19) | collective-permute-done | bytes 65568 | tf_op jit(solution)/shard_map/ppermute | solution.py:35
  52.5 1.1 %collective-permute-done.20.refs_7_ = bf16[256,128]{1,0:T(8,128)(2,1)S(1)} collective-permute-done((bf16[256,128]{1,0:T(8,128)(2,1)S(1)}, bf16[256,128]{1,0:T(8,128)(2,1)S(1)}, u32[]{:S(2)}, u32[]{:S(2)}) %collective-permute-start.20) | collective-permute-done | bytes 65568 | tf_op jit(solution)/shard_map/ppermute | solution.py:35
  54.2 1.2 %collective-permute-done.21 = f32[112,128]{1,0:T(8,128)S(1)} collective-permute-done((f32[112,128]{1,0:T(8,128)S(1)}, f32[112,128]{1,0:T(8,128)S(1)}, u32[]{:S(2)}, u32[]{:S(2)}) %collective-permute-start.21) | collective-permute-done | bytes 57376 | tf_op jit(solution)/shard_map/ppermute | solution.py:35
  55.5 1.3 %collective-permute-start.22 = (f32[112,128]{1,0:T(8,128)S(1)}, f32[112,128]{1,0:T(8,128)S(1)}, u32[]{:S(2)}, u32[]{:S(2)}) collective-permute-start(f32[112,128]{1,0:T(8,128)S(1)} %add.19), channel_id=1, source_target_pairs={{0,8},{4,12},{8,0},{12,4},{1,9},{5,13},{9,1},{13,5},{2,10},{6,14},... | collective-permute-start | bytes 172040 | tf_op jit(solution)/shard_map/ppermute | solution.py:35
  56.8 2.9 %collective-permute-done.22 = f32[112,128]{1,0:T(8,128)S(1)} collective-permute-done((f32[112,128]{1,0:T(8,128)S(1)}, f32[112,128]{1,0:T(8,128)S(1)}, u32[]{:S(2)}, u32[]{:S(2)}) %collective-permute-start.22) | collective-permute-done | bytes 57376 | tf_op jit(solution)/shard_map/ppermute | solution.py:35
  59.7 2.9 %collective-permute-start.25 = (f32[112,128]{1,0:T(8,128)S(1)}, f32[112,128]{1,0:T(8,128)S(1)}, u32[]{:S(2)}, u32[]{:S(2)}) collective-permute-start(f32[112,128]{1,0:T(8,128)S(1)} %add.20), channel_id=1, source_target_pairs={{0,3},{1,2},{2,1},{3,0},{4,7},{5,6},{6,5},{7,4},{8,11},{9,10},{10,... | collective-permute-start | bytes 172040 | tf_op jit(solution)/shard_map/ppermute | solution.py:35
  62.6 1.6 %collective-permute-start.23 = (f32[112,128]{1,0:T(8,128)S(1)}, f32[112,128]{1,0:T(8,128)S(1)}, u32[]{:S(2)}, u32[]{:S(2)}) collective-permute-start(f32[112,128]{1,0:T(8,128)S(1)} %add.20), channel_id=1, source_target_pairs={{0,1},{1,0},{2,3},{3,2},{4,5},{5,4},{6,7},{7,6},{8,9},{9,8},{10,11... | collective-permute-start | bytes 172040 | tf_op jit(solution)/shard_map/ppermute | solution.py:35
  64.2 1.7 %collective-permute-done.25 = f32[112,128]{1,0:T(8,128)S(1)} collective-permute-done((f32[112,128]{1,0:T(8,128)S(1)}, f32[112,128]{1,0:T(8,128)S(1)}, u32[]{:S(2)}, u32[]{:S(2)}) %collective-permute-start.25) | collective-permute-done | bytes 57376 | tf_op jit(solution)/shard_map/ppermute | solution.py:35
  65.9 1.9 %collective-permute-done.24 = f32[112,128]{1,0:T(8,128)S(1)} collective-permute-done((f32[112,128]{1,0:T(8,128)S(1)}, f32[112,128]{1,0:T(8,128)S(1)}, u32[]{:S(2)}, u32[]{:S(2)}) %collective-permute-start.24) | collective-permute-done | bytes 57376 | tf_op jit(solution)/shard_map/ppermute | solution.py:35
  67.8 1.9 %corner.1.corner_ref = f32[64,64]{1,0:T(8,128)S(1)} custom-call(f32[112,128]{1,0:T(8,128)S(1)} %add_add_fusion.keep_ref), custom_call_target="tpu_custom_call" | custom-call | flops 1000000000 | bytes 1000 | tf_op jit(solution)/shard_map/corner/pallas_call | solution.py:423
  69.7 6.0 %orthonormalize.1 = f32[192,512]{1,0:T(8,128)} custom-call(f32[112,128]{1,0:T(8,128)S(1)} %add_add_fusion.keep_ref, f32[112,128]{1,0:T(8,128)S(1)} %collective-permute-done.26.other_ref, f32[64,64]{1,0:T(8,128)S(1)} %corner.1.corner_ref, bf16[512,128]{1,0:T(8,128)(2,1)S(1)} %get-tuple-element.77.wide_ref, bf16[256,128]{1,0:T(8,128)(2,1)S(1)} %get-tuple-element.78.thin_ref), custom_call_target="tpu_custom_call" | custom-call | flops 1000 | bytes 1000 | tf_op jit(solution)/shard_map/orthonormalize/pallas_call | solution.py:426
  (55 shorter events, 8.7 us)
Async XLA Ops:
  0.0 8.1 %collective-permute-start.1 = (bf16[192,512]{1,0:T(8,128)(2,1)}, bf16[192,512]{1,0:T(8,128)(2,1)S(1)}, u32[]{:S(2)}, u32[]{:S(2)}) collective-permute-start(bf16[192,512]{1,0:T(8,128)(2,1)} %bitcast.3), channel_id=1, source_target_pairs={{0,8},{4,12},{8,0},{12,4},{1,9},{5,13},{9,1},{13,5},{2,10},{6,14},... | collective-permute-start | bytes 589832 | tf_op jit(solution)/shard_map/ppermute | solution.py:35
  4.3 1.4 %copy-start = (bf16[32,64,384]{2,1,0:T(8,128)(2,1)S(1)}, bf16[32,64,384]{2,1,0:T(8,128)(2,1)}, u32[]{:S(2)}) copy-start(bf16[32,64,384]{2,1,0:T(8,128)(2,1)} %ham_ref.9) | copy-start | bytes 4718596
  5.7 0.9 %copy-start.2 = (bf16[512,192]{0,1:T(8,128)(2,1)S(1)}, bf16[512,192]{0,1:T(8,128)(2,1)}, u32[]{:S(2)}) copy-start(bf16[512,192]{0,1:T(8,128)(2,1)} %param.7) | copy-start | bytes 589828
  6.6 0.7 copy-start.3
  7.3 2.4 %copy-start.1 = (bf16[32,64,384]{2,1,0:T(8,128)(2,1)S(1)}, bf16[32,64,384]{2,1,0:T(8,128)(2,1)}, u32[]{:S(2)}) copy-start(bf16[32,64,384]{2,1,0:T(8,128)(2,1)} %ham_ref.9) | copy-start | bytes 4718596
  7.3 1.5 %collective-permute-start = (bf16[192,512]{1,0:T(8,128)(2,1)S(1)}, bf16[192,512]{1,0:T(8,128)(2,1)S(1)}, u32[]{:S(2)}, u32[]{:S(2)}) collective-permute-start(bf16[192,512]{1,0:T(8,128)(2,1)S(1)} %get-tuple-element.45), channel_id=1, source_target_pairs={{0,4},{4,0},{8,12},{12,8},{1,5},{5,1},{9,13},{13,9},{2,6},{6,2},{1... | collective-permute-start | bytes 589832 | tf_op jit(solution)/shard_map/ppermute | solution.py:35
  8.1 1.4 %collective-permute-start.2 = (bf16[192,512]{1,0:T(8,128)(2,1)S(1)}, bf16[192,512]{1,0:T(8,128)(2,1)S(1)}, u32[]{:S(2)}, u32[]{:S(2)}) collective-permute-start(bf16[192,512]{1,0:T(8,128)(2,1)S(1)} %collective-permute-done.1.turned_ref), channel_id=1, source_target_pairs={{0,4},{4,0},{8,12},{12,8},{1,5},{5,1},{9,13},{13,9},{2,6},{6,2},{1... | collective-permute-start | bytes 589832 | tf_op jit(solution)/shard_map/ppermute | solution.py:35
  10.8 6.4 %collective-permute-start.3 = (bf16[512,128]{1,0:T(8,128)(2,1)S(1)}, bf16[512,128]{1,0:T(8,128)(2,1)S(1)}, u32[]{:S(2)}, u32[]{:S(2)}) collective-permute-start(bf16[512,128]{1,0:T(8,128)(2,1)S(1)} %get-tuple-element.55), channel_id=1, source_target_pairs={{0,1},{1,0},{2,3},{3,2},{4,5},{5,4},{6,7},{7,6},{8,9},{9,8},{10,11... | collective-permute-start | bytes 393224 | tf_op jit(solution)/shard_map/ppermute | solution.py:35
  12.6 7.4 %collective-permute-start.5 = (bf16[256,128]{1,0:T(8,128)(2,1)S(1)}, bf16[256,128]{1,0:T(8,128)(2,1)S(1)}, u32[]{:S(2)}, u32[]{:S(2)}) collective-permute-start(bf16[256,128]{1,0:T(8,128)(2,1)S(1)} %get-tuple-element.57), channel_id=1, source_target_pairs={{0,1},{1,0},{2,3},{3,2},{4,5},{5,4},{6,7},{7,6},{8,9},{9,8},{10,11... | collective-permute-start | bytes 196616 | tf_op jit(solution)/shard_map/ppermute | solution.py:35
  17.2 9.3 %collective-permute-start.4 = (bf16[512,128]{1,0:T(8,128)(2,1)S(1)}, bf16[512,128]{1,0:T(8,128)(2,1)S(1)}, u32[]{:S(2)}, u32[]{:S(2)}) collective-permute-start(bf16[512,128]{1,0:T(8,128)(2,1)S(1)} %add.27.refs_0_), channel_id=1, source_target_pairs={{0,2},{1,3},{2,0},{3,1},{4,6},{5,7},{6,4},{7,5},{8,10},{9,11},{10,... | collective-permute-start | bytes 393224 | tf_op jit(solution)/shard_map/ppermute | solution.py:35
  20.0 7.5 %collective-permute-start.6 = (bf16[512,128]{1,0:T(8,128)(2,1)S(1)}, bf16[512,128]{1,0:T(8,128)(2,1)S(1)}, u32[]{:S(2)}, u32[]{:S(2)}) collective-permute-start(bf16[512,128]{1,0:T(8,128)(2,1)S(1)} %get-tuple-element.60), channel_id=1, source_target_pairs={{0,1},{1,0},{2,3},{3,2},{4,5},{5,4},{6,7},{7,6},{8,9},{9,8},{10,11... | collective-permute-start | bytes 393224 | tf_op jit(solution)/shard_map/ppermute | solution.py:35
  21.7 7.6 %collective-permute-start.10 = (bf16[256,128]{1,0:T(8,128)(2,1)S(1)}, bf16[256,128]{1,0:T(8,128)(2,1)S(1)}, u32[]{:S(2)}, u32[]{:S(2)}) collective-permute-start(bf16[256,128]{1,0:T(8,128)(2,1)S(1)} %get-tuple-element.62), channel_id=1, source_target_pairs={{0,2},{1,3},{2,0},{3,1},{4,6},{5,7},{6,4},{7,5},{8,10},{9,11},{10,... | collective-permute-start | bytes 196616 | tf_op jit(solution)/shard_map/ppermute | solution.py:35
  22.3 7.0 %collective-permute-start.11 = (bf16[256,128]{1,0:T(8,128)(2,1)S(1)}, bf16[256,128]{1,0:T(8,128)(2,1)S(1)}, u32[]{:S(2)}, u32[]{:S(2)}) collective-permute-start(bf16[256,128]{1,0:T(8,128)(2,1)S(1)} %get-tuple-element.63), channel_id=1, source_target_pairs={{0,1},{1,0},{2,3},{3,2},{4,5},{5,4},{6,7},{7,6},{8,9},{9,8},{10,11... | collective-permute-start | bytes 196616 | tf_op jit(solution)/shard_map/ppermute | solution.py:35
  27.6 5.0 %collective-permute-start.8 = (bf16[512,128]{1,0:T(8,128)(2,1)S(1)}, bf16[512,128]{1,0:T(8,128)(2,1)S(1)}, u32[]{:S(2)}, u32[]{:S(2)}) collective-permute-start(bf16[512,128]{1,0:T(8,128)(2,1)S(1)} %first_filter.2.refs_0_.refs_1_), channel_id=1, source_target_pairs={{0,8},{4,12},{8,0},{12,4},{1,9},{5,13},{9,1},{13,5},{2,10},{6,14},... | collective-permute-start | bytes 393224 | tf_op jit(solution)/shard_map/ppermute | solution.py:35
  29.4 4.3 %collective-permute-start.13 = (bf16[256,128]{1,0:T(8,128)(2,1)S(1)}, bf16[256,128]{1,0:T(8,128)(2,1)S(1)}, u32[]{:S(2)}, u32[]{:S(2)}) collective-permute-start(bf16[256,128]{1,0:T(8,128)(2,1)S(1)} %first_filter.3.refs_4_.refs_5_), channel_id=1, source_target_pairs={{0,8},{4,12},{8,0},{12,4},{1,9},{5,13},{9,1},{13,5},{2,10},{6,14},... | collective-permute-start | bytes 196616 | tf_op jit(solution)/shard_map/ppermute | solution.py:35
  30.0 5.0 %collective-permute-start.7 = (bf16[512,128]{1,0:T(8,128)(2,1)S(1)}, bf16[512,128]{1,0:T(8,128)(2,1)S(1)}, u32[]{:S(2)}, u32[]{:S(2)}) collective-permute-start(bf16[512,128]{1,0:T(8,128)(2,1)S(1)} %first_filter.2.refs_0_.refs_1_), channel_id=1, source_target_pairs={{0,4},{4,0},{8,12},{12,8},{1,5},{5,1},{9,13},{13,9},{2,6},{6,2},{1... | collective-permute-start | bytes 393224 | tf_op jit(solution)/shard_map/ppermute | solution.py:35
  32.7 2.3 %collective-permute-start.9 = (bf16[512,128]{1,0:T(8,128)(2,1)S(1)}, bf16[512,128]{1,0:T(8,128)(2,1)S(1)}, u32[]{:S(2)}, u32[]{:S(2)}) collective-permute-start(bf16[512,128]{1,0:T(8,128)(2,1)S(1)} %collective-permute-done.8.refs_2_), channel_id=1, source_target_pairs={{0,4},{4,0},{8,12},{12,8},{1,5},{5,1},{9,13},{13,9},{2,6},{6,2},{1... | collective-permute-start | bytes 393224 | tf_op jit(solution)/shard_map/ppermute | solution.py:35
  32.7 1.4 %collective-permute-start.12 = (bf16[256,128]{1,0:T(8,128)(2,1)S(1)}, bf16[256,128]{1,0:T(8,128)(2,1)S(1)}, u32[]{:S(2)}, u32[]{:S(2)}) collective-permute-start(bf16[256,128]{1,0:T(8,128)(2,1)S(1)} %first_filter.3.refs_4_.refs_5_), channel_id=1, source_target_pairs={{0,4},{4,0},{8,12},{12,8},{1,5},{5,1},{9,13},{13,9},{2,6},{6,2},{1... | collective-permute-start | bytes 196616 | tf_op jit(solution)/shard_map/ppermute | solution.py:35
  33.7 1.3 %collective-permute-start.14 = (bf16[256,128]{1,0:T(8,128)(2,1)S(1)}, bf16[256,128]{1,0:T(8,128)(2,1)S(1)}, u32[]{:S(2)}, u32[]{:S(2)}) collective-permute-start(bf16[256,128]{1,0:T(8,128)(2,1)S(1)} %collective-permute-done.13.refs_6_), channel_id=1, source_target_pairs={{0,4},{4,0},{8,12},{12,8},{1,5},{5,1},{9,13},{13,9},{2,6},{6,2},{1... | collective-permute-start | bytes 196616 | tf_op jit(solution)/shard_map/ppermute | solution.py:35
  36.1 6.3 %collective-permute-start.15 = (bf16[512,128]{1,0:T(8,128)(2,1)S(1)}, bf16[512,128]{1,0:T(8,128)(2,1)S(1)}, u32[]{:S(2)}, u32[]{:S(2)}) collective-permute-start(bf16[512,128]{1,0:T(8,128)(2,1)S(1)} %get-tuple-element.66), channel_id=1, source_target_pairs={{0,1},{1,0},{2,3},{3,2},{4,5},{5,4},{6,7},{7,6},{8,9},{9,8},{10,11... | collective-permute-start | bytes 393224 | tf_op jit(solution)/shard_map/ppermute | solution.py:35
  36.8 7.4 %collective-permute-start.17 = (bf16[256,128]{1,0:T(8,128)(2,1)S(1)}, bf16[256,128]{1,0:T(8,128)(2,1)S(1)}, u32[]{:S(2)}, u32[]{:S(2)}) collective-permute-start(bf16[256,128]{1,0:T(8,128)(2,1)S(1)} %get-tuple-element.68), channel_id=1, source_target_pairs={{0,1},{1,0},{2,3},{3,2},{4,5},{5,4},{6,7},{7,6},{8,9},{9,8},{10,11... | collective-permute-start | bytes 196616 | tf_op jit(solution)/shard_map/ppermute | solution.py:35
  42.4 10.0 %collective-permute-start.16 = (bf16[512,128]{1,0:T(8,128)(2,1)S(1)}, bf16[512,128]{1,0:T(8,128)(2,1)S(1)}, u32[]{:S(2)}, u32[]{:S(2)}) collective-permute-start(bf16[512,128]{1,0:T(8,128)(2,1)S(1)} %add.29.refs_0_), channel_id=1, source_target_pairs={{0,2},{1,3},{2,0},{3,1},{4,6},{5,7},{6,4},{7,5},{8,10},{9,11},{10,... | collective-permute-start | bytes 393224 | tf_op jit(solution)/shard_map/ppermute | solution.py:35
  44.2 9.5 %collective-permute-start.18 = (bf16[512,128]{1,0:T(8,128)(2,1)S(1)}, bf16[512,128]{1,0:T(8,128)(2,1)S(1)}, u32[]{:S(2)}, u32[]{:S(2)}) collective-permute-start(bf16[512,128]{1,0:T(8,128)(2,1)S(1)} %get-tuple-element.71), channel_id=1, source_target_pairs={{0,1},{1,0},{2,3},{3,2},{4,5},{5,4},{6,7},{7,6},{8,9},{9,8},{10,11... | collective-permute-start | bytes 393224 | tf_op jit(solution)/shard_map/ppermute | solution.py:35
  46.2 6.2 %collective-permute-start.19 = (bf16[256,128]{1,0:T(8,128)(2,1)S(1)}, bf16[256,128]{1,0:T(8,128)(2,1)S(1)}, u32[]{:S(2)}, u32[]{:S(2)}) collective-permute-start(bf16[256,128]{1,0:T(8,128)(2,1)S(1)} %get-tuple-element.73), channel_id=1, source_target_pairs={{0,2},{1,3},{2,0},{3,1},{4,6},{5,7},{6,4},{7,5},{8,10},{9,11},{10,... | collective-permute-start | bytes 196616 | tf_op jit(solution)/shard_map/ppermute | solution.py:35
  46.8 6.8 %collective-permute-start.20 = (bf16[256,128]{1,0:T(8,128)(2,1)S(1)}, bf16[256,128]{1,0:T(8,128)(2,1)S(1)}, u32[]{:S(2)}, u32[]{:S(2)}) collective-permute-start(bf16[256,128]{1,0:T(8,128)(2,1)S(1)} %get-tuple-element.74), channel_id=1, source_target_pairs={{0,1},{1,0},{2,3},{3,2},{4,5},{5,4},{6,7},{7,6},{8,9},{9,8},{10,11... | collective-permute-start | bytes 196616 | tf_op jit(solution)/shard_map/ppermute | solution.py:35
  54.1 1.3 %collective-permute-start.21 = (f32[112,128]{1,0:T(8,128)S(1)}, f32[112,128]{1,0:T(8,128)S(1)}, u32[]{:S(2)}, u32[]{:S(2)}) collective-permute-start(f32[112,128]{1,0:T(8,128)S(1)} %get-tuple-element.76), channel_id=1, source_target_pairs={{0,4},{4,0},{8,12},{12,8},{1,5},{5,1},{9,13},{13,9},{2,6},{6,2},{1... | collective-permute-start | bytes 172040 | tf_op jit(solution)/shard_map/ppermute | solution.py:35
  55.5 4.2 %collective-permute-start.22 = (f32[112,128]{1,0:T(8,128)S(1)}, f32[112,128]{1,0:T(8,128)S(1)}, u32[]{:S(2)}, u32[]{:S(2)}) collective-permute-start(f32[112,128]{1,0:T(8,128)S(1)} %add.19), channel_id=1, source_target_pairs={{0,8},{4,12},{8,0},{12,4},{1,9},{5,13},{9,1},{13,5},{2,10},{6,14},... | collective-permute-start | bytes 172040 | tf_op jit(solution)/shard_map/ppermute | solution.py:35
  59.7 6.1 %collective-permute-start.25 = (f32[112,128]{1,0:T(8,128)S(1)}, f32[112,128]{1,0:T(8,128)S(1)}, u32[]{:S(2)}, u32[]{:S(2)}) collective-permute-start(f32[112,128]{1,0:T(8,128)S(1)} %add.20), channel_id=1, source_target_pairs={{0,3},{1,2},{2,1},{3,0},{4,7},{5,6},{6,5},{7,4},{8,11},{9,10},{10,... | collective-permute-start | bytes 172040 | tf_op jit(solution)/shard_map/ppermute | solution.py:35
  62.6 5.1 %collective-permute-start.24 = (f32[112,128]{1,0:T(8,128)S(1)}, f32[112,128]{1,0:T(8,128)S(1)}, u32[]{:S(2)}, u32[]{:S(2)}) collective-permute-start(f32[112,128]{1,0:T(8,128)S(1)} %add.20), channel_id=1, source_target_pairs={{0,2},{1,3},{2,0},{3,1},{4,6},{5,7},{6,4},{7,5},{8,10},{9,11},{10,... | collective-permute-start | bytes 172040 | tf_op jit(solution)/shard_map/ppermute | solution.py:35
  62.6 5.1 %collective-permute-start.23 = (f32[112,128]{1,0:T(8,128)S(1)}, f32[112,128]{1,0:T(8,128)S(1)}, u32[]{:S(2)}, u32[]{:S(2)}) collective-permute-start(f32[112,128]{1,0:T(8,128)S(1)} %add.20), channel_id=1, source_target_pairs={{0,1},{1,0},{2,3},{3,2},{4,5},{5,4},{6,7},{7,6},{8,9},{9,8},{10,11... | collective-permute-start | bytes 172040 | tf_op jit(solution)/shard_map/ppermute | solution.py:35
  67.7 2.0 %collective-permute-start.26 = (f32[112,128]{1,0:T(8,128)S(1)}, f32[112,128]{1,0:T(8,128)S(1)}, u32[]{:S(2)}, u32[]{:S(2)}) collective-permute-start(f32[112,128]{1,0:T(8,128)S(1)} %add_add_fusion.keep_ref), channel_id=1, source_target_pairs={{0,4},{4,0},{8,12},{12,8},{1,5},{5,1},{9,13},{13,9},{2,6},{6,2},{1... | collective-permute-start | bytes 172040 | tf_op jit(solution)/shard_map/ppermute | solution.py:35

commit v8 on v7

--- a/solution.py
+++ b/solution.py
@@ -328,8 +328,6 @@
     l21 = dot_t(rest[size:], x1)
     last = g22 - dot_t(l20, l20) - dot_t(l21, l21)
     n10 = -dot(x1, dot(l10, x0))
-    below0 = dot(l20, x0) + dot(l21, n10)
-    below1 = dot(l21, x1)
     zero = jnp.zeros((size, size), F32)
     factor[pl.ds(0, size), :] = jnp.concatenate([x0, zero], axis=1)
     factor[pl.ds(size, size), :] = jnp.concatenate([n10, x1], axis=1)
@@ -348,18 +346,11 @@
     result[head, :] = apply(factor[head, :], wide)
     early = pltpu.make_async_copy(result.at[head], out_ref.at[head], sems.at[0])
     early.start()
+    turned = thin.astype(F32).T
+    turned = jnp.concatenate([turned[:size], turned[size:]], axis=1)
+    rest = turned - dot(jnp.concatenate([l20, l21], axis=1), result[head, :])
     x2 = inverse_factor(last)
-    n20 = -dot(x2, below0)
-    n21 = -dot(x2, below1)
-    factor[foot, :] = jnp.concatenate([n20, n21], axis=1)
-    tail = jnp.concatenate(
-        [
-            apply(jnp.concatenate([x2, zero], axis=1), thin),
-            apply(jnp.concatenate([zero, x2], axis=1), thin),
-        ],
-        axis=1,
-    )
-    result[foot, :] = apply(factor[foot, :], wide) + tail
+    result[foot, :] = dot(x2, rest)
     late = pltpu.make_async_copy(result.at[foot], out_ref.at[foot], sems.at[1])
     late.start()
     early.wait()

time: 75.9 us -> 75.7 us (level)
  no operation moved by 1% of the time
where the time goes in v8:
time: 75.7 us; the launch traced here: 75.5 us
  waiting for transfers between devices  30.1 us (40%)
  starting transfers between devices  26.5 us (35%)
  Pallas kernels  14.4 us (19%)
  local copies, waits for them, and re-layouts  3.02 us (4%)
  between operations  1.47 us (2%)
    ppermute x27, waiting for transfers between devices, swap(): return lax.ppermute(x, axis, [(i, i ^ key) for i in range(count)])  30.1 us
    ppermute x27, starting transfers between devices, swap(): return lax.ppermute(x, axis, [(i, i ^ key) for i in range(count)])  26.5 us
    pallas_call x1, Pallas kernels, per_device(): call(last_kernel, jax.ShapeDtypeStruct((LANES + SIZE, rows), F32), [VMEM]...  5.77 us
    pallas_call x4, Pallas kernels, product(): call(functools.partial(product_kernel, keys, n_row, own_blocks), [jax.Sha...  5.33 us
    unnamed x8, local copies, waits for them, and re-layouts  3.02 us
    pallas_call x1, Pallas kernels, per_device(): call(corner_kernel, jax.ShapeDtypeStruct((SIZE, SIZE), F32), [VMEM], flop...  1.88 us
  transfers between devices with their start and end apart: 27, of which 17 were waited for; matrix products, arithmetic and copies ran while one was open for 0% of the time, Pallas kernels for 8%

profile of v8, /device:TPU:0, one launch (start us, length us, event | category | flops | bytes accessed | tf_op | source)
XLA Modules:
  0.0 75.5 jit_solution(16261582273242126814)
XLA Ops:
  0.0 3.0 %collective-permute-start.1 = (bf16[192,512]{1,0:T(8,128)(2,1)}, bf16[192,512]{1,0:T(8,128)(2,1)S(1)}, u32[]{:S(2)}, u32[]{:S(2)}) collective-permute-start(bf16[192,512]{1,0:T(8,128)(2,1)} %bitcast.3), channel_id=1, source_target_pairs={{0,8},{4,12},{8,0},{12,4},{1,9},{5,13},{9,1},{13,5},{2,10},{6,14},... | collective-permute-start | bytes 589832 | tf_op jit(solution)/shard_map/ppermute | solution.py:35
  4.3 1.4 %copy-done = bf16[32,64,384]{2,1,0:T(8,128)(2,1)S(1)} copy-done((bf16[32,64,384]{2,1,0:T(8,128)(2,1)S(1)}, bf16[32,64,384]{2,1,0:T(8,128)(2,1)}, u32[]{:S(2)}) %copy-start) | copy-done | bytes 1572888
  5.7 0.9 %copy-done.2 = bf16[512,192]{0,1:T(8,128)(2,1)S(1)} copy-done((bf16[512,192]{0,1:T(8,128)(2,1)S(1)}, bf16[512,192]{0,1:T(8,128)(2,1)}, u32[]{:S(2)}) %copy-start.2) | copy-done | bytes 196632
  9.7 1.1 %product.5 = (bf16[512,128]{1,0:T(8,128)(2,1)S(1)}, bf16[256,128]{1,0:T(8,128)(2,1)S(1)}) custom-call(s32[6,32]{1,0:T(8,128)S(1)} %get-tuple-element.44.at_vmem, bf16[32,64,384]{2,1,0:T(8,128)(2,1)S(1)} %copy-done.1, bf16[512,128]{1,0:T(8,128)(2,1)S(1)} %get-tuple-element.43.refs_0_.start, bf16[512,128]{1,0:T(8,128)(2,1)S(1)} %get-tuple-element.46.refs_1_, ...), custom_call_target="tpu_custom_call" | custom-call | flops 100663296 | bytes 1000 | tf_op jit(solution)/shard_map/product/pallas_call | solution.py:127
  10.8 1.9 %collective-permute-start.3 = (bf16[512,128]{1,0:T(8,128)(2,1)S(1)}, bf16[512,128]{1,0:T(8,128)(2,1)S(1)}, u32[]{:S(2)}, u32[]{:S(2)}) collective-permute-start(bf16[512,128]{1,0:T(8,128)(2,1)S(1)} %get-tuple-element.55), channel_id=1, source_target_pairs={{0,1},{1,0},{2,3},{3,2},{4,5},{5,4},{6,7},{7,6},{8,9},{9,8},{10,11... | collective-permute-start | bytes 393224 | tf_op jit(solution)/shard_map/ppermute | solution.py:35
  12.9 1.6 %product.4 = (bf16[512,128]{1,0:T(8,128)(2,1)S(1)}, bf16[512,128]{1,0:T(8,128)(2,1)S(1)}, bf16[512,128]{1,0:T(8,128)(2,1)S(1)}, bf16[256,128]{1,0:T(8,128)(2,1)S...) custom-call(s32[6,32]{1,0:T(8,128)S(1)} %get-tuple-element.44.at_vmem, ...), custom_call_target="tpu_custom_call" | custom-call | flops 301989888 | bytes 1000 | tf_op jit(solution)/shard_map/product/pallas_call | solution.py:127
  14.4 2.7 %collective-permute-done.3.refs_1_ = bf16[512,128]{1,0:T(8,128)(2,1)S(1)} collective-permute-done((bf16[512,128]{1,0:T(8,128)(2,1)S(1)}, bf16[512,128]{1,0:T(8,128)(2,1)S(1)}, u32[]{:S(2)}, u32[]{:S(2)}) %collective-permute-start.3) | collective-permute-done | bytes 131104 | tf_op jit(solution)/shard_map/ppermute | solution.py:35
  17.2 2.8 %collective-permute-start.4 = (bf16[512,128]{1,0:T(8,128)(2,1)S(1)}, bf16[512,128]{1,0:T(8,128)(2,1)S(1)}, u32[]{:S(2)}, u32[]{:S(2)}) collective-permute-start(bf16[512,128]{1,0:T(8,128)(2,1)S(1)} %add.27.refs_0_), channel_id=1, source_target_pairs={{0,2},{1,3},{2,0},{3,1},{4,6},{5,7},{6,4},{7,5},{8,10},{9,11},{10,... | collective-permute-start | bytes 393224 | tf_op jit(solution)/shard_map/ppermute | solution.py:35
  20.0 1.6 %collective-permute-start.6 = (bf16[512,128]{1,0:T(8,128)(2,1)S(1)}, bf16[512,128]{1,0:T(8,128)(2,1)S(1)}, u32[]{:S(2)}, u32[]{:S(2)}) collective-permute-start(bf16[512,128]{1,0:T(8,128)(2,1)S(1)} %get-tuple-element.60), channel_id=1, source_target_pairs={{0,1},{1,0},{2,3},{3,2},{4,5},{5,4},{6,7},{7,6},{8,9},{9,8},{10,11... | collective-permute-start | bytes 393224 | tf_op jit(solution)/shard_map/ppermute | solution.py:35
  22.7 3.7 %collective-permute-done.4.b = bf16[512,128]{1,0:T(8,128)(2,1)S(1)} collective-permute-done((bf16[512,128]{1,0:T(8,128)(2,1)S(1)}, bf16[512,128]{1,0:T(8,128)(2,1)S(1)}, u32[]{:S(2)}, u32[]{:S(2)}) %collective-permute-start.4) | collective-permute-done | bytes 131104 | tf_op jit(solution)/shard_map/ppermute | solution.py:35
  26.5 1.1 %collective-permute-done.6.refs_1_ = bf16[512,128]{1,0:T(8,128)(2,1)S(1)} collective-permute-done((bf16[512,128]{1,0:T(8,128)(2,1)S(1)}, bf16[512,128]{1,0:T(8,128)(2,1)S(1)}, u32[]{:S(2)}, u32[]{:S(2)}) %collective-permute-start.6) | collective-permute-done | bytes 131104 | tf_op jit(solution)/shard_map/ppermute | solution.py:35
  27.6 1.6 %collective-permute-start.8 = (bf16[512,128]{1,0:T(8,128)(2,1)S(1)}, bf16[512,128]{1,0:T(8,128)(2,1)S(1)}, u32[]{:S(2)}, u32[]{:S(2)}) collective-permute-start(bf16[512,128]{1,0:T(8,128)(2,1)S(1)} %first_filter.2.refs_0_.refs_1_), channel_id=1, source_target_pairs={{0,8},{4,12},{8,0},{12,4},{1,9},{5,13},{9,1},{13,5},{2,10},{6,14},... | collective-permute-start | bytes 393224 | tf_op jit(solution)/shard_map/ppermute | solution.py:35
  30.0 2.7 %collective-permute-done.8.refs_2_ = bf16[512,128]{1,0:T(8,128)(2,1)S(1)} collective-permute-done((bf16[512,128]{1,0:T(8,128)(2,1)S(1)}, bf16[512,128]{1,0:T(8,128)(2,1)S(1)}, u32[]{:S(2)}, u32[]{:S(2)}) %collective-permute-start.8) | collective-permute-done | bytes 131104 | tf_op jit(solution)/shard_map/ppermute | solution.py:35
  34.1 0.8 %collective-permute-done.14.refs_7_ = bf16[256,128]{1,0:T(8,128)(2,1)S(1)} collective-permute-done((bf16[256,128]{1,0:T(8,128)(2,1)S(1)}, bf16[256,128]{1,0:T(8,128)(2,1)S(1)}, u32[]{:S(2)}, u32[]{:S(2)}) %collective-permute-start.14) | collective-permute-done | bytes 65568 | tf_op jit(solution)/shard_map/ppermute | solution.py:35
  34.9 1.1 %product.7 = (bf16[512,128]{1,0:T(8,128)(2,1)S(1)}, bf16[256,128]{1,0:T(8,128)(2,1)S(1)}) custom-call(s32[6,32]{1,0:T(8,128)S(1)} %get-tuple-element.44.at_vmem, bf16[32,64,384]{2,1,0:T(8,128)(2,1)S(1)} %copy-done.1, bf16[512,128]{1,0:T(8,128)(2,1)S(1)} %first_filter.2.refs_0_.refs_1_, bf16[512,128]{1,0:T(8,128)(2,1)S(1)} %collective-permute-done.7.refs_1_, ...), custom_call_target="tpu_custom_call" | custom-call | flops 100663296 | bytes 1000 | tf_op jit(solution)/shard_map/product/pallas_call | solution.py:127
  36.8 1.4 %collective-permute-start.17 = (bf16[256,128]{1,0:T(8,128)(2,1)S(1)}, bf16[256,128]{1,0:T(8,128)(2,1)S(1)}, u32[]{:S(2)}, u32[]{:S(2)}) collective-permute-start(bf16[256,128]{1,0:T(8,128)(2,1)S(1)} %get-tuple-element.68), channel_id=1, source_target_pairs={{0,1},{1,0},{2,3},{3,2},{4,5},{5,4},{6,7},{7,6},{8,9},{9,8},{10,11... | collective-permute-start | bytes 196616 | tf_op jit(solution)/shard_map/ppermute | solution.py:35
  38.1 1.6 %product.6 = (bf16[512,128]{1,0:T(8,128)(2,1)S(1)}, bf16[512,128]{1,0:T(8,128)(2,1)S(1)}, bf16[512,128]{1,0:T(8,128)(2,1)S(1)}, bf16[256,128]{1,0:T(8,128)(2,1)S...) custom-call(s32[6,32]{1,0:T(8,128)S(1)} %get-tuple-element.44.at_vmem, ...), custom_call_target="tpu_custom_call" | custom-call | flops 301989888 | bytes 1000 | tf_op jit(solution)/shard_map/product/pallas_call | solution.py:127
  39.7 2.7 %collective-permute-done.15.refs_1_ = bf16[512,128]{1,0:T(8,128)(2,1)S(1)} collective-permute-done((bf16[512,128]{1,0:T(8,128)(2,1)S(1)}, bf16[512,128]{1,0:T(8,128)(2,1)S(1)}, u32[]{:S(2)}, u32[]{:S(2)}) %collective-permute-start.15) | collective-permute-done | bytes 131104 | tf_op jit(solution)/shard_map/ppermute | solution.py:35
  42.4 1.7 %collective-permute-start.16 = (bf16[512,128]{1,0:T(8,128)(2,1)S(1)}, bf16[512,128]{1,0:T(8,128)(2,1)S(1)}, u32[]{:S(2)}, u32[]{:S(2)}) collective-permute-start(bf16[512,128]{1,0:T(8,128)(2,1)S(1)} %add.29.refs_0_), channel_id=1, source_target_pairs={{0,2},{1,3},{2,0},{3,1},{4,6},{5,7},{6,4},{7,5},{8,10},{9,11},{10,... | collective-permute-start | bytes 393224 | tf_op jit(solution)/shard_map/ppermute | solution.py:35
  44.2 2.0 %collective-permute-start.18 = (bf16[512,128]{1,0:T(8,128)(2,1)S(1)}, bf16[512,128]{1,0:T(8,128)(2,1)S(1)}, u32[]{:S(2)}, u32[]{:S(2)}) collective-permute-start(bf16[512,128]{1,0:T(8,128)(2,1)S(1)} %get-tuple-element.71), channel_id=1, source_target_pairs={{0,1},{1,0},{2,3},{3,2},{4,5},{5,4},{6,7},{7,6},{8,9},{9,8},{10,11... | collective-permute-start | bytes 393224 | tf_op jit(solution)/shard_map/ppermute | solution.py:35
  46.8 0.7 collective-permute-start.20
  47.5 4.9 %collective-permute-done.19.b = bf16[256,128]{1,0:T(8,128)(2,1)S(1)} collective-permute-done((bf16[256,128]{1,0:T(8,128)(2,1)S(1)}, bf16[256,128]{1,0:T(8,128)(2,1)S(1)}, u32[]{:S(2)}, u32[]{:S(2)}) %collective-permute-start.19) | collective-permute-done | bytes 65568 | tf_op jit(solution)/shard_map/ppermute | solution.py:35
  52.5 1.1 %collective-permute-done.20.refs_7_ = bf16[256,128]{1,0:T(8,128)(2,1)S(1)} collective-permute-done((bf16[256,128]{1,0:T(8,128)(2,1)S(1)}, bf16[256,128]{1,0:T(8,128)(2,1)S(1)}, u32[]{:S(2)}, u32[]{:S(2)}) %collective-permute-start.20) | collective-permute-done | bytes 65568 | tf_op jit(solution)/shard_map/ppermute | solution.py:35
  54.2 1.2 %collective-permute-done.21 = f32[112,128]{1,0:T(8,128)S(1)} collective-permute-done((f32[112,128]{1,0:T(8,128)S(1)}, f32[112,128]{1,0:T(8,128)S(1)}, u32[]{:S(2)}, u32[]{:S(2)}) %collective-permute-start.21) | collective-permute-done | bytes 57376 | tf_op jit(solution)/shard_map/ppermute | solution.py:35
  55.5 1.3 %collective-permute-start.22 = (f32[112,128]{1,0:T(8,128)S(1)}, f32[112,128]{1,0:T(8,128)S(1)}, u32[]{:S(2)}, u32[]{:S(2)}) collective-permute-start(f32[112,128]{1,0:T(8,128)S(1)} %add.19), channel_id=1, source_target_pairs={{0,8},{4,12},{8,0},{12,4},{1,9},{5,13},{9,1},{13,5},{2,10},{6,14},... | collective-permute-start | bytes 172040 | tf_op jit(solution)/shard_map/ppermute | solution.py:35
  56.8 2.9 %collective-permute-done.22 = f32[112,128]{1,0:T(8,128)S(1)} collective-permute-done((f32[112,128]{1,0:T(8,128)S(1)}, f32[112,128]{1,0:T(8,128)S(1)}, u32[]{:S(2)}, u32[]{:S(2)}) %collective-permute-start.22) | collective-permute-done | bytes 57376 | tf_op jit(solution)/shard_map/ppermute | solution.py:35
  59.7 2.9 %collective-permute-start.25 = (f32[112,128]{1,0:T(8,128)S(1)}, f32[112,128]{1,0:T(8,128)S(1)}, u32[]{:S(2)}, u32[]{:S(2)}) collective-permute-start(f32[112,128]{1,0:T(8,128)S(1)} %add.20), channel_id=1, source_target_pairs={{0,3},{1,2},{2,1},{3,0},{4,7},{5,6},{6,5},{7,4},{8,11},{9,10},{10,... | collective-permute-start | bytes 172040 | tf_op jit(solution)/shard_map/ppermute | solution.py:35
  62.6 1.6 %collective-permute-start.23 = (f32[112,128]{1,0:T(8,128)S(1)}, f32[112,128]{1,0:T(8,128)S(1)}, u32[]{:S(2)}, u32[]{:S(2)}) collective-permute-start(f32[112,128]{1,0:T(8,128)S(1)} %add.20), channel_id=1, source_target_pairs={{0,1},{1,0},{2,3},{3,2},{4,5},{5,4},{6,7},{7,6},{8,9},{9,8},{10,11... | collective-permute-start | bytes 172040 | tf_op jit(solution)/shard_map/ppermute | solution.py:35
  64.2 1.7 %collective-permute-done.25 = f32[112,128]{1,0:T(8,128)S(1)} collective-permute-done((f32[112,128]{1,0:T(8,128)S(1)}, f32[112,128]{1,0:T(8,128)S(1)}, u32[]{:S(2)}, u32[]{:S(2)}) %collective-permute-start.25) | collective-permute-done | bytes 57376 | tf_op jit(solution)/shard_map/ppermute | solution.py:35
  65.9 1.9 %collective-permute-done.24 = f32[112,128]{1,0:T(8,128)S(1)} collective-permute-done((f32[112,128]{1,0:T(8,128)S(1)}, f32[112,128]{1,0:T(8,128)S(1)}, u32[]{:S(2)}, u32[]{:S(2)}) %collective-permute-start.24) | collective-permute-done | bytes 57376 | tf_op jit(solution)/shard_map/ppermute | solution.py:35
  67.8 1.9 %corner.1.corner_ref = f32[64,64]{1,0:T(8,128)S(1)} custom-call(f32[112,128]{1,0:T(8,128)S(1)} %add_add_fusion.keep_ref), custom_call_target="tpu_custom_call" | custom-call | flops 1000000000 | bytes 1000 | tf_op jit(solution)/shard_map/corner/pallas_call | solution.py:414
  69.7 5.8 %orthonormalize.1 = f32[192,512]{1,0:T(8,128)} custom-call(f32[112,128]{1,0:T(8,128)S(1)} %add_add_fusion.keep_ref, f32[112,128]{1,0:T(8,128)S(1)} %collective-permute-done.26.other_ref, f32[64,64]{1,0:T(8,128)S(1)} %corner.1.corner_ref, bf16[512,128]{1,0:T(8,128)(2,1)S(1)} %get-tuple-element.77.wide_ref, bf16[256,128]{1,0:T(8,128)(2,1)S(1)} %get-tuple-element.78.thin_ref), custom_call_target="tpu_custom_call" | custom-call | flops 1000 | bytes 1000 | tf_op jit(solution)/shard_map/orthonormalize/pallas_call | solution.py:417
  (55 shorter events, 8.7 us)
Async XLA Ops:
  0.0 8.1 %collective-permute-start.1 = (bf16[192,512]{1,0:T(8,128)(2,1)}, bf16[192,512]{1,0:T(8,128)(2,1)S(1)}, u32[]{:S(2)}, u32[]{:S(2)}) collective-permute-start(bf16[192,512]{1,0:T(8,128)(2,1)} %bitcast.3), channel_id=1, source_target_pairs={{0,8},{4,12},{8,0},{12,4},{1,9},{5,13},{9,1},{13,5},{2,10},{6,14},... | collective-permute-start | bytes 589832 | tf_op jit(solution)/shard_map/ppermute | solution.py:35
  4.3 1.4 %copy-start = (bf16[32,64,384]{2,1,0:T(8,128)(2,1)S(1)}, bf16[32,64,384]{2,1,0:T(8,128)(2,1)}, u32[]{:S(2)}) copy-start(bf16[32,64,384]{2,1,0:T(8,128)(2,1)} %ham_ref.9) | copy-start | bytes 4718596
  5.7 0.9 %copy-start.2 = (bf16[512,192]{0,1:T(8,128)(2,1)S(1)}, bf16[512,192]{0,1:T(8,128)(2,1)}, u32[]{:S(2)}) copy-start(bf16[512,192]{0,1:T(8,128)(2,1)} %param.7) | copy-start | bytes 589828
  6.6 0.7 copy-start.3
  7.3 2.4 %copy-start.1 = (bf16[32,64,384]{2,1,0:T(8,128)(2,1)S(1)}, bf16[32,64,384]{2,1,0:T(8,128)(2,1)}, u32[]{:S(2)}) copy-start(bf16[32,64,384]{2,1,0:T(8,128)(2,1)} %ham_ref.9) | copy-start | bytes 4718596
  7.3 1.5 %collective-permute-start = (bf16[192,512]{1,0:T(8,128)(2,1)S(1)}, bf16[192,512]{1,0:T(8,128)(2,1)S(1)}, u32[]{:S(2)}, u32[]{:S(2)}) collective-permute-start(bf16[192,512]{1,0:T(8,128)(2,1)S(1)} %get-tuple-element.45), channel_id=1, source_target_pairs={{0,4},{4,0},{8,12},{12,8},{1,5},{5,1},{9,13},{13,9},{2,6},{6,2},{1... | collective-permute-start | bytes 589832 | tf_op jit(solution)/shard_map/ppermute | solution.py:35
  8.1 1.4 %collective-permute-start.2 = (bf16[192,512]{1,0:T(8,128)(2,1)S(1)}, bf16[192,512]{1,0:T(8,128)(2,1)S(1)}, u32[]{:S(2)}, u32[]{:S(2)}) collective-permute-start(bf16[192,512]{1,0:T(8,128)(2,1)S(1)} %collective-permute-done.1.turned_ref), channel_id=1, source_target_pairs={{0,4},{4,0},{8,12},{12,8},{1,5},{5,1},{9,13},{13,9},{2,6},{6,2},{1... | collective-permute-start | bytes 589832 | tf_op jit(solution)/shard_map/ppermute | solution.py:35
  10.8 6.4 %collective-permute-start.3 = (bf16[512,128]{1,0:T(8,128)(2,1)S(1)}, bf16[512,128]{1,0:T(8,128)(2,1)S(1)}, u32[]{:S(2)}, u32[]{:S(2)}) collective-permute-start(bf16[512,128]{1,0:T(8,128)(2,1)S(1)} %get-tuple-element.55), channel_id=1, source_target_pairs={{0,1},{1,0},{2,3},{3,2},{4,5},{5,4},{6,7},{7,6},{8,9},{9,8},{10,11... | collective-permute-start | bytes 393224 | tf_op jit(solution)/shard_map/ppermute | solution.py:35
  12.6 7.4 %collective-permute-start.5 = (bf16[256,128]{1,0:T(8,128)(2,1)S(1)}, bf16[256,128]{1,0:T(8,128)(2,1)S(1)}, u32[]{:S(2)}, u32[]{:S(2)}) collective-permute-start(bf16[256,128]{1,0:T(8,128)(2,1)S(1)} %get-tuple-element.57), channel_id=1, source_target_pairs={{0,1},{1,0},{2,3},{3,2},{4,5},{5,4},{6,7},{7,6},{8,9},{9,8},{10,11... | collective-permute-start | bytes 196616 | tf_op jit(solution)/shard_map/ppermute | solution.py:35
  17.2 9.3 %collective-permute-start.4 = (bf16[512,128]{1,0:T(8,128)(2,1)S(1)}, bf16[512,128]{1,0:T(8,128)(2,1)S(1)}, u32[]{:S(2)}, u32[]{:S(2)}) collective-permute-start(bf16[512,128]{1,0:T(8,128)(2,1)S(1)} %add.27.refs_0_), channel_id=1, source_target_pairs={{0,2},{1,3},{2,0},{3,1},{4,6},{5,7},{6,4},{7,5},{8,10},{9,11},{10,... | collective-permute-start | bytes 393224 | tf_op jit(solution)/shard_map/ppermute | solution.py:35
  20.0 7.5 %collective-permute-start.6 = (bf16[512,128]{1,0:T(8,128)(2,1)S(1)}, bf16[512,128]{1,0:T(8,128)(2,1)S(1)}, u32[]{:S(2)}, u32[]{:S(2)}) collective-permute-start(bf16[512,128]{1,0:T(8,128)(2,1)S(1)} %get-tuple-element.60), channel_id=1, source_target_pairs={{0,1},{1,0},{2,3},{3,2},{4,5},{5,4},{6,7},{7,6},{8,9},{9,8},{10,11... | collective-permute-start | bytes 393224 | tf_op jit(solution)/shard_map/ppermute | solution.py:35
  21.7 7.6 %collective-permute-start.10 = (bf16[256,128]{1,0:T(8,128)(2,1)S(1)}, bf16[256,128]{1,0:T(8,128)(2,1)S(1)}, u32[]{:S(2)}, u32[]{:S(2)}) collective-permute-start(bf16[256,128]{1,0:T(8,128)(2,1)S(1)} %get-tuple-element.62), channel_id=1, source_target_pairs={{0,2},{1,3},{2,0},{3,1},{4,6},{5,7},{6,4},{7,5},{8,10},{9,11},{10,... | collective-permute-start | bytes 196616 | tf_op jit(solution)/shard_map/ppermute | solution.py:35
  22.3 7.0 %collective-permute-start.11 = (bf16[256,128]{1,0:T(8,128)(2,1)S(1)}, bf16[256,128]{1,0:T(8,128)(2,1)S(1)}, u32[]{:S(2)}, u32[]{:S(2)}) collective-permute-start(bf16[256,128]{1,0:T(8,128)(2,1)S(1)} %get-tuple-element.63), channel_id=1, source_target_pairs={{0,1},{1,0},{2,3},{3,2},{4,5},{5,4},{6,7},{7,6},{8,9},{9,8},{10,11... | collective-permute-start | bytes 196616 | tf_op jit(solution)/shard_map/ppermute | solution.py:35
  27.6 5.0 %collective-permute-start.8 = (bf16[512,128]{1,0:T(8,128)(2,1)S(1)}, bf16[512,128]{1,0:T(8,128)(2,1)S(1)}, u32[]{:S(2)}, u32[]{:S(2)}) collective-permute-start(bf16[512,128]{1,0:T(8,128)(2,1)S(1)} %first_filter.2.refs_0_.refs_1_), channel_id=1, source_target_pairs={{0,8},{4,12},{8,0},{12,4},{1,9},{5,13},{9,1},{13,5},{2,10},{6,14},... | collective-permute-start | bytes 393224 | tf_op jit(solution)/shard_map/ppermute | solution.py:35
  29.4 4.3 %collective-permute-start.13 = (bf16[256,128]{1,0:T(8,128)(2,1)S(1)}, bf16[256,128]{1,0:T(8,128)(2,1)S(1)}, u32[]{:S(2)}, u32[]{:S(2)}) collective-permute-start(bf16[256,128]{1,0:T(8,128)(2,1)S(1)} %first_filter.3.refs_4_.refs_5_), channel_id=1, source_target_pairs={{0,8},{4,12},{8,0},{12,4},{1,9},{5,13},{9,1},{13,5},{2,10},{6,14},... | collective-permute-start | bytes 196616 | tf_op jit(solution)/shard_map/ppermute | solution.py:35
  30.0 5.0 %collective-permute-start.7 = (bf16[512,128]{1,0:T(8,128)(2,1)S(1)}, bf16[512,128]{1,0:T(8,128)(2,1)S(1)}, u32[]{:S(2)}, u32[]{:S(2)}) collective-permute-start(bf16[512,128]{1,0:T(8,128)(2,1)S(1)} %first_filter.2.refs_0_.refs_1_), channel_id=1, source_target_pairs={{0,4},{4,0},{8,12},{12,8},{1,5},{5,1},{9,13},{13,9},{2,6},{6,2},{1... | collective-permute-start | bytes 393224 | tf_op jit(solution)/shard_map/ppermute | solution.py:35
  32.7 2.3 %collective-permute-start.9 = (bf16[512,128]{1,0:T(8,128)(2,1)S(1)}, bf16[512,128]{1,0:T(8,128)(2,1)S(1)}, u32[]{:S(2)}, u32[]{:S(2)}) collective-permute-start(bf16[512,128]{1,0:T(8,128)(2,1)S(1)} %collective-permute-done.8.refs_2_), channel_id=1, source_target_pairs={{0,4},{4,0},{8,12},{12,8},{1,5},{5,1},{9,13},{13,9},{2,6},{6,2},{1... | collective-permute-start | bytes 393224 | tf_op jit(solution)/shard_map/ppermute | solution.py:35
  32.7 1.4 %collective-permute-start.12 = (bf16[256,128]{1,0:T(8,128)(2,1)S(1)}, bf16[256,128]{1,0:T(8,128)(2,1)S(1)}, u32[]{:S(2)}, u32[]{:S(2)}) collective-permute-start(bf16[256,128]{1,0:T(8,128)(2,1)S(1)} %first_filter.3.refs_4_.refs_5_), channel_id=1, source_target_pairs={{0,4},{4,0},{8,12},{12,8},{1,5},{5,1},{9,13},{13,9},{2,6},{6,2},{1... | collective-permute-start | bytes 196616 | tf_op jit(solution)/shard_map/ppermute | solution.py:35
  33.7 1.3 %collective-permute-start.14 = (bf16[256,128]{1,0:T(8,128)(2,1)S(1)}, bf16[256,128]{1,0:T(8,128)(2,1)S(1)}, u32[]{:S(2)}, u32[]{:S(2)}) collective-permute-start(bf16[256,128]{1,0:T(8,128)(2,1)S(1)} %collective-permute-done.13.refs_6_), channel_id=1, source_target_pairs={{0,4},{4,0},{8,12},{12,8},{1,5},{5,1},{9,13},{13,9},{2,6},{6,2},{1... | collective-permute-start | bytes 196616 | tf_op jit(solution)/shard_map/ppermute | solution.py:35
  36.1 6.3 %collective-permute-start.15 = (bf16[512,128]{1,0:T(8,128)(2,1)S(1)}, bf16[512,128]{1,0:T(8,128)(2,1)S(1)}, u32[]{:S(2)}, u32[]{:S(2)}) collective-permute-start(bf16[512,128]{1,0:T(8,128)(2,1)S(1)} %get-tuple-element.66), channel_id=1, source_target_pairs={{0,1},{1,0},{2,3},{3,2},{4,5},{5,4},{6,7},{7,6},{8,9},{9,8},{10,11... | collective-permute-start | bytes 393224 | tf_op jit(solution)/shard_map/ppermute | solution.py:35
  36.8 7.4 %collective-permute-start.17 = (bf16[256,128]{1,0:T(8,128)(2,1)S(1)}, bf16[256,128]{1,0:T(8,128)(2,1)S(1)}, u32[]{:S(2)}, u32[]{:S(2)}) collective-permute-start(bf16[256,128]{1,0:T(8,128)(2,1)S(1)} %get-tuple-element.68), channel_id=1, source_target_pairs={{0,1},{1,0},{2,3},{3,2},{4,5},{5,4},{6,7},{7,6},{8,9},{9,8},{10,11... | collective-permute-start | bytes 196616 | tf_op jit(solution)/shard_map/ppermute | solution.py:35
  42.4 10.0 %collective-permute-start.16 = (bf16[512,128]{1,0:T(8,128)(2,1)S(1)}, bf16[512,128]{1,0:T(8,128)(2,1)S(1)}, u32[]{:S(2)}, u32[]{:S(2)}) collective-permute-start(bf16[512,128]{1,0:T(8,128)(2,1)S(1)} %add.29.refs_0_), channel_id=1, source_target_pairs={{0,2},{1,3},{2,0},{3,1},{4,6},{5,7},{6,4},{7,5},{8,10},{9,11},{10,... | collective-permute-start | bytes 393224 | tf_op jit(solution)/shard_map/ppermute | solution.py:35
  44.2 9.5 %collective-permute-start.18 = (bf16[512,128]{1,0:T(8,128)(2,1)S(1)}, bf16[512,128]{1,0:T(8,128)(2,1)S(1)}, u32[]{:S(2)}, u32[]{:S(2)}) collective-permute-start(bf16[512,128]{1,0:T(8,128)(2,1)S(1)} %get-tuple-element.71), channel_id=1, source_target_pairs={{0,1},{1,0},{2,3},{3,2},{4,5},{5,4},{6,7},{7,6},{8,9},{9,8},{10,11... | collective-permute-start | bytes 393224 | tf_op jit(solution)/shard_map/ppermute | solution.py:35
  46.2 6.2 %collective-permute-start.19 = (bf16[256,128]{1,0:T(8,128)(2,1)S(1)}, bf16[256,128]{1,0:T(8,128)(2,1)S(1)}, u32[]{:S(2)}, u32[]{:S(2)}) collective-permute-start(bf16[256,128]{1,0:T(8,128)(2,1)S(1)} %get-tuple-element.73), channel_id=1, source_target_pairs={{0,2},{1,3},{2,0},{3,1},{4,6},{5,7},{6,4},{7,5},{8,10},{9,11},{10,... | collective-permute-start | bytes 196616 | tf_op jit(solution)/shard_map/ppermute | solution.py:35
  46.8 6.8 %collective-permute-start.20 = (bf16[256,128]{1,0:T(8,128)(2,1)S(1)}, bf16[256,128]{1,0:T(8,128)(2,1)S(1)}, u32[]{:S(2)}, u32[]{:S(2)}) collective-permute-start(bf16[256,128]{1,0:T(8,128)(2,1)S(1)} %get-tuple-element.74), channel_id=1, source_target_pairs={{0,1},{1,0},{2,3},{3,2},{4,5},{5,4},{6,7},{7,6},{8,9},{9,8},{10,11... | collective-permute-start | bytes 196616 | tf_op jit(solution)/shard_map/ppermute | solution.py:35
  54.1 1.3 %collective-permute-start.21 = (f32[112,128]{1,0:T(8,128)S(1)}, f32[112,128]{1,0:T(8,128)S(1)}, u32[]{:S(2)}, u32[]{:S(2)}) collective-permute-start(f32[112,128]{1,0:T(8,128)S(1)} %get-tuple-element.76), channel_id=1, source_target_pairs={{0,4},{4,0},{8,12},{12,8},{1,5},{5,1},{9,13},{13,9},{2,6},{6,2},{1... | collective-permute-start | bytes 172040 | tf_op jit(solution)/shard_map/ppermute | solution.py:35
  55.5 4.2 %collective-permute-start.22 = (f32[112,128]{1,0:T(8,128)S(1)}, f32[112,128]{1,0:T(8,128)S(1)}, u32[]{:S(2)}, u32[]{:S(2)}) collective-permute-start(f32[112,128]{1,0:T(8,128)S(1)} %add.19), channel_id=1, source_target_pairs={{0,8},{4,12},{8,0},{12,4},{1,9},{5,13},{9,1},{13,5},{2,10},{6,14},... | collective-permute-start | bytes 172040 | tf_op jit(solution)/shard_map/ppermute | solution.py:35
  59.7 6.1 %collective-permute-start.25 = (f32[112,128]{1,0:T(8,128)S(1)}, f32[112,128]{1,0:T(8,128)S(1)}, u32[]{:S(2)}, u32[]{:S(2)}) collective-permute-start(f32[112,128]{1,0:T(8,128)S(1)} %add.20), channel_id=1, source_target_pairs={{0,3},{1,2},{2,1},{3,0},{4,7},{5,6},{6,5},{7,4},{8,11},{9,10},{10,... | collective-permute-start | bytes 172040 | tf_op jit(solution)/shard_map/ppermute | solution.py:35
  62.6 5.1 %collective-permute-start.24 = (f32[112,128]{1,0:T(8,128)S(1)}, f32[112,128]{1,0:T(8,128)S(1)}, u32[]{:S(2)}, u32[]{:S(2)}) collective-permute-start(f32[112,128]{1,0:T(8,128)S(1)} %add.20), channel_id=1, source_target_pairs={{0,2},{1,3},{2,0},{3,1},{4,6},{5,7},{6,4},{7,5},{8,10},{9,11},{10,... | collective-permute-start | bytes 172040 | tf_op jit(solution)/shard_map/ppermute | solution.py:35
  62.6 5.1 %collective-permute-start.23 = (f32[112,128]{1,0:T(8,128)S(1)}, f32[112,128]{1,0:T(8,128)S(1)}, u32[]{:S(2)}, u32[]{:S(2)}) collective-permute-start(f32[112,128]{1,0:T(8,128)S(1)} %add.20), channel_id=1, source_target_pairs={{0,1},{1,0},{2,3},{3,2},{4,5},{5,4},{6,7},{7,6},{8,9},{9,8},{10,11... | collective-permute-start | bytes 172040 | tf_op jit(solution)/shard_map/ppermute | solution.py:35
  67.7 2.0 %collective-permute-start.26 = (f32[112,128]{1,0:T(8,128)S(1)}, f32[112,128]{1,0:T(8,128)S(1)}, u32[]{:S(2)}, u32[]{:S(2)}) collective-permute-start(f32[112,128]{1,0:T(8,128)S(1)} %add_add_fusion.keep_ref), channel_id=1, source_target_pairs={{0,4},{4,0},{8,12},{12,8},{1,5},{5,1},{9,13},{13,9},{2,6},{6,2},{1... | collective-permute-start | bytes 172040 | tf_op jit(solution)/shard_map/ppermute | solution.py:35

commit v9 on v8

--- a/solution.py
+++ b/solution.py
@@ -10,7 +10,7 @@
 LANES = 128
 SIZE = LANES // 2
 GIGA = 10**9
-COSTS = ((3, 1, 3), (3, 0, 0))
+COSTS = ((3, 1, 3, 0, 1), (3, 0, 0, 1))
 F32 = jnp.float32
 BF16 = jnp.bfloat16
 VMEM = pl.BlockSpec(memory_space=pltpu.VMEM)
@@ -173,11 +173,15 @@
     wide, thin = swap(wide, "col", 1), swap(thin, "col", 1)
     across, near, own = product((2, 1, 0), own_blocks, at, ham, parts)
     (wide,) = add(across[0], wide)
-    thin, *near = add(across[1], thin, *near, after=[wide], flops=costs[0] * GIGA + 1000)
+    held = costs[3:]
+    thin, *late = add(
+        across[1], thin, *(near[i] for i in held), after=[wide], flops=costs[0] * GIGA + 1000
+    )
+    near = [late[held.index(i)] if i in held else near[i] for i in range(2)]
     near = [swap(x, "col", 1) for x in near]
     across = [swap(x, "col", 2) for x in (wide, thin)]
     sums = [
-        partial_sum(a, b, cost * GIGA + 1000) for a, b, cost in zip(own, across, costs[1:])
+        partial_sum(a, b, cost * GIGA + 1000) for a, b, cost in zip(own, across, costs[1:3])
     ]
     return list(zip(sums, near))
 

time: 75.7 us -> 75.7 us (level)
  transfers between devices with their start and end apart: 27 -> 27, of which waited for: 17 -> 16; matrix products, arithmetic and copies ran while one was open for 0% -> 0% of each run, Pallas kernels for 8% -> 8%
where the time goes in v9:
time: 75.7 us; the launch traced here: 75.4 us
  waiting for transfers between devices  29.4 us (39%)
  starting transfers between devices  27.1 us (36%)
  Pallas kernels  14.3 us (19%)
  local copies, waits for them, and re-layouts  3.02 us (4%)
  between operations  1.49 us (2%)
    ppermute x27, waiting for transfers between devices, swap(): return lax.ppermute(x, axis, [(i, i ^ key) for i in range(count)])  29.4 us
    ppermute x27, starting transfers between devices, swap(): return lax.ppermute(x, axis, [(i, i ^ key) for i in range(count)])  27.1 us
    pallas_call x1, Pallas kernels, per_device(): call(last_kernel, jax.ShapeDtypeStruct((LANES + SIZE, rows), F32), [VMEM]...  5.77 us
    pallas_call x4, Pallas kernels, product(): call(functools.partial(product_kernel, keys, n_row, own_blocks), [jax.Sha...  5.33 us
    unnamed x8, local copies, waits for them, and re-layouts  3.02 us
    pallas_call x1, Pallas kernels, per_device(): call(corner_kernel, jax.ShapeDtypeStruct((SIZE, SIZE), F32), [VMEM], flop...  1.88 us
  transfers between devices with their start and end apart: 27, of which 16 were waited for; matrix products, arithmetic and copies ran while one was open for 0% of the time, Pallas kernels for 8%

profile of v9, /device:TPU:0, one launch (start us, length us, event | category | flops | bytes accessed | tf_op | source)
XLA Modules:
  0.0 75.4 jit_solution(17175142375916693660)
XLA Ops:
  0.0 3.0 %collective-permute-start.1 = (bf16[192,512]{1,0:T(8,128)(2,1)}, bf16[192,512]{1,0:T(8,128)(2,1)S(1)}, u32[]{:S(2)}, u32[]{:S(2)}) collective-permute-start(bf16[192,512]{1,0:T(8,128)(2,1)} %bitcast.3), channel_id=1, source_target_pairs={{0,8},{4,12},{8,0},{12,4},{1,9},{5,13},{9,1},{13,5},{2,10},{6,14},... | collective-permute-start | bytes 589832 | tf_op jit(solution)/shard_map/ppermute | solution.py:35
  4.3 1.4 %copy-done = bf16[32,64,384]{2,1,0:T(8,128)(2,1)S(1)} copy-done((bf16[32,64,384]{2,1,0:T(8,128)(2,1)S(1)}, bf16[32,64,384]{2,1,0:T(8,128)(2,1)}, u32[]{:S(2)}) %copy-start) | copy-done | bytes 1572888
  5.7 0.9 %copy-done.2 = bf16[512,192]{0,1:T(8,128)(2,1)S(1)} copy-done((bf16[512,192]{0,1:T(8,128)(2,1)S(1)}, bf16[512,192]{0,1:T(8,128)(2,1)}, u32[]{:S(2)}) %copy-start.2) | copy-done | bytes 196632
  9.7 1.1 %product.5 = (bf16[512,128]{1,0:T(8,128)(2,1)S(1)}, bf16[256,128]{1,0:T(8,128)(2,1)S(1)}) custom-call(s32[6,32]{1,0:T(8,128)S(1)} %get-tuple-element.43.at_vmem, bf16[32,64,384]{2,1,0:T(8,128)(2,1)S(1)} %copy-done.1, bf16[512,128]{1,0:T(8,128)(2,1)S(1)} %get-tuple-element.42.refs_0_.start, bf16[512,128]{1,0:T(8,128)(2,1)S(1)} %get-tuple-element.45.refs_1_, ...), custom_call_target="tpu_custom_call" | custom-call | flops 100663296 | bytes 1000 | tf_op jit(solution)/shard_map/product/pallas_call | solution.py:127
  10.8 1.9 %collective-permute-start.3 = (bf16[512,128]{1,0:T(8,128)(2,1)S(1)}, bf16[512,128]{1,0:T(8,128)(2,1)S(1)}, u32[]{:S(2)}, u32[]{:S(2)}) collective-permute-start(bf16[512,128]{1,0:T(8,128)(2,1)S(1)} %get-tuple-element.54), channel_id=1, source_target_pairs={{0,1},{1,0},{2,3},{3,2},{4,5},{5,4},{6,7},{7,6},{8,9},{9,8},{10,11... | collective-permute-start | bytes 393224 | tf_op jit(solution)/shard_map/ppermute | solution.py:35
  12.9 1.6 %product.4 = (bf16[512,128]{1,0:T(8,128)(2,1)S(1)}, bf16[512,128]{1,0:T(8,128)(2,1)S(1)}, bf16[512,128]{1,0:T(8,128)(2,1)S(1)}, bf16[256,128]{1,0:T(8,128)(2,1)S...) custom-call(s32[6,32]{1,0:T(8,128)S(1)} %get-tuple-element.43.at_vmem, ...), custom_call_target="tpu_custom_call" | custom-call | flops 301989888 | bytes 1000 | tf_op jit(solution)/shard_map/product/pallas_call | solution.py:127
  14.4 2.7 %collective-permute-done.3.refs_1_ = bf16[512,128]{1,0:T(8,128)(2,1)S(1)} collective-permute-done((bf16[512,128]{1,0:T(8,128)(2,1)S(1)}, bf16[512,128]{1,0:T(8,128)(2,1)S(1)}, u32[]{:S(2)}, u32[]{:S(2)}) %collective-permute-start.3) | collective-permute-done | bytes 131104 | tf_op jit(solution)/shard_map/ppermute | solution.py:35
  17.2 2.8 %collective-permute-start.4 = (bf16[512,128]{1,0:T(8,128)(2,1)S(1)}, bf16[512,128]{1,0:T(8,128)(2,1)S(1)}, u32[]{:S(2)}, u32[]{:S(2)}) collective-permute-start(bf16[512,128]{1,0:T(8,128)(2,1)S(1)} %add.27.refs_0_), channel_id=1, source_target_pairs={{0,2},{1,3},{2,0},{3,1},{4,6},{5,7},{6,4},{7,5},{8,10},{9,11},{10,... | collective-permute-start | bytes 393224 | tf_op jit(solution)/shard_map/ppermute | solution.py:35
  20.0 1.6 %collective-permute-start.6 = (bf16[512,128]{1,0:T(8,128)(2,1)S(1)}, bf16[512,128]{1,0:T(8,128)(2,1)S(1)}, u32[]{:S(2)}, u32[]{:S(2)}) collective-permute-start(bf16[512,128]{1,0:T(8,128)(2,1)S(1)} %get-tuple-element.59), channel_id=1, source_target_pairs={{0,1},{1,0},{2,3},{3,2},{4,5},{5,4},{6,7},{7,6},{8,9},{9,8},{10,11... | collective-permute-start | bytes 393224 | tf_op jit(solution)/shard_map/ppermute | solution.py:35
  22.7 3.7 %collective-permute-done.4.b = bf16[512,128]{1,0:T(8,128)(2,1)S(1)} collective-permute-done((bf16[512,128]{1,0:T(8,128)(2,1)S(1)}, bf16[512,128]{1,0:T(8,128)(2,1)S(1)}, u32[]{:S(2)}, u32[]{:S(2)}) %collective-permute-start.4) | collective-permute-done | bytes 131104 | tf_op jit(solution)/shard_map/ppermute | solution.py:35
  26.5 1.1 %collective-permute-done.6.refs_1_ = bf16[512,128]{1,0:T(8,128)(2,1)S(1)} collective-permute-done((bf16[512,128]{1,0:T(8,128)(2,1)S(1)}, bf16[512,128]{1,0:T(8,128)(2,1)S(1)}, u32[]{:S(2)}, u32[]{:S(2)}) %collective-permute-start.6) | collective-permute-done | bytes 131104 | tf_op jit(solution)/shard_map/ppermute | solution.py:35
  27.6 1.6 %collective-permute-start.8 = (bf16[512,128]{1,0:T(8,128)(2,1)S(1)}, bf16[512,128]{1,0:T(8,128)(2,1)S(1)}, u32[]{:S(2)}, u32[]{:S(2)}) collective-permute-start(bf16[512,128]{1,0:T(8,128)(2,1)S(1)} %first_filter.2.refs_0_.refs_1_), channel_id=1, source_target_pairs={{0,8},{4,12},{8,0},{12,4},{1,9},{5,13},{9,1},{13,5},{2,10},{6,14},... | collective-permute-start | bytes 393224 | tf_op jit(solution)/shard_map/ppermute | solution.py:35
  30.0 2.7 %collective-permute-done.8.refs_2_ = bf16[512,128]{1,0:T(8,128)(2,1)S(1)} collective-permute-done((bf16[512,128]{1,0:T(8,128)(2,1)S(1)}, bf16[512,128]{1,0:T(8,128)(2,1)S(1)}, u32[]{:S(2)}, u32[]{:S(2)}) %collective-permute-start.8) | collective-permute-done | bytes 131104 | tf_op jit(solution)/shard_map/ppermute | solution.py:35
  34.1 0.8 %collective-permute-done.14.refs_7_ = bf16[256,128]{1,0:T(8,128)(2,1)S(1)} collective-permute-done((bf16[256,128]{1,0:T(8,128)(2,1)S(1)}, bf16[256,128]{1,0:T(8,128)(2,1)S(1)}, u32[]{:S(2)}, u32[]{:S(2)}) %collective-permute-start.14) | collective-permute-done | bytes 65568 | tf_op jit(solution)/shard_map/ppermute | solution.py:35
  34.9 1.1 %product.7 = (bf16[512,128]{1,0:T(8,128)(2,1)S(1)}, bf16[256,128]{1,0:T(8,128)(2,1)S(1)}) custom-call(s32[6,32]{1,0:T(8,128)S(1)} %get-tuple-element.43.at_vmem, bf16[32,64,384]{2,1,0:T(8,128)(2,1)S(1)} %copy-done.1, bf16[512,128]{1,0:T(8,128)(2,1)S(1)} %first_filter.2.refs_0_.refs_1_, bf16[512,128]{1,0:T(8,128)(2,1)S(1)} %collective-permute-done.7.refs_1_, ...), custom_call_target="tpu_custom_call" | custom-call | flops 100663296 | bytes 1000 | tf_op jit(solution)/shard_map/product/pallas_call | solution.py:127
  36.1 0.7 collective-permute-start.15
  36.8 1.4 %collective-permute-start.18 = (bf16[256,128]{1,0:T(8,128)(2,1)S(1)}, bf16[256,128]{1,0:T(8,128)(2,1)S(1)}, u32[]{:S(2)}, u32[]{:S(2)}) collective-permute-start(bf16[256,128]{1,0:T(8,128)(2,1)S(1)} %get-tuple-element.69), channel_id=1, source_target_pairs={{0,1},{1,0},{2,3},{3,2},{4,5},{5,4},{6,7},{7,6},{8,9},{9,8},{10,11... | collective-permute-start | bytes 196616 | tf_op jit(solution)/shard_map/ppermute | solution.py:35
  38.1 1.6 %product.6 = (bf16[512,128]{1,0:T(8,128)(2,1)S(1)}, bf16[512,128]{1,0:T(8,128)(2,1)S(1)}, bf16[512,128]{1,0:T(8,128)(2,1)S(1)}, bf16[256,128]{1,0:T(8,128)(2,1)S...) custom-call(s32[6,32]{1,0:T(8,128)S(1)} %get-tuple-element.43.at_vmem, ...), custom_call_target="tpu_custom_call" | custom-call | flops 301989888 | bytes 1000 | tf_op jit(solution)/shard_map/product/pallas_call | solution.py:127
  40.4 2.0 %collective-permute-done.15.refs_1_ = bf16[512,128]{1,0:T(8,128)(2,1)S(1)} collective-permute-done((bf16[512,128]{1,0:T(8,128)(2,1)S(1)}, bf16[512,128]{1,0:T(8,128)(2,1)S(1)}, u32[]{:S(2)}, u32[]{:S(2)}) %collective-permute-start.15) | collective-permute-done | bytes 131104 | tf_op jit(solution)/shard_map/ppermute | solution.py:35
  42.5 1.6 %collective-permute-start.16 = (bf16[512,128]{1,0:T(8,128)(2,1)S(1)}, bf16[512,128]{1,0:T(8,128)(2,1)S(1)}, u32[]{:S(2)}, u32[]{:S(2)}) collective-permute-start(bf16[512,128]{1,0:T(8,128)(2,1)S(1)} %add.29.refs_0_), channel_id=1, source_target_pairs={{0,2},{1,3},{2,0},{3,1},{4,6},{5,7},{6,4},{7,5},{8,10},{9,11},{10,... | collective-permute-start | bytes 393224 | tf_op jit(solution)/shard_map/ppermute | solution.py:35
  44.1 1.4 %collective-permute-start.19 = (bf16[256,128]{1,0:T(8,128)(2,1)S(1)}, bf16[256,128]{1,0:T(8,128)(2,1)S(1)}, u32[]{:S(2)}, u32[]{:S(2)}) collective-permute-start(bf16[256,128]{1,0:T(8,128)(2,1)S(1)} %get-tuple-element.71), channel_id=1, source_target_pairs={{0,2},{1,3},{2,0},{3,1},{4,6},{5,7},{6,4},{7,5},{8,10},{9,11},{10,... | collective-permute-start | bytes 196616 | tf_op jit(solution)/shard_map/ppermute | solution.py:35
  45.6 2.0 %collective-permute-start.20 = (bf16[256,128]{1,0:T(8,128)(2,1)S(1)}, bf16[256,128]{1,0:T(8,128)(2,1)S(1)}, u32[]{:S(2)}, u32[]{:S(2)}) collective-permute-start(bf16[256,128]{1,0:T(8,128)(2,1)S(1)} %get-tuple-element.72), channel_id=1, source_target_pairs={{0,1},{1,0},{2,3},{3,2},{4,5},{5,4},{6,7},{7,6},{8,9},{9,8},{10,11... | collective-permute-start | bytes 196616 | tf_op jit(solution)/shard_map/ppermute | solution.py:35
  47.6 6.1 %collective-permute-done.19.b = bf16[256,128]{1,0:T(8,128)(2,1)S(1)} collective-permute-done((bf16[256,128]{1,0:T(8,128)(2,1)S(1)}, bf16[256,128]{1,0:T(8,128)(2,1)S(1)}, u32[]{:S(2)}, u32[]{:S(2)}) %collective-permute-start.19) | collective-permute-done | bytes 65568 | tf_op jit(solution)/shard_map/ppermute | solution.py:35
  54.3 1.2 %collective-permute-done.21 = f32[112,128]{1,0:T(8,128)S(1)} collective-permute-done((f32[112,128]{1,0:T(8,128)S(1)}, f32[112,128]{1,0:T(8,128)S(1)}, u32[]{:S(2)}, u32[]{:S(2)}) %collective-permute-start.21) | collective-permute-done | bytes 57376 | tf_op jit(solution)/shard_map/ppermute | solution.py:35
  55.5 1.3 %collective-permute-start.22 = (f32[112,128]{1,0:T(8,128)S(1)}, f32[112,128]{1,0:T(8,128)S(1)}, u32[]{:S(2)}, u32[]{:S(2)}) collective-permute-start(f32[112,128]{1,0:T(8,128)S(1)} %add.19), channel_id=1, source_target_pairs={{0,8},{4,12},{8,0},{12,4},{1,9},{5,13},{9,1},{13,5},{2,10},{6,14},... | collective-permute-start | bytes 172040 | tf_op jit(solution)/shard_map/ppermute | solution.py:35
  56.9 2.9 %collective-permute-done.22 = f32[112,128]{1,0:T(8,128)S(1)} collective-permute-done((f32[112,128]{1,0:T(8,128)S(1)}, f32[112,128]{1,0:T(8,128)S(1)}, u32[]{:S(2)}, u32[]{:S(2)}) %collective-permute-start.22) | collective-permute-done | bytes 57376 | tf_op jit(solution)/shard_map/ppermute | solution.py:35
  59.8 2.5 %collective-permute-start.25 = (f32[112,128]{1,0:T(8,128)S(1)}, f32[112,128]{1,0:T(8,128)S(1)}, u32[]{:S(2)}, u32[]{:S(2)}) collective-permute-start(f32[112,128]{1,0:T(8,128)S(1)} %add.20), channel_id=1, source_target_pairs={{0,3},{1,2},{2,1},{3,0},{4,7},{5,6},{6,5},{7,4},{8,11},{9,10},{10,... | collective-permute-start | bytes 172040 | tf_op jit(solution)/shard_map/ppermute | solution.py:35
  62.3 1.9 %collective-permute-start.23 = (f32[112,128]{1,0:T(8,128)S(1)}, f32[112,128]{1,0:T(8,128)S(1)}, u32[]{:S(2)}, u32[]{:S(2)}) collective-permute-start(f32[112,128]{1,0:T(8,128)S(1)} %add.20), channel_id=1, source_target_pairs={{0,1},{1,0},{2,3},{3,2},{4,5},{5,4},{6,7},{7,6},{8,9},{9,8},{10,11... | collective-permute-start | bytes 172040 | tf_op jit(solution)/shard_map/ppermute | solution.py:35
  64.3 1.8 %collective-permute-done.25 = f32[112,128]{1,0:T(8,128)S(1)} collective-permute-done((f32[112,128]{1,0:T(8,128)S(1)}, f32[112,128]{1,0:T(8,128)S(1)}, u32[]{:S(2)}, u32[]{:S(2)}) %collective-permute-start.25) | collective-permute-done | bytes 57376 | tf_op jit(solution)/shard_map/ppermute | solution.py:35
  66.1 1.6 %collective-permute-done.24 = f32[112,128]{1,0:T(8,128)S(1)} collective-permute-done((f32[112,128]{1,0:T(8,128)S(1)}, f32[112,128]{1,0:T(8,128)S(1)}, u32[]{:S(2)}, u32[]{:S(2)}) %collective-permute-start.24) | collective-permute-done | bytes 57376 | tf_op jit(solution)/shard_map/ppermute | solution.py:35
  67.8 1.9 %corner.1.corner_ref = f32[64,64]{1,0:T(8,128)S(1)} custom-call(f32[112,128]{1,0:T(8,128)S(1)} %add_add_fusion.keep_ref), custom_call_target="tpu_custom_call" | custom-call | flops 1000000000 | bytes 1000 | tf_op jit(solution)/shard_map/corner/pallas_call | solution.py:418
  69.6 5.8 %orthonormalize.1 = f32[192,512]{1,0:T(8,128)} custom-call(f32[112,128]{1,0:T(8,128)S(1)} %add_add_fusion.keep_ref, f32[112,128]{1,0:T(8,128)S(1)} %collective-permute-done.26.other_ref, f32[64,64]{1,0:T(8,128)S(1)} %corner.1.corner_ref, bf16[512,128]{1,0:T(8,128)(2,1)S(1)} %get-tuple-element.75.wide_ref, bf16[256,128]{1,0:T(8,128)(2,1)S(1)} %get-tuple-element.76.thin_ref), custom_call_target="tpu_custom_call" | custom-call | flops 1000 | bytes 1000 | tf_op jit(solution)/shard_map/orthonormalize/pallas_call | solution.py:421
  (55 shorter events, 8.1 us)
Async XLA Ops:
  0.0 8.1 %collective-permute-start.1 = (bf16[192,512]{1,0:T(8,128)(2,1)}, bf16[192,512]{1,0:T(8,128)(2,1)S(1)}, u32[]{:S(2)}, u32[]{:S(2)}) collective-permute-start(bf16[192,512]{1,0:T(8,128)(2,1)} %bitcast.3), channel_id=1, source_target_pairs={{0,8},{4,12},{8,0},{12,4},{1,9},{5,13},{9,1},{13,5},{2,10},{6,14},... | collective-permute-start | bytes 589832 | tf_op jit(solution)/shard_map/ppermute | solution.py:35
  4.3 1.4 %copy-start = (bf16[32,64,384]{2,1,0:T(8,128)(2,1)S(1)}, bf16[32,64,384]{2,1,0:T(8,128)(2,1)}, u32[]{:S(2)}) copy-start(bf16[32,64,384]{2,1,0:T(8,128)(2,1)} %ham_ref.9) | copy-start | bytes 4718596
  5.7 0.9 %copy-start.2 = (bf16[512,192]{0,1:T(8,128)(2,1)S(1)}, bf16[512,192]{0,1:T(8,128)(2,1)}, u32[]{:S(2)}) copy-start(bf16[512,192]{0,1:T(8,128)(2,1)} %param.7) | copy-start | bytes 589828
  6.6 0.7 copy-start.3
  7.3 2.4 %copy-start.1 = (bf16[32,64,384]{2,1,0:T(8,128)(2,1)S(1)}, bf16[32,64,384]{2,1,0:T(8,128)(2,1)}, u32[]{:S(2)}) copy-start(bf16[32,64,384]{2,1,0:T(8,128)(2,1)} %ham_ref.9) | copy-start | bytes 4718596
  7.3 1.5 %collective-permute-start = (bf16[192,512]{1,0:T(8,128)(2,1)S(1)}, bf16[192,512]{1,0:T(8,128)(2,1)S(1)}, u32[]{:S(2)}, u32[]{:S(2)}) collective-permute-start(bf16[192,512]{1,0:T(8,128)(2,1)S(1)} %get-tuple-element.44), channel_id=1, source_target_pairs={{0,4},{4,0},{8,12},{12,8},{1,5},{5,1},{9,13},{13,9},{2,6},{6,2},{1... | collective-permute-start | bytes 589832 | tf_op jit(solution)/shard_map/ppermute | solution.py:35
  8.1 1.4 %collective-permute-start.2 = (bf16[192,512]{1,0:T(8,128)(2,1)S(1)}, bf16[192,512]{1,0:T(8,128)(2,1)S(1)}, u32[]{:S(2)}, u32[]{:S(2)}) collective-permute-start(bf16[192,512]{1,0:T(8,128)(2,1)S(1)} %collective-permute-done.1.turned_ref), channel_id=1, source_target_pairs={{0,4},{4,0},{8,12},{12,8},{1,5},{5,1},{9,13},{13,9},{2,6},{6,2},{1... | collective-permute-start | bytes 589832 | tf_op jit(solution)/shard_map/ppermute | solution.py:35
  10.8 6.4 %collective-permute-start.3 = (bf16[512,128]{1,0:T(8,128)(2,1)S(1)}, bf16[512,128]{1,0:T(8,128)(2,1)S(1)}, u32[]{:S(2)}, u32[]{:S(2)}) collective-permute-start(bf16[512,128]{1,0:T(8,128)(2,1)S(1)} %get-tuple-element.54), channel_id=1, source_target_pairs={{0,1},{1,0},{2,3},{3,2},{4,5},{5,4},{6,7},{7,6},{8,9},{9,8},{10,11... | collective-permute-start | bytes 393224 | tf_op jit(solution)/shard_map/ppermute | solution.py:35
  12.6 7.4 %collective-permute-start.5 = (bf16[256,128]{1,0:T(8,128)(2,1)S(1)}, bf16[256,128]{1,0:T(8,128)(2,1)S(1)}, u32[]{:S(2)}, u32[]{:S(2)}) collective-permute-start(bf16[256,128]{1,0:T(8,128)(2,1)S(1)} %get-tuple-element.56), channel_id=1, source_target_pairs={{0,1},{1,0},{2,3},{3,2},{4,5},{5,4},{6,7},{7,6},{8,9},{9,8},{10,11... | collective-permute-start | bytes 196616 | tf_op jit(solution)/shard_map/ppermute | solution.py:35
  17.2 9.3 %collective-permute-start.4 = (bf16[512,128]{1,0:T(8,128)(2,1)S(1)}, bf16[512,128]{1,0:T(8,128)(2,1)S(1)}, u32[]{:S(2)}, u32[]{:S(2)}) collective-permute-start(bf16[512,128]{1,0:T(8,128)(2,1)S(1)} %add.27.refs_0_), channel_id=1, source_target_pairs={{0,2},{1,3},{2,0},{3,1},{4,6},{5,7},{6,4},{7,5},{8,10},{9,11},{10,... | collective-permute-start | bytes 393224 | tf_op jit(solution)/shard_map/ppermute | solution.py:35
  20.0 7.5 %collective-permute-start.6 = (bf16[512,128]{1,0:T(8,128)(2,1)S(1)}, bf16[512,128]{1,0:T(8,128)(2,1)S(1)}, u32[]{:S(2)}, u32[]{:S(2)}) collective-permute-start(bf16[512,128]{1,0:T(8,128)(2,1)S(1)} %get-tuple-element.59), channel_id=1, source_target_pairs={{0,1},{1,0},{2,3},{3,2},{4,5},{5,4},{6,7},{7,6},{8,9},{9,8},{10,11... | collective-permute-start | bytes 393224 | tf_op jit(solution)/shard_map/ppermute | solution.py:35
  21.7 7.6 %collective-permute-start.10 = (bf16[256,128]{1,0:T(8,128)(2,1)S(1)}, bf16[256,128]{1,0:T(8,128)(2,1)S(1)}, u32[]{:S(2)}, u32[]{:S(2)}) collective-permute-start(bf16[256,128]{1,0:T(8,128)(2,1)S(1)} %get-tuple-element.61), channel_id=1, source_target_pairs={{0,2},{1,3},{2,0},{3,1},{4,6},{5,7},{6,4},{7,5},{8,10},{9,11},{10,... | collective-permute-start | bytes 196616 | tf_op jit(solution)/shard_map/ppermute | solution.py:35
  22.3 7.0 %collective-permute-start.11 = (bf16[256,128]{1,0:T(8,128)(2,1)S(1)}, bf16[256,128]{1,0:T(8,128)(2,1)S(1)}, u32[]{:S(2)}, u32[]{:S(2)}) collective-permute-start(bf16[256,128]{1,0:T(8,128)(2,1)S(1)} %get-tuple-element.62), channel_id=1, source_target_pairs={{0,1},{1,0},{2,3},{3,2},{4,5},{5,4},{6,7},{7,6},{8,9},{9,8},{10,11... | collective-permute-start | bytes 196616 | tf_op jit(solution)/shard_map/ppermute | solution.py:35
  27.6 5.0 %collective-permute-start.8 = (bf16[512,128]{1,0:T(8,128)(2,1)S(1)}, bf16[512,128]{1,0:T(8,128)(2,1)S(1)}, u32[]{:S(2)}, u32[]{:S(2)}) collective-permute-start(bf16[512,128]{1,0:T(8,128)(2,1)S(1)} %first_filter.2.refs_0_.refs_1_), channel_id=1, source_target_pairs={{0,8},{4,12},{8,0},{12,4},{1,9},{5,13},{9,1},{13,5},{2,10},{6,14},... | collective-permute-start | bytes 393224 | tf_op jit(solution)/shard_map/ppermute | solution.py:35
  29.4 4.3 %collective-permute-start.13 = (bf16[256,128]{1,0:T(8,128)(2,1)S(1)}, bf16[256,128]{1,0:T(8,128)(2,1)S(1)}, u32[]{:S(2)}, u32[]{:S(2)}) collective-permute-start(bf16[256,128]{1,0:T(8,128)(2,1)S(1)} %first_filter.3.refs_4_.refs_5_), channel_id=1, source_target_pairs={{0,8},{4,12},{8,0},{12,4},{1,9},{5,13},{9,1},{13,5},{2,10},{6,14},... | collective-permute-start | bytes 196616 | tf_op jit(solution)/shard_map/ppermute | solution.py:35
  30.0 5.0 %collective-permute-start.7 = (bf16[512,128]{1,0:T(8,128)(2,1)S(1)}, bf16[512,128]{1,0:T(8,128)(2,1)S(1)}, u32[]{:S(2)}, u32[]{:S(2)}) collective-permute-start(bf16[512,128]{1,0:T(8,128)(2,1)S(1)} %first_filter.2.refs_0_.refs_1_), channel_id=1, source_target_pairs={{0,4},{4,0},{8,12},{12,8},{1,5},{5,1},{9,13},{13,9},{2,6},{6,2},{1... | collective-permute-start | bytes 393224 | tf_op jit(solution)/shard_map/ppermute | solution.py:35
  32.7 2.3 %collective-permute-start.9 = (bf16[512,128]{1,0:T(8,128)(2,1)S(1)}, bf16[512,128]{1,0:T(8,128)(2,1)S(1)}, u32[]{:S(2)}, u32[]{:S(2)}) collective-permute-start(bf16[512,128]{1,0:T(8,128)(2,1)S(1)} %collective-permute-done.8.refs_2_), channel_id=1, source_target_pairs={{0,4},{4,0},{8,12},{12,8},{1,5},{5,1},{9,13},{13,9},{2,6},{6,2},{1... | collective-permute-start | bytes 393224 | tf_op jit(solution)/shard_map/ppermute | solution.py:35
  32.7 1.4 %collective-permute-start.12 = (bf16[256,128]{1,0:T(8,128)(2,1)S(1)}, bf16[256,128]{1,0:T(8,128)(2,1)S(1)}, u32[]{:S(2)}, u32[]{:S(2)}) collective-permute-start(bf16[256,128]{1,0:T(8,128)(2,1)S(1)} %first_filter.3.refs_4_.refs_5_), channel_id=1, source_target_pairs={{0,4},{4,0},{8,12},{12,8},{1,5},{5,1},{9,13},{13,9},{2,6},{6,2},{1... | collective-permute-start | bytes 196616 | tf_op jit(solution)/shard_map/ppermute | solution.py:35
  33.7 1.3 %collective-permute-start.14 = (bf16[256,128]{1,0:T(8,128)(2,1)S(1)}, bf16[256,128]{1,0:T(8,128)(2,1)S(1)}, u32[]{:S(2)}, u32[]{:S(2)}) collective-permute-start(bf16[256,128]{1,0:T(8,128)(2,1)S(1)} %collective-permute-done.13.refs_6_), channel_id=1, source_target_pairs={{0,4},{4,0},{8,12},{12,8},{1,5},{5,1},{9,13},{13,9},{2,6},{6,2},{1... | collective-permute-start | bytes 196616 | tf_op jit(solution)/shard_map/ppermute | solution.py:35
  36.1 6.4 %collective-permute-start.15 = (bf16[512,128]{1,0:T(8,128)(2,1)S(1)}, bf16[512,128]{1,0:T(8,128)(2,1)S(1)}, u32[]{:S(2)}, u32[]{:S(2)}) collective-permute-start(bf16[512,128]{1,0:T(8,128)(2,1)S(1)} %get-tuple-element.65), channel_id=1, source_target_pairs={{0,1},{1,0},{2,3},{3,2},{4,5},{5,4},{6,7},{7,6},{8,9},{9,8},{10,11... | collective-permute-start | bytes 393224 | tf_op jit(solution)/shard_map/ppermute | solution.py:35
  36.8 7.4 %collective-permute-start.18 = (bf16[256,128]{1,0:T(8,128)(2,1)S(1)}, bf16[256,128]{1,0:T(8,128)(2,1)S(1)}, u32[]{:S(2)}, u32[]{:S(2)}) collective-permute-start(bf16[256,128]{1,0:T(8,128)(2,1)S(1)} %get-tuple-element.69), channel_id=1, source_target_pairs={{0,1},{1,0},{2,3},{3,2},{4,5},{5,4},{6,7},{7,6},{8,9},{9,8},{10,11... | collective-permute-start | bytes 196616 | tf_op jit(solution)/shard_map/ppermute | solution.py:35
  39.7 14.0 %collective-permute-start.17 = (bf16[512,128]{1,0:T(8,128)(2,1)S(1)}, bf16[512,128]{1,0:T(8,128)(2,1)S(1)}, u32[]{:S(2)}, u32[]{:S(2)}) collective-permute-start(bf16[512,128]{1,0:T(8,128)(2,1)S(1)} %get-tuple-element.66), channel_id=1, source_target_pairs={{0,1},{1,0},{2,3},{3,2},{4,5},{5,4},{6,7},{7,6},{8,9},{9,8},{10,11... | collective-permute-start | bytes 393224 | tf_op jit(solution)/shard_map/ppermute | solution.py:35
  42.5 11.1 %collective-permute-start.16 = (bf16[512,128]{1,0:T(8,128)(2,1)S(1)}, bf16[512,128]{1,0:T(8,128)(2,1)S(1)}, u32[]{:S(2)}, u32[]{:S(2)}) collective-permute-start(bf16[512,128]{1,0:T(8,128)(2,1)S(1)} %add.29.refs_0_), channel_id=1, source_target_pairs={{0,2},{1,3},{2,0},{3,1},{4,6},{5,7},{6,4},{7,5},{8,10},{9,11},{10,... | collective-permute-start | bytes 393224 | tf_op jit(solution)/shard_map/ppermute | solution.py:35
  44.1 9.5 %collective-permute-start.19 = (bf16[256,128]{1,0:T(8,128)(2,1)S(1)}, bf16[256,128]{1,0:T(8,128)(2,1)S(1)}, u32[]{:S(2)}, u32[]{:S(2)}) collective-permute-start(bf16[256,128]{1,0:T(8,128)(2,1)S(1)} %get-tuple-element.71), channel_id=1, source_target_pairs={{0,2},{1,3},{2,0},{3,1},{4,6},{5,7},{6,4},{7,5},{8,10},{9,11},{10,... | collective-permute-start | bytes 196616 | tf_op jit(solution)/shard_map/ppermute | solution.py:35
  45.6 8.1 %collective-permute-start.20 = (bf16[256,128]{1,0:T(8,128)(2,1)S(1)}, bf16[256,128]{1,0:T(8,128)(2,1)S(1)}, u32[]{:S(2)}, u32[]{:S(2)}) collective-permute-start(bf16[256,128]{1,0:T(8,128)(2,1)S(1)} %get-tuple-element.72), channel_id=1, source_target_pairs={{0,1},{1,0},{2,3},{3,2},{4,5},{5,4},{6,7},{7,6},{8,9},{9,8},{10,11... | collective-permute-start | bytes 196616 | tf_op jit(solution)/shard_map/ppermute | solution.py:35
  54.2 1.3 %collective-permute-start.21 = (f32[112,128]{1,0:T(8,128)S(1)}, f32[112,128]{1,0:T(8,128)S(1)}, u32[]{:S(2)}, u32[]{:S(2)}) collective-permute-start(f32[112,128]{1,0:T(8,128)S(1)} %get-tuple-element.74), channel_id=1, source_target_pairs={{0,4},{4,0},{8,12},{12,8},{1,5},{5,1},{9,13},{13,9},{2,6},{6,2},{1... | collective-permute-start | bytes 172040 | tf_op jit(solution)/shard_map/ppermute | solution.py:35
  55.5 4.2 %collective-permute-start.22 = (f32[112,128]{1,0:T(8,128)S(1)}, f32[112,128]{1,0:T(8,128)S(1)}, u32[]{:S(2)}, u32[]{:S(2)}) collective-permute-start(f32[112,128]{1,0:T(8,128)S(1)} %add.19), channel_id=1, source_target_pairs={{0,8},{4,12},{8,0},{12,4},{1,9},{5,13},{9,1},{13,5},{2,10},{6,14},... | collective-permute-start | bytes 172040 | tf_op jit(solution)/shard_map/ppermute | solution.py:35
  59.8 6.3 %collective-permute-start.25 = (f32[112,128]{1,0:T(8,128)S(1)}, f32[112,128]{1,0:T(8,128)S(1)}, u32[]{:S(2)}, u32[]{:S(2)}) collective-permute-start(f32[112,128]{1,0:T(8,128)S(1)} %add.20), channel_id=1, source_target_pairs={{0,3},{1,2},{2,1},{3,0},{4,7},{5,6},{6,5},{7,4},{8,11},{9,10},{10,... | collective-permute-start | bytes 172040 | tf_op jit(solution)/shard_map/ppermute | solution.py:35
  62.3 5.3 %collective-permute-start.24 = (f32[112,128]{1,0:T(8,128)S(1)}, f32[112,128]{1,0:T(8,128)S(1)}, u32[]{:S(2)}, u32[]{:S(2)}) collective-permute-start(f32[112,128]{1,0:T(8,128)S(1)} %add.20), channel_id=1, source_target_pairs={{0,2},{1,3},{2,0},{3,1},{4,6},{5,7},{6,4},{7,5},{8,10},{9,11},{10,... | collective-permute-start | bytes 172040 | tf_op jit(solution)/shard_map/ppermute | solution.py:35
  62.3 5.3 %collective-permute-start.23 = (f32[112,128]{1,0:T(8,128)S(1)}, f32[112,128]{1,0:T(8,128)S(1)}, u32[]{:S(2)}, u32[]{:S(2)}) collective-permute-start(f32[112,128]{1,0:T(8,128)S(1)} %add.20), channel_id=1, source_target_pairs={{0,1},{1,0},{2,3},{3,2},{4,5},{5,4},{6,7},{7,6},{8,9},{9,8},{10,11... | collective-permute-start | bytes 172040 | tf_op jit(solution)/shard_map/ppermute | solution.py:35
  67.7 2.0 %collective-permute-start.26 = (f32[112,128]{1,0:T(8,128)S(1)}, f32[112,128]{1,0:T(8,128)S(1)}, u32[]{:S(2)}, u32[]{:S(2)}) collective-permute-start(f32[112,128]{1,0:T(8,128)S(1)} %add_add_fusion.keep_ref), channel_id=1, source_target_pairs={{0,4},{4,0},{8,12},{12,8},{1,5},{5,1},{9,13},{13,9},{2,6},{6,2},{1... | collective-permute-start | bytes 172040 | tf_op jit(solution)/shard_map/ppermute | solution.py:35
